TPU v7x, 128 devices: a whole 4x4x4 slice. The times are simulated.
128 devices in a mesh: dp: 4 (over z), fsdp: 32 (over x, y, core).
Axes of the slice: x: 4, y: 4, z: 4, core: 2. Of those that a mesh axis runs over, the one named last changes fastest.
Arguments:
- grads: bfloat16 [4, 2, 6144, 6144], P('dp', None, 'fsdp'), may hold values from -200 to 200, as said below
- errors: bfloat16 [4, 2, 6144, 6144], P('dp', None, 'fsdp'), may hold values from -3 to 3
- q_init: float32 [2, 6144, 8], replicated, may hold values from -6 to 6
Outputs:
- approx: bfloat16 [2, 6144, 6144], P(None, 'fsdp')
- errors_next: bfloat16 [4, 2, 6144, 6144], P('dp', None, 'fsdp')
- q_next: float32 [2, 6144, 8], replicated
Inputs may be any that keep to these rules, and one draw needn't show every extreme that they name: `grads`: gradients of one matrix differ from replica to replica.
All inputs are finite; a program needn't handle non-finite values.
Results may differ from a plain program's by a relative error of at most 0.0027.
Values sent between devices are 32-bit elements; how exact they have to be, the bound alone decides.
No kernel may reach another device: no remote copies, remote signals or barrier semaphores. Data moves between devices by JAX's collectives and lax.ppermute only.
A program may use at most 128 MiB of HBM per device.

v0:
```python
import jax
import jax.numpy as jnp
from jax import lax
from jax.sharding import PartitionSpec as P

ITERS = 2


def per_device(grads, errors, q_init):
    replicas = lax.axis_size("dp")
    working = grads[0].astype(jnp.float32) + errors[0].astype(jnp.float32)
    q_basis = q_init
    p_hat = None
    for iteration in range(ITERS):
        p_terms = jnp.einsum("mij,mjk->mik", working, q_basis, precision=lax.Precision.HIGHEST)
        p_basis = lax.psum(p_terms, "dp") / replicas
        gram_terms = jnp.einsum("mik,mil->mkl", p_basis, p_basis, precision=lax.Precision.HIGHEST)
        gram = lax.psum(gram_terms, "fsdp")
        lower_factor = jnp.linalg.cholesky(gram)
        solved = lax.linalg.triangular_solve(
            lower_factor, jnp.swapaxes(p_basis, 1, 2), left_side=True, lower=True
        )
        p_hat = jnp.swapaxes(solved, 1, 2)
        q_terms = jnp.einsum("mij,mik->mjk", working, p_hat, precision=lax.Precision.HIGHEST)
        q_basis = lax.psum(q_terms, ("dp", "fsdp")) / replicas
    full = jnp.einsum("mik,mjk->mij", p_hat, q_basis, precision=lax.Precision.HIGHEST)
    approx = full.astype(jnp.bfloat16)
    errors_next = (working - full)[None].astype(jnp.bfloat16)
    return (approx, errors_next, q_basis)


def solution(mesh):
    in_specs = (P("dp", None, "fsdp", None), P("dp", None, "fsdp", None), P())
    out_specs = (P(None, "fsdp", None), P("dp", None, "fsdp", None), P())
    return jax.shard_map(
        per_device, mesh=mesh, in_specs=in_specs, out_specs=out_specs, check_vma=False
    )
```

profile of v0, /device:TPU:1, one launch (start us, length us, event | category | flops | bytes accessed | tf_op | source)
XLA Modules:
  0.0 513.4 jit_solution(16314256231737076995)
XLA Ops:
  7.2 0.0 copy-start
  7.2 0.0 all-reduce.3.cloned.1.call-start
  7.3 0.9 copy-done
  8.2 10.2 %fusion.6 = f32[2,192,8]{1,2,0:T(8,128)S(1)} fusion(f32[2,6144,8]{1,2,0:T(8,128)S(1)} %copy-done, bf16[1,2,192,6144]{3,2,1,0:T(8,128)(2,1)} %param.7, bf16[1,2,192,6144]{3,2,1,0:T(8,128)(2,1)} %param.6), kind=kOutput, calls=%fused_computation.7 | convolution fusion | flops 233570304 | bytes 9842688 | tf_op jit(solution)/shard_map/mij,mjk->mik/dot_general | solution.py:15
  18.4 15.3 %psum.42 = f32[2,192,8]{1,2,0:T(8,128)S(1)} all-reduce(f32[2,192,8]{1,2,0:T(8,128)S(1)} %fusion.6), channel_id=1, replica_groups=mesh['dp'=4,'fsdp'=32] {'dp'}, use_global_device_ids=true, to_apply=%region_0.0 | all-reduce | flops 3072 | bytes 24576 | tf_op jit(solution)/shard_map/psum | solution.py:16
  33.6 0.1 fusion.20
  33.8 67.7 %psum.43 = f32[2,8,8]{1,2,0:T(8,128)S(1)} all-reduce(f32[2,8,8]{1,2,0:T(8,128)S(1)} %fusion.20), channel_id=1, replica_groups=mesh['dp'=4,'fsdp'=32] {'fsdp'}, use_global_device_ids=true, to_apply=%region_1.0 | all-reduce | flops 128 | bytes 1024 | tf_op jit(solution)/shard_map/psum | solution.py:18
  101.5 0.1 copy.15
  101.6 1.4 custom-call.8
  103.0 0.1 select_reduce_fusion.1
  103.0 0.1 compare_reduce_fusion.1
  103.2 0.1 select_bitcast_fusion.1
  103.2 1.3 custom-call.9
  104.5 0.2 fusion.14
  104.7 8.9 %fusion.4 = f32[2,6144,8]{1,2,0:T(8,128)} fusion(f32[2,8,192]{2,1,0:T(8,128)S(1)} %fusion.14, bf16[1,2,192,6144]{3,2,1,0:T(8,128)(2,1)} %param.7, bf16[1,2,192,6144]{3,2,1,0:T(8,128)(2,1)} %param.6), kind=kOutput, calls=%fused_computation.5 | convolution fusion | flops 233570304 | bytes 9842688 | tf_op jit(solution)/shard_map/mij,mik->mjk/dot_general | solution.py:24
  113.7 0.0 all-reduce.3.cloned.1.call-update
  113.7 0.0 all-reduce.5.cloned.1.call-start
  113.7 139.0 %all-reduce.3.cloned.1.call-done = f32[2,6144,8]{1,2,0:T(8,128)} async-done(((f32[2,6144,8]{1,2,0:T(8,128)}), f32[2,6144,8]{1,2,0:T(8,128)}) %all-reduce.3.cloned.1.call-update) | async-done | bytes 393232 | tf_op jit(solution)/shard_map/psum | solution.py:25
  252.7 10.2 %fusion.2 = f32[2,192,8]{1,2,0:T(8,128)S(1)} fusion(bf16[1,2,192,6144]{3,2,1,0:T(8,128)(2,1)} %param.7, bf16[1,2,192,6144]{3,2,1,0:T(8,128)(2,1)} %param.6, f32[2,6144,8]{1,2,0:T(8,128)} %all-reduce.3.cloned.1.call-done), kind=kOutput, calls=%fused_computation.3 | convolution fusion | flops 233668608 | bytes 9842688 | tf_op jit(solution)/shard_map/mij,mjk->mik/dot_general | solution.py:15
  262.9 12.6 %psum.45 = f32[2,192,8]{1,2,0:T(8,128)S(1)} all-reduce(f32[2,192,8]{1,2,0:T(8,128)S(1)} %fusion.2), channel_id=1, replica_groups=mesh['dp'=4,'fsdp'=32] {'dp'}, use_global_device_ids=true, to_apply=%region_5.8 | all-reduce | flops 3072 | bytes 24576 | tf_op jit(solution)/shard_map/psum | solution.py:16
  275.5 0.1 fusion.17
  275.7 66.6 %psum.46 = f32[2,8,8]{1,2,0:T(8,128)S(1)} all-reduce(f32[2,8,8]{1,2,0:T(8,128)S(1)} %fusion.17), channel_id=1, replica_groups=mesh['dp'=4,'fsdp'=32] {'fsdp'}, use_global_device_ids=true, to_apply=%region_6.9 | all-reduce | flops 128 | bytes 1024 | tf_op jit(solution)/shard_map/psum | solution.py:18
  342.2 0.1 copy.19
  342.3 1.4 custom-call.10
  343.7 0.1 select_reduce_fusion
  343.8 0.1 compare_reduce_fusion
  343.9 0.1 select_bitcast_fusion
  344.0 1.3 custom-call.11
  345.3 0.2 fusion.12
  345.5 8.9 %fusion = f32[2,6144,8]{1,2,0:T(8,128)} fusion(f32[2,8,192]{2,1,0:T(8,128)S(1)} %fusion.12, bf16[1,2,192,6144]{3,2,1,0:T(8,128)(2,1)} %param.7, bf16[1,2,192,6144]{3,2,1,0:T(8,128)(2,1)} %param.6), kind=kOutput, calls=%fused_computation.1 | convolution fusion | flops 233570304 | bytes 9842688 | tf_op jit(solution)/shard_map/mij,mik->mjk/dot_general | solution.py:24
  354.4 0.0 all-reduce.5.cloned.1.call-update
  354.5 138.4 %all-reduce.5.cloned.1.call-done = f32[2,6144,8]{1,2,0:T(8,128)} async-done(((f32[2,6144,8]{1,2,0:T(8,128)}), f32[2,6144,8]{1,2,0:T(8,128)}) %all-reduce.5.cloned.1.call-update) | async-done | bytes 393232 | tf_op jit(solution)/shard_map/psum | solution.py:25
  492.8 1.0 broadcast_multiply_fusion
  493.8 0.0 copy-start.1
  493.9 12.7 %fusion.9 = (bf16[1,2,192,6144]{3,2,1,0:T(8,128)(2,1)}, bf16[2,192,6144]{2,1,0:T(8,128)(2,1)}) fusion(bf16[1,2,192,6144]{3,2,1,0:T(8,128)(2,1)} %param.7, bf16[1,2,192,6144]{3,2,1,0:T(8,128)(2,1)} %param.6, f32[2,8,192]{2,1,0:T(8,128)S(1)} %fusion.12, f32[2,6144,8]{1,2,0:T(8,128)S(1)} %broadcast_multiply_fusion), kind=kOutput, calls=%fused_computation.11 | convolution fusion | flops 240648192 | bytes 19279872 | tf_op jit(solution)/shard_map/mik,mjk->mij/dot_general | solution.py:26
  506.6 0.0 copy-done.1
  (4 shorter events, 0.0 us)
Async XLA Ops:
  7.2 1.0 copy-start
  7.2 245.5 %all-reduce.3.cloned.1.call-start = ((), (), s32[]{:S(2)}) async-start(), calls=%async_computation | async-start | bytes 786432 | tf_op jit(solution)/shard_map/psum | solution.py:25
  113.7 379.1 %all-reduce.5.cloned.1.call-start = ((), (), s32[]{:S(2)}) async-start(), calls=%async_computation.1 | async-start | bytes 786432 | tf_op jit(solution)/shard_map/psum | solution.py:25
  493.8 12.7 %copy-start.1 = (f32[2,6144,8]{1,2,0:T(8,128)}, f32[2,6144,8]{1,2,0:T(8,128)S(1)}, u32[]{:S(2)}) copy-start(f32[2,6144,8]{1,2,0:T(8,128)S(1)} %broadcast_multiply_fusion) | copy-start | bytes 1179652
Sparse Core Ops, SparseCore 0:
  113.8 138.8 all-reduce.2
  354.6 138.2 all-reduce.4
where the time goes:
time: 514 us; the launch traced here: 513 us
  waiting for transfers between devices  277 us (54%)
  blocking collectives  162 us (32%)
  matrix products  51.7 us (10%)
  between operations  14.1 us (3%)
  other arithmetic  6.92 us (1%)
    psum x2, waiting for transfers between devices, per_device(): q_basis = lax.psum(q_terms, ('dp', 'fsdp')) / replicas  277 us
    psum x2, blocking collectives, per_device(): gram = lax.psum(gram_terms, 'fsdp')  134 us
    psum x2, blocking collectives, per_device(): p_basis = lax.psum(p_terms, 'dp') / replicas  27.9 us
    dot_general x2, matrix products, per_device(): jnp.einsum('mij,mjk->mik', working, q_basis, precision=lax.Precision.HIGH...  20.4 us
    dot_general x2, matrix products, per_device(): jnp.einsum('mij,mik->mjk', working, p_hat, precision=lax.Precision.HIGHEST)  17.9 us
    dot_general x1, matrix products, per_device(): jnp.einsum('mik,mjk->mij', p_hat, q_basis, precision=lax.Precision.HIGHEST)  12.7 us
  transfers between devices with their start and end apart: 2, of which 2 were waited for; matrix products, arithmetic and copies ran while one was open for 0% of the time, Pallas kernels for 0%

commit v1 on v0

v1 whole, which is shorter than its diff:
```python
import functools

import jax
import jax.numpy as jnp
from jax import lax
from jax.experimental import pallas as pl
from jax.experimental.pallas import tpu as pltpu
from jax.sharding import Mesh, PartitionSpec as P

F32, BF16 = jnp.float32, jnp.bfloat16
MATS, RANK, ROWS, COLS = 2, 8, 192, 6144
CHUNK = 1024
STEPS = COLS // CHUNK
TILES = CHUNK // 128
GRAM = MATS * COLS // 128
N_DEV, N_DP = 128, 4
VMEM = 48 * 1024 * 1024
ALL = ("dp", "x", "y", "core")


def split3(a):
    one = a.astype(BF16).astype(F32)
    rest = a - one
    two = rest.astype(BF16).astype(F32)
    return one, two, rest - two


def three(a):
    return jnp.concatenate(split3(a), axis=0).astype(BF16)


def fold(r):
    return r[0:8] + r[8:16] + r[16:24]


def small_dot(a, b):
    total = a[:, 0:1] * b[0:1, :]
    for k in range(1, RANK):
        total = total + a[:, k : k + 1] * b[k : k + 1, :]
    return total


def inverse_lower(gram):
    row = lax.broadcasted_iota(jnp.int32, (8, 128), 0)
    lane = lax.broadcasted_iota(jnp.int32, (8, 128), 1)
    a = jnp.where(lane < RANK, gram, jnp.where(lane == row + RANK, 1.0, 0.0).astype(F32))
    for k in range(RANK):
        pivot = a[k : k + 1, k : k + 1]
        inv = lax.rsqrt(pivot)
        inv = inv * (1.5 - 0.5 * pivot * inv * inv)
        top = a[k : k + 1, :] * inv
        below = a - (a[:, k : k + 1] * inv) * top
        a = jnp.where(row == k, top, jnp.where(row > k, below, a))
    return a[:, RANK : 2 * RANK]


def left_kernel(tiled, g_ref, e_ref, q_ref, *refs):
    if tiled:
        gram_ref, o_ref, acc = refs
    else:
        o_ref, acc = refs
    j = pl.program_id(0)

    @pl.when(j == 0)
    def _():
        acc[...] = jnp.zeros_like(acc)

    for m in range(MATS):
        if tiled:
            q = jnp.concatenate([q_ref[m * TILES + c] for c in range(TILES)], axis=1)
        else:
            q = q_ref[m]
        q = three(q)
        dims = (((1,), (1,)), ((), ()))
        r = lax.dot_general(q, g_ref[0, m], dims, preferred_element_type=F32)
        r = r + lax.dot_general(q, e_ref[0, m], dims, preferred_element_type=F32)
        acc[m] += r

    @pl.when(j == STEPS - 1)
    def _():
        for m in range(MATS):
            p = fold(acc[m])
            if tiled:
                lower_inv = inverse_lower(gram_ref[m])
                p = small_dot(lower_inv, p)
            o_ref[m * 8 : (m + 1) * 8, :] = p


def left(g, e, q, gram_from=None):
    tiled = gram_from is not None
    w_spec = pl.BlockSpec((1, MATS, ROWS, CHUNK), lambda j: (0, 0, 0, j))
    if tiled:
        specs = [w_spec, w_spec, pl.BlockSpec((MATS * TILES, 8, 128), lambda j: (j, 0, 0)),
                 pl.BlockSpec((MATS, 8, 128), lambda j: (GRAM // MATS, 0, 0))]
        args = (g, e, q, gram_from)
    else:
        specs = [w_spec, w_spec, pl.BlockSpec((MATS, RANK, CHUNK), lambda j: (0, 0, j))]
        args = (g, e, q)
    return pl.pallas_call(
        functools.partial(left_kernel, tiled),
        grid=(STEPS,),
        in_specs=specs,
        out_specs=pl.BlockSpec((16, ROWS), lambda j: (0, 0)),
        out_shape=jax.ShapeDtypeStruct((16, ROWS), F32),
        scratch_shapes=[pltpu.VMEM((MATS, 24, ROWS), F32)],
        compiler_params=pltpu.CompilerParams(vmem_limit_bytes=VMEM),
        name="left_factor",
    )(*args)


def right_kernel(p_ref, g_ref, e_ref, o_ref, psum_ref, p3):
    j = pl.program_id(0)

    @pl.when(j == 0)
    def _():
        p = (p_ref[0] + p_ref[1] + p_ref[2] + p_ref[3]) * (1.0 / N_DP)
        psum_ref[...] = p
        for m in range(MATS):
            p3[m] = three(p[m * 8 : (m + 1) * 8])

    @pl.when(j < STEPS)
    def _():
        for m in range(MATS):
            r = jnp.dot(p3[m], g_ref[0, m], preferred_element_type=F32)
            r = fold(r + jnp.dot(p3[m], e_ref[0, m], preferred_element_type=F32))
            for c in range(TILES):
                o_ref[m * TILES + c] = r[:, c * 128 : (c + 1) * 128]

    @pl.when(j >= STEPS)
    def _():
        o_ref[...] = jnp.zeros_like(o_ref)

    @pl.when(j == STEPS)
    def _():
        for m in range(MATS):
            p = psum_ref[m * 8 : (m + 1) * 8, :]
            gram = lax.dot_general(p, p, (((1,), (1,)), ((), ())), precision=lax.Precision.HIGHEST, preferred_element_type=F32)
            o_ref[m] = jnp.concatenate([gram, jnp.zeros((8, 120), F32)], axis=1)


def right(p_all, g, e):
    w_spec = pl.BlockSpec((1, MATS, ROWS, CHUNK), lambda j: (0, 0, 0, jnp.minimum(j, STEPS - 1)))
    return pl.pallas_call(
        right_kernel,
        grid=(N_DEV // (MATS * TILES),),
        in_specs=[pl.BlockSpec((N_DP, 16, ROWS), lambda j: (0, 0, 0)), w_spec, w_spec],
        out_specs=(pl.BlockSpec((MATS * TILES, 8, 128), lambda j: (j, 0, 0)), pl.BlockSpec((16, ROWS), lambda j: (0, 0))),
        out_shape=(jax.ShapeDtypeStruct((N_DEV, 8, 128), F32), jax.ShapeDtypeStruct((16, ROWS), F32)),
        scratch_shapes=[pltpu.VMEM((MATS, 24, ROWS), BF16)],
        compiler_params=pltpu.CompilerParams(vmem_limit_bytes=VMEM),
        name="right_factor",
    )(p_all, g, e)


def spread_kernel(t_ref, o_ref):
    total = jnp.sum(t_ref[...], axis=0, keepdims=True) * (1.0 / N_DP)
    o_ref[...] = jnp.broadcast_to(total, o_ref.shape)


def sum_everywhere(tiles):
    mine = lax.all_to_all(tiles, ALL, 0, 0)
    copies = pl.pallas_call(
        spread_kernel,
        out_shape=jax.ShapeDtypeStruct((N_DEV, 8, 128), F32),
        name="sum_tiles",
    )(mine)
    return lax.all_to_all(copies, ALL, 0, 0)


def final_kernel(g_ref, e_ref, z_ref, gram_ref, p_ref, a_ref, n_ref, q_ref, lower, p6):
    j = pl.program_id(0)

    @pl.when(j == 0)
    def _():
        for m in range(MATS):
            lower_inv = inverse_lower(gram_ref[m])
            lower[m] = jnp.concatenate([lower_inv, jnp.zeros((8, 120), F32)], axis=1)
            one, two, rest = split3(small_dot(lower_inv, p_ref[m * 8 : (m + 1) * 8, :]))
            pieces = jnp.concatenate([one, one, two, two, one, rest, jnp.zeros((80, ROWS), F32)], axis=0)
            pieces = jnp.concatenate([pieces, jnp.zeros((128, 64), F32)], axis=1)
            p6[m] = pieces.T.astype(BF16)

    for m in range(MATS):
        z = jnp.concatenate([z_ref[m * TILES + c] for c in range(TILES)], axis=1)
        q = small_dot(lower[m], z)
        q_ref[m] = q
        one, two, rest = split3(q)
        pieces = jnp.concatenate([one, two, one, two, rest, one], axis=0).astype(BF16)
        full = jnp.dot(p6[m, 0:ROWS, 0:48], pieces, preferred_element_type=F32)
        a_ref[m] = full.astype(BF16)
        n_ref[0, m] = (g_ref[0, m].astype(F32) + e_ref[0, m].astype(F32) - full).astype(BF16)


def final(g, e, z, p):
    w_spec = pl.BlockSpec((1, MATS, ROWS, CHUNK), lambda j: (0, 0, 0, j))
    return pl.pallas_call(
        final_kernel,
        grid=(STEPS,),
        in_specs=[w_spec, w_spec, pl.BlockSpec((MATS * TILES, 8, 128), lambda j: (j, 0, 0)),
                  pl.BlockSpec((MATS, 8, 128), lambda j: (GRAM // MATS, 0, 0)), pl.BlockSpec((16, ROWS), lambda j: (0, 0))],
        out_specs=(pl.BlockSpec((MATS, ROWS, CHUNK), lambda j: (0, 0, j)), w_spec,
                   pl.BlockSpec((MATS, RANK, CHUNK), lambda j: (0, 0, j))),
        out_shape=(jax.ShapeDtypeStruct((MATS, ROWS, COLS), BF16), jax.ShapeDtypeStruct((1, MATS, ROWS, COLS), BF16),
                   jax.ShapeDtypeStruct((MATS, RANK, COLS), F32)),
        scratch_shapes=[pltpu.VMEM((MATS, 8, 128), F32), pltpu.VMEM((MATS, 256, 128), BF16)],
        compiler_params=pltpu.CompilerParams(vmem_limit_bytes=VMEM),
        name="residual",
    )(g, e, z, z, p)


def everyones(p):
    return lax.all_to_all(jnp.broadcast_to(p[None], (N_DP,) + p.shape), "dp", 0, 0)


def per_device(grads, errors, q_init):
    p_own = left(grads, errors, jnp.swapaxes(q_init, 1, 2))
    tiles, _ = right(everyones(p_own), grads, errors)
    z = sum_everywhere(tiles)
    p_own = left(grads, errors, z, z)
    tiles, p = right(everyones(p_own), grads, errors)
    z = sum_everywhere(tiles)
    approx, errors_next, q_next = final(grads, errors, z, p)
    return approx, errors_next, jnp.swapaxes(q_next, 1, 2)


def solution(mesh):
    fine = Mesh(mesh.devices.reshape(4, 4, 4, 2), ALL)
    fsdp = ("x", "y", "core")
    in_specs = (P("dp", None, fsdp, None), P("dp", None, fsdp, None), P())
    out_specs = (P(None, fsdp, None), P("dp", None, fsdp, None), P())
    return jax.shard_map(per_device, mesh=fine, in_specs=in_specs, out_specs=out_specs, check_vma=False)
```

time: 514 us -> 143 us (0.28)
  waiting for transfers between devices: 277 us -> 0 us
  blocking collectives: 162 us -> 95.7 us
  matrix products: 51.7 us -> 0 us
  Pallas kernels: 0 us -> 37.6 us
  between operations: 14.1 us -> 0.68 us
  local copies, waits for them, and re-layouts: 1.07 us -> 8.01 us
  other arithmetic: 6.92 us -> 0 us
    psum x2 -> x0, waiting for transfers between devices: 277 us -> none  [per_device(): q_basis = lax.psum(q_terms, ('dp', 'fsdp')) / replicas]
    psum x4 -> x0, blocking collectives: 162 us -> none  [the longest x2 134 us: per_device(): gram = lax.psum(gram_terms, 'fsdp')]
    all_to_all x0 -> x6, blocking collectives: none -> 95.7 us  [the longest x2 42 us: sum_everywhere(): mine = lax.all_to_all(tiles, ALL, 0, 0)]
    dot_general x7 -> x0, matrix products: 51.3 us -> none  [the longest x2 20.4 us: per_device(): jnp.einsum('mij,mjk->mik', working, q_basis, precision=lax.Precision.HIGH...]
    pallas_call x0 -> x7, Pallas kernels: none -> 37.6 us  [the longest x2 13 us: left(): pl.pallas_call(functools.partial(left_kernel, tiled), grid=(STEPS,), in_s...]
    unnamed x4 -> x8, local copies, waits for them, and re-layouts: 0.93 us -> 8 us
    another operation x12 -> x0, other arithmetic: 5.89 us -> none  [the longest x7 3.22 us: per_device(): lower_factor = jnp.linalg.cholesky(gram)]
  transfers between devices with their start and end apart: 2 -> 0, of which waited for: 2 -> 0; matrix products, arithmetic and copies ran while one was open for 0% -> 0% of each run, Pallas kernels for 0% -> 0%
where the time goes in v1:
time: 143 us; the launch traced here: 142 us
  blocking collectives  95.7 us (67%)
  Pallas kernels  37.6 us (26%)
  local copies, waits for them, and re-layouts  8.01 us (6%)
    all_to_all x2, blocking collectives, sum_everywhere(): mine = lax.all_to_all(tiles, ALL, 0, 0)  42 us
    all_to_all x2, blocking collectives, sum_everywhere(): return lax.all_to_all(copies, ALL, 0, 0)  36.7 us
    all_to_all x2, blocking collectives, everyones(): lax.all_to_all(jnp.broadcast_to(p[None], (N_DP,) + p.shape), 'dp', 0, 0)  17 us
    pallas_call x2, Pallas kernels, left(): pl.pallas_call(functools.partial(left_kernel, tiled), grid=(STEPS,), in_s...  13 us
    pallas_call x2, Pallas kernels, right(): pl.pallas_call(right_kernel, grid=(N_DEV // (MATS * TILES),), in_specs=[p...  11.7 us
    pallas_call x1, Pallas kernels, final(): pl.pallas_call(final_kernel, grid=(STEPS,), in_specs=[w_spec, w_spec, pl....  8.94 us
    unnamed x8, local copies, waits for them, and re-layouts  8 us
    pallas_call x2, Pallas kernels, sum_everywhere(): pl.pallas_call(spread_kernel, out_shape=jax.ShapeDtypeStruct((N_DEV, 8, 1...  4.01 us

profile of v1, /device:TPU:1, one launch (start us, length us, event | category | flops | bytes accessed | tf_op | source)
XLA Modules:
  0.0 142.0 jit_solution(14878262624186690632)
XLA Ops:
  0.6 0.0 copy-start
  0.6 2.3 %copy-done = bf16[1,2,192,6144]{3,2,1,0:T(8,128)(2,1)S(1)} copy-done((bf16[1,2,192,6144]{3,2,1,0:T(8,128)(2,1)S(1)}, bf16[1,2,192,6144]{3,2,1,0:T(8,128)(2,1)}, u32[]{:S(2)}) %copy-start) | copy-done | bytes 4718616
  3.0 0.0 copy-start.3
  3.0 1.0 copy-done.3
  4.0 6.2 %left_factor.2 = f32[16,192]{1,0:T(8,128)S(1)} custom-call(bf16[1,2,192,6144]{3,2,1,0:T(8,128)(2,1)S(1)} %copy-done, bf16[1,2,192,6144]{3,2,1,0:T(8,128)(2,1)} %e_ref.9, f32[2,8,6144]{2,1,0:T(8,128)S(1)} %bitcast.2), custom_call_target="tpu_custom_call" | custom-call | tf_op jit(solution)/shard_map/left_factor/pallas_call | solution.py:99
  10.1 10.1 %all_to_all.30.p_ref = f32[4,16,192]{2,1,0:T(8,128)S(1)} all-to-all(f32[4,16,192]{2,1,0:T(8,128)S(1)} %broadcast_in_dim.4), channel_id=1, replica_groups=mesh['dp'=4,'x'=4,'y'=4,'core'=2] {'dp'}, dimensions={0} | all-to-all | bytes 98304 | tf_op jit(solution)/shard_map/all_to_all | solution.py:212
  20.3 6.1 %right_factor.2 = (f32[128,8,128]{2,1,0:T(8,128)S(1)}, f32[16,192]{1,0:T(8,128)}) custom-call(f32[4,16,192]{2,1,0:T(8,128)S(1)} %all_to_all.30.p_ref, bf16[1,2,192,6144]{3,2,1,0:T(8,128)(2,1)S(1)} %copy-done, bf16[1,2,192,6144]{3,2,1,0:T(8,128)(2,1)} %e_ref.9), custom_call_target="tpu_custom_call" | custom-call | tf_op jit(solution)/shard_map/right_factor/pallas_call | solution.py:143
  26.4 22.6 %all_to_all.31.t_ref = f32[128,8,128]{2,1,0:T(8,128)} all-to-all(f32[128,8,128]{2,1,0:T(8,128)S(1)} %get-tuple-element.9), channel_id=1, replica_groups=mesh['dp'=4,'x'=4,'y'=4,'core'=2] {'dp','x','y','core'}, dimensions={0} | all-to-all | bytes 1048576 | tf_op jit(solution)/shard_map/all_to_all | solution.py:161
  49.0 2.0 %sum_tiles.2 = f32[128,8,128]{2,1,0:T(8,128)} custom-call(f32[128,8,128]{2,1,0:T(8,128)} %all_to_all.31.t_ref), custom_call_target="tpu_custom_call" | custom-call | tf_op jit(solution)/shard_map/sum_tiles/pallas_call | solution.py:162
  51.1 18.4 %all_to_all.32.q_ref.refs_0_ = f32[128,8,128]{2,1,0:T(8,128)S(1)} all-to-all(f32[128,8,128]{2,1,0:T(8,128)} %sum_tiles.2), channel_id=1, replica_groups=mesh['dp'=4,'x'=4,'y'=4,'core'=2] {'dp','x','y','core'}, dimensions={0} | all-to-all | bytes 1048576 | tf_op jit(solution)/shard_map/all_to_all | solution.py:167
  69.4 0.0 copy-start.1
  69.4 2.3 %copy-done.1 = bf16[1,2,192,6144]{3,2,1,0:T(8,128)(2,1)S(1)} copy-done((bf16[1,2,192,6144]{3,2,1,0:T(8,128)(2,1)S(1)}, bf16[1,2,192,6144]{3,2,1,0:T(8,128)(2,1)}, u32[]{:S(2)}) %copy-start.1) | copy-done | bytes 4718616
  71.8 6.9 %left_factor.3 = f32[16,192]{1,0:T(8,128)S(1)} custom-call(bf16[1,2,192,6144]{3,2,1,0:T(8,128)(2,1)S(1)} %copy-done.1, bf16[1,2,192,6144]{3,2,1,0:T(8,128)(2,1)} %e_ref.9, f32[128,8,128]{2,1,0:T(8,128)S(1)} %all_to_all.32.q_ref.refs_0_, f32[128,8,128]{2,1,0:T(8,128)S(1)} %all_to_all.32.q_ref.refs_0_), custom_call_target="tpu_custom_call" | custom-call | tf_op jit(solution)/shard_map/left_factor/pallas_call | solution.py:99
  78.7 6.8 %all_to_all.33.p_ref = f32[4,16,192]{2,1,0:T(8,128)S(1)} all-to-all(f32[4,16,192]{2,1,0:T(8,128)S(1)} %broadcast_in_dim.5), channel_id=1, replica_groups=mesh['dp'=4,'x'=4,'y'=4,'core'=2] {'dp'}, dimensions={0} | all-to-all | bytes 98304 | tf_op jit(solution)/shard_map/all_to_all | solution.py:212
  85.5 5.5 %right_factor.3 = (f32[128,8,128]{2,1,0:T(8,128)S(1)}, f32[16,192]{1,0:T(8,128)S(1)}) custom-call(f32[4,16,192]{2,1,0:T(8,128)S(1)} %all_to_all.33.p_ref, bf16[1,2,192,6144]{3,2,1,0:T(8,128)(2,1)S(1)} %copy-done.1, bf16[1,2,192,6144]{3,2,1,0:T(8,128)(2,1)} %e_ref.9), custom_call_target="tpu_custom_call" | custom-call | tf_op jit(solution)/shard_map/right_factor/pallas_call | solution.py:143
  91.0 19.3 %all_to_all.34.t_ref = f32[128,8,128]{2,1,0:T(8,128)} all-to-all(f32[128,8,128]{2,1,0:T(8,128)S(1)} %get-tuple-element.10), channel_id=1, replica_groups=mesh['dp'=4,'x'=4,'y'=4,'core'=2] {'dp','x','y','core'}, dimensions={0} | all-to-all | bytes 1048576 | tf_op jit(solution)/shard_map/all_to_all | solution.py:161
  110.3 2.0 %sum_tiles.3 = f32[128,8,128]{2,1,0:T(8,128)} custom-call(f32[128,8,128]{2,1,0:T(8,128)} %all_to_all.34.t_ref), custom_call_target="tpu_custom_call" | custom-call | tf_op jit(solution)/shard_map/sum_tiles/pallas_call | solution.py:162
  112.3 18.4 %all_to_all.35.z_ref.gram_ref = f32[128,8,128]{2,1,0:T(8,128)S(1)} all-to-all(f32[128,8,128]{2,1,0:T(8,128)} %sum_tiles.3), channel_id=1, replica_groups=mesh['dp'=4,'x'=4,'y'=4,'core'=2] {'dp','x','y','core'}, dimensions={0} | all-to-all | bytes 1048576 | tf_op jit(solution)/shard_map/all_to_all | solution.py:167
  130.7 0.0 copy-start.2
  130.7 2.3 %copy-done.2 = bf16[1,2,192,6144]{3,2,1,0:T(8,128)(2,1)S(1)} copy-done((bf16[1,2,192,6144]{3,2,1,0:T(8,128)(2,1)S(1)}, bf16[1,2,192,6144]{3,2,1,0:T(8,128)(2,1)}, u32[]{:S(2)}) %copy-start.2) | copy-done | bytes 4718616
  133.0 8.9 %residual.1 = (bf16[2,192,6144]{2,1,0:T(8,128)(2,1)}, bf16[1,2,192,6144]{3,2,1,0:T(8,128)(2,1)}, f32[2,8,6144]{2,1,0:T(8,128)}) custom-call(bf16[1,2,192,6144]{3,2,1,0:T(8,128)(2,1)S(1)} %copy-done.2, bf16[1,2,192,6144]{3,2,1,0:T(8,128)(2,1)} %e_ref.9, f32[128,8,128]{2,1,0:T(8,128)S(1)} %all_to_all.35.z_ref.gram_ref, ...), custom_call_target="tpu_custom_call" | custom-call | tf_op jit(solution)/shard_map/residual/pallas_call | solution.py:196
  (2 shorter events, 0.0 us)
Async XLA Ops:
  0.6 2.3 %copy-start = (bf16[1,2,192,6144]{3,2,1,0:T(8,128)(2,1)S(1)}, bf16[1,2,192,6144]{3,2,1,0:T(8,128)(2,1)}, u32[]{:S(2)}) copy-start(bf16[1,2,192,6144]{3,2,1,0:T(8,128)(2,1)} %g_ref.9) | copy-start | bytes 14155780
  3.0 1.0 copy-start.3
  69.4 2.3 %copy-start.1 = (bf16[1,2,192,6144]{3,2,1,0:T(8,128)(2,1)S(1)}, bf16[1,2,192,6144]{3,2,1,0:T(8,128)(2,1)}, u32[]{:S(2)}) copy-start(bf16[1,2,192,6144]{3,2,1,0:T(8,128)(2,1)} %g_ref.9) | copy-start | bytes 14155780
  130.7 2.3 %copy-start.2 = (bf16[1,2,192,6144]{3,2,1,0:T(8,128)(2,1)S(1)}, bf16[1,2,192,6144]{3,2,1,0:T(8,128)(2,1)}, u32[]{:S(2)}) copy-start(bf16[1,2,192,6144]{3,2,1,0:T(8,128)(2,1)} %g_ref.9) | copy-start | bytes 14155780

commit v2 on v0

v2 whole, which is shorter than its diff:
```python
import functools

import jax
import jax.numpy as jnp
from jax import lax
from jax.experimental import pallas as pl
from jax.experimental.pallas import tpu as pltpu
from jax.sharding import Mesh, PartitionSpec as P

F32, BF16 = jnp.float32, jnp.bfloat16
MATS, RANK, ROWS, COLS = 2, 8, 192, 6144
CHUNK = 1024
STEPS = COLS // CHUNK
TILES = CHUNK // 128
N_DP, PLANE = 4, 16
DEEP = COLS // 128 * RANK // PLANE
NT = (((1,), (1,)), ((), ()))
IN_VMEM = pl.BlockSpec(memory_space=pltpu.VMEM)
IN_SMEM = pl.BlockSpec(memory_space=pltpu.SMEM)
ANYWHERE = pl.BlockSpec(memory_space=pl.ANY)


def vmem(a):
    return pltpu.with_memory_space_constraint(a, pltpu.VMEM)


def hbm(a):
    return pltpu.with_memory_space_constraint(a, pltpu.HBM)


def kernel(body, out_shape, in_specs, name, scratch=(), limit=16, flops=10**7):
    many = isinstance(out_shape, tuple)
    out_specs = tuple(ANYWHERE if isinstance(s, jax.ShapeDtypeStruct) else IN_VMEM for s in (out_shape if many else (out_shape,)))
    return pl.pallas_call(
        body,
        in_specs=in_specs,
        out_specs=out_specs if many else out_specs[0],
        out_shape=out_shape,
        scratch_shapes=list(scratch),
        compiler_params=pltpu.CompilerParams(vmem_limit_bytes=limit * 1024 * 1024),
        cost_estimate=pl.CostEstimate(flops=flops, bytes_accessed=10**6, transcendentals=0),
        name=name,
    )


def split3(a):
    one = a.astype(BF16).astype(F32)
    rest = a - one
    two = rest.astype(BF16).astype(F32)
    return one, two, rest - two


def three(a):
    return jnp.concatenate(split3(a), axis=0).astype(BF16)


def fold(r):
    return r[0:8] + r[8:16] + r[16:24]


def small_dot(a, b):
    total = a[:, 0:1] * b[0:1, :]
    for k in range(1, RANK):
        total = total + a[:, k : k + 1] * b[k : k + 1, :]
    return total


def inverse_lower(gram):
    row = lax.broadcasted_iota(jnp.int32, (8, 128), 0)
    lane = lax.broadcasted_iota(jnp.int32, (8, 128), 1)
    a = jnp.where(lane < RANK, gram, jnp.where(lane == row + RANK, 1.0, 0.0).astype(F32))
    for k in range(RANK):
        pivot = a[k : k + 1, k : k + 1]
        inv = lax.rsqrt(pivot)
        inv = inv * (1.5 - 0.5 * pivot * inv * inv)
        top = a[k : k + 1, :] * inv
        below = a - (a[:, k : k + 1] * inv) * top
        a = jnp.where(row == k, top, jnp.where(row > k, below, a))
    return jnp.concatenate([a[:, RANK : 2 * RANK], jnp.zeros((8, 120), F32)], axis=1)


def chunk_of(q_ref, c):
    tiles = range(c * TILES, (c + 1) * TILES)
    return jnp.concatenate([q_ref[t // 3, t % 3 * 8 : t % 3 * 8 + 8, :] for t in tiles], axis=1)


def cols(c):
    return slice(c * CHUNK, (c + 1) * CHUNK)


def first_left_kernel(core_ref, g_hbm, e_hbm, q_ref, p_ref, g_ref, e_ref, g_sem, e_sem):
    core = core_ref[0]
    copies = []
    for c in range(STEPS):
        s = pl.ds(c * CHUNK, CHUNK)
        copies.append((
            pltpu.make_async_copy(g_hbm.at[0, :, :, s], g_ref.at[:, :, s], g_sem.at[c]),
            pltpu.make_async_copy(e_hbm.at[0, :, :, s], e_ref.at[:, :, s], e_sem.at[c]),
        ))
        copies[-1][0].start()
        copies[-1][1].start()
    acc = [jnp.zeros((24, ROWS), F32)] * MATS
    for c in range(STEPS):
        q = [three(q_ref[m, :, cols(c)]) for m in range(MATS)]
        copies[c][0].wait()
        copies[c][1].wait()
        for m in range(MATS):
            r = lax.dot_general(q[m], g_ref[m, :, cols(c)], NT, preferred_element_type=F32)
            r = r + lax.dot_general(q[m], e_ref[m, :, cols(c)], NT, preferred_element_type=F32)
            acc[m] = acc[m] + r
    for m in range(MATS):
        place = pl.multiple_of((m + core) % 2 * 8, 8)
        p_ref[pl.ds(place, 8), :] = fold(acc[m])


def first_left(core, grads, errors, q):
    wide = pltpu.VMEM((MATS, ROWS, COLS), BF16)
    return kernel(
        first_left_kernel, (pltpu.VMEM((16, ROWS), F32), wide, wide), [IN_SMEM, ANYWHERE, ANYWHERE, IN_VMEM], "first_left",
        [pltpu.SemaphoreType.DMA((STEPS,)), pltpu.SemaphoreType.DMA((STEPS,))],
    )(core, hbm(grads), hbm(errors), vmem(q))


def left_kernel(slot, core_ref, q_ref, g_ref, e_ref, *refs):
    p_ref = refs[-1]
    m = (core_ref[0] + slot) % 2
    acc = jnp.zeros((24, ROWS), F32)
    for c in range(STEPS):
        q = three(chunk_of(q_ref, c))
        acc = acc + lax.dot_general(q, g_ref[m, :, cols(c)], NT, preferred_element_type=F32)
        acc = acc + lax.dot_general(q, e_ref[m, :, cols(c)], NT, preferred_element_type=F32)
    if slot == 0:
        p_ref[...] = fold(acc)
    else:
        p_ref[0:8, :] = refs[0][...]
        p_ref[8:16, :] = fold(acc)


def left(core, q_own, q_other, g, e):
    own = kernel(functools.partial(left_kernel, 0), pltpu.VMEM((8, ROWS), F32), [IN_SMEM] + [IN_VMEM] * 3, "left_own", flops=10**9)(
        core, vmem(q_own), vmem(g), vmem(e))
    return kernel(functools.partial(left_kernel, 1), pltpu.VMEM((16, ROWS), F32), [IN_SMEM] + [IN_VMEM] * 4, "left_other")(
        core, vmem(q_other), vmem(g), vmem(e), vmem(own))


def right_kernel(slot, core_ref, p0, p1, p2, p3, g_ref, e_ref, o_ref, mean_ref):
    m = (core_ref[0] + slot) % 2
    mean_ref[...] = (p0[...] + p1[...] + p2[...] + p3[...]) * (1.0 / N_DP)
    p = mean_ref[slot * 8 : slot * 8 + 8, :]
    pieces = three(p)
    gram = lax.dot_general(p, p, NT, precision=lax.Precision.HIGHEST, preferred_element_type=F32)
    gram = jnp.concatenate([gram, jnp.zeros((8, 120), F32)], axis=1)
    for k in range(PLANE):
        o_ref[k, DEEP : DEEP + 8, :] = gram
    for c in range(STEPS):
        r = jnp.dot(pieces, g_ref[m, :, cols(c)], preferred_element_type=F32)
        r = fold(r + jnp.dot(pieces, e_ref[m, :, cols(c)], preferred_element_type=F32))
        for i in range(TILES):
            t = c * TILES + i
            o_ref[t // 3, t % 3 * 8 : t % 3 * 8 + 8, :] = r[:, i * 128 : (i + 1) * 128]


def right(slot, core, p_all, g, e):
    return kernel(
        functools.partial(right_kernel, slot), (pltpu.VMEM((PLANE, DEEP + 8, 128), F32), pltpu.VMEM((16, ROWS), F32)),
        [IN_SMEM] + [IN_VMEM] * 6, "right_own" if slot == 0 else "right_other", flops=10**9,
    )(core, *map(vmem, p_all), vmem(g), vmem(e))


def plane_sum_kernel(t_ref, z_ref, gram_ref):
    total = jnp.sum(t_ref[...], axis=0)
    z_ref[...] = total[0:DEEP]
    gram_ref[...] = total[DEEP : DEEP + 8]


def plane_sum(t):
    return kernel(plane_sum_kernel, (pltpu.VMEM((DEEP, 128), F32), pltpu.VMEM((8, 128), F32)), [IN_VMEM], "plane_sum")(vmem(t))


def lower_kernel(gram_ref, o_ref):
    o_ref[...] = inverse_lower(gram_ref[...])


def lower_inverse(gram):
    return kernel(lower_kernel, pltpu.VMEM((8, 128), F32), [IN_VMEM], "lower_inverse", flops=10**9)(vmem(gram))


def spread_kernel(z0, z1, z2, z3, lower_ref, o_ref):
    total = (z0[...] + z1[...] + z2[...] + z3[...]) * (1.0 / N_DP)
    lower = lower_ref[...]
    q = jnp.concatenate([small_dot(lower, total[i * 8 : i * 8 + 8]) for i in range(DEEP // 8)], axis=0)
    o_ref[...] = jnp.broadcast_to(q[None], o_ref.shape)


def spread(z_all, lower):
    return kernel(spread_kernel, pltpu.VMEM((PLANE, DEEP, 128), F32), [IN_VMEM] * 5, "spread")(*map(vmem, z_all), vmem(lower))


def final_kernel(core_ref, lower_own, lower_other, q_own, q_other, p_ref, g_ref, e_ref, a_hbm, n_hbm, q_hbm,
                 p6, a_buf, n_buf, q_buf, a_sem, n_sem, q_sem):
    copies = []
    for slot, (lower_ref, q_ref) in enumerate(((lower_own, q_own), (lower_other, q_other))):
        m = (core_ref[0] + slot) % 2
        one, two, rest = split3(small_dot(lower_ref[...], p_ref[slot * 8 : slot * 8 + 8, :]))
        pieces = jnp.concatenate([one, one, two, two, one, rest, jnp.zeros((80, ROWS), F32)], axis=0)
        pieces = jnp.concatenate([pieces, jnp.zeros((128, 64), F32)], axis=1)
        p6[slot] = pieces.T.astype(BF16)
        left_pieces = p6[slot, 0:ROWS, 0:48]
        for c in range(STEPS):
            q = chunk_of(q_ref, c)
            q_buf[slot, :, cols(c)] = q
            one, two, rest = split3(q)
            pieces = jnp.concatenate([one, two, one, two, rest, one], axis=0).astype(BF16)
            full = jnp.dot(left_pieces, pieces, preferred_element_type=F32)
            a_buf[slot, :, cols(c)] = full.astype(BF16)
            n_buf[slot, :, cols(c)] = (g_ref[m, :, cols(c)].astype(F32) + e_ref[m, :, cols(c)].astype(F32) - full).astype(BF16)
            s = pl.ds(c * CHUNK, CHUNK)
            i = slot * STEPS + c
            copies.append(pltpu.make_async_copy(a_buf.at[slot, :, s], a_hbm.at[m, :, s], a_sem.at[i]))
            copies.append(pltpu.make_async_copy(n_buf.at[slot, :, s], n_hbm.at[0, m, :, s], n_sem.at[i]))
            copies[-2].start()
            copies[-1].start()
        copies.append(pltpu.make_async_copy(q_buf.at[slot], q_hbm.at[m], q_sem.at[slot]))
        copies[-1].start()
    for copy in copies:
        copy.wait()


def final(core, lower_own, lower_other, q_own, q_other, p, g, e):
    n = MATS * STEPS
    return kernel(
        final_kernel,
        (jax.ShapeDtypeStruct((MATS, ROWS, COLS), BF16), jax.ShapeDtypeStruct((1, MATS, ROWS, COLS), BF16),
         jax.ShapeDtypeStruct((MATS, RANK, COLS), F32)),
        [IN_SMEM] + [IN_VMEM] * 7, "residual",
        [pltpu.VMEM((MATS, 256, 128), BF16), pltpu.VMEM((MATS, ROWS, COLS), BF16), pltpu.VMEM((MATS, ROWS, COLS), BF16),
         pltpu.VMEM((MATS, RANK, COLS), F32), pltpu.SemaphoreType.DMA((n,)), pltpu.SemaphoreType.DMA((n,)),
         pltpu.SemaphoreType.DMA((MATS,))],
        limit=24,
    )(core, *map(vmem, (lower_own, lower_other, q_own, q_other, p, g, e)))


def swap(a, axis, n, k):
    return lax.ppermute(a, axis, [(i, i ^ k) for i in range(n)])


def everyones(a):
    return (a,) + tuple(swap(a, "dp", N_DP, k) for k in (1, 2, 3))


def right_sum(core, p_own, g, e):
    p_all = everyones(p_own)
    theirs, _ = right(1, core, p_all, g, e)
    arrived = swap(theirs, "core", 2, 1)
    mine, p = right(0, core, p_all, g, e)
    z, gram = plane_sum(lax.all_to_all(mine + arrived, ("x", "y"), 0, 0))
    z_all = everyones(z)
    lower = lower_inverse(gram)
    return lax.all_to_all(spread(z_all, lower), ("x", "y"), 0, 0), lower, p


def per_device(grads, errors, q_init):
    core = lax.axis_index("core").astype(jnp.int32).reshape(1)
    p_own, g, e = first_left(core, grads, errors, jnp.swapaxes(q_init, 1, 2))
    q_own, _, _ = right_sum(core, p_own, g, e)
    p_own = left(core, q_own, swap(q_own, "core", 2, 1), g, e)
    q_own, lower, p = right_sum(core, p_own, g, e)
    lower_other = swap(lower, "core", 2, 1)
    approx, errors_next, q_next = final(core, lower, lower_other, q_own, swap(q_own, "core", 2, 1), p, g, e)
    return approx, errors_next, jnp.swapaxes(q_next, 1, 2)


def solution(mesh):
    fine = Mesh(mesh.devices.reshape(4, 4, 4, 2), ("dp", "x", "y", "core"))
    fsdp = ("x", "y", "core")
    in_specs = (P("dp", None, fsdp, None), P("dp", None, fsdp, None), P())
    out_specs = (P(None, fsdp, None), P("dp", None, fsdp, None), P())
    return jax.shard_map(per_device, mesh=fine, in_specs=in_specs, out_specs=out_specs, check_vma=False)
```

time: 514 us -> 104 us (0.20)
  waiting for transfers between devices: 277 us -> 9.2 us
  blocking collectives: 162 us -> 46.1 us
  matrix products: 51.7 us -> 0 us
  starting transfers between devices: 0.08 us -> 27.3 us
  Pallas kernels: 0 us -> 19.6 us
  between operations: 14.1 us -> 0.73 us
  other arithmetic: 6.92 us -> 0.07 us
    psum x2 -> x0, waiting for transfers between devices: 277 us -> none  [per_device(): q_basis = lax.psum(q_terms, ('dp', 'fsdp')) / replicas]
    psum x4 -> x0, blocking collectives: 162 us -> none  [the longest x2 134 us: per_device(): gram = lax.psum(gram_terms, 'fsdp')]
    dot_general x7 -> x0, matrix products: 51.3 us -> none  [the longest x2 20.4 us: per_device(): jnp.einsum('mij,mjk->mik', working, q_basis, precision=lax.Precision.HIGH...]
    all_to_all x0 -> x4, blocking collectives: none -> 46.1 us  [the longest x2 25.1 us: right_sum(): z, gram = plane_sum(lax.all_to_all(mine + arrived, ('x', 'y'), 0, 0))]
    ppermute x0 -> x17, starting transfers between devices: none -> 27.3 us  [swap(): return lax.ppermute(a, axis, [(i, i ^ k) for i in range(n)])]
    pallas_call x0 -> x14, Pallas kernels: none -> 19.6 us  [the longest x4 5.35 us: right(): kernel(functools.partial(right_kernel, slot), (pltpu.VMEM((PLANE, DEEP +...]
    ppermute x0 -> x17, waiting for transfers between devices: none -> 9.2 us  [swap(): return lax.ppermute(a, axis, [(i, i ^ k) for i in range(n)])]
    another operation x12 -> x0, other arithmetic: 5.89 us -> none  [the longest x7 3.22 us: per_device(): lower_factor = jnp.linalg.cholesky(gram)]
  transfers between devices with their start and end apart: 2 -> 17, of which waited for: 2 -> 8; matrix products, arithmetic and copies ran while one was open for 0% -> 0% of each run, Pallas kernels for 0% -> 5%
where the time goes in v2:
time: 104 us
  blocking collectives  46.1 us (44%)
  starting transfers between devices  27.3 us (26%)
  Pallas kernels  19.6 us (19%)
  waiting for transfers between devices  9.2 us (9%)
    ppermute x17, starting transfers between devices, swap(): return lax.ppermute(a, axis, [(i, i ^ k) for i in range(n)])  27.3 us
    all_to_all x2, blocking collectives, right_sum(): z, gram = plane_sum(lax.all_to_all(mine + arrived, ('x', 'y'), 0, 0))  25.1 us
    all_to_all x2, blocking collectives, right_sum(): return (lax.all_to_all(spread(z_all, lower), ('x', 'y'), 0, 0), lower, p)  21.1 us
    ppermute x17, waiting for transfers between devices, swap(): return lax.ppermute(a, axis, [(i, i ^ k) for i in range(n)])  9.2 us
    pallas_call x4, Pallas kernels, right(): kernel(functools.partial(right_kernel, slot), (pltpu.VMEM((PLANE, DEEP +...  5.35 us
    pallas_call x1, Pallas kernels, first_left(): kernel(first_left_kernel, (pltpu.VMEM((16, ROWS), F32), wide, wide), [IN_...  5.14 us
    pallas_call x1, Pallas kernels, final(): kernel(final_kernel, (jax.ShapeDtypeStruct((MATS, ROWS, COLS), BF16), jax...  4.35 us
  transfers between devices with their start and end apart: 17, of which 8 were waited for; matrix products, arithmetic and copies ran while one was open for 0% of the time, Pallas kernels for 5%

profile of v2, /device:TPU:1, one launch (start us, length us, event | category | flops | bytes accessed | tf_op | source)
XLA Modules:
  0.0 104.0 jit_solution(11654021537333831098)
XLA Ops:
  0.6 1.0 copy-done
  1.6 5.1 %first_left.1 = (f32[16,192]{1,0:T(8,128)S(1)}, bf16[2,192,6144]{2,1,0:T(8,128)(2,1)S(1)}, bf16[2,192,6144]{2,1,0:T(8,128)(2,1)S(1)}) custom-call(s32[1]{0:T(128)} %bitcast.core_ref, bf16[1,2,192,6144]{3,2,1,0:T(8,128)(2,1)} %g_hbm.1, bf16[1,2,192,6144]{3,2,1,0:T(8,128)(2,1)} %e_hbm.1, f32[2,8,6144]{2,1,0:T(8,128)S(1)} %bitcast.3), custom_call_target="tpu_custom_call" | custom-call | flops 10000000 | bytes 1000000 | tf_op jit(solution)/shard_map/first_left/pallas_call | solution.py:118
  6.8 4.7 %collective-permute-start.2 = (f32[16,192]{1,0:T(8,128)S(1)}, f32[16,192]{1,0:T(8,128)S(1)}, u32[]{:S(2)}, u32[]{:S(2)}) collective-permute-start(f32[16,192]{1,0:T(8,128)S(1)} %get-tuple-element.18.p0), channel_id=1, source_target_pairs={{0,96},{32,64},{64,32},{96,0},{1,97},{33,65},{65,33},{97,1},{2,98}... | collective-permute-start | bytes 36872 | tf_op jit(solution)/shard_map/ppermute | solution.py:244
  11.4 0.0 collective-permute-start.1
  11.4 0.7 collective-permute-start
  12.1 0.5 collective-permute-done.2.p3
  12.6 3.0 %collective-permute-done.1.p2 = f32[16,192]{1,0:T(8,128)S(1)} collective-permute-done((f32[16,192]{1,0:T(8,128)S(1)}, f32[16,192]{1,0:T(8,128)S(1)}, u32[]{:S(2)}, u32[]{:S(2)}) %collective-permute-start.1) | collective-permute-done | bytes 12320 | tf_op jit(solution)/shard_map/ppermute | solution.py:244
  15.5 0.0 collective-permute-done.p1
  15.5 1.5 %right_other.2 = (f32[16,32,128]{2,1,0:T(8,128)S(1)}, f32[16,192]{1,0:T(8,128)}) custom-call(s32[1]{0:T(128)} %bitcast.core_ref, f32[16,192]{1,0:T(8,128)S(1)} %get-tuple-element.18.p0, f32[16,192]{1,0:T(8,128)S(1)} %collective-permute-done.p1, f32[16,192]{1,0:T(8,128)S(1)} %collective-permute-done.1.p2, f32[16,192]{1,0:T(8,128)S(1)} %collective-permute-done.2.p3, ...), custom_call_target="tpu_custom_call" | custom-call | flops 1000000000 | bytes 1000000 | tf_op jit(solution)/shard_map/right_other/pallas_call | solution.py:164
  17.0 2.1 %collective-permute-start.3 = (f32[16,32,128]{2,1,0:T(8,128)S(1)}, f32[16,32,128]{2,1,0:T(8,128)S(1)}, u32[]{:S(2)}, u32[]{:S(2)}) collective-permute-start(f32[16,32,128]{2,1,0:T(8,128)S(1)} %get-tuple-element.22), channel_id=1, source_target_pairs={{0,1},{1,0},{2,3},{3,2},{4,5},{5,4},{6,7},{7,6},{8,9},{9,8},{10,11... | collective-permute-start | bytes 786440 | tf_op jit(solution)/shard_map/ppermute | solution.py:244
  19.1 1.5 %right_own.2 = (f32[16,32,128]{2,1,0:T(8,128)S(1)}, f32[16,192]{1,0:T(8,128)}) custom-call(s32[1]{0:T(128)} %bitcast.core_ref, f32[16,192]{1,0:T(8,128)S(1)} %get-tuple-element.18.p0, f32[16,192]{1,0:T(8,128)S(1)} %collective-permute-done.p1, f32[16,192]{1,0:T(8,128)S(1)} %collective-permute-done.1.p2, f32[16,192]{1,0:T(8,128)S(1)} %collective-permute-done.2.p3, ...), custom_call_target="tpu_custom_call" | custom-call | flops 1000000000 | bytes 1000000 | tf_op jit(solution)/shard_map/right_own/pallas_call | solution.py:164
  20.6 0.0 collective-permute-done.3
  20.6 14.3 %all_to_all.20.t_ref = f32[16,32,128]{2,1,0:T(8,128)S(1)} all-to-all(f32[16,32,128]{2,1,0:T(8,128)S(1)} %add.6), channel_id=1, replica_groups=mesh['dp'=4,'x'=4,'y'=4,'core'=2] {'x','y'}, dimensions={0} | all-to-all | bytes 524288 | tf_op jit(solution)/shard_map/all_to_all | solution.py:256
  34.9 0.8 collective-permute-start.6
  35.7 1.2 %collective-permute-start.5 = (f32[24,128]{1,0:T(8,128)S(1)}, f32[24,128]{1,0:T(8,128)S(1)}, u32[]{:S(2)}, u32[]{:S(2)}) collective-permute-start(f32[24,128]{1,0:T(8,128)S(1)} %get-tuple-element.23.z0), channel_id=1, source_target_pairs={{0,64},{32,96},{64,0},{96,32},{1,65},{33,97},{65,1},{97,33},{2,66}... | collective-permute-start | bytes 36872 | tf_op jit(solution)/shard_map/ppermute | solution.py:244
  36.8 1.4 %collective-permute-start.4 = (f32[24,128]{1,0:T(8,128)S(1)}, f32[24,128]{1,0:T(8,128)S(1)}, u32[]{:S(2)}, u32[]{:S(2)}) collective-permute-start(f32[24,128]{1,0:T(8,128)S(1)} %get-tuple-element.23.z0), channel_id=1, source_target_pairs={{0,32},{32,0},{64,96},{96,64},{1,33},{33,1},{65,97},{97,65},{2,34}... | collective-permute-start | bytes 36872 | tf_op jit(solution)/shard_map/ppermute | solution.py:244
  38.2 0.7 lower_inverse.2.lower_ref
  38.9 0.0 collective-permute-done.6.z3
  38.9 0.8 collective-permute-done.5.z2
  39.7 0.0 collective-permute-done.4.z1
  39.7 0.1 spread.2
  39.8 10.6 %all_to_all.21.q_ref = f32[16,24,128]{2,1,0:T(8,128)S(1)} all-to-all(f32[16,24,128]{2,1,0:T(8,128)S(1)} %spread.2), channel_id=1, replica_groups=mesh['dp'=4,'x'=4,'y'=4,'core'=2] {'x','y'}, dimensions={0} | all-to-all | bytes 393216 | tf_op jit(solution)/shard_map/all_to_all | solution.py:259
  50.4 4.0 %collective-permute-start.7 = (f32[16,24,128]{2,1,0:T(8,128)S(1)}, f32[16,24,128]{2,1,0:T(8,128)S(1)}, u32[]{:S(2)}, u32[]{:S(2)}) collective-permute-start(f32[16,24,128]{2,1,0:T(8,128)S(1)} %all_to_all.21.q_ref), channel_id=1, source_target_pairs={{0,1},{1,0},{2,3},{3,2},{4,5},{5,4},{6,7},{7,6},{8,9},{9,8},{10,11... | collective-permute-start | bytes 589832 | tf_op jit(solution)/shard_map/ppermute | solution.py:244
  54.5 1.6 %left_own.1.refs_0_ = f32[8,192]{1,0:T(8,128)S(1)} custom-call(s32[1]{0:T(128)} %bitcast.core_ref, f32[16,24,128]{2,1,0:T(8,128)S(1)} %all_to_all.21.q_ref, bf16[2,192,6144]{2,1,0:T(8,128)(2,1)S(1)} %get-tuple-element.19.g_ref, bf16[2,192,6144]{2,1,0:T(8,128)(2,1)S(1)} %get-tuple-element.20.e_ref), custom_call_target="tpu_custom_call" | custom-call | flops 1000000000 | bytes 1000000 | tf_op jit(solution)/shard_map/left_own/pallas_call | solution.py:140
  56.1 1.6 %left_other.1.p0 = f32[16,192]{1,0:T(8,128)S(1)} custom-call(s32[1]{0:T(128)} %bitcast.core_ref, f32[16,24,128]{2,1,0:T(8,128)S(1)} %collective-permute-done.7.q_ref, bf16[2,192,6144]{2,1,0:T(8,128)(2,1)S(1)} %get-tuple-element.19.g_ref, bf16[2,192,6144]{2,1,0:T(8,128)(2,1)S(1)} %get-tuple-element.20.e_ref, f32[8,192]{1,0:T(8,128)S(1)} %left_own.1.refs_0_), custom_call_target="tpu_custom_call" | custom-call | flops 10000000 | bytes 1000000 | tf_op jit(solution)/shard_map/left_other/pallas_call | solution.py:142
  57.7 2.1 %collective-permute-start.10 = (f32[16,192]{1,0:T(8,128)S(1)}, f32[16,192]{1,0:T(8,128)S(1)}, u32[]{:S(2)}, u32[]{:S(2)}) collective-permute-start(f32[16,192]{1,0:T(8,128)S(1)} %left_other.1.p0), channel_id=1, source_target_pairs={{0,96},{32,64},{64,32},{96,0},{1,97},{33,65},{65,33},{97,1},{2,98}... | collective-permute-start | bytes 36872 | tf_op jit(solution)/shard_map/ppermute | solution.py:244
  59.7 1.1 %collective-permute-start.9 = (f32[16,192]{1,0:T(8,128)S(1)}, f32[16,192]{1,0:T(8,128)S(1)}, u32[]{:S(2)}, u32[]{:S(2)}) collective-permute-start(f32[16,192]{1,0:T(8,128)S(1)} %left_other.1.p0), channel_id=1, source_target_pairs={{0,64},{32,96},{64,0},{96,32},{1,65},{33,97},{65,1},{97,33},{2,66}... | collective-permute-start | bytes 36872 | tf_op jit(solution)/shard_map/ppermute | solution.py:244
  60.9 0.1 collective-permute-start.8
  61.0 0.5 collective-permute-done.10.p3
  61.5 2.3 %collective-permute-done.9.p2 = f32[16,192]{1,0:T(8,128)S(1)} collective-permute-done((f32[16,192]{1,0:T(8,128)S(1)}, f32[16,192]{1,0:T(8,128)S(1)}, u32[]{:S(2)}, u32[]{:S(2)}) %collective-permute-start.9) | collective-permute-done | bytes 12320 | tf_op jit(solution)/shard_map/ppermute | solution.py:244
  63.8 0.0 collective-permute-done.8.p1
  63.8 1.5 %right_other.3 = (f32[16,32,128]{2,1,0:T(8,128)S(1)}, f32[16,192]{1,0:T(8,128)}) custom-call(s32[1]{0:T(128)} %bitcast.core_ref, f32[16,192]{1,0:T(8,128)S(1)} %left_other.1.p0, f32[16,192]{1,0:T(8,128)S(1)} %collective-permute-done.8.p1, f32[16,192]{1,0:T(8,128)S(1)} %collective-permute-done.9.p2, f32[16,192]{1,0:T(8,128)S(1)} %collective-permute-done.10.p3, ...), custom_call_target="tpu_custom_call" | custom-call | flops 1000000000 | bytes 1000000 | tf_op jit(solution)/shard_map/right_other/pallas_call | solution.py:164
  65.3 1.4 %collective-permute-start.11 = (f32[16,32,128]{2,1,0:T(8,128)S(1)}, f32[16,32,128]{2,1,0:T(8,128)S(1)}, u32[]{:S(2)}, u32[]{:S(2)}) collective-permute-start(f32[16,32,128]{2,1,0:T(8,128)S(1)} %get-tuple-element.26), channel_id=1, source_target_pairs={{0,1},{1,0},{2,3},{3,2},{4,5},{5,4},{6,7},{7,6},{8,9},{9,8},{10,11... | collective-permute-start | bytes 786440 | tf_op jit(solution)/shard_map/ppermute | solution.py:244
  66.7 1.0 right_own.3
  67.7 0.2 collective-permute-done.11
  67.9 10.8 %all_to_all.22.t_ref = f32[16,32,128]{2,1,0:T(8,128)S(1)} all-to-all(f32[16,32,128]{2,1,0:T(8,128)S(1)} %add.7), channel_id=1, replica_groups=mesh['dp'=4,'x'=4,'y'=4,'core'=2] {'x','y'}, dimensions={0} | all-to-all | bytes 524288 | tf_op jit(solution)/shard_map/all_to_all | solution.py:256
  78.8 0.8 collective-permute-start.15
  79.5 1.2 %collective-permute-start.14 = (f32[24,128]{1,0:T(8,128)S(1)}, f32[24,128]{1,0:T(8,128)S(1)}, u32[]{:S(2)}, u32[]{:S(2)}) collective-permute-start(f32[24,128]{1,0:T(8,128)S(1)} %get-tuple-element.28.z0), channel_id=1, source_target_pairs={{0,64},{32,96},{64,0},{96,32},{1,65},{33,97},{65,1},{97,33},{2,66}... | collective-permute-start | bytes 36872 | tf_op jit(solution)/shard_map/ppermute | solution.py:244
  80.7 1.4 %collective-permute-start.13 = (f32[24,128]{1,0:T(8,128)S(1)}, f32[24,128]{1,0:T(8,128)S(1)}, u32[]{:S(2)}, u32[]{:S(2)}) collective-permute-start(f32[24,128]{1,0:T(8,128)S(1)} %get-tuple-element.28.z0), channel_id=1, source_target_pairs={{0,32},{32,0},{64,96},{96,64},{1,33},{33,1},{65,97},{97,65},{2,34}... | collective-permute-start | bytes 36872 | tf_op jit(solution)/shard_map/ppermute | solution.py:244
  82.1 0.7 lower_inverse.3.lower_ref.lower_own
  82.8 0.8 collective-permute-done.14.z2
  83.6 0.1 spread.3
  83.7 10.5 %all_to_all.23.q_own = f32[16,24,128]{2,1,0:T(8,128)S(1)} all-to-all(f32[16,24,128]{2,1,0:T(8,128)S(1)} %spread.3), channel_id=1, replica_groups=mesh['dp'=4,'x'=4,'y'=4,'core'=2] {'x','y'}, dimensions={0} | all-to-all | bytes 393216 | tf_op jit(solution)/shard_map/all_to_all | solution.py:259
  94.1 4.4 %collective-permute-start.16 = (f32[16,24,128]{2,1,0:T(8,128)S(1)}, f32[16,24,128]{2,1,0:T(8,128)S(1)}, u32[]{:S(2)}, u32[]{:S(2)}) collective-permute-start(f32[16,24,128]{2,1,0:T(8,128)S(1)} %all_to_all.23.q_own), channel_id=1, source_target_pairs={{0,1},{1,0},{2,3},{3,2},{4,5},{5,4},{6,7},{7,6},{8,9},{9,8},{10,11... | collective-permute-start | bytes 589832 | tf_op jit(solution)/shard_map/ppermute | solution.py:244
  98.5 0.0 collective-permute-start.12
  98.5 1.2 %collective-permute-done.12.lower_other = f32[8,128]{1,0:T(8,128)S(1)} collective-permute-done((f32[8,128]{1,0:T(8,128)S(1)}, f32[8,128]{1,0:T(8,128)S(1)}, u32[]{:S(2)}, u32[]{:S(2)}) %collective-permute-start.12) | collective-permute-done | bytes 4128 | tf_op jit(solution)/shard_map/ppermute | solution.py:244
  99.7 0.0 collective-permute-done.16.q_other
  99.7 4.3 %residual.1 = (bf16[2,192,6144]{2,1,0:T(8,128)(2,1)}, bf16[1,2,192,6144]{3,2,1,0:T(8,128)(2,1)}, f32[2,8,6144]{2,1,0:T(8,128)}) custom-call(s32[1]{0:T(128)} %bitcast.core_ref, f32[8,128]{1,0:T(8,128)S(1)} %lower_inverse.3.lower_ref.lower_own, f32[8,128]{1,0:T(8,128)S(1)} %collective-permute-done.12.lower_other, f32[16,24,128]{2,1,0:T(8,128)S(1)} %all_to_all.23.q_own, ...), custom_call_target="tpu_custom_call" | custom-call | flops 10000000 | bytes 1000000 | tf_op jit(solution)/shard_map/residual/pallas_call | solution.py:231
  (8 shorter events, 0.1 us)
Async XLA Ops:
  0.6 1.0 copy-start
  6.8 5.8 %collective-permute-start.2 = (f32[16,192]{1,0:T(8,128)S(1)}, f32[16,192]{1,0:T(8,128)S(1)}, u32[]{:S(2)}, u32[]{:S(2)}) collective-permute-start(f32[16,192]{1,0:T(8,128)S(1)} %get-tuple-element.18.p0), channel_id=1, source_target_pairs={{0,96},{32,64},{64,32},{96,0},{1,97},{33,65},{65,33},{97,1},{2,98}... | collective-permute-start | bytes 36872 | tf_op jit(solution)/shard_map/ppermute | solution.py:244
  11.4 4.1 %collective-permute-start.1 = (f32[16,192]{1,0:T(8,128)S(1)}, f32[16,192]{1,0:T(8,128)S(1)}, u32[]{:S(2)}, u32[]{:S(2)}) collective-permute-start(f32[16,192]{1,0:T(8,128)S(1)} %get-tuple-element.18.p0), channel_id=1, source_target_pairs={{0,64},{32,96},{64,0},{96,32},{1,65},{33,97},{65,1},{97,33},{2,66}... | collective-permute-start | bytes 36872 | tf_op jit(solution)/shard_map/ppermute | solution.py:244
  11.4 4.1 %collective-permute-start = (f32[16,192]{1,0:T(8,128)S(1)}, f32[16,192]{1,0:T(8,128)S(1)}, u32[]{:S(2)}, u32[]{:S(2)}) collective-permute-start(f32[16,192]{1,0:T(8,128)S(1)} %get-tuple-element.18.p0), channel_id=1, source_target_pairs={{0,32},{32,0},{64,96},{96,64},{1,33},{33,1},{65,97},{97,65},{2,34}... | collective-permute-start | bytes 36872 | tf_op jit(solution)/shard_map/ppermute | solution.py:244
  17.0 3.6 %collective-permute-start.3 = (f32[16,32,128]{2,1,0:T(8,128)S(1)}, f32[16,32,128]{2,1,0:T(8,128)S(1)}, u32[]{:S(2)}, u32[]{:S(2)}) collective-permute-start(f32[16,32,128]{2,1,0:T(8,128)S(1)} %get-tuple-element.22), channel_id=1, source_target_pairs={{0,1},{1,0},{2,3},{3,2},{4,5},{5,4},{6,7},{7,6},{8,9},{9,8},{10,11... | collective-permute-start | bytes 786440 | tf_op jit(solution)/shard_map/ppermute | solution.py:244
  34.9 4.0 %collective-permute-start.6 = (f32[24,128]{1,0:T(8,128)S(1)}, f32[24,128]{1,0:T(8,128)S(1)}, u32[]{:S(2)}, u32[]{:S(2)}) collective-permute-start(f32[24,128]{1,0:T(8,128)S(1)} %get-tuple-element.23.z0), channel_id=1, source_target_pairs={{0,96},{32,64},{64,32},{96,0},{1,97},{33,65},{65,33},{97,1},{2,98}... | collective-permute-start | bytes 36872 | tf_op jit(solution)/shard_map/ppermute | solution.py:244
  35.7 4.0 %collective-permute-start.5 = (f32[24,128]{1,0:T(8,128)S(1)}, f32[24,128]{1,0:T(8,128)S(1)}, u32[]{:S(2)}, u32[]{:S(2)}) collective-permute-start(f32[24,128]{1,0:T(8,128)S(1)} %get-tuple-element.23.z0), channel_id=1, source_target_pairs={{0,64},{32,96},{64,0},{96,32},{1,65},{33,97},{65,1},{97,33},{2,66}... | collective-permute-start | bytes 36872 | tf_op jit(solution)/shard_map/ppermute | solution.py:244
  36.8 2.9 %collective-permute-start.4 = (f32[24,128]{1,0:T(8,128)S(1)}, f32[24,128]{1,0:T(8,128)S(1)}, u32[]{:S(2)}, u32[]{:S(2)}) collective-permute-start(f32[24,128]{1,0:T(8,128)S(1)} %get-tuple-element.23.z0), channel_id=1, source_target_pairs={{0,32},{32,0},{64,96},{96,64},{1,33},{33,1},{65,97},{97,65},{2,34}... | collective-permute-start | bytes 36872 | tf_op jit(solution)/shard_map/ppermute | solution.py:244
  50.4 5.6 %collective-permute-start.7 = (f32[16,24,128]{2,1,0:T(8,128)S(1)}, f32[16,24,128]{2,1,0:T(8,128)S(1)}, u32[]{:S(2)}, u32[]{:S(2)}) collective-permute-start(f32[16,24,128]{2,1,0:T(8,128)S(1)} %all_to_all.21.q_ref), channel_id=1, source_target_pairs={{0,1},{1,0},{2,3},{3,2},{4,5},{5,4},{6,7},{7,6},{8,9},{9,8},{10,11... | collective-permute-start | bytes 589832 | tf_op jit(solution)/shard_map/ppermute | solution.py:244
  57.7 3.9 %collective-permute-start.10 = (f32[16,192]{1,0:T(8,128)S(1)}, f32[16,192]{1,0:T(8,128)S(1)}, u32[]{:S(2)}, u32[]{:S(2)}) collective-permute-start(f32[16,192]{1,0:T(8,128)S(1)} %left_other.1.p0), channel_id=1, source_target_pairs={{0,96},{32,64},{64,32},{96,0},{1,97},{33,65},{65,33},{97,1},{2,98}... | collective-permute-start | bytes 36872 | tf_op jit(solution)/shard_map/ppermute | solution.py:244
  59.7 4.1 %collective-permute-start.9 = (f32[16,192]{1,0:T(8,128)S(1)}, f32[16,192]{1,0:T(8,128)S(1)}, u32[]{:S(2)}, u32[]{:S(2)}) collective-permute-start(f32[16,192]{1,0:T(8,128)S(1)} %left_other.1.p0), channel_id=1, source_target_pairs={{0,64},{32,96},{64,0},{96,32},{1,65},{33,97},{65,1},{97,33},{2,66}... | collective-permute-start | bytes 36872 | tf_op jit(solution)/shard_map/ppermute | solution.py:244
  60.9 3.0 %collective-permute-start.8 = (f32[16,192]{1,0:T(8,128)S(1)}, f32[16,192]{1,0:T(8,128)S(1)}, u32[]{:S(2)}, u32[]{:S(2)}) collective-permute-start(f32[16,192]{1,0:T(8,128)S(1)} %left_other.1.p0), channel_id=1, source_target_pairs={{0,32},{32,0},{64,96},{96,64},{1,33},{33,1},{65,97},{97,65},{2,34}... | collective-permute-start | bytes 36872 | tf_op jit(solution)/shard_map/ppermute | solution.py:244
  65.3 2.6 %collective-permute-start.11 = (f32[16,32,128]{2,1,0:T(8,128)S(1)}, f32[16,32,128]{2,1,0:T(8,128)S(1)}, u32[]{:S(2)}, u32[]{:S(2)}) collective-permute-start(f32[16,32,128]{2,1,0:T(8,128)S(1)} %get-tuple-element.26), channel_id=1, source_target_pairs={{0,1},{1,0},{2,3},{3,2},{4,5},{5,4},{6,7},{7,6},{8,9},{9,8},{10,11... | collective-permute-start | bytes 786440 | tf_op jit(solution)/shard_map/ppermute | solution.py:244
  78.8 4.0 %collective-permute-start.15 = (f32[24,128]{1,0:T(8,128)S(1)}, f32[24,128]{1,0:T(8,128)S(1)}, u32[]{:S(2)}, u32[]{:S(2)}) collective-permute-start(f32[24,128]{1,0:T(8,128)S(1)} %get-tuple-element.28.z0), channel_id=1, source_target_pairs={{0,96},{32,64},{64,32},{96,0},{1,97},{33,65},{65,33},{97,1},{2,98}... | collective-permute-start | bytes 36872 | tf_op jit(solution)/shard_map/ppermute | solution.py:244
  79.5 4.0 %collective-permute-start.14 = (f32[24,128]{1,0:T(8,128)S(1)}, f32[24,128]{1,0:T(8,128)S(1)}, u32[]{:S(2)}, u32[]{:S(2)}) collective-permute-start(f32[24,128]{1,0:T(8,128)S(1)} %get-tuple-element.28.z0), channel_id=1, source_target_pairs={{0,64},{32,96},{64,0},{96,32},{1,65},{33,97},{65,1},{97,33},{2,66}... | collective-permute-start | bytes 36872 | tf_op jit(solution)/shard_map/ppermute | solution.py:244
  80.7 2.9 %collective-permute-start.13 = (f32[24,128]{1,0:T(8,128)S(1)}, f32[24,128]{1,0:T(8,128)S(1)}, u32[]{:S(2)}, u32[]{:S(2)}) collective-permute-start(f32[24,128]{1,0:T(8,128)S(1)} %get-tuple-element.28.z0), channel_id=1, source_target_pairs={{0,32},{32,0},{64,96},{96,64},{1,33},{33,1},{65,97},{97,65},{2,34}... | collective-permute-start | bytes 36872 | tf_op jit(solution)/shard_map/ppermute | solution.py:244
  94.1 5.6 %collective-permute-start.16 = (f32[16,24,128]{2,1,0:T(8,128)S(1)}, f32[16,24,128]{2,1,0:T(8,128)S(1)}, u32[]{:S(2)}, u32[]{:S(2)}) collective-permute-start(f32[16,24,128]{2,1,0:T(8,128)S(1)} %all_to_all.23.q_own), channel_id=1, source_target_pairs={{0,1},{1,0},{2,3},{3,2},{4,5},{5,4},{6,7},{7,6},{8,9},{9,8},{10,11... | collective-permute-start | bytes 589832 | tf_op jit(solution)/shard_map/ppermute | solution.py:244
  98.5 1.2 %collective-permute-start.12 = (f32[8,128]{1,0:T(8,128)S(1)}, f32[8,128]{1,0:T(8,128)S(1)}, u32[]{:S(2)}, u32[]{:S(2)}) collective-permute-start(f32[8,128]{1,0:T(8,128)S(1)} %lower_inverse.3.lower_ref.lower_own), channel_id=1, source_target_pairs={{0,1},{1,0},{2,3},{3,2},{4,5},{5,4},{6,7},{7,6},{8,9},{9,8},{10,11... | collective-permute-start | bytes 12296 | tf_op jit(solution)/shard_map/ppermute | solution.py:244

commit v3 on v2

v3 whole, which is shorter than its diff:
```python
import functools

import jax
import jax.numpy as jnp
from jax import lax
from jax.experimental import pallas as pl
from jax.experimental.pallas import tpu as pltpu
from jax.sharding import Mesh, PartitionSpec as P

F32, BF16 = jnp.float32, jnp.bfloat16
MATS, RANK, ROWS, COLS = 2, 8, 192, 6144
CHUNK = 1024
STEPS = COLS // CHUNK
SIDE = 4
QUARTER = COLS // SIDE
DEEP = QUARTER // 128 * RANK
NT = (((1,), (1,)), ((), ()))
IN_VMEM = pl.BlockSpec(memory_space=pltpu.VMEM)
IN_SMEM = pl.BlockSpec(memory_space=pltpu.SMEM)
ANYWHERE = pl.BlockSpec(memory_space=pl.ANY)


def vmem(a):
    return pltpu.with_memory_space_constraint(a, pltpu.VMEM)


def hbm(a):
    return pltpu.with_memory_space_constraint(a, pltpu.HBM)


def kernel(body, out_shape, in_specs, name, scratch=(), limit=16, flops=10**7):
    many = isinstance(out_shape, tuple)
    out_specs = tuple(ANYWHERE if isinstance(s, jax.ShapeDtypeStruct) else IN_VMEM for s in (out_shape if many else (out_shape,)))
    return pl.pallas_call(
        body,
        in_specs=in_specs,
        out_specs=out_specs if many else out_specs[0],
        out_shape=out_shape,
        scratch_shapes=list(scratch),
        compiler_params=pltpu.CompilerParams(vmem_limit_bytes=limit * 1024 * 1024),
        cost_estimate=pl.CostEstimate(flops=flops, bytes_accessed=10**6, transcendentals=0),
        name=name,
    )


def split3(a):
    one = a.astype(BF16).astype(F32)
    rest = a - one
    two = rest.astype(BF16).astype(F32)
    return one, two, rest - two


def three(a):
    return jnp.concatenate(split3(a), axis=0).astype(BF16)


def fold(r):
    return r[0:8] + r[8:16] + r[16:24]


def small_dot(a, b):
    total = a[:, 0:1] * b[0:1, :]
    for k in range(1, RANK):
        total = total + a[:, k : k + 1] * b[k : k + 1, :]
    return total


def inverse_lower(gram):
    row = lax.broadcasted_iota(jnp.int32, (8, 128), 0)
    lane = lax.broadcasted_iota(jnp.int32, (8, 128), 1)
    a = jnp.where(lane < RANK, gram, jnp.where(lane == row + RANK, 1.0, 0.0).astype(F32))
    for k in range(RANK):
        pivot = a[k : k + 1, k : k + 1]
        inv = lax.rsqrt(pivot)
        inv = inv * (1.5 - 0.5 * pivot * inv * inv)
        top = a[k : k + 1, :] * inv
        below = a - (a[:, k : k + 1] * inv) * top
        a = jnp.where(row == k, top, jnp.where(row > k, below, a))
    return jnp.concatenate([a[:, RANK : 2 * RANK], jnp.zeros((8, 120), F32)], axis=1)


def block_of(q_ref):
    return jnp.concatenate([q_ref[t * 8 : t * 8 + 8, :] for t in range(DEEP // 8)], axis=1)


def quarter(place_ref, k):
    return pl.ds(pl.multiple_of((place_ref[1] ^ k) * QUARTER, QUARTER), QUARTER)


def cols(c):
    return slice(c * CHUNK, (c + 1) * CHUNK)


def first_left_kernel(place_ref, g_hbm, e_hbm, q_ref, p_ref, g_ref, e_ref, g_sem, e_sem):
    core = place_ref[0]
    copies = []
    for c in range(STEPS):
        s = pl.ds(c * CHUNK, CHUNK)
        copies.append((
            pltpu.make_async_copy(g_hbm.at[0, :, :, s], g_ref.at[:, :, s], g_sem.at[c]),
            pltpu.make_async_copy(e_hbm.at[0, :, :, s], e_ref.at[:, :, s], e_sem.at[c]),
        ))
        copies[-1][0].start()
        copies[-1][1].start()
    acc = [jnp.zeros((24, ROWS), F32)] * MATS
    for c in range(STEPS):
        q = [three(q_ref[m, :, cols(c)]) for m in range(MATS)]
        copies[c][0].wait()
        copies[c][1].wait()
        for m in range(MATS):
            r = lax.dot_general(q[m], g_ref[m, :, cols(c)], NT, preferred_element_type=F32)
            r = r + lax.dot_general(q[m], e_ref[m, :, cols(c)], NT, preferred_element_type=F32)
            acc[m] = acc[m] + r
    for m in range(MATS):
        place = pl.multiple_of((m + core) % 2 * 8, 8)
        p_ref[pl.ds(place, 8), :] = fold(acc[m])


def first_left(place, grads, errors, q):
    wide = pltpu.VMEM((MATS, ROWS, COLS), BF16)
    return kernel(
        first_left_kernel, (pltpu.VMEM((16, ROWS), F32), wide, wide), [IN_SMEM, ANYWHERE, ANYWHERE, IN_VMEM], "first_left",
        [pltpu.SemaphoreType.DMA((STEPS,)), pltpu.SemaphoreType.DMA((STEPS,))],
    )(place, hbm(grads), hbm(errors), vmem(q))


def left_kernel(slot, place_ref, q0, q1, q2, q3, g_ref, e_ref, *refs):
    p_ref = refs[-1]
    m = (place_ref[0] + slot) % 2
    acc = jnp.zeros((24, ROWS), F32)
    for k, q_ref in enumerate((q0, q1, q2, q3)):
        q = three(block_of(q_ref))
        acc = acc + lax.dot_general(q, g_ref[m, :, quarter(place_ref, k)], NT, preferred_element_type=F32)
        acc = acc + lax.dot_general(q, e_ref[m, :, quarter(place_ref, k)], NT, preferred_element_type=F32)
    if slot == 0:
        p_ref[...] = fold(acc)
    else:
        p_ref[0:8, :] = refs[0][...]
        p_ref[8:16, :] = fold(acc)


def left(place, q_own, q_other, g, e):
    own = kernel(functools.partial(left_kernel, 0), pltpu.VMEM((8, ROWS), F32), [IN_SMEM] + [IN_VMEM] * 6, "left_own", flops=10**9)(
        place, *map(vmem, q_own), vmem(g), vmem(e))
    return kernel(functools.partial(left_kernel, 1), pltpu.VMEM((16, ROWS), F32), [IN_SMEM] + [IN_VMEM] * 7, "left_other")(
        place, *map(vmem, q_other), vmem(g), vmem(e), vmem(own))


def right_kernel(slot, place_ref, p0, p1, p2, p3, g_ref, e_ref, o_ref, *mean_ref):
    m = (place_ref[0] + slot) % 2
    p = ((p0[...] + p1[...]) + (p2[...] + p3[...])) * (1.0 / SIDE)
    if mean_ref:
        mean_ref[0][...] = p
    p = p[slot * 8 : slot * 8 + 8, :]
    pieces = three(p)
    gram = lax.dot_general(p, p, NT, precision=lax.Precision.HIGHEST, preferred_element_type=F32)
    gram = jnp.concatenate([gram, jnp.zeros((8, 120), F32)], axis=1)
    for k in range(SIDE):
        o_ref[k, DEEP : DEEP + 8, :] = gram
        s = slice(k * QUARTER, (k + 1) * QUARTER)
        r = jnp.dot(pieces, g_ref[m, :, s], preferred_element_type=F32)
        r = fold(r + jnp.dot(pieces, e_ref[m, :, s], preferred_element_type=F32))
        for t in range(DEEP // 8):
            o_ref[k, t * 8 : t * 8 + 8, :] = r[:, t * 128 : (t + 1) * 128]


def right(slot, place, p_all, g, e, keep=False):
    out = (pltpu.VMEM((SIDE, DEEP + 8, 128), F32),) + ((pltpu.VMEM((16, ROWS), F32),) if keep else ())
    return kernel(
        functools.partial(right_kernel, slot), out, [IN_SMEM] + [IN_VMEM] * 6, "right_own" if slot == 0 else "right_other", flops=10**9,
    )(place, *map(vmem, p_all), vmem(g), vmem(e))


def pick_kernel(place_ref, mine_ref, arrived_ref, *o_refs):
    for k, o_ref in enumerate(o_refs):
        o_ref[...] = mine_ref[place_ref[1] ^ k] + arrived_ref[place_ref[1] ^ k]


def pick(place, mine, arrived):
    return kernel(pick_kernel, (pltpu.VMEM((DEEP + 8, 128), F32),) * SIDE, [IN_SMEM] + [IN_VMEM] * 2, "pick")(
        place, vmem(mine), vmem(arrived))


def add_kernel(a, b, c, d, *o_refs):
    total = (a[...] + b[...]) + (c[...] + d[...])
    o_refs[0][...] = total[0 : o_refs[0].shape[0]]
    if len(o_refs) > 1:
        o_refs[1][...] = total[DEEP : DEEP + 8]


def add(parts, *rows):
    return kernel(add_kernel, tuple(pltpu.VMEM((r, 128), F32) for r in rows), [IN_VMEM] * SIDE, "add")(*map(vmem, parts))


def lower_kernel(gram_ref, o_ref):
    o_ref[...] = inverse_lower(gram_ref[...])


def lower_inverse(gram):
    return kernel(lower_kernel, pltpu.VMEM((8, 128), F32), [IN_VMEM], "lower_inverse", flops=10**9)(vmem(gram))


def normal_kernel(z0, z1, z2, z3, lower_ref, o_ref):
    total = ((z0[...] + z1[...]) + (z2[...] + z3[...])) * (1.0 / SIDE)
    lower = lower_ref[...]
    for t in range(DEEP // 8):
        o_ref[t * 8 : t * 8 + 8, :] = small_dot(lower, total[t * 8 : t * 8 + 8])


def normal(z_all, lower):
    return kernel(normal_kernel, pltpu.VMEM((DEEP, 128), F32), [IN_VMEM] * 5, "normal")(*map(vmem, z_all), vmem(lower))


def final_kernel(place_ref, lower_own, lower_other, *refs):
    q_refs, (p_ref, g_ref, e_ref, a_hbm, n_hbm, q_hbm, p6, a_buf, n_buf, q_buf, a_sem, n_sem, q_sem) = refs[:8], refs[8:]
    copies = []
    for slot, lower_ref in enumerate((lower_own, lower_other)):
        m = (place_ref[0] + slot) % 2
        one, two, rest = split3(small_dot(lower_ref[...], p_ref[slot * 8 : slot * 8 + 8, :]))
        pieces = jnp.concatenate([one, one, two, two, one, rest, jnp.zeros((80, ROWS), F32)], axis=0)
        pieces = jnp.concatenate([pieces, jnp.zeros((128, 64), F32)], axis=1)
        p6[slot] = pieces.T.astype(BF16)
        left_pieces = p6[slot, 0:ROWS, 0:48]
        for k in range(SIDE):
            i = slot * SIDE + k
            s = quarter(place_ref, k)
            q = block_of(q_refs[i])
            q_buf[i] = q
            one, two, rest = split3(q)
            pieces = jnp.concatenate([one, two, one, two, rest, one], axis=0).astype(BF16)
            full = jnp.dot(left_pieces, pieces, preferred_element_type=F32)
            a_buf[i] = full.astype(BF16)
            n_buf[i] = (g_ref[m, :, s].astype(F32) + e_ref[m, :, s].astype(F32) - full).astype(BF16)
            copies.append(pltpu.make_async_copy(a_buf.at[i], a_hbm.at[m, :, s], a_sem.at[i]))
            copies.append(pltpu.make_async_copy(n_buf.at[i], n_hbm.at[0, m, :, s], n_sem.at[i]))
            copies.append(pltpu.make_async_copy(q_buf.at[i], q_hbm.at[m, :, s], q_sem.at[i]))
            for copy in copies[-3:]:
                copy.start()
    for copy in copies:
        copy.wait()


def final(place, lower_own, lower_other, q_own, q_other, p, g, e):
    n = MATS * SIDE
    return kernel(
        final_kernel,
        (jax.ShapeDtypeStruct((MATS, ROWS, COLS), BF16), jax.ShapeDtypeStruct((1, MATS, ROWS, COLS), BF16),
         jax.ShapeDtypeStruct((MATS, RANK, COLS), F32)),
        [IN_SMEM] + [IN_VMEM] * 13, "residual",
        [pltpu.VMEM((MATS, 256, 128), BF16), pltpu.VMEM((n, ROWS, QUARTER), BF16), pltpu.VMEM((n, ROWS, QUARTER), BF16),
         pltpu.VMEM((n, RANK, QUARTER), F32)] + [pltpu.SemaphoreType.DMA((n,))] * 3,
        limit=24,
    )(place, *map(vmem, (lower_own, lower_other, *q_own, *q_other, p, g, e)))


def swap(a, axis, k):
    n = lax.axis_size(axis)
    return lax.ppermute(a, axis, [(i, i ^ k) for i in range(n)])


def everyones(a, axis):
    return (a,) + tuple(swap(a, axis, k) for k in (1, 2, 3))


def right_sum(place, p_own, g, e, keep):
    p_all = everyones(p_own, "dp")
    (theirs,) = right(1, place, p_all, g, e)
    arrived = swap(theirs, "core", 1)
    mine, *p = right(0, place, p_all, g, e, keep)
    parts = pick(place, mine, arrived)
    (z,) = add((parts[0],) + tuple(swap(parts[k], "x", k) for k in (1, 2, 3)), DEEP + 8)
    z, gram = add(everyones(z, "y"), DEEP, 8)
    z_all = everyones(z, "dp")
    lower = lower_inverse(gram)
    return everyones(normal(z_all, lower), "x"), lower, p


def per_device(grads, errors, q_init):
    place = jnp.stack([lax.axis_index("core"), lax.axis_index("x")]).astype(jnp.int32)
    p_own, g, e = first_left(place, grads, errors, jnp.swapaxes(q_init, 1, 2))
    q_own, _, _ = right_sum(place, p_own, g, e, False)
    p_own = left(place, q_own, [swap(q, "core", 1) for q in q_own], g, e)
    q_own, lower, (p,) = right_sum(place, p_own, g, e, True)
    q_other = [swap(q, "core", 1) for q in q_own]
    approx, errors_next, q_next = final(place, lower, swap(lower, "core", 1), q_own, q_other, p, g, e)
    return approx, errors_next, jnp.swapaxes(q_next, 1, 2)


def solution(mesh):
    fine = Mesh(mesh.devices.reshape(4, 4, 4, 2), ("dp", "x", "y", "core"))
    fsdp = ("x", "y", "core")
    in_specs = (P("dp", None, fsdp, None), P("dp", None, fsdp, None), P())
    out_specs = (P(None, fsdp, None), P("dp", None, fsdp, None), P())
    return jax.shard_map(per_device, mesh=fine, in_specs=in_specs, out_specs=out_specs, check_vma=False)
```

time: 104 us -> 106 us (1.019)
  blocking collectives: 46.1 us -> 0 us
  starting transfers between devices: 27.3 us -> 56.4 us
  waiting for transfers between devices: 9.2 us -> 24.1 us
  Pallas kernels: 19.6 us -> 23.7 us
    all_to_all x4 -> x0, blocking collectives: 46.1 us -> none  [the longest x2 25.1 us: right_sum(): z, gram = plane_sum(lax.all_to_all(mine + arrived, ('x', 'y'), 0, 0))]
    ppermute x17 -> x41, starting transfers between devices: 27.3 us -> 56.4 us  [swap(): return lax.ppermute(a, axis, [(i, i ^ k) for i in range(n)])]
    ppermute x17 -> x41, waiting for transfers between devices: 9.2 us -> 24.1 us  [swap(): return lax.ppermute(a, axis, [(i, i ^ k) for i in range(n)])]
    pallas_call x8 -> x12, Pallas kernels: 5.59 us -> 7.43 us  [the longest x4 6.03 us: right(): kernel(functools.partial(right_kernel, slot), out, [IN_SMEM] + [IN_VMEM]...]
  transfers between devices with their start and end apart: 17 -> 41, of which waited for: 8 -> 18; matrix products, arithmetic and copies ran while one was open for 0% -> 0% of each run, Pallas kernels for 5% -> 6%
where the time goes in v3:
time: 106 us
  starting transfers between devices  56.4 us (53%)
  waiting for transfers between devices  24.1 us (23%)
  Pallas kernels  23.7 us (22%)
    ppermute x41, starting transfers between devices, swap(): return lax.ppermute(a, axis, [(i, i ^ k) for i in range(n)])  56.4 us
    ppermute x41, waiting for transfers between devices, swap(): return lax.ppermute(a, axis, [(i, i ^ k) for i in range(n)])  24.1 us
    pallas_call x4, Pallas kernels, right(): kernel(functools.partial(right_kernel, slot), out, [IN_SMEM] + [IN_VMEM]...  6.03 us
    pallas_call x1, Pallas kernels, first_left(): kernel(first_left_kernel, (pltpu.VMEM((16, ROWS), F32), wide, wide), [IN_...  5.67 us
    pallas_call x1, Pallas kernels, final(): kernel(final_kernel, (jax.ShapeDtypeStruct((MATS, ROWS, COLS), BF16), jax...  4.95 us
  transfers between devices with their start and end apart: 41, of which 18 were waited for; matrix products, arithmetic and copies ran while one was open for 0% of the time, Pallas kernels for 6%

profile of v3, /device:TPU:1, one launch (start us, length us, event | category | flops | bytes accessed | tf_op | source)
XLA Modules:
  0.0 106.2 jit_solution(18103247580711014504)
XLA Ops:
  0.7 1.0 copy-done
  1.7 5.7 %first_left.1 = (f32[16,192]{1,0:T(8,128)S(1)}, bf16[2,192,6144]{2,1,0:T(8,128)(2,1)S(1)}, bf16[2,192,6144]{2,1,0:T(8,128)(2,1)S(1)}) custom-call(s32[2]{0:T(128)S(1)} %pad_add_fusion.place_ref, bf16[1,2,192,6144]{3,2,1,0:T(8,128)(2,1)} %g_hbm.1, bf16[1,2,192,6144]{3,2,1,0:T(8,128)(2,1)} %e_hbm.1, f32[2,8,6144]{2,1,0:T(8,128)S(1)} %bitcast.4), custom_call_target="tpu_custom_call" | custom-call | flops 10000000 | bytes 1000000 | tf_op jit(solution)/shard_map/first_left/pallas_call | solution.py:121
  7.4 4.7 %collective-permute-start.2 = (f32[16,192]{1,0:T(8,128)S(1)}, f32[16,192]{1,0:T(8,128)S(1)}, u32[]{:S(2)}, u32[]{:S(2)}) collective-permute-start(f32[16,192]{1,0:T(8,128)S(1)} %get-tuple-element.23.p0), channel_id=1, source_target_pairs={{0,96},{32,64},{64,32},{96,0},{1,97},{33,65},{65,33},{97,1},{2,98}... | collective-permute-start | bytes 36872 | tf_op jit(solution)/shard_map/ppermute | solution.py:258
  13.2 3.0 %collective-permute-done.1.p2 = f32[16,192]{1,0:T(8,128)S(1)} collective-permute-done((f32[16,192]{1,0:T(8,128)S(1)}, f32[16,192]{1,0:T(8,128)S(1)}, u32[]{:S(2)}, u32[]{:S(2)}) %collective-permute-start.1) | collective-permute-done | bytes 12320 | tf_op jit(solution)/shard_map/ppermute | solution.py:258
  16.2 1.5 %right_other.2 = f32[4,104,128]{2,1,0:T(8,128)S(1)} custom-call(s32[2]{0:T(128)S(1)} %pad_add_fusion.place_ref, f32[16,192]{1,0:T(8,128)S(1)} %get-tuple-element.23.p0, f32[16,192]{1,0:T(8,128)S(1)} %collective-permute-done.p1, f32[16,192]{1,0:T(8,128)S(1)} %collective-permute-done.1.p2, f32[16,192]{1,0:T(8,128)S(1)} %collective-permute-done.2.p3, ...), custom_call_target="tpu_custom_call" | custom-call | flops 1000000000 | bytes 1000000 | tf_op jit(solution)/shard_map/right_other/pallas_call | solution.py:169
  17.7 2.2 %collective-permute-start.3 = (f32[4,104,128]{2,1,0:T(8,128)S(1)}, f32[4,104,128]{2,1,0:T(8,128)S(1)}, u32[]{:S(2)}, u32[]{:S(2)}) collective-permute-start(f32[4,104,128]{2,1,0:T(8,128)S(1)} %right_other.2), channel_id=1, source_target_pairs={{0,1},{1,0},{2,3},{3,2},{4,5},{5,4},{6,7},{7,6},{8,9},{9,8},{10,11... | collective-permute-start | bytes 638984 | tf_op jit(solution)/shard_map/ppermute | solution.py:258
  19.9 1.5 %right_own.2.mine_ref = f32[4,104,128]{2,1,0:T(8,128)S(1)} custom-call(s32[2]{0:T(128)S(1)} %pad_add_fusion.place_ref, f32[16,192]{1,0:T(8,128)S(1)} %get-tuple-element.23.p0, f32[16,192]{1,0:T(8,128)S(1)} %collective-permute-done.p1, f32[16,192]{1,0:T(8,128)S(1)} %collective-permute-done.1.p2, f32[16,192]{1,0:T(8,128)S(1)} %collective-permute-done.2.p3, ...), custom_call_target="tpu_custom_call" | custom-call | flops 1000000000 | bytes 1000000 | tf_op jit(solution)/shard_map/right_own/pallas_call | solution.py:169
  22.0 1.3 %collective-permute-start.4 = (f32[104,128]{1,0:T(8,128)S(1)}, f32[104,128]{1,0:T(8,128)S(1)}, u32[]{:S(2)}, u32[]{:S(2)}) collective-permute-start(f32[104,128]{1,0:T(8,128)S(1)} %get-tuple-element.27), channel_id=1, source_target_pairs={{0,8},{8,0},{16,24},{24,16},{1,9},{9,1},{17,25},{25,17},{2,10},{10... | collective-permute-start | bytes 159752 | tf_op jit(solution)/shard_map/ppermute | solution.py:258
  23.2 2.5 %collective-permute-start.5 = (f32[104,128]{1,0:T(8,128)S(1)}, f32[104,128]{1,0:T(8,128)S(1)}, u32[]{:S(2)}, u32[]{:S(2)}) collective-permute-start(f32[104,128]{1,0:T(8,128)S(1)} %get-tuple-element.28), channel_id=1, source_target_pairs={{0,16},{8,24},{16,0},{24,8},{1,17},{9,25},{17,1},{25,9},{2,18},{10... | collective-permute-start | bytes 159752 | tf_op jit(solution)/shard_map/ppermute | solution.py:258
  25.9 2.9 %collective-permute-done.5.c = f32[104,128]{1,0:T(8,128)S(1)} collective-permute-done((f32[104,128]{1,0:T(8,128)S(1)}, f32[104,128]{1,0:T(8,128)S(1)}, u32[]{:S(2)}, u32[]{:S(2)}) %collective-permute-start.5) | collective-permute-done | bytes 53280 | tf_op jit(solution)/shard_map/ppermute | solution.py:258
  28.8 1.1 %collective-permute-done.6.d = f32[104,128]{1,0:T(8,128)S(1)} collective-permute-done((f32[104,128]{1,0:T(8,128)S(1)}, f32[104,128]{1,0:T(8,128)S(1)}, u32[]{:S(2)}, u32[]{:S(2)}) %collective-permute-start.6) | collective-permute-done | bytes 53280 | tf_op jit(solution)/shard_map/ppermute | solution.py:258
  29.9 2.8 %collective-permute-start.9 = (f32[104,128]{1,0:T(8,128)S(1)}, f32[104,128]{1,0:T(8,128)S(1)}, u32[]{:S(2)}, u32[]{:S(2)}) collective-permute-start(f32[104,128]{1,0:T(8,128)S(1)} %add.6.a), channel_id=1, source_target_pairs={{0,6},{2,4},{4,2},{6,0},{1,7},{3,5},{5,3},{7,1},{8,14},{10,12},{12... | collective-permute-start | bytes 159752 | tf_op jit(solution)/shard_map/ppermute | solution.py:258
  33.4 0.9 collective-permute-done.9.d
  34.2 3.0 %collective-permute-done.8.c = f32[104,128]{1,0:T(8,128)S(1)} collective-permute-done((f32[104,128]{1,0:T(8,128)S(1)}, f32[104,128]{1,0:T(8,128)S(1)}, u32[]{:S(2)}, u32[]{:S(2)}) %collective-permute-start.8) | collective-permute-done | bytes 53280 | tf_op jit(solution)/shard_map/ppermute | solution.py:258
  38.0 1.2 %collective-permute-start.11 = (f32[96,128]{1,0:T(8,128)S(1)}, f32[96,128]{1,0:T(8,128)S(1)}, u32[]{:S(2)}, u32[]{:S(2)}) collective-permute-start(f32[96,128]{1,0:T(8,128)S(1)} %get-tuple-element.30.z0), channel_id=1, source_target_pairs={{0,64},{32,96},{64,0},{96,32},{1,65},{33,97},{65,1},{97,33},{2,66}... | collective-permute-start | bytes 147464 | tf_op jit(solution)/shard_map/ppermute | solution.py:258
  39.1 1.4 %collective-permute-start.10 = (f32[96,128]{1,0:T(8,128)S(1)}, f32[96,128]{1,0:T(8,128)S(1)}, u32[]{:S(2)}, u32[]{:S(2)}) collective-permute-start(f32[96,128]{1,0:T(8,128)S(1)} %get-tuple-element.30.z0), channel_id=1, source_target_pairs={{0,32},{32,0},{64,96},{96,64},{1,33},{33,1},{65,97},{97,65},{2,34}... | collective-permute-start | bytes 147464 | tf_op jit(solution)/shard_map/ppermute | solution.py:258
  41.5 1.0 collective-permute-done.11.z2
  42.7 1.3 %collective-permute-start.18 = (f32[96,128]{1,0:T(8,128)S(1)}, f32[96,128]{1,0:T(8,128)S(1)}, u32[]{:S(2)}, u32[]{:S(2)}) collective-permute-start(f32[96,128]{1,0:T(8,128)S(1)} %normal.2.q0), channel_id=1, source_target_pairs={{0,24},{8,16},{16,8},{24,0},{1,25},{9,17},{17,9},{25,1},{2,26},{10... | collective-permute-start | bytes 147464 | tf_op jit(solution)/shard_map/ppermute | solution.py:258
  44.7 1.3 %collective-permute-start.14 = (f32[96,128]{1,0:T(8,128)S(1)}, f32[96,128]{1,0:T(8,128)S(1)}, u32[]{:S(2)}, u32[]{:S(2)}) collective-permute-start(f32[96,128]{1,0:T(8,128)S(1)} %normal.2.q0), channel_id=1, source_target_pairs={{0,8},{8,0},{16,24},{24,16},{1,9},{9,1},{17,25},{25,17},{2,10},{10... | collective-permute-start | bytes 147464 | tf_op jit(solution)/shard_map/ppermute | solution.py:258
  46.0 5.4 %collective-permute-start.13 = (f32[96,128]{1,0:T(8,128)S(1)}, f32[96,128]{1,0:T(8,128)S(1)}, u32[]{:S(2)}, u32[]{:S(2)}) collective-permute-start(f32[96,128]{1,0:T(8,128)S(1)} %normal.2.q0), channel_id=1, source_target_pairs={{0,1},{1,0},{2,3},{3,2},{4,5},{5,4},{6,7},{7,6},{8,9},{9,8},{10,11... | collective-permute-start | bytes 147464 | tf_op jit(solution)/shard_map/ppermute | solution.py:258
  51.4 1.2 %collective-permute-start.19 = (f32[96,128]{1,0:T(8,128)S(1)}, f32[96,128]{1,0:T(8,128)S(1)}, u32[]{:S(2)}, u32[]{:S(2)}) collective-permute-start(f32[96,128]{1,0:T(8,128)S(1)} %collective-permute-done.18.q3), channel_id=1, source_target_pairs={{0,1},{1,0},{2,3},{3,2},{4,5},{5,4},{6,7},{7,6},{8,9},{9,8},{10,11... | collective-permute-start | bytes 147464 | tf_op jit(solution)/shard_map/ppermute | solution.py:258
  52.6 0.9 collective-permute-start.17
  54.0 2.1 %left_own.1.refs_0_ = f32[8,192]{1,0:T(8,128)S(1)} custom-call(s32[2]{0:T(128)S(1)} %pad_add_fusion.place_ref, f32[96,128]{1,0:T(8,128)S(1)} %normal.2.q0, f32[96,128]{1,0:T(8,128)S(1)} %collective-permute-done.14.q1, f32[96,128]{1,0:T(8,128)S(1)} %collective-permute-done.16.q2, f32[96,128]{1,0:T(8,128)S(1)} %collective-permute-done.18.q3, ...), custom_call_target="tpu_custom_call" | custom-call | flops 1000000000 | bytes 1000000 | tf_op jit(solution)/shard_map/left_own/pallas_call | solution.py:143
  56.2 2.1 %left_other.1.p0 = f32[16,192]{1,0:T(8,128)S(1)} custom-call(s32[2]{0:T(128)S(1)} %pad_add_fusion.place_ref, f32[96,128]{1,0:T(8,128)S(1)} %collective-permute-done.13.q0, f32[96,128]{1,0:T(8,128)S(1)} %collective-permute-done.15.q1, f32[96,128]{1,0:T(8,128)S(1)} %collective-permute-done.17.q2, f32[96,128]{1,0:T(8,128)S(1)} %collective-permute-done.19.q3, ...), custom_call_target="tpu_custom_call" | custom-call | flops 10000000 | bytes 1000000 | tf_op jit(solution)/shard_map/left_other/pallas_call | solution.py:145
  58.3 1.9 %collective-permute-start.22 = (f32[16,192]{1,0:T(8,128)S(1)}, f32[16,192]{1,0:T(8,128)S(1)}, u32[]{:S(2)}, u32[]{:S(2)}) collective-permute-start(f32[16,192]{1,0:T(8,128)S(1)} %left_other.1.p0), channel_id=1, source_target_pairs={{0,96},{32,64},{64,32},{96,0},{1,97},{33,65},{65,33},{97,1},{2,98}... | collective-permute-start | bytes 36872 | tf_op jit(solution)/shard_map/ppermute | solution.py:258
  60.3 1.1 %collective-permute-start.21 = (f32[16,192]{1,0:T(8,128)S(1)}, f32[16,192]{1,0:T(8,128)S(1)}, u32[]{:S(2)}, u32[]{:S(2)}) collective-permute-start(f32[16,192]{1,0:T(8,128)S(1)} %left_other.1.p0), channel_id=1, source_target_pairs={{0,64},{32,96},{64,0},{96,32},{1,65},{33,97},{65,1},{97,33},{2,66}... | collective-permute-start | bytes 36872 | tf_op jit(solution)/shard_map/ppermute | solution.py:258
  62.2 2.2 %collective-permute-done.21.p2 = f32[16,192]{1,0:T(8,128)S(1)} collective-permute-done((f32[16,192]{1,0:T(8,128)S(1)}, f32[16,192]{1,0:T(8,128)S(1)}, u32[]{:S(2)}, u32[]{:S(2)}) %collective-permute-start.21) | collective-permute-done | bytes 12320 | tf_op jit(solution)/shard_map/ppermute | solution.py:258
  64.4 1.5 %right_other.3 = f32[4,104,128]{2,1,0:T(8,128)S(1)} custom-call(s32[2]{0:T(128)S(1)} %pad_add_fusion.place_ref, f32[16,192]{1,0:T(8,128)S(1)} %left_other.1.p0, f32[16,192]{1,0:T(8,128)S(1)} %collective-permute-done.20.p1, f32[16,192]{1,0:T(8,128)S(1)} %collective-permute-done.21.p2, f32[16,192]{1,0:T(8,128)S(1)} %collective-permute-done.22.p3, ...), custom_call_target="tpu_custom_call" | custom-call | flops 1000000000 | bytes 1000000 | tf_op jit(solution)/shard_map/right_other/pallas_call | solution.py:169
  65.9 1.5 %collective-permute-start.23 = (f32[4,104,128]{2,1,0:T(8,128)S(1)}, f32[4,104,128]{2,1,0:T(8,128)S(1)}, u32[]{:S(2)}, u32[]{:S(2)}) collective-permute-start(f32[4,104,128]{2,1,0:T(8,128)S(1)} %right_other.3), channel_id=1, source_target_pairs={{0,1},{1,0},{2,3},{3,2},{4,5},{5,4},{6,7},{7,6},{8,9},{9,8},{10,11... | collective-permute-start | bytes 638984 | tf_op jit(solution)/shard_map/ppermute | solution.py:258
  67.4 1.5 %right_own.3 = (f32[4,104,128]{2,1,0:T(8,128)S(1)}, f32[16,192]{1,0:T(8,128)S(1)}) custom-call(s32[2]{0:T(128)S(1)} %pad_add_fusion.place_ref, f32[16,192]{1,0:T(8,128)S(1)} %left_other.1.p0, f32[16,192]{1,0:T(8,128)S(1)} %collective-permute-done.20.p1, f32[16,192]{1,0:T(8,128)S(1)} %collective-permute-done.21.p2, f32[16,192]{1,0:T(8,128)S(1)} %collective-permute-done.22.p3, ...), custom_call_target="tpu_custom_call" | custom-call | flops 1000000000 | bytes 1000000 | tf_op jit(solution)/shard_map/right_own/pallas_call | solution.py:169
  69.5 1.3 %collective-permute-start.24 = (f32[104,128]{1,0:T(8,128)S(1)}, f32[104,128]{1,0:T(8,128)S(1)}, u32[]{:S(2)}, u32[]{:S(2)}) collective-permute-start(f32[104,128]{1,0:T(8,128)S(1)} %get-tuple-element.34), channel_id=1, source_target_pairs={{0,8},{8,0},{16,24},{24,16},{1,9},{9,1},{17,25},{25,17},{2,10},{10... | collective-permute-start | bytes 159752 | tf_op jit(solution)/shard_map/ppermute | solution.py:258
  70.8 2.3 %collective-permute-start.25 = (f32[104,128]{1,0:T(8,128)S(1)}, f32[104,128]{1,0:T(8,128)S(1)}, u32[]{:S(2)}, u32[]{:S(2)}) collective-permute-start(f32[104,128]{1,0:T(8,128)S(1)} %get-tuple-element.35), channel_id=1, source_target_pairs={{0,16},{8,24},{16,0},{24,8},{1,17},{9,25},{17,1},{25,9},{2,18},{10... | collective-permute-start | bytes 159752 | tf_op jit(solution)/shard_map/ppermute | solution.py:258
  73.5 2.8 %collective-permute-done.25.c = f32[104,128]{1,0:T(8,128)S(1)} collective-permute-done((f32[104,128]{1,0:T(8,128)S(1)}, f32[104,128]{1,0:T(8,128)S(1)}, u32[]{:S(2)}, u32[]{:S(2)}) %collective-permute-start.25) | collective-permute-done | bytes 53280 | tf_op jit(solution)/shard_map/ppermute | solution.py:258
  76.2 1.1 %collective-permute-done.26.d = f32[104,128]{1,0:T(8,128)S(1)} collective-permute-done((f32[104,128]{1,0:T(8,128)S(1)}, f32[104,128]{1,0:T(8,128)S(1)}, u32[]{:S(2)}, u32[]{:S(2)}) %collective-permute-start.26) | collective-permute-done | bytes 53280 | tf_op jit(solution)/shard_map/ppermute | solution.py:258
  77.3 1.1 %collective-permute-start.29 = (f32[104,128]{1,0:T(8,128)S(1)}, f32[104,128]{1,0:T(8,128)S(1)}, u32[]{:S(2)}, u32[]{:S(2)}) collective-permute-start(f32[104,128]{1,0:T(8,128)S(1)} %add.8.a), channel_id=1, source_target_pairs={{0,6},{2,4},{4,2},{6,0},{1,7},{3,5},{5,3},{7,1},{8,14},{10,12},{12... | collective-permute-start | bytes 159752 | tf_op jit(solution)/shard_map/ppermute | solution.py:258
  79.2 1.4 %collective-permute-start.27 = (f32[104,128]{1,0:T(8,128)S(1)}, f32[104,128]{1,0:T(8,128)S(1)}, u32[]{:S(2)}, u32[]{:S(2)}) collective-permute-start(f32[104,128]{1,0:T(8,128)S(1)} %add.8.a), channel_id=1, source_target_pairs={{0,2},{2,0},{4,6},{6,4},{1,3},{3,1},{5,7},{7,5},{8,10},{10,8},{12,... | collective-permute-start | bytes 159752 | tf_op jit(solution)/shard_map/ppermute | solution.py:258
  80.7 0.9 collective-permute-done.29.d
  81.6 1.3 %collective-permute-done.28.c = f32[104,128]{1,0:T(8,128)S(1)} collective-permute-done((f32[104,128]{1,0:T(8,128)S(1)}, f32[104,128]{1,0:T(8,128)S(1)}, u32[]{:S(2)}, u32[]{:S(2)}) %collective-permute-start.28) | collective-permute-done | bytes 53280 | tf_op jit(solution)/shard_map/ppermute | solution.py:258
  82.9 1.0 collective-permute-start.33
  84.0 1.0 collective-permute-start.32
  85.0 1.3 %collective-permute-start.31 = (f32[96,128]{1,0:T(8,128)S(1)}, f32[96,128]{1,0:T(8,128)S(1)}, u32[]{:S(2)}, u32[]{:S(2)}) collective-permute-start(f32[96,128]{1,0:T(8,128)S(1)} %get-tuple-element.38.z0), channel_id=1, source_target_pairs={{0,32},{32,0},{64,96},{96,64},{1,33},{33,1},{65,97},{97,65},{2,34}... | collective-permute-start | bytes 147464 | tf_op jit(solution)/shard_map/ppermute | solution.py:258
  87.2 1.3 %collective-permute-done.32.z2 = f32[96,128]{1,0:T(8,128)S(1)} collective-permute-done((f32[96,128]{1,0:T(8,128)S(1)}, f32[96,128]{1,0:T(8,128)S(1)}, u32[]{:S(2)}, u32[]{:S(2)}) %collective-permute-start.32) | collective-permute-done | bytes 49184 | tf_op jit(solution)/shard_map/ppermute | solution.py:258
  89.0 1.5 %collective-permute-start.35 = (f32[96,128]{1,0:T(8,128)S(1)}, f32[96,128]{1,0:T(8,128)S(1)}, u32[]{:S(2)}, u32[]{:S(2)}) collective-permute-start(f32[96,128]{1,0:T(8,128)S(1)} %normal.3.refs_0_), channel_id=1, source_target_pairs={{0,16},{8,24},{16,0},{24,8},{1,17},{9,25},{17,1},{25,9},{2,18},{10... | collective-permute-start | bytes 147464 | tf_op jit(solution)/shard_map/ppermute | solution.py:258
  90.4 1.4 %collective-permute-start.34 = (f32[96,128]{1,0:T(8,128)S(1)}, f32[96,128]{1,0:T(8,128)S(1)}, u32[]{:S(2)}, u32[]{:S(2)}) collective-permute-start(f32[96,128]{1,0:T(8,128)S(1)} %normal.3.refs_0_), channel_id=1, source_target_pairs={{0,8},{8,0},{16,24},{24,16},{1,9},{9,1},{17,25},{25,17},{2,10},{10... | collective-permute-start | bytes 147464 | tf_op jit(solution)/shard_map/ppermute | solution.py:258
  91.9 5.4 %collective-permute-start.37 = (f32[96,128]{1,0:T(8,128)S(1)}, f32[96,128]{1,0:T(8,128)S(1)}, u32[]{:S(2)}, u32[]{:S(2)}) collective-permute-start(f32[96,128]{1,0:T(8,128)S(1)} %normal.3.refs_0_), channel_id=1, source_target_pairs={{0,1},{1,0},{2,3},{3,2},{4,5},{5,4},{6,7},{7,6},{8,9},{9,8},{10,11... | collective-permute-start | bytes 147464 | tf_op jit(solution)/shard_map/ppermute | solution.py:258
  97.3 1.2 %collective-permute-start.40 = (f32[96,128]{1,0:T(8,128)S(1)}, f32[96,128]{1,0:T(8,128)S(1)}, u32[]{:S(2)}, u32[]{:S(2)}) collective-permute-start(f32[96,128]{1,0:T(8,128)S(1)} %collective-permute-done.36.refs_3_), channel_id=1, source_target_pairs={{0,1},{1,0},{2,3},{3,2},{4,5},{5,4},{6,7},{7,6},{8,9},{9,8},{10,11... | collective-permute-start | bytes 147464 | tf_op jit(solution)/shard_map/ppermute | solution.py:258
  99.9 1.2 %collective-permute-done.30.lower_other = f32[8,128]{1,0:T(8,128)S(1)} collective-permute-done((f32[8,128]{1,0:T(8,128)S(1)}, f32[8,128]{1,0:T(8,128)S(1)}, u32[]{:S(2)}, u32[]{:S(2)}) %collective-permute-start.30) | collective-permute-done | bytes 4128 | tf_op jit(solution)/shard_map/ppermute | solution.py:258
  101.1 5.0 %residual.1 = (bf16[2,192,6144]{2,1,0:T(8,128)(2,1)}, bf16[1,2,192,6144]{3,2,1,0:T(8,128)(2,1)}, f32[2,8,6144]{2,1,0:T(8,128)}) custom-call(s32[2]{0:T(128)S(1)} %pad_add_fusion.place_ref, f32[8,128]{1,0:T(8,128)S(1)} %lower_inverse.3.lower_ref.lower_own, f32[8,128]{1,0:T(8,128)S(1)} %collective-permute-done.30.lower_other, f32[96,128]{1,0:T(8,128)S(1)} %normal.3.refs_0_, ...), custom_call_target="tpu_custom_call" | custom-call | flops 10000000 | bytes 1000000 | tf_op jit(solution)/shard_map/residual/pallas_call | solution.py:245
  (55 shorter events, 11.2 us)
Async XLA Ops:
  0.7 1.0 copy-start
  7.4 5.8 %collective-permute-start.2 = (f32[16,192]{1,0:T(8,128)S(1)}, f32[16,192]{1,0:T(8,128)S(1)}, u32[]{:S(2)}, u32[]{:S(2)}) collective-permute-start(f32[16,192]{1,0:T(8,128)S(1)} %get-tuple-element.23.p0), channel_id=1, source_target_pairs={{0,96},{32,64},{64,32},{96,0},{1,97},{33,65},{65,33},{97,1},{2,98}... | collective-permute-start | bytes 36872 | tf_op jit(solution)/shard_map/ppermute | solution.py:258
  12.1 4.1 %collective-permute-start.1 = (f32[16,192]{1,0:T(8,128)S(1)}, f32[16,192]{1,0:T(8,128)S(1)}, u32[]{:S(2)}, u32[]{:S(2)}) collective-permute-start(f32[16,192]{1,0:T(8,128)S(1)} %get-tuple-element.23.p0), channel_id=1, source_target_pairs={{0,64},{32,96},{64,0},{96,32},{1,65},{33,97},{65,1},{97,33},{2,66}... | collective-permute-start | bytes 36872 | tf_op jit(solution)/shard_map/ppermute | solution.py:258
  12.1 4.1 %collective-permute-start = (f32[16,192]{1,0:T(8,128)S(1)}, f32[16,192]{1,0:T(8,128)S(1)}, u32[]{:S(2)}, u32[]{:S(2)}) collective-permute-start(f32[16,192]{1,0:T(8,128)S(1)} %get-tuple-element.23.p0), channel_id=1, source_target_pairs={{0,32},{32,0},{64,96},{96,64},{1,33},{33,1},{65,97},{97,65},{2,34}... | collective-permute-start | bytes 36872 | tf_op jit(solution)/shard_map/ppermute | solution.py:258
  17.7 3.7 %collective-permute-start.3 = (f32[4,104,128]{2,1,0:T(8,128)S(1)}, f32[4,104,128]{2,1,0:T(8,128)S(1)}, u32[]{:S(2)}, u32[]{:S(2)}) collective-permute-start(f32[4,104,128]{2,1,0:T(8,128)S(1)} %right_other.2), channel_id=1, source_target_pairs={{0,1},{1,0},{2,3},{3,2},{4,5},{5,4},{6,7},{7,6},{8,9},{9,8},{10,11... | collective-permute-start | bytes 638984 | tf_op jit(solution)/shard_map/ppermute | solution.py:258
  22.0 3.9 %collective-permute-start.4 = (f32[104,128]{1,0:T(8,128)S(1)}, f32[104,128]{1,0:T(8,128)S(1)}, u32[]{:S(2)}, u32[]{:S(2)}) collective-permute-start(f32[104,128]{1,0:T(8,128)S(1)} %get-tuple-element.27), channel_id=1, source_target_pairs={{0,8},{8,0},{16,24},{24,16},{1,9},{9,1},{17,25},{25,17},{2,10},{10... | collective-permute-start | bytes 159752 | tf_op jit(solution)/shard_map/ppermute | solution.py:258
  23.2 5.6 %collective-permute-start.5 = (f32[104,128]{1,0:T(8,128)S(1)}, f32[104,128]{1,0:T(8,128)S(1)}, u32[]{:S(2)}, u32[]{:S(2)}) collective-permute-start(f32[104,128]{1,0:T(8,128)S(1)} %get-tuple-element.28), channel_id=1, source_target_pairs={{0,16},{8,24},{16,0},{24,8},{1,17},{9,25},{17,1},{25,9},{2,18},{10... | collective-permute-start | bytes 159752 | tf_op jit(solution)/shard_map/ppermute | solution.py:258
  25.7 4.2 %collective-permute-start.6 = (f32[104,128]{1,0:T(8,128)S(1)}, f32[104,128]{1,0:T(8,128)S(1)}, u32[]{:S(2)}, u32[]{:S(2)}) collective-permute-start(f32[104,128]{1,0:T(8,128)S(1)} %get-tuple-element.29), channel_id=1, source_target_pairs={{0,24},{8,16},{16,8},{24,0},{1,25},{9,17},{17,9},{25,1},{2,26},{10... | collective-permute-start | bytes 159752 | tf_op jit(solution)/shard_map/ppermute | solution.py:258
  29.9 4.3 %collective-permute-start.9 = (f32[104,128]{1,0:T(8,128)S(1)}, f32[104,128]{1,0:T(8,128)S(1)}, u32[]{:S(2)}, u32[]{:S(2)}) collective-permute-start(f32[104,128]{1,0:T(8,128)S(1)} %add.6.a), channel_id=1, source_target_pairs={{0,6},{2,4},{4,2},{6,0},{1,7},{3,5},{5,3},{7,1},{8,14},{10,12},{12... | collective-permute-start | bytes 159752 | tf_op jit(solution)/shard_map/ppermute | solution.py:258
  32.7 4.5 %collective-permute-start.8 = (f32[104,128]{1,0:T(8,128)S(1)}, f32[104,128]{1,0:T(8,128)S(1)}, u32[]{:S(2)}, u32[]{:S(2)}) collective-permute-start(f32[104,128]{1,0:T(8,128)S(1)} %add.6.a), channel_id=1, source_target_pairs={{0,4},{2,6},{4,0},{6,2},{1,5},{3,7},{5,1},{7,3},{8,12},{10,14},{12... | collective-permute-start | bytes 159752 | tf_op jit(solution)/shard_map/ppermute | solution.py:258
  33.1 4.1 %collective-permute-start.7 = (f32[104,128]{1,0:T(8,128)S(1)}, f32[104,128]{1,0:T(8,128)S(1)}, u32[]{:S(2)}, u32[]{:S(2)}) collective-permute-start(f32[104,128]{1,0:T(8,128)S(1)} %add.6.a), channel_id=1, source_target_pairs={{0,2},{2,0},{4,6},{6,4},{1,3},{3,1},{5,7},{7,5},{8,10},{10,8},{12,... | collective-permute-start | bytes 159752 | tf_op jit(solution)/shard_map/ppermute | solution.py:258
  37.2 4.2 %collective-permute-start.12 = (f32[96,128]{1,0:T(8,128)S(1)}, f32[96,128]{1,0:T(8,128)S(1)}, u32[]{:S(2)}, u32[]{:S(2)}) collective-permute-start(f32[96,128]{1,0:T(8,128)S(1)} %get-tuple-element.30.z0), channel_id=1, source_target_pairs={{0,96},{32,64},{64,32},{96,0},{1,97},{33,65},{65,33},{97,1},{2,98}... | collective-permute-start | bytes 147464 | tf_op jit(solution)/shard_map/ppermute | solution.py:258
  38.0 4.4 %collective-permute-start.11 = (f32[96,128]{1,0:T(8,128)S(1)}, f32[96,128]{1,0:T(8,128)S(1)}, u32[]{:S(2)}, u32[]{:S(2)}) collective-permute-start(f32[96,128]{1,0:T(8,128)S(1)} %get-tuple-element.30.z0), channel_id=1, source_target_pairs={{0,64},{32,96},{64,0},{96,32},{1,65},{33,97},{65,1},{97,33},{2,66}... | collective-permute-start | bytes 147464 | tf_op jit(solution)/shard_map/ppermute | solution.py:258
  39.1 3.4 %collective-permute-start.10 = (f32[96,128]{1,0:T(8,128)S(1)}, f32[96,128]{1,0:T(8,128)S(1)}, u32[]{:S(2)}, u32[]{:S(2)}) collective-permute-start(f32[96,128]{1,0:T(8,128)S(1)} %get-tuple-element.30.z0), channel_id=1, source_target_pairs={{0,32},{32,0},{64,96},{96,64},{1,33},{33,1},{65,97},{97,65},{2,34}... | collective-permute-start | bytes 147464 | tf_op jit(solution)/shard_map/ppermute | solution.py:258
  42.7 8.8 %collective-permute-start.18 = (f32[96,128]{1,0:T(8,128)S(1)}, f32[96,128]{1,0:T(8,128)S(1)}, u32[]{:S(2)}, u32[]{:S(2)}) collective-permute-start(f32[96,128]{1,0:T(8,128)S(1)} %normal.2.q0), channel_id=1, source_target_pairs={{0,24},{8,16},{16,8},{24,0},{1,25},{9,17},{17,9},{25,1},{2,26},{10... | collective-permute-start | bytes 147464 | tf_op jit(solution)/shard_map/ppermute | solution.py:258
  44.0 8.7 %collective-permute-start.16 = (f32[96,128]{1,0:T(8,128)S(1)}, f32[96,128]{1,0:T(8,128)S(1)}, u32[]{:S(2)}, u32[]{:S(2)}) collective-permute-start(f32[96,128]{1,0:T(8,128)S(1)} %normal.2.q0), channel_id=1, source_target_pairs={{0,16},{8,24},{16,0},{24,8},{1,17},{9,25},{17,1},{25,9},{2,18},{10... | collective-permute-start | bytes 147464 | tf_op jit(solution)/shard_map/ppermute | solution.py:258
  44.7 8.8 %collective-permute-start.14 = (f32[96,128]{1,0:T(8,128)S(1)}, f32[96,128]{1,0:T(8,128)S(1)}, u32[]{:S(2)}, u32[]{:S(2)}) collective-permute-start(f32[96,128]{1,0:T(8,128)S(1)} %normal.2.q0), channel_id=1, source_target_pairs={{0,8},{8,0},{16,24},{24,16},{1,9},{9,1},{17,25},{25,17},{2,10},{10... | collective-permute-start | bytes 147464 | tf_op jit(solution)/shard_map/ppermute | solution.py:258
  46.0 10.1 %collective-permute-start.13 = (f32[96,128]{1,0:T(8,128)S(1)}, f32[96,128]{1,0:T(8,128)S(1)}, u32[]{:S(2)}, u32[]{:S(2)}) collective-permute-start(f32[96,128]{1,0:T(8,128)S(1)} %normal.2.q0), channel_id=1, source_target_pairs={{0,1},{1,0},{2,3},{3,2},{4,5},{5,4},{6,7},{7,6},{8,9},{9,8},{10,11... | collective-permute-start | bytes 147464 | tf_op jit(solution)/shard_map/ppermute | solution.py:258
  51.4 4.7 %collective-permute-start.19 = (f32[96,128]{1,0:T(8,128)S(1)}, f32[96,128]{1,0:T(8,128)S(1)}, u32[]{:S(2)}, u32[]{:S(2)}) collective-permute-start(f32[96,128]{1,0:T(8,128)S(1)} %collective-permute-done.18.q3), channel_id=1, source_target_pairs={{0,1},{1,0},{2,3},{3,2},{4,5},{5,4},{6,7},{7,6},{8,9},{9,8},{10,11... | collective-permute-start | bytes 147464 | tf_op jit(solution)/shard_map/ppermute | solution.py:258
  52.6 3.5 %collective-permute-start.17 = (f32[96,128]{1,0:T(8,128)S(1)}, f32[96,128]{1,0:T(8,128)S(1)}, u32[]{:S(2)}, u32[]{:S(2)}) collective-permute-start(f32[96,128]{1,0:T(8,128)S(1)} %collective-permute-done.16.q2), channel_id=1, source_target_pairs={{0,1},{1,0},{2,3},{3,2},{4,5},{5,4},{6,7},{7,6},{8,9},{9,8},{10,11... | collective-permute-start | bytes 147464 | tf_op jit(solution)/shard_map/ppermute | solution.py:258
  53.5 2.6 %collective-permute-start.15 = (f32[96,128]{1,0:T(8,128)S(1)}, f32[96,128]{1,0:T(8,128)S(1)}, u32[]{:S(2)}, u32[]{:S(2)}) collective-permute-start(f32[96,128]{1,0:T(8,128)S(1)} %collective-permute-done.14.q1), channel_id=1, source_target_pairs={{0,1},{1,0},{2,3},{3,2},{4,5},{5,4},{6,7},{7,6},{8,9},{9,8},{10,11... | collective-permute-start | bytes 147464 | tf_op jit(solution)/shard_map/ppermute | solution.py:258
  58.3 3.9 %collective-permute-start.22 = (f32[16,192]{1,0:T(8,128)S(1)}, f32[16,192]{1,0:T(8,128)S(1)}, u32[]{:S(2)}, u32[]{:S(2)}) collective-permute-start(f32[16,192]{1,0:T(8,128)S(1)} %left_other.1.p0), channel_id=1, source_target_pairs={{0,96},{32,64},{64,32},{96,0},{1,97},{33,65},{65,33},{97,1},{2,98}... | collective-permute-start | bytes 36872 | tf_op jit(solution)/shard_map/ppermute | solution.py:258
  60.3 4.1 %collective-permute-start.21 = (f32[16,192]{1,0:T(8,128)S(1)}, f32[16,192]{1,0:T(8,128)S(1)}, u32[]{:S(2)}, u32[]{:S(2)}) collective-permute-start(f32[16,192]{1,0:T(8,128)S(1)} %left_other.1.p0), channel_id=1, source_target_pairs={{0,64},{32,96},{64,0},{96,32},{1,65},{33,97},{65,1},{97,33},{2,66}... | collective-permute-start | bytes 36872 | tf_op jit(solution)/shard_map/ppermute | solution.py:258
  61.4 3.0 %collective-permute-start.20 = (f32[16,192]{1,0:T(8,128)S(1)}, f32[16,192]{1,0:T(8,128)S(1)}, u32[]{:S(2)}, u32[]{:S(2)}) collective-permute-start(f32[16,192]{1,0:T(8,128)S(1)} %left_other.1.p0), channel_id=1, source_target_pairs={{0,32},{32,0},{64,96},{96,64},{1,33},{33,1},{65,97},{97,65},{2,34}... | collective-permute-start | bytes 36872 | tf_op jit(solution)/shard_map/ppermute | solution.py:258
  65.9 3.1 %collective-permute-start.23 = (f32[4,104,128]{2,1,0:T(8,128)S(1)}, f32[4,104,128]{2,1,0:T(8,128)S(1)}, u32[]{:S(2)}, u32[]{:S(2)}) collective-permute-start(f32[4,104,128]{2,1,0:T(8,128)S(1)} %right_other.3), channel_id=1, source_target_pairs={{0,1},{1,0},{2,3},{3,2},{4,5},{5,4},{6,7},{7,6},{8,9},{9,8},{10,11... | collective-permute-start | bytes 638984 | tf_op jit(solution)/shard_map/ppermute | solution.py:258
  69.5 3.9 %collective-permute-start.24 = (f32[104,128]{1,0:T(8,128)S(1)}, f32[104,128]{1,0:T(8,128)S(1)}, u32[]{:S(2)}, u32[]{:S(2)}) collective-permute-start(f32[104,128]{1,0:T(8,128)S(1)} %get-tuple-element.34), channel_id=1, source_target_pairs={{0,8},{8,0},{16,24},{24,16},{1,9},{9,1},{17,25},{25,17},{2,10},{10... | collective-permute-start | bytes 159752 | tf_op jit(solution)/shard_map/ppermute | solution.py:258
  70.8 5.5 %collective-permute-start.25 = (f32[104,128]{1,0:T(8,128)S(1)}, f32[104,128]{1,0:T(8,128)S(1)}, u32[]{:S(2)}, u32[]{:S(2)}) collective-permute-start(f32[104,128]{1,0:T(8,128)S(1)} %get-tuple-element.35), channel_id=1, source_target_pairs={{0,16},{8,24},{16,0},{24,8},{1,17},{9,25},{17,1},{25,9},{2,18},{10... | collective-permute-start | bytes 159752 | tf_op jit(solution)/shard_map/ppermute | solution.py:258
  73.1 4.2 %collective-permute-start.26 = (f32[104,128]{1,0:T(8,128)S(1)}, f32[104,128]{1,0:T(8,128)S(1)}, u32[]{:S(2)}, u32[]{:S(2)}) collective-permute-start(f32[104,128]{1,0:T(8,128)S(1)} %get-tuple-element.36), channel_id=1, source_target_pairs={{0,24},{8,16},{16,8},{24,0},{1,25},{9,17},{17,9},{25,1},{2,26},{10... | collective-permute-start | bytes 159752 | tf_op jit(solution)/shard_map/ppermute | solution.py:258
  77.3 4.3 %collective-permute-start.29 = (f32[104,128]{1,0:T(8,128)S(1)}, f32[104,128]{1,0:T(8,128)S(1)}, u32[]{:S(2)}, u32[]{:S(2)}) collective-permute-start(f32[104,128]{1,0:T(8,128)S(1)} %add.8.a), channel_id=1, source_target_pairs={{0,6},{2,4},{4,2},{6,0},{1,7},{3,5},{5,3},{7,1},{8,14},{10,12},{12... | collective-permute-start | bytes 159752 | tf_op jit(solution)/shard_map/ppermute | solution.py:258
  78.4 4.5 %collective-permute-start.28 = (f32[104,128]{1,0:T(8,128)S(1)}, f32[104,128]{1,0:T(8,128)S(1)}, u32[]{:S(2)}, u32[]{:S(2)}) collective-permute-start(f32[104,128]{1,0:T(8,128)S(1)} %add.8.a), channel_id=1, source_target_pairs={{0,4},{2,6},{4,0},{6,2},{1,5},{3,7},{5,1},{7,3},{8,12},{10,14},{12... | collective-permute-start | bytes 159752 | tf_op jit(solution)/shard_map/ppermute | solution.py:258
  79.2 3.7 %collective-permute-start.27 = (f32[104,128]{1,0:T(8,128)S(1)}, f32[104,128]{1,0:T(8,128)S(1)}, u32[]{:S(2)}, u32[]{:S(2)}) collective-permute-start(f32[104,128]{1,0:T(8,128)S(1)} %add.8.a), channel_id=1, source_target_pairs={{0,2},{2,0},{4,6},{6,4},{1,3},{3,1},{5,7},{7,5},{8,10},{10,8},{12,... | collective-permute-start | bytes 159752 | tf_op jit(solution)/shard_map/ppermute | solution.py:258
  82.9 4.2 %collective-permute-start.33 = (f32[96,128]{1,0:T(8,128)S(1)}, f32[96,128]{1,0:T(8,128)S(1)}, u32[]{:S(2)}, u32[]{:S(2)}) collective-permute-start(f32[96,128]{1,0:T(8,128)S(1)} %get-tuple-element.38.z0), channel_id=1, source_target_pairs={{0,96},{32,64},{64,32},{96,0},{1,97},{33,65},{65,33},{97,1},{2,98}... | collective-permute-start | bytes 147464 | tf_op jit(solution)/shard_map/ppermute | solution.py:258
  84.0 4.4 %collective-permute-start.32 = (f32[96,128]{1,0:T(8,128)S(1)}, f32[96,128]{1,0:T(8,128)S(1)}, u32[]{:S(2)}, u32[]{:S(2)}) collective-permute-start(f32[96,128]{1,0:T(8,128)S(1)} %get-tuple-element.38.z0), channel_id=1, source_target_pairs={{0,64},{32,96},{64,0},{96,32},{1,65},{33,97},{65,1},{97,33},{2,66}... | collective-permute-start | bytes 147464 | tf_op jit(solution)/shard_map/ppermute | solution.py:258
  85.0 3.5 %collective-permute-start.31 = (f32[96,128]{1,0:T(8,128)S(1)}, f32[96,128]{1,0:T(8,128)S(1)}, u32[]{:S(2)}, u32[]{:S(2)}) collective-permute-start(f32[96,128]{1,0:T(8,128)S(1)} %get-tuple-element.38.z0), channel_id=1, source_target_pairs={{0,32},{32,0},{64,96},{96,64},{1,33},{33,1},{65,97},{97,65},{2,34}... | collective-permute-start | bytes 147464 | tf_op jit(solution)/shard_map/ppermute | solution.py:258
  88.5 8.8 %collective-permute-start.36 = (f32[96,128]{1,0:T(8,128)S(1)}, f32[96,128]{1,0:T(8,128)S(1)}, u32[]{:S(2)}, u32[]{:S(2)}) collective-permute-start(f32[96,128]{1,0:T(8,128)S(1)} %normal.3.refs_0_), channel_id=1, source_target_pairs={{0,24},{8,16},{16,8},{24,0},{1,25},{9,17},{17,9},{25,1},{2,26},{10... | collective-permute-start | bytes 147464 | tf_op jit(solution)/shard_map/ppermute | solution.py:258
  89.0 9.5 %collective-permute-start.35 = (f32[96,128]{1,0:T(8,128)S(1)}, f32[96,128]{1,0:T(8,128)S(1)}, u32[]{:S(2)}, u32[]{:S(2)}) collective-permute-start(f32[96,128]{1,0:T(8,128)S(1)} %normal.3.refs_0_), channel_id=1, source_target_pairs={{0,16},{8,24},{16,0},{24,8},{1,17},{9,25},{17,1},{25,9},{2,18},{10... | collective-permute-start | bytes 147464 | tf_op jit(solution)/shard_map/ppermute | solution.py:258
  90.4 8.8 %collective-permute-start.34 = (f32[96,128]{1,0:T(8,128)S(1)}, f32[96,128]{1,0:T(8,128)S(1)}, u32[]{:S(2)}, u32[]{:S(2)}) collective-permute-start(f32[96,128]{1,0:T(8,128)S(1)} %normal.3.refs_0_), channel_id=1, source_target_pairs={{0,8},{8,0},{16,24},{24,16},{1,9},{9,1},{17,25},{25,17},{2,10},{10... | collective-permute-start | bytes 147464 | tf_op jit(solution)/shard_map/ppermute | solution.py:258
  91.9 9.2 %collective-permute-start.37 = (f32[96,128]{1,0:T(8,128)S(1)}, f32[96,128]{1,0:T(8,128)S(1)}, u32[]{:S(2)}, u32[]{:S(2)}) collective-permute-start(f32[96,128]{1,0:T(8,128)S(1)} %normal.3.refs_0_), channel_id=1, source_target_pairs={{0,1},{1,0},{2,3},{3,2},{4,5},{5,4},{6,7},{7,6},{8,9},{9,8},{10,11... | collective-permute-start | bytes 147464 | tf_op jit(solution)/shard_map/ppermute | solution.py:258
  97.3 3.8 %collective-permute-start.40 = (f32[96,128]{1,0:T(8,128)S(1)}, f32[96,128]{1,0:T(8,128)S(1)}, u32[]{:S(2)}, u32[]{:S(2)}) collective-permute-start(f32[96,128]{1,0:T(8,128)S(1)} %collective-permute-done.36.refs_3_), channel_id=1, source_target_pairs={{0,1},{1,0},{2,3},{3,2},{4,5},{5,4},{6,7},{7,6},{8,9},{9,8},{10,11... | collective-permute-start | bytes 147464 | tf_op jit(solution)/shard_map/ppermute | solution.py:258
  98.5 2.6 %collective-permute-start.39 = (f32[96,128]{1,0:T(8,128)S(1)}, f32[96,128]{1,0:T(8,128)S(1)}, u32[]{:S(2)}, u32[]{:S(2)}) collective-permute-start(f32[96,128]{1,0:T(8,128)S(1)} %collective-permute-done.35.refs_2_), channel_id=1, source_target_pairs={{0,1},{1,0},{2,3},{3,2},{4,5},{5,4},{6,7},{7,6},{8,9},{9,8},{10,11... | collective-permute-start | bytes 147464 | tf_op jit(solution)/shard_map/ppermute | solution.py:258
  99.3 1.8 %collective-permute-start.38 = (f32[96,128]{1,0:T(8,128)S(1)}, f32[96,128]{1,0:T(8,128)S(1)}, u32[]{:S(2)}, u32[]{:S(2)}) collective-permute-start(f32[96,128]{1,0:T(8,128)S(1)} %collective-permute-done.34.refs_1_), channel_id=1, source_target_pairs={{0,1},{1,0},{2,3},{3,2},{4,5},{5,4},{6,7},{7,6},{8,9},{9,8},{10,11... | collective-permute-start | bytes 147464 | tf_op jit(solution)/shard_map/ppermute | solution.py:258
  99.9 1.2 %collective-permute-start.30 = (f32[8,128]{1,0:T(8,128)S(1)}, f32[8,128]{1,0:T(8,128)S(1)}, u32[]{:S(2)}, u32[]{:S(2)}) collective-permute-start(f32[8,128]{1,0:T(8,128)S(1)} %lower_inverse.3.lower_ref.lower_own), channel_id=1, source_target_pairs={{0,1},{1,0},{2,3},{3,2},{4,5},{5,4},{6,7},{7,6},{8,9},{9,8},{10,11... | collective-permute-start | bytes 12296 | tf_op jit(solution)/shard_map/ppermute | solution.py:258

commit v4 on v3

v4 whole, which is shorter than its diff:
```python
import functools

import jax
import jax.numpy as jnp
from jax import lax
from jax.experimental import pallas as pl
from jax.experimental.pallas import tpu as pltpu
from jax.sharding import Mesh, PartitionSpec as P

F32, BF16 = jnp.float32, jnp.bfloat16
MATS, RANK, ROWS, COLS = 2, 8, 192, 6144
CHUNK = 1024
STEPS = COLS // CHUNK
SIDE = 4
QUARTER = COLS // SIDE
BLOCK = QUARTER // 2
DEEP = QUARTER // 128 * RANK
NT = (((1,), (1,)), ((), ()))
IN_VMEM = pl.BlockSpec(memory_space=pltpu.VMEM)
ANYWHERE = pl.BlockSpec(memory_space=pl.ANY)


def vmem(a):
    return pltpu.with_memory_space_constraint(a, pltpu.VMEM)


def hbm(a):
    return pltpu.with_memory_space_constraint(a, pltpu.HBM)


def kernel(body, out_shape, in_specs, name, scratch=(), limit=16, flops=10**7):
    many = isinstance(out_shape, tuple)
    out_specs = tuple(ANYWHERE if isinstance(s, jax.ShapeDtypeStruct) else IN_VMEM for s in (out_shape if many else (out_shape,)))
    return pl.pallas_call(
        body,
        in_specs=in_specs,
        out_specs=out_specs if many else out_specs[0],
        out_shape=out_shape,
        scratch_shapes=list(scratch),
        compiler_params=pltpu.CompilerParams(vmem_limit_bytes=limit * 1024 * 1024),
        cost_estimate=pl.CostEstimate(flops=flops, bytes_accessed=10**6, transcendentals=0),
        name=name,
    )


def split3(a):
    one = a.astype(BF16).astype(F32)
    rest = a - one
    two = rest.astype(BF16).astype(F32)
    return one, two, rest - two


def three(a):
    return jnp.concatenate(split3(a), axis=0).astype(BF16)


def fold(r):
    return r[0:8] + r[8:16] + r[16:24]


def small_dot(a, b):
    total = a[:, 0:1] * b[0:1, :]
    for k in range(1, RANK):
        total = total + a[:, k : k + 1] * b[k : k + 1, :]
    return total


def inverse_lower(gram):
    row = lax.broadcasted_iota(jnp.int32, (8, 128), 0)
    lane = lax.broadcasted_iota(jnp.int32, (8, 128), 1)
    a = jnp.where(lane < RANK, gram, jnp.where(lane == row + RANK, 1.0, 0.0).astype(F32))
    for k in range(RANK):
        pivot = a[k : k + 1, k : k + 1]
        inv = lax.rsqrt(pivot)
        inv = inv * (1.5 - 0.5 * pivot * inv * inv)
        top = a[k : k + 1, :] * inv
        below = a - (a[:, k : k + 1] * inv) * top
        a = jnp.where(row == k, top, jnp.where(row > k, below, a))
    return jnp.concatenate([a[:, RANK : 2 * RANK], jnp.zeros((8, 120), F32)], axis=1)


def block_of(q, h):
    tiles = range(h * (BLOCK // 128), (h + 1) * (BLOCK // 128))
    return jnp.concatenate([q[t * 8 : t * 8 + 8, :] for t in tiles], axis=1)


def half(k, h):
    return pl.ds(pl.multiple_of((lax.axis_index("x") ^ k) * QUARTER + h * BLOCK, BLOCK), BLOCK)


def cols(c):
    return slice(c * CHUNK, (c + 1) * CHUNK)


def first_left_kernel(g_hbm, e_hbm, q_hbm, p_ref, g_ref, e_ref, q_ref, g_sem, e_sem, q_sem):
    core = lax.axis_index("core")
    copies = []
    q_copy = pltpu.make_async_copy(q_hbm, q_ref, q_sem)
    q_copy.start()
    for c in range(STEPS):
        s = pl.ds(c * CHUNK, CHUNK)
        copies.append((
            pltpu.make_async_copy(g_hbm.at[0, :, :, s], g_ref.at[:, :, s], g_sem.at[c]),
            pltpu.make_async_copy(e_hbm.at[0, :, :, s], e_ref.at[:, :, s], e_sem.at[c]),
        ))
        copies[-1][0].start()
        copies[-1][1].start()
    acc = [jnp.zeros((24, ROWS), F32)] * MATS
    q_copy.wait()
    for c in range(STEPS):
        q = [three(q_ref[m, :, cols(c)]) for m in range(MATS)]
        copies[c][0].wait()
        copies[c][1].wait()
        for m in range(MATS):
            r = lax.dot_general(q[m], g_ref[m, :, cols(c)], NT, preferred_element_type=F32)
            r = r + lax.dot_general(q[m], e_ref[m, :, cols(c)], NT, preferred_element_type=F32)
            acc[m] = acc[m] + r
    for m in range(MATS):
        place = pl.multiple_of((core ^ m) * 8, 8)
        p_ref[pl.ds(place, 8), :] = fold(acc[m])


def first_left(grads, errors, q):
    wide = pltpu.VMEM((MATS, ROWS, COLS), BF16)
    return kernel(
        first_left_kernel, (pltpu.VMEM((16, ROWS), F32), wide, wide), [ANYWHERE] * 3, "first_left",
        [pltpu.VMEM((MATS, RANK, COLS), F32), pltpu.SemaphoreType.DMA((STEPS,)), pltpu.SemaphoreType.DMA((STEPS,)), pltpu.SemaphoreType.DMA],
    )(hbm(grads), hbm(errors), hbm(q))


def left_kernel(slot, q_ref, g_ref, e_ref, *refs):
    p_ref = refs[-1]
    m = lax.axis_index("core") ^ slot
    acc = jnp.zeros((24, ROWS), F32)
    for k in range(SIDE):
        for h in range(2):
            q = three(block_of(q_ref[k], h))
            acc = acc + lax.dot_general(q, g_ref[m, :, half(k, h)], NT, preferred_element_type=F32)
            acc = acc + lax.dot_general(q, e_ref[m, :, half(k, h)], NT, preferred_element_type=F32)
    if slot == 0:
        p_ref[...] = fold(acc)
    else:
        p_ref[0:8, :] = refs[0][...]
        p_ref[8:16, :] = fold(acc)


def left(q_own, q_other, g, e):
    own = kernel(functools.partial(left_kernel, 0), pltpu.VMEM((8, ROWS), F32), [IN_VMEM] * 3, "left_own", flops=10**9)(
        vmem(q_own), vmem(g), vmem(e))
    return kernel(functools.partial(left_kernel, 1), pltpu.VMEM((16, ROWS), F32), [IN_VMEM] * 4, "left_other")(
        vmem(q_other), vmem(g), vmem(e), vmem(own))


def right_kernel(slot, p0, p1, p2, p3, g_ref, e_ref, o_ref, *mean_ref):
    m = lax.axis_index("core") ^ slot
    p = ((p0[...] + p1[...]) + (p2[...] + p3[...])) * (1.0 / SIDE)
    if mean_ref:
        mean_ref[0][...] = p
    p = p[slot * 8 : slot * 8 + 8, :]
    pieces = three(p)
    gram = lax.dot_general(p, p, NT, precision=lax.Precision.HIGHEST, preferred_element_type=F32)
    gram = jnp.concatenate([gram, jnp.zeros((8, 120), F32)], axis=1)
    for k in range(SIDE):
        o_ref[k, DEEP : DEEP + 8, :] = gram
        for h in range(2):
            s = slice(k * QUARTER + h * BLOCK, k * QUARTER + (h + 1) * BLOCK)
            r = jnp.dot(pieces, g_ref[m, :, s], preferred_element_type=F32)
            r = fold(r + jnp.dot(pieces, e_ref[m, :, s], preferred_element_type=F32))
            for i in range(BLOCK // 128):
                t = h * (BLOCK // 128) + i
                o_ref[k, t * 8 : t * 8 + 8, :] = r[:, i * 128 : (i + 1) * 128]


def right(slot, p_all, g, e, keep=False):
    out = (pltpu.VMEM((SIDE, DEEP + 8, 128), F32),) + ((pltpu.VMEM((16, ROWS), F32),) if keep else ())
    return kernel(
        functools.partial(right_kernel, slot), out, [IN_VMEM] * 6, "right_own" if slot == 0 else "right_other", flops=10**9,
    )(*map(vmem, p_all), vmem(g), vmem(e))


def pick_kernel(mine_ref, arrived_ref, *o_refs):
    for k, o_ref in enumerate(o_refs):
        o_ref[...] = mine_ref[lax.axis_index("x") ^ k] + arrived_ref[lax.axis_index("x") ^ k]


def pick(mine, arrived):
    return kernel(pick_kernel, (pltpu.VMEM((DEEP + 8, 128), F32),) * SIDE, [IN_VMEM] * 2, "pick")(
        vmem(mine), vmem(arrived))


def add_kernel(a, b, c, d, *o_refs):
    total = (a[...] + b[...]) + (c[...] + d[...])
    o_refs[0][...] = total[0 : o_refs[0].shape[0]]
    if len(o_refs) > 1:
        o_refs[1][...] = total[DEEP : DEEP + 8]


def add(parts, *rows):
    return kernel(add_kernel, tuple(pltpu.VMEM((r, 128), F32) for r in rows), [IN_VMEM] * SIDE, "add")(*map(vmem, parts))


def lower_kernel(gram_ref, o_ref):
    o_ref[...] = inverse_lower(gram_ref[...])


def lower_inverse(gram):
    return kernel(lower_kernel, pltpu.VMEM((8, 128), F32), [IN_VMEM], "lower_inverse", flops=10**9)(vmem(gram))


def normal_kernel(z0, z1, z2, z3, lower_ref, o_ref):
    total = ((z0[...] + z1[...]) + (z2[...] + z3[...])) * (1.0 / SIDE)
    lower = lower_ref[...]
    for t in range(DEEP // 8):
        o_ref[t * 8 : t * 8 + 8, :] = small_dot(lower, total[t * 8 : t * 8 + 8])


def normal(z_all, lower):
    return kernel(normal_kernel, pltpu.VMEM((DEEP, 128), F32), [IN_VMEM] * 5, "normal")(*map(vmem, z_all), vmem(lower))


def join_kernel(q0, q1, q2, q3, o_ref):
    for k, q_ref in enumerate((q0, q1, q2, q3)):
        o_ref[k] = q_ref[...]


def join(parts):
    return kernel(join_kernel, pltpu.VMEM((SIDE, DEEP, 128), F32), [IN_VMEM] * SIDE, "join")(*map(vmem, parts))


def final_kernel(lower_own, lower_other, q_own, q_other, p_ref, g_ref, e_ref, a_hbm, n_hbm, q_hbm,
                 p6, a_buf, n_buf, q_buf, a_sem, n_sem, q_sem):
    copies = []
    for slot, (lower_ref, q_ref) in enumerate(((lower_own, q_own), (lower_other, q_other))):
        m = lax.axis_index("core") ^ slot
        one, two, rest = split3(small_dot(lower_ref[...], p_ref[slot * 8 : slot * 8 + 8, :]))
        pieces = jnp.concatenate([one, one, two, two, one, rest, jnp.zeros((80, ROWS), F32)], axis=0)
        pieces = jnp.concatenate([pieces, jnp.zeros((128, 64), F32)], axis=1)
        p6[slot] = pieces.T.astype(BF16)
        left_pieces = p6[slot, 0:ROWS, 0:48]
        for k in range(SIDE):
            for h in range(2):
                i = (slot * SIDE + k) * 2 + h
                s = half(k, h)
                q = block_of(q_ref[k], h)
                q_buf[i] = q
                one, two, rest = split3(q)
                pieces = jnp.concatenate([one, two, one, two, rest, one], axis=0).astype(BF16)
                full = jnp.dot(left_pieces, pieces, preferred_element_type=F32)
                a_buf[i] = full.astype(BF16)
                n_buf[i] = (g_ref[m, :, s].astype(F32) + e_ref[m, :, s].astype(F32) - full).astype(BF16)
                copies.append(pltpu.make_async_copy(a_buf.at[i], a_hbm.at[m, :, s], a_sem.at[i]))
                copies.append(pltpu.make_async_copy(n_buf.at[i], n_hbm.at[0, m, :, s], n_sem.at[i]))
                copies.append(pltpu.make_async_copy(q_buf.at[i], q_hbm.at[m, :, s], q_sem.at[i]))
                for copy in copies[-3:]:
                    copy.start()
    for copy in copies:
        copy.wait()


def final(lower_own, lower_other, q_own, q_other, p, g, e):
    n = MATS * SIDE * 2
    return kernel(
        final_kernel,
        (jax.ShapeDtypeStruct((MATS, ROWS, COLS), BF16), jax.ShapeDtypeStruct((1, MATS, ROWS, COLS), BF16),
         jax.ShapeDtypeStruct((MATS, RANK, COLS), F32)),
        [IN_VMEM] * 7, "residual",
        [pltpu.VMEM((MATS, 256, 128), BF16), pltpu.VMEM((n, ROWS, BLOCK), BF16), pltpu.VMEM((n, ROWS, BLOCK), BF16),
         pltpu.VMEM((n, RANK, BLOCK), F32)] + [pltpu.SemaphoreType.DMA((n,))] * 3,
        limit=24,
    )(*map(vmem, (lower_own, lower_other, q_own, q_other, p, g, e)))


def swap(a, axis, k):
    n = lax.axis_size(axis)
    return lax.ppermute(a, axis, [(i, i ^ k) for i in range(n)])


def everyones(a, axis):
    return (a,) + tuple(swap(a, axis, k) for k in (1, 2, 3))


def right_sum(p_own, g, e, keep):
    p_all = everyones(p_own, "dp")
    (theirs,) = right(1, p_all, g, e)
    arrived = swap(theirs, "core", 1)
    mine, *p = right(0, p_all, g, e, keep)
    parts = pick(mine, arrived)
    (z,) = add((parts[0],) + tuple(swap(parts[k], "x", k) for k in (1, 2, 3)), DEEP + 8)
    z, gram = add(everyones(z, "y"), DEEP, 8)
    z_all = everyones(z, "dp")
    lower = lower_inverse(gram)
    return join(everyones(normal(z_all, lower), "x")), lower, p


def per_device(grads, errors, q_init):
    p_own, g, e = first_left(grads, errors, jnp.swapaxes(q_init, 1, 2))
    q_own, _, _ = right_sum(p_own, g, e, False)
    p_own = left(q_own, swap(q_own, "core", 1), g, e)
    q_own, lower, (p,) = right_sum(p_own, g, e, True)
    approx, errors_next, q_next = final(lower, swap(lower, "core", 1), q_own, swap(q_own, "core", 1), p, g, e)
    return approx, errors_next, jnp.swapaxes(q_next, 1, 2)


def solution(mesh):
    fine = Mesh(mesh.devices.reshape(4, 4, 4, 2), ("dp", "x", "y", "core"))
    fsdp = ("x", "y", "core")
    in_specs = (P("dp", None, fsdp, None), P("dp", None, fsdp, None), P())
    out_specs = (P(None, fsdp, None), P("dp", None, fsdp, None), P())
    return jax.shard_map(per_device, mesh=fine, in_specs=in_specs, out_specs=out_specs, check_vma=False)
```

time: 106 us -> 103 us (0.972)
  waiting for transfers between devices: 24.1 us -> 27.8 us
  Pallas kernels: 23.7 us -> 20.4 us
  starting transfers between devices: 56.4 us -> 53.4 us
    ppermute x41 -> x35, waiting for transfers between devices: 24.1 us -> 27.8 us  [swap(): return lax.ppermute(a, axis, [(i, i ^ k) for i in range(n)])]
    ppermute x41 -> x35, starting transfers between devices: 56.4 us -> 53.4 us  [swap(): return lax.ppermute(a, axis, [(i, i ^ k) for i in range(n)])]
    pallas_call x7 -> x9, Pallas kernels: 12.8 us -> 11.1 us  [the longest x1 7.15 us: first_left(): kernel(first_left_kernel, (pltpu.VMEM((16, ROWS), F32), wide, wide), [ANY...]
  transfers between devices with their start and end apart: 41 -> 35, of which waited for: 18 -> 26; matrix products, arithmetic and copies ran while one was open for 0% -> 0% of each run, Pallas kernels for 6% -> 5%
where the time goes in v4:
time: 103 us; the launch traced here: 102 us
  starting transfers between devices  53.4 us (52%)
  waiting for transfers between devices  27.8 us (27%)
  Pallas kernels  20.4 us (20%)
    ppermute x35, starting transfers between devices, swap(): return lax.ppermute(a, axis, [(i, i ^ k) for i in range(n)])  53.4 us
    ppermute x35, waiting for transfers between devices, swap(): return lax.ppermute(a, axis, [(i, i ^ k) for i in range(n)])  27.8 us
    pallas_call x1, Pallas kernels, first_left(): kernel(first_left_kernel, (pltpu.VMEM((16, ROWS), F32), wide, wide), [ANY...  7.15 us
    pallas_call x1, Pallas kernels, final(): kernel(final_kernel, (jax.ShapeDtypeStruct((MATS, ROWS, COLS), BF16), jax...  4.54 us
    pallas_call x4, Pallas kernels, right(): kernel(functools.partial(right_kernel, slot), out, [IN_VMEM] * 6, 'right_...  3.87 us
  transfers between devices with their start and end apart: 35, of which 26 were waited for; matrix products, arithmetic and copies ran while one was open for 0% of the time, Pallas kernels for 5%

profile of v4, /device:TPU:1, one launch (start us, length us, event | category | flops | bytes accessed | tf_op | source)
XLA Modules:
  0.0 102.5 jit_solution(14879567987258238044)
XLA Ops:
  0.6 7.1 %first_left.1 = (f32[16,192]{1,0:T(8,128)S(1)}, bf16[2,192,6144]{2,1,0:T(8,128)(2,1)S(1)}, bf16[2,192,6144]{2,1,0:T(8,128)(2,1)S(1)}) custom-call(bf16[1,2,192,6144]{3,2,1,0:T(8,128)(2,1)} %g_hbm.1, bf16[1,2,192,6144]{3,2,1,0:T(8,128)(2,1)} %e_hbm.1, f32[2,8,6144]{2,1,0:T(8,128)} %bitcast.2), custom_call_target="tpu_custom_call" | custom-call | flops 10000000 | bytes 1000000 | tf_op jit(solution)/shard_map/first_left/pallas_call | solution.py:125
  7.8 4.7 %collective-permute-start.2 = (f32[16,192]{1,0:T(8,128)S(1)}, f32[16,192]{1,0:T(8,128)S(1)}, u32[]{:S(2)}, u32[]{:S(2)}) collective-permute-start(f32[16,192]{1,0:T(8,128)S(1)} %get-tuple-element.23.p0), channel_id=1, source_target_pairs={{0,96},{32,64},{64,32},{96,0},{1,97},{33,65},{65,33},{97,1},{2,98}... | collective-permute-start | bytes 36872 | tf_op jit(solution)/shard_map/ppermute | solution.py:275
  13.6 3.0 %collective-permute-done.1.p2 = f32[16,192]{1,0:T(8,128)S(1)} collective-permute-done((f32[16,192]{1,0:T(8,128)S(1)}, f32[16,192]{1,0:T(8,128)S(1)}, u32[]{:S(2)}, u32[]{:S(2)}) %collective-permute-start.1) | collective-permute-done | bytes 12320 | tf_op jit(solution)/shard_map/ppermute | solution.py:275
  16.5 1.0 right_other.2
  17.5 2.2 %collective-permute-start.3 = (f32[4,104,128]{2,1,0:T(8,128)S(1)}, f32[4,104,128]{2,1,0:T(8,128)S(1)}, u32[]{:S(2)}, u32[]{:S(2)}) collective-permute-start(f32[4,104,128]{2,1,0:T(8,128)S(1)} %right_other.2), channel_id=1, source_target_pairs={{0,1},{1,0},{2,3},{3,2},{4,5},{5,4},{6,7},{7,6},{8,9},{9,8},{10,11... | collective-permute-start | bytes 638984 | tf_op jit(solution)/shard_map/ppermute | solution.py:275
  19.7 1.0 right_own.2.mine_ref
  20.8 1.3 %collective-permute-start.4 = (f32[104,128]{1,0:T(8,128)S(1)}, f32[104,128]{1,0:T(8,128)S(1)}, u32[]{:S(2)}, u32[]{:S(2)}) collective-permute-start(f32[104,128]{1,0:T(8,128)S(1)} %get-tuple-element.27), channel_id=1, source_target_pairs={{0,8},{8,0},{16,24},{24,16},{1,9},{9,1},{17,25},{25,17},{2,10},{10... | collective-permute-start | bytes 159752 | tf_op jit(solution)/shard_map/ppermute | solution.py:275
  22.1 2.4 %collective-permute-start.5 = (f32[104,128]{1,0:T(8,128)S(1)}, f32[104,128]{1,0:T(8,128)S(1)}, u32[]{:S(2)}, u32[]{:S(2)}) collective-permute-start(f32[104,128]{1,0:T(8,128)S(1)} %get-tuple-element.28), channel_id=1, source_target_pairs={{0,16},{8,24},{16,0},{24,8},{1,17},{9,25},{17,1},{25,9},{2,18},{10... | collective-permute-start | bytes 159752 | tf_op jit(solution)/shard_map/ppermute | solution.py:275
  24.8 2.2 %collective-permute-done.5.c = f32[104,128]{1,0:T(8,128)S(1)} collective-permute-done((f32[104,128]{1,0:T(8,128)S(1)}, f32[104,128]{1,0:T(8,128)S(1)}, u32[]{:S(2)}, u32[]{:S(2)}) %collective-permute-start.5) | collective-permute-done | bytes 53280 | tf_op jit(solution)/shard_map/ppermute | solution.py:275
  27.0 1.8 %collective-permute-done.6.d = f32[104,128]{1,0:T(8,128)S(1)} collective-permute-done((f32[104,128]{1,0:T(8,128)S(1)}, f32[104,128]{1,0:T(8,128)S(1)}, u32[]{:S(2)}, u32[]{:S(2)}) %collective-permute-start.6) | collective-permute-done | bytes 53280 | tf_op jit(solution)/shard_map/ppermute | solution.py:275
  28.8 2.8 %collective-permute-start.9 = (f32[104,128]{1,0:T(8,128)S(1)}, f32[104,128]{1,0:T(8,128)S(1)}, u32[]{:S(2)}, u32[]{:S(2)}) collective-permute-start(f32[104,128]{1,0:T(8,128)S(1)} %add.4.a), channel_id=1, source_target_pairs={{0,6},{2,4},{4,2},{6,0},{1,7},{3,5},{5,3},{7,1},{8,14},{10,12},{12... | collective-permute-start | bytes 159752 | tf_op jit(solution)/shard_map/ppermute | solution.py:275
  32.3 0.9 collective-permute-done.9.d
  33.1 3.0 %collective-permute-done.8.c = f32[104,128]{1,0:T(8,128)S(1)} collective-permute-done((f32[104,128]{1,0:T(8,128)S(1)}, f32[104,128]{1,0:T(8,128)S(1)}, u32[]{:S(2)}, u32[]{:S(2)}) %collective-permute-start.8) | collective-permute-done | bytes 53280 | tf_op jit(solution)/shard_map/ppermute | solution.py:275
  37.0 1.2 %collective-permute-start.11 = (f32[96,128]{1,0:T(8,128)S(1)}, f32[96,128]{1,0:T(8,128)S(1)}, u32[]{:S(2)}, u32[]{:S(2)}) collective-permute-start(f32[96,128]{1,0:T(8,128)S(1)} %get-tuple-element.30.z0), channel_id=1, source_target_pairs={{0,64},{32,96},{64,0},{96,32},{1,65},{33,97},{65,1},{97,33},{2,66}... | collective-permute-start | bytes 147464 | tf_op jit(solution)/shard_map/ppermute | solution.py:275
  38.1 1.4 %collective-permute-start.10 = (f32[96,128]{1,0:T(8,128)S(1)}, f32[96,128]{1,0:T(8,128)S(1)}, u32[]{:S(2)}, u32[]{:S(2)}) collective-permute-start(f32[96,128]{1,0:T(8,128)S(1)} %get-tuple-element.30.z0), channel_id=1, source_target_pairs={{0,32},{32,0},{64,96},{96,64},{1,33},{33,1},{65,97},{97,65},{2,34}... | collective-permute-start | bytes 147464 | tf_op jit(solution)/shard_map/ppermute | solution.py:275
  40.4 1.0 collective-permute-done.11.z2
  43.0 2.0 %collective-permute-start.13 = (f32[96,128]{1,0:T(8,128)S(1)}, f32[96,128]{1,0:T(8,128)S(1)}, u32[]{:S(2)}, u32[]{:S(2)}) collective-permute-start(f32[96,128]{1,0:T(8,128)S(1)} %normal.2.q0), channel_id=1, source_target_pairs={{0,8},{8,0},{16,24},{24,16},{1,9},{9,1},{17,25},{25,17},{2,10},{10... | collective-permute-start | bytes 147464 | tf_op jit(solution)/shard_map/ppermute | solution.py:275
  45.0 0.9 collective-permute-done.15.q3
  45.9 0.9 collective-permute-done.14.q2
  47.0 6.4 %collective-permute-start.16 = (f32[4,96,128]{2,1,0:T(8,128)S(1)}, f32[4,96,128]{2,1,0:T(8,128)S(1)}, u32[]{:S(2)}, u32[]{:S(2)}) collective-permute-start(f32[4,96,128]{2,1,0:T(8,128)S(1)} %join.2.q_ref), channel_id=1, source_target_pairs={{0,1},{1,0},{2,3},{3,2},{4,5},{5,4},{6,7},{7,6},{8,9},{9,8},{10,11... | collective-permute-start | bytes 589832 | tf_op jit(solution)/shard_map/ppermute | solution.py:275
  53.3 1.6 %left_own.1.refs_0_ = f32[8,192]{1,0:T(8,128)S(1)} custom-call(f32[4,96,128]{2,1,0:T(8,128)S(1)} %join.2.q_ref, bf16[2,192,6144]{2,1,0:T(8,128)(2,1)S(1)} %get-tuple-element.24.g_ref, bf16[2,192,6144]{2,1,0:T(8,128)(2,1)S(1)} %get-tuple-element.25.e_ref), custom_call_target="tpu_custom_call" | custom-call | flops 1000000000 | bytes 1000000 | tf_op jit(solution)/shard_map/left_own/pallas_call | solution.py:148
  54.9 1.6 %left_other.1.p0 = f32[16,192]{1,0:T(8,128)S(1)} custom-call(f32[4,96,128]{2,1,0:T(8,128)S(1)} %collective-permute-done.16.q_ref, bf16[2,192,6144]{2,1,0:T(8,128)(2,1)S(1)} %get-tuple-element.24.g_ref, bf16[2,192,6144]{2,1,0:T(8,128)(2,1)S(1)} %get-tuple-element.25.e_ref, f32[8,192]{1,0:T(8,128)S(1)} %left_own.1.refs_0_), custom_call_target="tpu_custom_call" | custom-call | flops 10000000 | bytes 1000000 | tf_op jit(solution)/shard_map/left_other/pallas_call | solution.py:150
  56.5 1.9 %collective-permute-start.19 = (f32[16,192]{1,0:T(8,128)S(1)}, f32[16,192]{1,0:T(8,128)S(1)}, u32[]{:S(2)}, u32[]{:S(2)}) collective-permute-start(f32[16,192]{1,0:T(8,128)S(1)} %left_other.1.p0), channel_id=1, source_target_pairs={{0,96},{32,64},{64,32},{96,0},{1,97},{33,65},{65,33},{97,1},{2,98}... | collective-permute-start | bytes 36872 | tf_op jit(solution)/shard_map/ppermute | solution.py:275
  58.5 1.1 %collective-permute-start.18 = (f32[16,192]{1,0:T(8,128)S(1)}, f32[16,192]{1,0:T(8,128)S(1)}, u32[]{:S(2)}, u32[]{:S(2)}) collective-permute-start(f32[16,192]{1,0:T(8,128)S(1)} %left_other.1.p0), channel_id=1, source_target_pairs={{0,64},{32,96},{64,0},{96,32},{1,65},{33,97},{65,1},{97,33},{2,66}... | collective-permute-start | bytes 36872 | tf_op jit(solution)/shard_map/ppermute | solution.py:275
  60.4 2.2 %collective-permute-done.18.p2 = f32[16,192]{1,0:T(8,128)S(1)} collective-permute-done((f32[16,192]{1,0:T(8,128)S(1)}, f32[16,192]{1,0:T(8,128)S(1)}, u32[]{:S(2)}, u32[]{:S(2)}) %collective-permute-start.18) | collective-permute-done | bytes 12320 | tf_op jit(solution)/shard_map/ppermute | solution.py:275
  62.6 1.0 right_other.3
  63.6 1.7 %collective-permute-start.20 = (f32[4,104,128]{2,1,0:T(8,128)S(1)}, f32[4,104,128]{2,1,0:T(8,128)S(1)}, u32[]{:S(2)}, u32[]{:S(2)}) collective-permute-start(f32[4,104,128]{2,1,0:T(8,128)S(1)} %right_other.3), channel_id=1, source_target_pairs={{0,1},{1,0},{2,3},{3,2},{4,5},{5,4},{6,7},{7,6},{8,9},{9,8},{10,11... | collective-permute-start | bytes 638984 | tf_op jit(solution)/shard_map/ppermute | solution.py:275
  65.3 1.0 right_own.3
  66.4 1.3 %collective-permute-start.21 = (f32[104,128]{1,0:T(8,128)S(1)}, f32[104,128]{1,0:T(8,128)S(1)}, u32[]{:S(2)}, u32[]{:S(2)}) collective-permute-start(f32[104,128]{1,0:T(8,128)S(1)} %get-tuple-element.34), channel_id=1, source_target_pairs={{0,8},{8,0},{16,24},{24,16},{1,9},{9,1},{17,25},{25,17},{2,10},{10... | collective-permute-start | bytes 159752 | tf_op jit(solution)/shard_map/ppermute | solution.py:275
  67.7 1.8 %collective-permute-start.22 = (f32[104,128]{1,0:T(8,128)S(1)}, f32[104,128]{1,0:T(8,128)S(1)}, u32[]{:S(2)}, u32[]{:S(2)}) collective-permute-start(f32[104,128]{1,0:T(8,128)S(1)} %get-tuple-element.35), channel_id=1, source_target_pairs={{0,16},{8,24},{16,0},{24,8},{1,17},{9,25},{17,1},{25,9},{2,18},{10... | collective-permute-start | bytes 159752 | tf_op jit(solution)/shard_map/ppermute | solution.py:275
  69.5 0.8 collective-permute-start.23
  70.3 2.1 %collective-permute-done.22.c = f32[104,128]{1,0:T(8,128)S(1)} collective-permute-done((f32[104,128]{1,0:T(8,128)S(1)}, f32[104,128]{1,0:T(8,128)S(1)}, u32[]{:S(2)}, u32[]{:S(2)}) %collective-permute-start.22) | collective-permute-done | bytes 53280 | tf_op jit(solution)/shard_map/ppermute | solution.py:275
  72.4 1.4 %collective-permute-done.23.d = f32[104,128]{1,0:T(8,128)S(1)} collective-permute-done((f32[104,128]{1,0:T(8,128)S(1)}, f32[104,128]{1,0:T(8,128)S(1)}, u32[]{:S(2)}, u32[]{:S(2)}) %collective-permute-start.23) | collective-permute-done | bytes 53280 | tf_op jit(solution)/shard_map/ppermute | solution.py:275
  73.9 1.1 %collective-permute-start.26 = (f32[104,128]{1,0:T(8,128)S(1)}, f32[104,128]{1,0:T(8,128)S(1)}, u32[]{:S(2)}, u32[]{:S(2)}) collective-permute-start(f32[104,128]{1,0:T(8,128)S(1)} %add.6.a), channel_id=1, source_target_pairs={{0,6},{2,4},{4,2},{6,0},{1,7},{3,5},{5,3},{7,1},{8,14},{10,12},{12... | collective-permute-start | bytes 159752 | tf_op jit(solution)/shard_map/ppermute | solution.py:275
  75.0 0.8 collective-permute-start.25
  75.8 1.4 %collective-permute-start.24 = (f32[104,128]{1,0:T(8,128)S(1)}, f32[104,128]{1,0:T(8,128)S(1)}, u32[]{:S(2)}, u32[]{:S(2)}) collective-permute-start(f32[104,128]{1,0:T(8,128)S(1)} %add.6.a), channel_id=1, source_target_pairs={{0,2},{2,0},{4,6},{6,4},{1,3},{3,1},{5,7},{7,5},{8,10},{10,8},{12,... | collective-permute-start | bytes 159752 | tf_op jit(solution)/shard_map/ppermute | solution.py:275
  77.2 0.9 collective-permute-done.26.d
  78.1 1.3 %collective-permute-done.25.c = f32[104,128]{1,0:T(8,128)S(1)} collective-permute-done((f32[104,128]{1,0:T(8,128)S(1)}, f32[104,128]{1,0:T(8,128)S(1)}, u32[]{:S(2)}, u32[]{:S(2)}) %collective-permute-start.25) | collective-permute-done | bytes 53280 | tf_op jit(solution)/shard_map/ppermute | solution.py:275
  79.5 0.9 collective-permute-start.30
  80.4 1.1 %collective-permute-start.29 = (f32[96,128]{1,0:T(8,128)S(1)}, f32[96,128]{1,0:T(8,128)S(1)}, u32[]{:S(2)}, u32[]{:S(2)}) collective-permute-start(f32[96,128]{1,0:T(8,128)S(1)} %get-tuple-element.38.z0), channel_id=1, source_target_pairs={{0,64},{32,96},{64,0},{96,32},{1,65},{33,97},{65,1},{97,33},{2,66}... | collective-permute-start | bytes 147464 | tf_op jit(solution)/shard_map/ppermute | solution.py:275
  81.5 1.3 %collective-permute-start.28 = (f32[96,128]{1,0:T(8,128)S(1)}, f32[96,128]{1,0:T(8,128)S(1)}, u32[]{:S(2)}, u32[]{:S(2)}) collective-permute-start(f32[96,128]{1,0:T(8,128)S(1)} %get-tuple-element.38.z0), channel_id=1, source_target_pairs={{0,32},{32,0},{64,96},{96,64},{1,33},{33,1},{65,97},{97,65},{2,34}... | collective-permute-start | bytes 147464 | tf_op jit(solution)/shard_map/ppermute | solution.py:275
  83.7 1.1 %collective-permute-done.29.z2 = f32[96,128]{1,0:T(8,128)S(1)} collective-permute-done((f32[96,128]{1,0:T(8,128)S(1)}, f32[96,128]{1,0:T(8,128)S(1)}, u32[]{:S(2)}, u32[]{:S(2)}) %collective-permute-start.29) | collective-permute-done | bytes 49184 | tf_op jit(solution)/shard_map/ppermute | solution.py:275
  85.8 2.5 %collective-permute-start.31 = (f32[96,128]{1,0:T(8,128)S(1)}, f32[96,128]{1,0:T(8,128)S(1)}, u32[]{:S(2)}, u32[]{:S(2)}) collective-permute-start(f32[96,128]{1,0:T(8,128)S(1)} %normal.3.q0), channel_id=1, source_target_pairs={{0,8},{8,0},{16,24},{24,16},{1,9},{9,1},{17,25},{25,17},{2,10},{10... | collective-permute-start | bytes 147464 | tf_op jit(solution)/shard_map/ppermute | solution.py:275
  88.3 1.0 collective-permute-done.33.q3
  89.2 0.9 collective-permute-done.32.q2
  90.3 6.3 %collective-permute-start.34 = (f32[4,96,128]{2,1,0:T(8,128)S(1)}, f32[4,96,128]{2,1,0:T(8,128)S(1)}, u32[]{:S(2)}, u32[]{:S(2)}) collective-permute-start(f32[4,96,128]{2,1,0:T(8,128)S(1)} %join.3.q_own), channel_id=1, source_target_pairs={{0,1},{1,0},{2,3},{3,2},{4,5},{5,4},{6,7},{7,6},{8,9},{9,8},{10,11... | collective-permute-start | bytes 589832 | tf_op jit(solution)/shard_map/ppermute | solution.py:275
  96.7 1.1 %collective-permute-done.27.lower_other = f32[8,128]{1,0:T(8,128)S(1)} collective-permute-done((f32[8,128]{1,0:T(8,128)S(1)}, f32[8,128]{1,0:T(8,128)S(1)}, u32[]{:S(2)}, u32[]{:S(2)}) %collective-permute-start.27) | collective-permute-done | bytes 4128 | tf_op jit(solution)/shard_map/ppermute | solution.py:275
  97.8 4.5 %residual.1 = (bf16[2,192,6144]{2,1,0:T(8,128)(2,1)}, bf16[1,2,192,6144]{3,2,1,0:T(8,128)(2,1)}, f32[2,8,6144]{2,1,0:T(8,128)}) custom-call(f32[8,128]{1,0:T(8,128)S(1)} %lower_inverse.3.lower_ref.lower_own, f32[8,128]{1,0:T(8,128)S(1)} %collective-permute-done.27.lower_other, f32[4,96,128]{2,1,0:T(8,128)S(1)} %join.3.q_own, ...), custom_call_target="tpu_custom_call" | custom-call | flops 10000000 | bytes 1000000 | tf_op jit(solution)/shard_map/residual/pallas_call | solution.py:262
  (42 shorter events, 8.7 us)
Async XLA Ops:
  7.8 5.8 %collective-permute-start.2 = (f32[16,192]{1,0:T(8,128)S(1)}, f32[16,192]{1,0:T(8,128)S(1)}, u32[]{:S(2)}, u32[]{:S(2)}) collective-permute-start(f32[16,192]{1,0:T(8,128)S(1)} %get-tuple-element.23.p0), channel_id=1, source_target_pairs={{0,96},{32,64},{64,32},{96,0},{1,97},{33,65},{65,33},{97,1},{2,98}... | collective-permute-start | bytes 36872 | tf_op jit(solution)/shard_map/ppermute | solution.py:275
  12.4 4.1 %collective-permute-start.1 = (f32[16,192]{1,0:T(8,128)S(1)}, f32[16,192]{1,0:T(8,128)S(1)}, u32[]{:S(2)}, u32[]{:S(2)}) collective-permute-start(f32[16,192]{1,0:T(8,128)S(1)} %get-tuple-element.23.p0), channel_id=1, source_target_pairs={{0,64},{32,96},{64,0},{96,32},{1,65},{33,97},{65,1},{97,33},{2,66}... | collective-permute-start | bytes 36872 | tf_op jit(solution)/shard_map/ppermute | solution.py:275
  12.4 4.1 %collective-permute-start = (f32[16,192]{1,0:T(8,128)S(1)}, f32[16,192]{1,0:T(8,128)S(1)}, u32[]{:S(2)}, u32[]{:S(2)}) collective-permute-start(f32[16,192]{1,0:T(8,128)S(1)} %get-tuple-element.23.p0), channel_id=1, source_target_pairs={{0,32},{32,0},{64,96},{96,64},{1,33},{33,1},{65,97},{97,65},{2,34}... | collective-permute-start | bytes 36872 | tf_op jit(solution)/shard_map/ppermute | solution.py:275
  17.5 3.3 %collective-permute-start.3 = (f32[4,104,128]{2,1,0:T(8,128)S(1)}, f32[4,104,128]{2,1,0:T(8,128)S(1)}, u32[]{:S(2)}, u32[]{:S(2)}) collective-permute-start(f32[4,104,128]{2,1,0:T(8,128)S(1)} %right_other.2), channel_id=1, source_target_pairs={{0,1},{1,0},{2,3},{3,2},{4,5},{5,4},{6,7},{7,6},{8,9},{9,8},{10,11... | collective-permute-start | bytes 638984 | tf_op jit(solution)/shard_map/ppermute | solution.py:275
  20.8 3.9 %collective-permute-start.4 = (f32[104,128]{1,0:T(8,128)S(1)}, f32[104,128]{1,0:T(8,128)S(1)}, u32[]{:S(2)}, u32[]{:S(2)}) collective-permute-start(f32[104,128]{1,0:T(8,128)S(1)} %get-tuple-element.27), channel_id=1, source_target_pairs={{0,8},{8,0},{16,24},{24,16},{1,9},{9,1},{17,25},{25,17},{2,10},{10... | collective-permute-start | bytes 159752 | tf_op jit(solution)/shard_map/ppermute | solution.py:275
  22.1 4.9 %collective-permute-start.5 = (f32[104,128]{1,0:T(8,128)S(1)}, f32[104,128]{1,0:T(8,128)S(1)}, u32[]{:S(2)}, u32[]{:S(2)}) collective-permute-start(f32[104,128]{1,0:T(8,128)S(1)} %get-tuple-element.28), channel_id=1, source_target_pairs={{0,16},{8,24},{16,0},{24,8},{1,17},{9,25},{17,1},{25,9},{2,18},{10... | collective-permute-start | bytes 159752 | tf_op jit(solution)/shard_map/ppermute | solution.py:275
  24.6 4.2 %collective-permute-start.6 = (f32[104,128]{1,0:T(8,128)S(1)}, f32[104,128]{1,0:T(8,128)S(1)}, u32[]{:S(2)}, u32[]{:S(2)}) collective-permute-start(f32[104,128]{1,0:T(8,128)S(1)} %get-tuple-element.29), channel_id=1, source_target_pairs={{0,24},{8,16},{16,8},{24,0},{1,25},{9,17},{17,9},{25,1},{2,26},{10... | collective-permute-start | bytes 159752 | tf_op jit(solution)/shard_map/ppermute | solution.py:275
  28.8 4.3 %collective-permute-start.9 = (f32[104,128]{1,0:T(8,128)S(1)}, f32[104,128]{1,0:T(8,128)S(1)}, u32[]{:S(2)}, u32[]{:S(2)}) collective-permute-start(f32[104,128]{1,0:T(8,128)S(1)} %add.4.a), channel_id=1, source_target_pairs={{0,6},{2,4},{4,2},{6,0},{1,7},{3,5},{5,3},{7,1},{8,14},{10,12},{12... | collective-permute-start | bytes 159752 | tf_op jit(solution)/shard_map/ppermute | solution.py:275
  31.6 4.6 %collective-permute-start.8 = (f32[104,128]{1,0:T(8,128)S(1)}, f32[104,128]{1,0:T(8,128)S(1)}, u32[]{:S(2)}, u32[]{:S(2)}) collective-permute-start(f32[104,128]{1,0:T(8,128)S(1)} %add.4.a), channel_id=1, source_target_pairs={{0,4},{2,6},{4,0},{6,2},{1,5},{3,7},{5,1},{7,3},{8,12},{10,14},{12... | collective-permute-start | bytes 159752 | tf_op jit(solution)/shard_map/ppermute | solution.py:275
  31.9 4.2 %collective-permute-start.7 = (f32[104,128]{1,0:T(8,128)S(1)}, f32[104,128]{1,0:T(8,128)S(1)}, u32[]{:S(2)}, u32[]{:S(2)}) collective-permute-start(f32[104,128]{1,0:T(8,128)S(1)} %add.4.a), channel_id=1, source_target_pairs={{0,2},{2,0},{4,6},{6,4},{1,3},{3,1},{5,7},{7,5},{8,10},{10,8},{12,... | collective-permute-start | bytes 159752 | tf_op jit(solution)/shard_map/ppermute | solution.py:275
  36.2 4.2 %collective-permute-start.12 = (f32[96,128]{1,0:T(8,128)S(1)}, f32[96,128]{1,0:T(8,128)S(1)}, u32[]{:S(2)}, u32[]{:S(2)}) collective-permute-start(f32[96,128]{1,0:T(8,128)S(1)} %get-tuple-element.30.z0), channel_id=1, source_target_pairs={{0,96},{32,64},{64,32},{96,0},{1,97},{33,65},{65,33},{97,1},{2,98}... | collective-permute-start | bytes 147464 | tf_op jit(solution)/shard_map/ppermute | solution.py:275
  37.0 4.4 %collective-permute-start.11 = (f32[96,128]{1,0:T(8,128)S(1)}, f32[96,128]{1,0:T(8,128)S(1)}, u32[]{:S(2)}, u32[]{:S(2)}) collective-permute-start(f32[96,128]{1,0:T(8,128)S(1)} %get-tuple-element.30.z0), channel_id=1, source_target_pairs={{0,64},{32,96},{64,0},{96,32},{1,65},{33,97},{65,1},{97,33},{2,66}... | collective-permute-start | bytes 147464 | tf_op jit(solution)/shard_map/ppermute | solution.py:275
  38.1 3.4 %collective-permute-start.10 = (f32[96,128]{1,0:T(8,128)S(1)}, f32[96,128]{1,0:T(8,128)S(1)}, u32[]{:S(2)}, u32[]{:S(2)}) collective-permute-start(f32[96,128]{1,0:T(8,128)S(1)} %get-tuple-element.30.z0), channel_id=1, source_target_pairs={{0,32},{32,0},{64,96},{96,64},{1,33},{33,1},{65,97},{97,65},{2,34}... | collective-permute-start | bytes 147464 | tf_op jit(solution)/shard_map/ppermute | solution.py:275
  41.6 4.2 %collective-permute-start.15 = (f32[96,128]{1,0:T(8,128)S(1)}, f32[96,128]{1,0:T(8,128)S(1)}, u32[]{:S(2)}, u32[]{:S(2)}) collective-permute-start(f32[96,128]{1,0:T(8,128)S(1)} %normal.2.q0), channel_id=1, source_target_pairs={{0,24},{8,16},{16,8},{24,0},{1,25},{9,17},{17,9},{25,1},{2,26},{10... | collective-permute-start | bytes 147464 | tf_op jit(solution)/shard_map/ppermute | solution.py:275
  42.3 4.4 %collective-permute-start.14 = (f32[96,128]{1,0:T(8,128)S(1)}, f32[96,128]{1,0:T(8,128)S(1)}, u32[]{:S(2)}, u32[]{:S(2)}) collective-permute-start(f32[96,128]{1,0:T(8,128)S(1)} %normal.2.q0), channel_id=1, source_target_pairs={{0,16},{8,24},{16,0},{24,8},{1,17},{9,25},{17,1},{25,9},{2,18},{10... | collective-permute-start | bytes 147464 | tf_op jit(solution)/shard_map/ppermute | solution.py:275
  43.0 4.0 %collective-permute-start.13 = (f32[96,128]{1,0:T(8,128)S(1)}, f32[96,128]{1,0:T(8,128)S(1)}, u32[]{:S(2)}, u32[]{:S(2)}) collective-permute-start(f32[96,128]{1,0:T(8,128)S(1)} %normal.2.q0), channel_id=1, source_target_pairs={{0,8},{8,0},{16,24},{24,16},{1,9},{9,1},{17,25},{25,17},{2,10},{10... | collective-permute-start | bytes 147464 | tf_op jit(solution)/shard_map/ppermute | solution.py:275
  47.0 8.0 %collective-permute-start.16 = (f32[4,96,128]{2,1,0:T(8,128)S(1)}, f32[4,96,128]{2,1,0:T(8,128)S(1)}, u32[]{:S(2)}, u32[]{:S(2)}) collective-permute-start(f32[4,96,128]{2,1,0:T(8,128)S(1)} %join.2.q_ref), channel_id=1, source_target_pairs={{0,1},{1,0},{2,3},{3,2},{4,5},{5,4},{6,7},{7,6},{8,9},{9,8},{10,11... | collective-permute-start | bytes 589832 | tf_op jit(solution)/shard_map/ppermute | solution.py:275
  56.5 3.9 %collective-permute-start.19 = (f32[16,192]{1,0:T(8,128)S(1)}, f32[16,192]{1,0:T(8,128)S(1)}, u32[]{:S(2)}, u32[]{:S(2)}) collective-permute-start(f32[16,192]{1,0:T(8,128)S(1)} %left_other.1.p0), channel_id=1, source_target_pairs={{0,96},{32,64},{64,32},{96,0},{1,97},{33,65},{65,33},{97,1},{2,98}... | collective-permute-start | bytes 36872 | tf_op jit(solution)/shard_map/ppermute | solution.py:275
  58.5 4.1 %collective-permute-start.18 = (f32[16,192]{1,0:T(8,128)S(1)}, f32[16,192]{1,0:T(8,128)S(1)}, u32[]{:S(2)}, u32[]{:S(2)}) collective-permute-start(f32[16,192]{1,0:T(8,128)S(1)} %left_other.1.p0), channel_id=1, source_target_pairs={{0,64},{32,96},{64,0},{96,32},{1,65},{33,97},{65,1},{97,33},{2,66}... | collective-permute-start | bytes 36872 | tf_op jit(solution)/shard_map/ppermute | solution.py:275
  59.6 3.0 %collective-permute-start.17 = (f32[16,192]{1,0:T(8,128)S(1)}, f32[16,192]{1,0:T(8,128)S(1)}, u32[]{:S(2)}, u32[]{:S(2)}) collective-permute-start(f32[16,192]{1,0:T(8,128)S(1)} %left_other.1.p0), channel_id=1, source_target_pairs={{0,32},{32,0},{64,96},{96,64},{1,33},{33,1},{65,97},{97,65},{2,34}... | collective-permute-start | bytes 36872 | tf_op jit(solution)/shard_map/ppermute | solution.py:275
  63.6 2.8 %collective-permute-start.20 = (f32[4,104,128]{2,1,0:T(8,128)S(1)}, f32[4,104,128]{2,1,0:T(8,128)S(1)}, u32[]{:S(2)}, u32[]{:S(2)}) collective-permute-start(f32[4,104,128]{2,1,0:T(8,128)S(1)} %right_other.3), channel_id=1, source_target_pairs={{0,1},{1,0},{2,3},{3,2},{4,5},{5,4},{6,7},{7,6},{8,9},{9,8},{10,11... | collective-permute-start | bytes 638984 | tf_op jit(solution)/shard_map/ppermute | solution.py:275
  66.4 3.9 %collective-permute-start.21 = (f32[104,128]{1,0:T(8,128)S(1)}, f32[104,128]{1,0:T(8,128)S(1)}, u32[]{:S(2)}, u32[]{:S(2)}) collective-permute-start(f32[104,128]{1,0:T(8,128)S(1)} %get-tuple-element.34), channel_id=1, source_target_pairs={{0,8},{8,0},{16,24},{24,16},{1,9},{9,1},{17,25},{25,17},{2,10},{10... | collective-permute-start | bytes 159752 | tf_op jit(solution)/shard_map/ppermute | solution.py:275
  67.7 4.8 %collective-permute-start.22 = (f32[104,128]{1,0:T(8,128)S(1)}, f32[104,128]{1,0:T(8,128)S(1)}, u32[]{:S(2)}, u32[]{:S(2)}) collective-permute-start(f32[104,128]{1,0:T(8,128)S(1)} %get-tuple-element.35), channel_id=1, source_target_pairs={{0,16},{8,24},{16,0},{24,8},{1,17},{9,25},{17,1},{25,9},{2,18},{10... | collective-permute-start | bytes 159752 | tf_op jit(solution)/shard_map/ppermute | solution.py:275
  69.5 4.3 %collective-permute-start.23 = (f32[104,128]{1,0:T(8,128)S(1)}, f32[104,128]{1,0:T(8,128)S(1)}, u32[]{:S(2)}, u32[]{:S(2)}) collective-permute-start(f32[104,128]{1,0:T(8,128)S(1)} %get-tuple-element.36), channel_id=1, source_target_pairs={{0,24},{8,16},{16,8},{24,0},{1,25},{9,17},{17,9},{25,1},{2,26},{10... | collective-permute-start | bytes 159752 | tf_op jit(solution)/shard_map/ppermute | solution.py:275
  73.9 4.3 %collective-permute-start.26 = (f32[104,128]{1,0:T(8,128)S(1)}, f32[104,128]{1,0:T(8,128)S(1)}, u32[]{:S(2)}, u32[]{:S(2)}) collective-permute-start(f32[104,128]{1,0:T(8,128)S(1)} %add.6.a), channel_id=1, source_target_pairs={{0,6},{2,4},{4,2},{6,0},{1,7},{3,5},{5,3},{7,1},{8,14},{10,12},{12... | collective-permute-start | bytes 159752 | tf_op jit(solution)/shard_map/ppermute | solution.py:275
  75.0 4.5 %collective-permute-start.25 = (f32[104,128]{1,0:T(8,128)S(1)}, f32[104,128]{1,0:T(8,128)S(1)}, u32[]{:S(2)}, u32[]{:S(2)}) collective-permute-start(f32[104,128]{1,0:T(8,128)S(1)} %add.6.a), channel_id=1, source_target_pairs={{0,4},{2,6},{4,0},{6,2},{1,5},{3,7},{5,1},{7,3},{8,12},{10,14},{12... | collective-permute-start | bytes 159752 | tf_op jit(solution)/shard_map/ppermute | solution.py:275
  75.8 3.7 %collective-permute-start.24 = (f32[104,128]{1,0:T(8,128)S(1)}, f32[104,128]{1,0:T(8,128)S(1)}, u32[]{:S(2)}, u32[]{:S(2)}) collective-permute-start(f32[104,128]{1,0:T(8,128)S(1)} %add.6.a), channel_id=1, source_target_pairs={{0,2},{2,0},{4,6},{6,4},{1,3},{3,1},{5,7},{7,5},{8,10},{10,8},{12,... | collective-permute-start | bytes 159752 | tf_op jit(solution)/shard_map/ppermute | solution.py:275
  79.5 4.2 %collective-permute-start.30 = (f32[96,128]{1,0:T(8,128)S(1)}, f32[96,128]{1,0:T(8,128)S(1)}, u32[]{:S(2)}, u32[]{:S(2)}) collective-permute-start(f32[96,128]{1,0:T(8,128)S(1)} %get-tuple-element.38.z0), channel_id=1, source_target_pairs={{0,96},{32,64},{64,32},{96,0},{1,97},{33,65},{65,33},{97,1},{2,98}... | collective-permute-start | bytes 147464 | tf_op jit(solution)/shard_map/ppermute | solution.py:275
  80.4 4.4 %collective-permute-start.29 = (f32[96,128]{1,0:T(8,128)S(1)}, f32[96,128]{1,0:T(8,128)S(1)}, u32[]{:S(2)}, u32[]{:S(2)}) collective-permute-start(f32[96,128]{1,0:T(8,128)S(1)} %get-tuple-element.38.z0), channel_id=1, source_target_pairs={{0,64},{32,96},{64,0},{96,32},{1,65},{33,97},{65,1},{97,33},{2,66}... | collective-permute-start | bytes 147464 | tf_op jit(solution)/shard_map/ppermute | solution.py:275
  81.5 3.3 %collective-permute-start.28 = (f32[96,128]{1,0:T(8,128)S(1)}, f32[96,128]{1,0:T(8,128)S(1)}, u32[]{:S(2)}, u32[]{:S(2)}) collective-permute-start(f32[96,128]{1,0:T(8,128)S(1)} %get-tuple-element.38.z0), channel_id=1, source_target_pairs={{0,32},{32,0},{64,96},{96,64},{1,33},{33,1},{65,97},{97,65},{2,34}... | collective-permute-start | bytes 147464 | tf_op jit(solution)/shard_map/ppermute | solution.py:275
  84.9 4.3 %collective-permute-start.33 = (f32[96,128]{1,0:T(8,128)S(1)}, f32[96,128]{1,0:T(8,128)S(1)}, u32[]{:S(2)}, u32[]{:S(2)}) collective-permute-start(f32[96,128]{1,0:T(8,128)S(1)} %normal.3.q0), channel_id=1, source_target_pairs={{0,24},{8,16},{16,8},{24,0},{1,25},{9,17},{17,9},{25,1},{2,26},{10... | collective-permute-start | bytes 147464 | tf_op jit(solution)/shard_map/ppermute | solution.py:275
  85.7 4.4 %collective-permute-start.32 = (f32[96,128]{1,0:T(8,128)S(1)}, f32[96,128]{1,0:T(8,128)S(1)}, u32[]{:S(2)}, u32[]{:S(2)}) collective-permute-start(f32[96,128]{1,0:T(8,128)S(1)} %normal.3.q0), channel_id=1, source_target_pairs={{0,16},{8,24},{16,0},{24,8},{1,17},{9,25},{17,1},{25,9},{2,18},{10... | collective-permute-start | bytes 147464 | tf_op jit(solution)/shard_map/ppermute | solution.py:275
  85.8 4.5 %collective-permute-start.31 = (f32[96,128]{1,0:T(8,128)S(1)}, f32[96,128]{1,0:T(8,128)S(1)}, u32[]{:S(2)}, u32[]{:S(2)}) collective-permute-start(f32[96,128]{1,0:T(8,128)S(1)} %normal.3.q0), channel_id=1, source_target_pairs={{0,8},{8,0},{16,24},{24,16},{1,9},{9,1},{17,25},{25,17},{2,10},{10... | collective-permute-start | bytes 147464 | tf_op jit(solution)/shard_map/ppermute | solution.py:275
  90.3 7.5 %collective-permute-start.34 = (f32[4,96,128]{2,1,0:T(8,128)S(1)}, f32[4,96,128]{2,1,0:T(8,128)S(1)}, u32[]{:S(2)}, u32[]{:S(2)}) collective-permute-start(f32[4,96,128]{2,1,0:T(8,128)S(1)} %join.3.q_own), channel_id=1, source_target_pairs={{0,1},{1,0},{2,3},{3,2},{4,5},{5,4},{6,7},{7,6},{8,9},{9,8},{10,11... | collective-permute-start | bytes 589832 | tf_op jit(solution)/shard_map/ppermute | solution.py:275
  96.6 1.2 %collective-permute-start.27 = (f32[8,128]{1,0:T(8,128)S(1)}, f32[8,128]{1,0:T(8,128)S(1)}, u32[]{:S(2)}, u32[]{:S(2)}) collective-permute-start(f32[8,128]{1,0:T(8,128)S(1)} %lower_inverse.3.lower_ref.lower_own), channel_id=1, source_target_pairs={{0,1},{1,0},{2,3},{3,2},{4,5},{5,4},{6,7},{7,6},{8,9},{9,8},{10,11... | collective-permute-start | bytes 12296 | tf_op jit(solution)/shard_map/ppermute | solution.py:275

commit v5 on v4

--- a/solution.py
+++ b/solution.py
@@ -79,69 +79,75 @@
     return jnp.concatenate([a[:, RANK : 2 * RANK], jnp.zeros((8, 120), F32)], axis=1)
 
 
-def block_of(q, h):
-    tiles = range(h * (BLOCK // 128), (h + 1) * (BLOCK // 128))
-    return jnp.concatenate([q[t * 8 : t * 8 + 8, :] for t in tiles], axis=1)
+def block_of(q_ref, k, h):
+    first = k * DEEP + h * (BLOCK // 128) * 8
+    return jnp.concatenate([q_ref[first + i * 8 : first + i * 8 + 8, :] for i in range(BLOCK // 128)], axis=1)
 
 
 def half(k, h):
     return pl.ds(pl.multiple_of((lax.axis_index("x") ^ k) * QUARTER + h * BLOCK, BLOCK), BLOCK)
 
 
+def matrix(slot):
+    parity = lax.axis_index("x") ^ lax.axis_index("y") ^ lax.axis_index("dp")
+    return lax.axis_index("core") ^ (parity & 1) ^ slot
+
+
+def rows(m):
+    return pl.ds(pl.multiple_of(m * 8, 8), 8)
+
+
 def cols(c):
     return slice(c * CHUNK, (c + 1) * CHUNK)
 
 
 def first_left_kernel(g_hbm, e_hbm, q_hbm, p_ref, g_ref, e_ref, q_ref, g_sem, e_sem, q_sem):
-    core = lax.axis_index("core")
     copies = []
-    q_copy = pltpu.make_async_copy(q_hbm, q_ref, q_sem)
-    q_copy.start()
     for c in range(STEPS):
         s = pl.ds(c * CHUNK, CHUNK)
         copies.append((
+            pltpu.make_async_copy(q_hbm.at[:, :, s], q_ref.at[:, :, s], q_sem.at[c]),
             pltpu.make_async_copy(g_hbm.at[0, :, :, s], g_ref.at[:, :, s], g_sem.at[c]),
             pltpu.make_async_copy(e_hbm.at[0, :, :, s], e_ref.at[:, :, s], e_sem.at[c]),
         ))
-        copies[-1][0].start()
-        copies[-1][1].start()
+        for copy in copies[c]:
+            copy.start()
     acc = [jnp.zeros((24, ROWS), F32)] * MATS
-    q_copy.wait()
     for c in range(STEPS):
+        copies[c][0].wait()
         q = [three(q_ref[m, :, cols(c)]) for m in range(MATS)]
-        copies[c][0].wait()
         copies[c][1].wait()
+        copies[c][2].wait()
         for m in range(MATS):
             r = lax.dot_general(q[m], g_ref[m, :, cols(c)], NT, preferred_element_type=F32)
             r = r + lax.dot_general(q[m], e_ref[m, :, cols(c)], NT, preferred_element_type=F32)
             acc[m] = acc[m] + r
     for m in range(MATS):
-        place = pl.multiple_of((core ^ m) * 8, 8)
-        p_ref[pl.ds(place, 8), :] = fold(acc[m])
+        p_ref[m * 8 : m * 8 + 8, :] = fold(acc[m])
 
 
 def first_left(grads, errors, q):
     wide = pltpu.VMEM((MATS, ROWS, COLS), BF16)
     return kernel(
         first_left_kernel, (pltpu.VMEM((16, ROWS), F32), wide, wide), [ANYWHERE] * 3, "first_left",
-        [pltpu.VMEM((MATS, RANK, COLS), F32), pltpu.SemaphoreType.DMA((STEPS,)), pltpu.SemaphoreType.DMA((STEPS,)), pltpu.SemaphoreType.DMA],
+        [pltpu.VMEM((MATS, RANK, COLS), F32)] + [pltpu.SemaphoreType.DMA((STEPS,))] * 3,
     )(hbm(grads), hbm(errors), hbm(q))
 
 
 def left_kernel(slot, q_ref, g_ref, e_ref, *refs):
     p_ref = refs[-1]
-    m = lax.axis_index("core") ^ slot
+    m = matrix(slot)
     acc = jnp.zeros((24, ROWS), F32)
     for k in range(SIDE):
         for h in range(2):
-            q = three(block_of(q_ref[k], h))
+            q = three(block_of(q_ref, k, h))
             acc = acc + lax.dot_general(q, g_ref[m, :, half(k, h)], NT, preferred_element_type=F32)
             acc = acc + lax.dot_general(q, e_ref[m, :, half(k, h)], NT, preferred_element_type=F32)
     if slot == 0:
         p_ref[...] = fold(acc)
     else:
-        p_ref[0:8, :] = refs[0][...]
-        p_ref[8:16, :] = fold(acc)
+        p_ref[rows(matrix(0)), :] = refs[0][...]
+        p_ref[rows(m), :] = fold(acc)
 
 
 def left(q_own, q_other, g, e):
@@ -152,11 +158,11 @@
 
 
 def right_kernel(slot, p0, p1, p2, p3, g_ref, e_ref, o_ref, *mean_ref):
-    m = lax.axis_index("core") ^ slot
+    m = matrix(slot)
     p = ((p0[...] + p1[...]) + (p2[...] + p3[...])) * (1.0 / SIDE)
     if mean_ref:
         mean_ref[0][...] = p
-    p = p[slot * 8 : slot * 8 + 8, :]
+    p = jnp.where(m == 0, p[0:8], p[8:16])
     pieces = three(p)
     gram = lax.dot_general(p, p, NT, precision=lax.Precision.HIGHEST, preferred_element_type=F32)
     gram = jnp.concatenate([gram, jnp.zeros((8, 120), F32)], axis=1)
@@ -218,86 +224,94 @@
     return kernel(normal_kernel, pltpu.VMEM((DEEP, 128), F32), [IN_VMEM] * 5, "normal")(*map(vmem, z_all), vmem(lower))
 
 
-def join_kernel(q0, q1, q2, q3, o_ref):
+def join_kernel(q0, q1, q2, q3, lower_ref, o_ref):
     for k, q_ref in enumerate((q0, q1, q2, q3)):
-        o_ref[k] = q_ref[...]
-
-
-def join(parts):
-    return kernel(join_kernel, pltpu.VMEM((SIDE, DEEP, 128), F32), [IN_VMEM] * SIDE, "join")(*map(vmem, parts))
-
-
-def final_kernel(lower_own, lower_other, q_own, q_other, p_ref, g_ref, e_ref, a_hbm, n_hbm, q_hbm,
-                 p6, a_buf, n_buf, q_buf, a_sem, n_sem, q_sem):
+        o_ref[k * DEEP : (k + 1) * DEEP, :] = q_ref[...]
+    o_ref[SIDE * DEEP :, :] = lower_ref[...]
+
+
+def join(parts, lower):
+    return kernel(join_kernel, pltpu.VMEM((SIDE * DEEP + 8, 128), F32), [IN_VMEM] * 5, "join")(*map(vmem, parts), vmem(lower))
+
+
+def final_kernel(slot, q_ref, p_ref, g_ref, e_ref, *refs):
+    a_hbm, n_hbm, q_hbm, p6, a_buf, n_buf, q_buf, a_sem, n_sem, q_sem = refs[-10:]
+    m = matrix(slot)
     copies = []
-    for slot, (lower_ref, q_ref) in enumerate(((lower_own, q_own), (lower_other, q_other))):
-        m = lax.axis_index("core") ^ slot
-        one, two, rest = split3(small_dot(lower_ref[...], p_ref[slot * 8 : slot * 8 + 8, :]))
-        pieces = jnp.concatenate([one, one, two, two, one, rest, jnp.zeros((80, ROWS), F32)], axis=0)
-        pieces = jnp.concatenate([pieces, jnp.zeros((128, 64), F32)], axis=1)
-        p6[slot] = pieces.T.astype(BF16)
-        left_pieces = p6[slot, 0:ROWS, 0:48]
-        for k in range(SIDE):
-            for h in range(2):
-                i = (slot * SIDE + k) * 2 + h
-                s = half(k, h)
-                q = block_of(q_ref[k], h)
-                q_buf[i] = q
-                one, two, rest = split3(q)
-                pieces = jnp.concatenate([one, two, one, two, rest, one], axis=0).astype(BF16)
-                full = jnp.dot(left_pieces, pieces, preferred_element_type=F32)
-                a_buf[i] = full.astype(BF16)
-                n_buf[i] = (g_ref[m, :, s].astype(F32) + e_ref[m, :, s].astype(F32) - full).astype(BF16)
-                copies.append(pltpu.make_async_copy(a_buf.at[i], a_hbm.at[m, :, s], a_sem.at[i]))
-                copies.append(pltpu.make_async_copy(n_buf.at[i], n_hbm.at[0, m, :, s], n_sem.at[i]))
-                copies.append(pltpu.make_async_copy(q_buf.at[i], q_hbm.at[m, :, s], q_sem.at[i]))
-                for copy in copies[-3:]:
-                    copy.start()
+    one, two, rest = split3(small_dot(q_ref[SIDE * DEEP :, :], p_ref[rows(m), :]))
+    pieces = jnp.concatenate([one, one, two, two, one, rest, jnp.zeros((80, ROWS), F32)], axis=0)
+    pieces = jnp.concatenate([pieces, jnp.zeros((128, 64), F32)], axis=1)
+    p6[...] = pieces.T.astype(BF16)
+    left_pieces = p6[0:ROWS, 0:48]
+    for k in range(SIDE):
+        for h in range(2):
+            i = k * 2 + h
+            s = half(k, h)
+            q = block_of(q_ref, k, h)
+            q_buf[i] = q
+            one, two, rest = split3(q)
+            pieces = jnp.concatenate([one, two, one, two, rest, one], axis=0).astype(BF16)
+            full = jnp.dot(left_pieces, pieces, preferred_element_type=F32)
+            a_buf[i] = full.astype(BF16)
+            n_buf[i] = (g_ref[m, :, s].astype(F32) + e_ref[m, :, s].astype(F32) - full).astype(BF16)
+            copies.append(pltpu.make_async_copy(a_buf.at[i], a_hbm.at[m, :, s], a_sem.at[i]))
+            copies.append(pltpu.make_async_copy(n_buf.at[i], n_hbm.at[0, m, :, s], n_sem.at[i]))
+            copies.append(pltpu.make_async_copy(q_buf.at[i], q_hbm.at[m, :, s], q_sem.at[i]))
+            for copy in copies[-3:]:
+                copy.start()
     for copy in copies:
         copy.wait()
 
 
-def final(lower_own, lower_other, q_own, q_other, p, g, e):
-    n = MATS * SIDE * 2
-    return kernel(
-        final_kernel,
-        (jax.ShapeDtypeStruct((MATS, ROWS, COLS), BF16), jax.ShapeDtypeStruct((1, MATS, ROWS, COLS), BF16),
-         jax.ShapeDtypeStruct((MATS, RANK, COLS), F32)),
-        [IN_VMEM] * 7, "residual",
-        [pltpu.VMEM((MATS, 256, 128), BF16), pltpu.VMEM((n, ROWS, BLOCK), BF16), pltpu.VMEM((n, ROWS, BLOCK), BF16),
-         pltpu.VMEM((n, RANK, BLOCK), F32)] + [pltpu.SemaphoreType.DMA((n,))] * 3,
-        limit=24,
-    )(*map(vmem, (lower_own, lower_other, q_own, q_other, p, g, e)))
+def final(slot, q, p, g, e, before=()):
+    n = SIDE * 2
+    return pl.pallas_call(
+        functools.partial(final_kernel, slot),
+        in_specs=[IN_VMEM] * 4 + [ANYWHERE] * len(before),
+        out_specs=(ANYWHERE,) * 3,
+        out_shape=(jax.ShapeDtypeStruct((MATS, ROWS, COLS), BF16), jax.ShapeDtypeStruct((1, MATS, ROWS, COLS), BF16),
+                   jax.ShapeDtypeStruct((MATS, RANK, COLS), F32)),
+        scratch_shapes=[pltpu.VMEM((256, 128), BF16), pltpu.VMEM((n, ROWS, BLOCK), BF16), pltpu.VMEM((n, ROWS, BLOCK), BF16),
+                        pltpu.VMEM((n, RANK, BLOCK), F32)] + [pltpu.SemaphoreType.DMA((n,))] * 3,
+        input_output_aliases={4 + i: i for i in range(len(before))},
+        compiler_params=pltpu.CompilerParams(vmem_limit_bytes=16 * 1024 * 1024),
+        cost_estimate=pl.CostEstimate(flops=10**9, bytes_accessed=10**7, transcendentals=0),
+        name="residual_own" if slot == 0 else "residual_other",
+    )(*map(vmem, (q, p, g, e)), *before)
 
 
 def swap(a, axis, k):
-    n = lax.axis_size(axis)
-    return lax.ppermute(a, axis, [(i, i ^ k) for i in range(n)])
-
-
-def everyones(a, axis):
-    return (a,) + tuple(swap(a, axis, k) for k in (1, 2, 3))
+    return lax.ppermute(a, axis, [(i, i ^ k) for i in range(lax.axis_size(axis))])
+
+
+def cross(a, axis, k):
+    return lax.ppermute(a, (axis, "core"), [(i * 2 + c, (i ^ k) * 2 + (c ^ (k & 1))) for i in range(SIDE) for c in range(2)])
+
+
+def everyones(a, axis, move):
+    return (a,) + tuple(move(a, axis, k) for k in (1, 2, 3))
 
 
 def right_sum(p_own, g, e, keep):
-    p_all = everyones(p_own, "dp")
+    p_all = everyones(p_own, "dp", swap)
     (theirs,) = right(1, p_all, g, e)
     arrived = swap(theirs, "core", 1)
     mine, *p = right(0, p_all, g, e, keep)
     parts = pick(mine, arrived)
-    (z,) = add((parts[0],) + tuple(swap(parts[k], "x", k) for k in (1, 2, 3)), DEEP + 8)
-    z, gram = add(everyones(z, "y"), DEEP, 8)
-    z_all = everyones(z, "dp")
+    (z,) = add((parts[0],) + tuple(cross(parts[k], "x", k) for k in (1, 2, 3)), DEEP + 8)
+    z, gram = add(everyones(z, "y", cross), DEEP, 8)
+    z_all = everyones(z, "dp", cross)
     lower = lower_inverse(gram)
-    return join(everyones(normal(z_all, lower), "x")), lower, p
+    return join(everyones(normal(z_all, lower), "x", cross), lower), p
 
 
 def per_device(grads, errors, q_init):
     p_own, g, e = first_left(grads, errors, jnp.swapaxes(q_init, 1, 2))
-    q_own, _, _ = right_sum(p_own, g, e, False)
+    q_own, _ = right_sum(p_own, g, e, False)
     p_own = left(q_own, swap(q_own, "core", 1), g, e)
-    q_own, lower, (p,) = right_sum(p_own, g, e, True)
-    approx, errors_next, q_next = final(lower, swap(lower, "core", 1), q_own, swap(q_own, "core", 1), p, g, e)
+    q_own, (p,) = right_sum(p_own, g, e, True)
+    q_other = swap(q_own, "core", 1)
+    approx, errors_next, q_next = final(1, q_other, p, g, e, final(0, q_own, p, g, e))
     return approx, errors_next, jnp.swapaxes(q_next, 1, 2)
 
 

time: 103 us -> 100 us (0.971)
  starting transfers between devices: 53.4 us -> 46.8 us
  waiting for transfers between devices: 27.8 us -> 32.5 us
    ppermute x35 -> x34, starting transfers between devices: 53.4 us -> 46.8 us  [the longest x24 32.5 us: cross(): lax.ppermute(a, (axis, 'core'), [(i * 2 + c, (i ^ k) * 2 + (c ^ k & 1)) f...]
    ppermute x35 -> x34, waiting for transfers between devices: 27.8 us -> 32.5 us  [the longest x24 26.7 us: cross(): lax.ppermute(a, (axis, 'core'), [(i * 2 + c, (i ^ k) * 2 + (c ^ k & 1)) f...]
    pallas_call x1, Pallas kernels: 7.15 us -> 5.25 us  [first_left(): kernel(first_left_kernel, (pltpu.VMEM((16, ROWS), F32), wide, wide), [ANY...]
    pallas_call x3 -> x4, Pallas kernels: 4.57 us -> 5.71 us  [the longest x2 5.68 us: final(): pl.pallas_call(functools.partial(final_kernel, slot), in_specs=[IN_VMEM]...]
  transfers between devices with their start and end apart: 35 -> 34, of which waited for: 26 -> 26; matrix products, arithmetic and copies ran while one was open for 0% -> 0% of each run, Pallas kernels for 5% -> 8%
where the time goes in v5:
time: 100 us; the launch traced here: 99.9 us
  starting transfers between devices  46.8 us (47%)
  waiting for transfers between devices  32.5 us (32%)
  Pallas kernels  19.7 us (20%)
    ppermute x24, starting transfers between devices, cross(): lax.ppermute(a, (axis, 'core'), [(i * 2 + c, (i ^ k) * 2 + (c ^ k & 1)) f...  32.5 us
    ppermute x24, waiting for transfers between devices, cross(): lax.ppermute(a, (axis, 'core'), [(i * 2 + c, (i ^ k) * 2 + (c ^ k & 1)) f...  26.7 us
    ppermute x10, starting transfers between devices, swap(): lax.ppermute(a, axis, [(i, i ^ k) for i in range(lax.axis_size(axis))])  14.2 us
    ppermute x10, waiting for transfers between devices, swap(): lax.ppermute(a, axis, [(i, i ^ k) for i in range(lax.axis_size(axis))])  5.77 us
    pallas_call x2, Pallas kernels, final(): pl.pallas_call(functools.partial(final_kernel, slot), in_specs=[IN_VMEM]...  5.68 us
    pallas_call x1, Pallas kernels, first_left(): kernel(first_left_kernel, (pltpu.VMEM((16, ROWS), F32), wide, wide), [ANY...  5.25 us
    pallas_call x4, Pallas kernels, right(): kernel(functools.partial(right_kernel, slot), out, [IN_VMEM] * 6, 'right_...  3.89 us
  transfers between devices with their start and end apart: 34, of which 26 were waited for; matrix products, arithmetic and copies ran while one was open for 0% of the time, Pallas kernels for 8%

profile of v5, /device:TPU:1, one launch (start us, length us, event | category | flops | bytes accessed | tf_op | source)
XLA Modules:
  0.0 99.9 jit_solution(11189047155870044910)
XLA Ops:
  0.6 5.3 %first_left.1 = (f32[16,192]{1,0:T(8,128)S(1)}, bf16[2,192,6144]{2,1,0:T(8,128)(2,1)S(1)}, bf16[2,192,6144]{2,1,0:T(8,128)(2,1)S(1)}) custom-call(bf16[1,2,192,6144]{3,2,1,0:T(8,128)(2,1)} %g_hbm.1, bf16[1,2,192,6144]{3,2,1,0:T(8,128)(2,1)} %e_hbm.1, f32[2,8,6144]{2,1,0:T(8,128)} %bitcast.2), custom_call_target="tpu_custom_call" | custom-call | flops 10000000 | bytes 1000000 | tf_op jit(solution)/shard_map/first_left/pallas_call | solution.py:131
  5.9 4.7 %collective-permute-start.2 = (f32[16,192]{1,0:T(8,128)S(1)}, f32[16,192]{1,0:T(8,128)S(1)}, u32[]{:S(2)}, u32[]{:S(2)}) collective-permute-start(f32[16,192]{1,0:T(8,128)S(1)} %get-tuple-element.26.p0), channel_id=1, source_target_pairs={{0,96},{32,64},{64,32},{96,0},{1,97},{33,65},{65,33},{97,1},{2,98}... | collective-permute-start | bytes 36872 | tf_op jit(solution)/shard_map/ppermute | solution.py:284
  11.7 3.0 %collective-permute-done.1.p2 = f32[16,192]{1,0:T(8,128)S(1)} collective-permute-done((f32[16,192]{1,0:T(8,128)S(1)}, f32[16,192]{1,0:T(8,128)S(1)}, u32[]{:S(2)}, u32[]{:S(2)}) %collective-permute-start.1) | collective-permute-done | bytes 12320 | tf_op jit(solution)/shard_map/ppermute | solution.py:284
  14.7 1.0 right_other.2
  15.6 2.2 %collective-permute-start.3 = (f32[4,104,128]{2,1,0:T(8,128)S(1)}, f32[4,104,128]{2,1,0:T(8,128)S(1)}, u32[]{:S(2)}, u32[]{:S(2)}) collective-permute-start(f32[4,104,128]{2,1,0:T(8,128)S(1)} %right_other.2), channel_id=1, source_target_pairs={{0,1},{1,0},{2,3},{3,2},{4,5},{5,4},{6,7},{7,6},{8,9},{9,8},{10,11... | collective-permute-start | bytes 638984 | tf_op jit(solution)/shard_map/ppermute | solution.py:284
  17.8 1.0 right_own.2.mine_ref
  18.9 1.6 %collective-permute-start.4 = (f32[104,128]{1,0:T(8,128)S(1)}, f32[104,128]{1,0:T(8,128)S(1)}, u32[]{:S(2)}, u32[]{:S(2)}) collective-permute-start(f32[104,128]{1,0:T(8,128)S(1)} %get-tuple-element.30), channel_id=1, source_target_pairs={{0,9},{1,8},{8,1},{9,0},{16,25},{17,24},{24,17},{25,16},{2,11},{3,... | collective-permute-start | bytes 159752 | tf_op jit(solution)/shard_map/ppermute | solution.py:288
  20.5 2.4 %collective-permute-start.5 = (f32[104,128]{1,0:T(8,128)S(1)}, f32[104,128]{1,0:T(8,128)S(1)}, u32[]{:S(2)}, u32[]{:S(2)}) collective-permute-start(f32[104,128]{1,0:T(8,128)S(1)} %get-tuple-element.31), channel_id=1, source_target_pairs={{0,16},{1,17},{8,24},{9,25},{16,0},{17,1},{24,8},{25,9},{2,18},{3,... | collective-permute-start | bytes 159752 | tf_op jit(solution)/shard_map/ppermute | solution.py:288
  23.5 2.7 %collective-permute-done.5.c = f32[104,128]{1,0:T(8,128)S(1)} collective-permute-done((f32[104,128]{1,0:T(8,128)S(1)}, f32[104,128]{1,0:T(8,128)S(1)}, u32[]{:S(2)}, u32[]{:S(2)}) %collective-permute-start.5) | collective-permute-done | bytes 53280 | tf_op jit(solution)/shard_map/ppermute | solution.py:288
  26.1 1.9 %collective-permute-done.6.d = f32[104,128]{1,0:T(8,128)S(1)} collective-permute-done((f32[104,128]{1,0:T(8,128)S(1)}, f32[104,128]{1,0:T(8,128)S(1)}, u32[]{:S(2)}, u32[]{:S(2)}) %collective-permute-start.6) | collective-permute-done | bytes 53280 | tf_op jit(solution)/shard_map/ppermute | solution.py:288
  28.1 3.1 %collective-permute-start.9 = (f32[104,128]{1,0:T(8,128)S(1)}, f32[104,128]{1,0:T(8,128)S(1)}, u32[]{:S(2)}, u32[]{:S(2)}) collective-permute-start(f32[104,128]{1,0:T(8,128)S(1)} %add.4.a), channel_id=1, source_target_pairs={{0,7},{1,6},{2,5},{3,4},{4,3},{5,2},{6,1},{7,0},{8,15},{9,14},{10,... | collective-permute-start | bytes 159752 | tf_op jit(solution)/shard_map/ppermute | solution.py:288
  32.1 1.4 %collective-permute-done.9.d = f32[104,128]{1,0:T(8,128)S(1)} collective-permute-done((f32[104,128]{1,0:T(8,128)S(1)}, f32[104,128]{1,0:T(8,128)S(1)}, u32[]{:S(2)}, u32[]{:S(2)}) %collective-permute-start.9) | collective-permute-done | bytes 53280 | tf_op jit(solution)/shard_map/ppermute | solution.py:288
  33.5 2.5 %collective-permute-done.8.c = f32[104,128]{1,0:T(8,128)S(1)} collective-permute-done((f32[104,128]{1,0:T(8,128)S(1)}, f32[104,128]{1,0:T(8,128)S(1)}, u32[]{:S(2)}, u32[]{:S(2)}) %collective-permute-start.8) | collective-permute-done | bytes 53280 | tf_op jit(solution)/shard_map/ppermute | solution.py:288
  36.1 1.9 %collective-permute-start.12 = (f32[96,128]{1,0:T(8,128)S(1)}, f32[96,128]{1,0:T(8,128)S(1)}, u32[]{:S(2)}, u32[]{:S(2)}) collective-permute-start(f32[96,128]{1,0:T(8,128)S(1)} %get-tuple-element.33.z0), channel_id=1, source_target_pairs={{0,97},{1,96},{32,65},{33,64},{64,33},{65,32},{96,1},{97,0},{2,99}... | collective-permute-start | bytes 147464 | tf_op jit(solution)/shard_map/ppermute | solution.py:288
  38.8 1.2 %collective-permute-start.10 = (f32[96,128]{1,0:T(8,128)S(1)}, f32[96,128]{1,0:T(8,128)S(1)}, u32[]{:S(2)}, u32[]{:S(2)}) collective-permute-start(f32[96,128]{1,0:T(8,128)S(1)} %get-tuple-element.33.z0), channel_id=1, source_target_pairs={{0,33},{1,32},{32,1},{33,0},{64,97},{65,96},{96,65},{97,64},{2,35}... | collective-permute-start | bytes 147464 | tf_op jit(solution)/shard_map/ppermute | solution.py:288
  40.9 2.4 %collective-permute-done.11.z2 = f32[96,128]{1,0:T(8,128)S(1)} collective-permute-done((f32[96,128]{1,0:T(8,128)S(1)}, f32[96,128]{1,0:T(8,128)S(1)}, u32[]{:S(2)}, u32[]{:S(2)}) %collective-permute-start.11) | collective-permute-done | bytes 49184 | tf_op jit(solution)/shard_map/ppermute | solution.py:288
  43.4 1.5 %collective-permute-start.15 = (f32[96,128]{1,0:T(8,128)S(1)}, f32[96,128]{1,0:T(8,128)S(1)}, u32[]{:S(2)}, u32[]{:S(2)}) collective-permute-start(f32[96,128]{1,0:T(8,128)S(1)} %normal.2.q0), channel_id=1, source_target_pairs={{0,25},{1,24},{8,17},{9,16},{16,9},{17,8},{24,1},{25,0},{2,27},{3,... | collective-permute-start | bytes 147464 | tf_op jit(solution)/shard_map/ppermute | solution.py:288
  45.4 1.9 %collective-permute-start.13 = (f32[96,128]{1,0:T(8,128)S(1)}, f32[96,128]{1,0:T(8,128)S(1)}, u32[]{:S(2)}, u32[]{:S(2)}) collective-permute-start(f32[96,128]{1,0:T(8,128)S(1)} %normal.2.q0), channel_id=1, source_target_pairs={{0,9},{1,8},{8,1},{9,0},{16,25},{17,24},{24,17},{25,16},{2,11},{3,... | collective-permute-start | bytes 147464 | tf_op jit(solution)/shard_map/ppermute | solution.py:288
  47.3 1.7 %collective-permute-done.15.q3 = f32[96,128]{1,0:T(8,128)S(1)} collective-permute-done((f32[96,128]{1,0:T(8,128)S(1)}, f32[96,128]{1,0:T(8,128)S(1)}, u32[]{:S(2)}, u32[]{:S(2)}) %collective-permute-start.15) | collective-permute-done | bytes 49184 | tf_op jit(solution)/shard_map/ppermute | solution.py:288
  51.0 1.6 %left_own.1.refs_0_ = f32[8,192]{1,0:T(8,128)S(1)} custom-call(f32[392,128]{1,0:T(8,128)S(1)} %join.2.q_ref, bf16[2,192,6144]{2,1,0:T(8,128)(2,1)S(1)} %get-tuple-element.27.g_ref, bf16[2,192,6144]{2,1,0:T(8,128)(2,1)S(1)} %get-tuple-element.28.e_ref), custom_call_target="tpu_custom_call" | custom-call | flops 1000000000 | bytes 1000000 | tf_op jit(solution)/shard_map/left_own/pallas_call | solution.py:154
  52.5 1.6 %left_other.1.p0 = f32[16,192]{1,0:T(8,128)S(1)} custom-call(f32[392,128]{1,0:T(8,128)S(1)} %collective-permute-done.16.q_ref, bf16[2,192,6144]{2,1,0:T(8,128)(2,1)S(1)} %get-tuple-element.27.g_ref, bf16[2,192,6144]{2,1,0:T(8,128)(2,1)S(1)} %get-tuple-element.28.e_ref, f32[8,192]{1,0:T(8,128)S(1)} %left_own.1.refs_0_), custom_call_target="tpu_custom_call" | custom-call | flops 10000000 | bytes 1000000 | tf_op jit(solution)/shard_map/left_other/pallas_call | solution.py:156
  54.1 1.4 %collective-permute-start.19 = (f32[16,192]{1,0:T(8,128)S(1)}, f32[16,192]{1,0:T(8,128)S(1)}, u32[]{:S(2)}, u32[]{:S(2)}) collective-permute-start(f32[16,192]{1,0:T(8,128)S(1)} %left_other.1.p0), channel_id=1, source_target_pairs={{0,96},{32,64},{64,32},{96,0},{1,97},{33,65},{65,33},{97,1},{2,98}... | collective-permute-start | bytes 36872 | tf_op jit(solution)/shard_map/ppermute | solution.py:284
  55.5 0.9 collective-permute-start.18
  56.4 1.1 %collective-permute-start.17 = (f32[16,192]{1,0:T(8,128)S(1)}, f32[16,192]{1,0:T(8,128)S(1)}, u32[]{:S(2)}, u32[]{:S(2)}) collective-permute-start(f32[16,192]{1,0:T(8,128)S(1)} %left_other.1.p0), channel_id=1, source_target_pairs={{0,32},{32,0},{64,96},{96,64},{1,33},{33,1},{65,97},{97,65},{2,34}... | collective-permute-start | bytes 36872 | tf_op jit(solution)/shard_map/ppermute | solution.py:284
  58.1 1.6 %collective-permute-done.18.p2 = f32[16,192]{1,0:T(8,128)S(1)} collective-permute-done((f32[16,192]{1,0:T(8,128)S(1)}, f32[16,192]{1,0:T(8,128)S(1)}, u32[]{:S(2)}, u32[]{:S(2)}) %collective-permute-start.18) | collective-permute-done | bytes 12320 | tf_op jit(solution)/shard_map/ppermute | solution.py:284
  59.6 1.0 right_other.3
  60.6 1.9 %collective-permute-start.20 = (f32[4,104,128]{2,1,0:T(8,128)S(1)}, f32[4,104,128]{2,1,0:T(8,128)S(1)}, u32[]{:S(2)}, u32[]{:S(2)}) collective-permute-start(f32[4,104,128]{2,1,0:T(8,128)S(1)} %right_other.3), channel_id=1, source_target_pairs={{0,1},{1,0},{2,3},{3,2},{4,5},{5,4},{6,7},{7,6},{8,9},{9,8},{10,11... | collective-permute-start | bytes 638984 | tf_op jit(solution)/shard_map/ppermute | solution.py:284
  62.5 1.0 right_own.3
  63.6 1.1 %collective-permute-start.21 = (f32[104,128]{1,0:T(8,128)S(1)}, f32[104,128]{1,0:T(8,128)S(1)}, u32[]{:S(2)}, u32[]{:S(2)}) collective-permute-start(f32[104,128]{1,0:T(8,128)S(1)} %get-tuple-element.37), channel_id=1, source_target_pairs={{0,9},{1,8},{8,1},{9,0},{16,25},{17,24},{24,17},{25,16},{2,11},{3,... | collective-permute-start | bytes 159752 | tf_op jit(solution)/shard_map/ppermute | solution.py:288
  64.7 2.1 %collective-permute-start.22 = (f32[104,128]{1,0:T(8,128)S(1)}, f32[104,128]{1,0:T(8,128)S(1)}, u32[]{:S(2)}, u32[]{:S(2)}) collective-permute-start(f32[104,128]{1,0:T(8,128)S(1)} %get-tuple-element.38), channel_id=1, source_target_pairs={{0,16},{1,17},{8,24},{9,25},{16,0},{17,1},{24,8},{25,9},{2,18},{3,... | collective-permute-start | bytes 159752 | tf_op jit(solution)/shard_map/ppermute | solution.py:288
  66.8 1.3 %collective-permute-start.23 = (f32[104,128]{1,0:T(8,128)S(1)}, f32[104,128]{1,0:T(8,128)S(1)}, u32[]{:S(2)}, u32[]{:S(2)}) collective-permute-start(f32[104,128]{1,0:T(8,128)S(1)} %get-tuple-element.39), channel_id=1, source_target_pairs={{0,25},{1,24},{8,17},{9,16},{16,9},{17,8},{24,1},{25,0},{2,27},{3,... | collective-permute-start | bytes 159752 | tf_op jit(solution)/shard_map/ppermute | solution.py:288
  68.1 1.9 %collective-permute-done.22.c = f32[104,128]{1,0:T(8,128)S(1)} collective-permute-done((f32[104,128]{1,0:T(8,128)S(1)}, f32[104,128]{1,0:T(8,128)S(1)}, u32[]{:S(2)}, u32[]{:S(2)}) %collective-permute-start.22) | collective-permute-done | bytes 53280 | tf_op jit(solution)/shard_map/ppermute | solution.py:288
  70.0 1.9 %collective-permute-done.23.d = f32[104,128]{1,0:T(8,128)S(1)} collective-permute-done((f32[104,128]{1,0:T(8,128)S(1)}, f32[104,128]{1,0:T(8,128)S(1)}, u32[]{:S(2)}, u32[]{:S(2)}) %collective-permute-start.23) | collective-permute-done | bytes 53280 | tf_op jit(solution)/shard_map/ppermute | solution.py:288
  71.9 1.6 %collective-permute-start.26 = (f32[104,128]{1,0:T(8,128)S(1)}, f32[104,128]{1,0:T(8,128)S(1)}, u32[]{:S(2)}, u32[]{:S(2)}) collective-permute-start(f32[104,128]{1,0:T(8,128)S(1)} %add.6.a), channel_id=1, source_target_pairs={{0,7},{1,6},{2,5},{3,4},{4,3},{5,2},{6,1},{7,0},{8,15},{9,14},{10,... | collective-permute-start | bytes 159752 | tf_op jit(solution)/shard_map/ppermute | solution.py:288
  74.2 1.6 %collective-permute-start.24 = (f32[104,128]{1,0:T(8,128)S(1)}, f32[104,128]{1,0:T(8,128)S(1)}, u32[]{:S(2)}, u32[]{:S(2)}) collective-permute-start(f32[104,128]{1,0:T(8,128)S(1)} %add.6.a), channel_id=1, source_target_pairs={{0,3},{1,2},{2,1},{3,0},{4,7},{5,6},{6,5},{7,4},{8,11},{9,10},{10,... | collective-permute-start | bytes 159752 | tf_op jit(solution)/shard_map/ppermute | solution.py:288
  75.8 1.2 %collective-permute-done.26.d = f32[104,128]{1,0:T(8,128)S(1)} collective-permute-done((f32[104,128]{1,0:T(8,128)S(1)}, f32[104,128]{1,0:T(8,128)S(1)}, u32[]{:S(2)}, u32[]{:S(2)}) %collective-permute-start.26) | collective-permute-done | bytes 53280 | tf_op jit(solution)/shard_map/ppermute | solution.py:288
  77.1 1.4 %collective-permute-done.25.c = f32[104,128]{1,0:T(8,128)S(1)} collective-permute-done((f32[104,128]{1,0:T(8,128)S(1)}, f32[104,128]{1,0:T(8,128)S(1)}, u32[]{:S(2)}, u32[]{:S(2)}) %collective-permute-start.25) | collective-permute-done | bytes 53280 | tf_op jit(solution)/shard_map/ppermute | solution.py:288
  79.1 1.3 %collective-permute-start.29 = (f32[96,128]{1,0:T(8,128)S(1)}, f32[96,128]{1,0:T(8,128)S(1)}, u32[]{:S(2)}, u32[]{:S(2)}) collective-permute-start(f32[96,128]{1,0:T(8,128)S(1)} %get-tuple-element.40.z0), channel_id=1, source_target_pairs={{0,97},{1,96},{32,65},{33,64},{64,33},{65,32},{96,1},{97,0},{2,99}... | collective-permute-start | bytes 147464 | tf_op jit(solution)/shard_map/ppermute | solution.py:288
  80.5 1.1 %collective-permute-start.28 = (f32[96,128]{1,0:T(8,128)S(1)}, f32[96,128]{1,0:T(8,128)S(1)}, u32[]{:S(2)}, u32[]{:S(2)}) collective-permute-start(f32[96,128]{1,0:T(8,128)S(1)} %get-tuple-element.40.z0), channel_id=1, source_target_pairs={{0,64},{1,65},{32,96},{33,97},{64,0},{65,1},{96,32},{97,33},{2,66}... | collective-permute-start | bytes 147464 | tf_op jit(solution)/shard_map/ppermute | solution.py:288
  81.5 1.5 %collective-permute-start.27 = (f32[96,128]{1,0:T(8,128)S(1)}, f32[96,128]{1,0:T(8,128)S(1)}, u32[]{:S(2)}, u32[]{:S(2)}) collective-permute-start(f32[96,128]{1,0:T(8,128)S(1)} %get-tuple-element.40.z0), channel_id=1, source_target_pairs={{0,33},{1,32},{32,1},{33,0},{64,97},{65,96},{96,65},{97,64},{2,35}... | collective-permute-start | bytes 147464 | tf_op jit(solution)/shard_map/ppermute | solution.py:288
  84.9 1.1 %collective-permute-done.27.z1 = f32[96,128]{1,0:T(8,128)S(1)} collective-permute-done((f32[96,128]{1,0:T(8,128)S(1)}, f32[96,128]{1,0:T(8,128)S(1)}, u32[]{:S(2)}, u32[]{:S(2)}) %collective-permute-start.27) | collective-permute-done | bytes 49184 | tf_op jit(solution)/shard_map/ppermute | solution.py:288
  86.1 1.7 %collective-permute-start.32 = (f32[96,128]{1,0:T(8,128)S(1)}, f32[96,128]{1,0:T(8,128)S(1)}, u32[]{:S(2)}, u32[]{:S(2)}) collective-permute-start(f32[96,128]{1,0:T(8,128)S(1)} %normal.3.q0), channel_id=1, source_target_pairs={{0,25},{1,24},{8,17},{9,16},{16,9},{17,8},{24,1},{25,0},{2,27},{3,... | collective-permute-start | bytes 147464 | tf_op jit(solution)/shard_map/ppermute | solution.py:288
  87.9 2.1 %collective-permute-start.30 = (f32[96,128]{1,0:T(8,128)S(1)}, f32[96,128]{1,0:T(8,128)S(1)}, u32[]{:S(2)}, u32[]{:S(2)}) collective-permute-start(f32[96,128]{1,0:T(8,128)S(1)} %normal.3.q0), channel_id=1, source_target_pairs={{0,9},{1,8},{8,1},{9,0},{16,25},{17,24},{24,17},{25,16},{2,11},{3,... | collective-permute-start | bytes 147464 | tf_op jit(solution)/shard_map/ppermute | solution.py:288
  90.0 1.1 %collective-permute-done.32.q3 = f32[96,128]{1,0:T(8,128)S(1)} collective-permute-done((f32[96,128]{1,0:T(8,128)S(1)}, f32[96,128]{1,0:T(8,128)S(1)}, u32[]{:S(2)}, u32[]{:S(2)}) %collective-permute-start.32) | collective-permute-done | bytes 49184 | tf_op jit(solution)/shard_map/ppermute | solution.py:288
  91.1 1.1 %collective-permute-done.31.q2 = f32[96,128]{1,0:T(8,128)S(1)} collective-permute-done((f32[96,128]{1,0:T(8,128)S(1)}, f32[96,128]{1,0:T(8,128)S(1)}, u32[]{:S(2)}, u32[]{:S(2)}) %collective-permute-start.31) | collective-permute-done | bytes 49184 | tf_op jit(solution)/shard_map/ppermute | solution.py:288
  93.0 1.0 collective-permute-start.33
  94.0 2.8 %residual_own.1 = (bf16[2,192,6144]{2,1,0:T(8,128)(2,1)}, bf16[1,2,192,6144]{3,2,1,0:T(8,128)(2,1)}, f32[2,8,6144]{2,1,0:T(8,128)}) custom-call(f32[392,128]{1,0:T(8,128)S(1)} %join.3.q_ref, f32[16,192]{1,0:T(8,128)S(1)} %get-tuple-element.42.p_ref, bf16[2,192,6144]{2,1,0:T(8,128)(2,1)S(1)} %get-tuple-element.27.g_ref, ...), custom_call_target="tpu_custom_call" | custom-call | flops 1000000000 | bytes 10000000 | tf_op jit(solution)/shard_map/residual_own/pallas_call | solution.py:268
  96.9 2.8 %residual_other.1 = (bf16[2,192,6144]{2,1,0:T(8,128)(2,1)}, bf16[1,2,192,6144]{3,2,1,0:T(8,128)(2,1)}, f32[2,8,6144]{2,1,0:T(8,128)}) custom-call(f32[392,128]{1,0:T(8,128)S(1)} %collective-permute-done.33.q_ref, f32[16,192]{1,0:T(8,128)S(1)} %get-tuple-element.42.p_ref, ...), custom_call_target="tpu_custom_call", output_to_operand_aliasing={{0}: (4, {}), {1}: (5, {}), {2}: (6, {})} | custom-call | flops 1000000000 | bytes 10000000 | tf_op jit(solution)/shard_map/residual_other/pallas_call | solution.py:268
  (41 shorter events, 11.9 us)
Async XLA Ops:
  5.9 5.8 %collective-permute-start.2 = (f32[16,192]{1,0:T(8,128)S(1)}, f32[16,192]{1,0:T(8,128)S(1)}, u32[]{:S(2)}, u32[]{:S(2)}) collective-permute-start(f32[16,192]{1,0:T(8,128)S(1)} %get-tuple-element.26.p0), channel_id=1, source_target_pairs={{0,96},{32,64},{64,32},{96,0},{1,97},{33,65},{65,33},{97,1},{2,98}... | collective-permute-start | bytes 36872 | tf_op jit(solution)/shard_map/ppermute | solution.py:284
  10.6 4.1 %collective-permute-start.1 = (f32[16,192]{1,0:T(8,128)S(1)}, f32[16,192]{1,0:T(8,128)S(1)}, u32[]{:S(2)}, u32[]{:S(2)}) collective-permute-start(f32[16,192]{1,0:T(8,128)S(1)} %get-tuple-element.26.p0), channel_id=1, source_target_pairs={{0,64},{32,96},{64,0},{96,32},{1,65},{33,97},{65,1},{97,33},{2,66}... | collective-permute-start | bytes 36872 | tf_op jit(solution)/shard_map/ppermute | solution.py:284
  10.6 4.1 %collective-permute-start = (f32[16,192]{1,0:T(8,128)S(1)}, f32[16,192]{1,0:T(8,128)S(1)}, u32[]{:S(2)}, u32[]{:S(2)}) collective-permute-start(f32[16,192]{1,0:T(8,128)S(1)} %get-tuple-element.26.p0), channel_id=1, source_target_pairs={{0,32},{32,0},{64,96},{96,64},{1,33},{33,1},{65,97},{97,65},{2,34}... | collective-permute-start | bytes 36872 | tf_op jit(solution)/shard_map/ppermute | solution.py:284
  15.6 3.3 %collective-permute-start.3 = (f32[4,104,128]{2,1,0:T(8,128)S(1)}, f32[4,104,128]{2,1,0:T(8,128)S(1)}, u32[]{:S(2)}, u32[]{:S(2)}) collective-permute-start(f32[4,104,128]{2,1,0:T(8,128)S(1)} %right_other.2), channel_id=1, source_target_pairs={{0,1},{1,0},{2,3},{3,2},{4,5},{5,4},{6,7},{7,6},{8,9},{9,8},{10,11... | collective-permute-start | bytes 638984 | tf_op jit(solution)/shard_map/ppermute | solution.py:284
  18.9 4.5 %collective-permute-start.4 = (f32[104,128]{1,0:T(8,128)S(1)}, f32[104,128]{1,0:T(8,128)S(1)}, u32[]{:S(2)}, u32[]{:S(2)}) collective-permute-start(f32[104,128]{1,0:T(8,128)S(1)} %get-tuple-element.30), channel_id=1, source_target_pairs={{0,9},{1,8},{8,1},{9,0},{16,25},{17,24},{24,17},{25,16},{2,11},{3,... | collective-permute-start | bytes 159752 | tf_op jit(solution)/shard_map/ppermute | solution.py:288
  20.5 5.7 %collective-permute-start.5 = (f32[104,128]{1,0:T(8,128)S(1)}, f32[104,128]{1,0:T(8,128)S(1)}, u32[]{:S(2)}, u32[]{:S(2)}) collective-permute-start(f32[104,128]{1,0:T(8,128)S(1)} %get-tuple-element.31), channel_id=1, source_target_pairs={{0,16},{1,17},{8,24},{9,25},{16,0},{17,1},{24,8},{25,9},{2,18},{3,... | collective-permute-start | bytes 159752 | tf_op jit(solution)/shard_map/ppermute | solution.py:288
  22.9 5.1 %collective-permute-start.6 = (f32[104,128]{1,0:T(8,128)S(1)}, f32[104,128]{1,0:T(8,128)S(1)}, u32[]{:S(2)}, u32[]{:S(2)}) collective-permute-start(f32[104,128]{1,0:T(8,128)S(1)} %get-tuple-element.32), channel_id=1, source_target_pairs={{0,25},{1,24},{8,17},{9,16},{16,9},{17,8},{24,1},{25,0},{2,27},{3,... | collective-permute-start | bytes 159752 | tf_op jit(solution)/shard_map/ppermute | solution.py:288
  28.1 5.5 %collective-permute-start.9 = (f32[104,128]{1,0:T(8,128)S(1)}, f32[104,128]{1,0:T(8,128)S(1)}, u32[]{:S(2)}, u32[]{:S(2)}) collective-permute-start(f32[104,128]{1,0:T(8,128)S(1)} %add.4.a), channel_id=1, source_target_pairs={{0,7},{1,6},{2,5},{3,4},{4,3},{5,2},{6,1},{7,0},{8,15},{9,14},{10,... | collective-permute-start | bytes 159752 | tf_op jit(solution)/shard_map/ppermute | solution.py:288
  31.2 4.9 %collective-permute-start.8 = (f32[104,128]{1,0:T(8,128)S(1)}, f32[104,128]{1,0:T(8,128)S(1)}, u32[]{:S(2)}, u32[]{:S(2)}) collective-permute-start(f32[104,128]{1,0:T(8,128)S(1)} %add.4.a), channel_id=1, source_target_pairs={{0,4},{1,5},{2,6},{3,7},{4,0},{5,1},{6,2},{7,3},{8,12},{9,13},{10,... | collective-permute-start | bytes 159752 | tf_op jit(solution)/shard_map/ppermute | solution.py:288
  31.5 4.5 %collective-permute-start.7 = (f32[104,128]{1,0:T(8,128)S(1)}, f32[104,128]{1,0:T(8,128)S(1)}, u32[]{:S(2)}, u32[]{:S(2)}) collective-permute-start(f32[104,128]{1,0:T(8,128)S(1)} %add.4.a), channel_id=1, source_target_pairs={{0,3},{1,2},{2,1},{3,0},{4,7},{5,6},{6,5},{7,4},{8,11},{9,10},{10,... | collective-permute-start | bytes 159752 | tf_op jit(solution)/shard_map/ppermute | solution.py:288
  36.1 4.8 %collective-permute-start.12 = (f32[96,128]{1,0:T(8,128)S(1)}, f32[96,128]{1,0:T(8,128)S(1)}, u32[]{:S(2)}, u32[]{:S(2)}) collective-permute-start(f32[96,128]{1,0:T(8,128)S(1)} %get-tuple-element.33.z0), channel_id=1, source_target_pairs={{0,97},{1,96},{32,65},{33,64},{64,33},{65,32},{96,1},{97,0},{2,99}... | collective-permute-start | bytes 147464 | tf_op jit(solution)/shard_map/ppermute | solution.py:288
  38.0 5.2 %collective-permute-start.11 = (f32[96,128]{1,0:T(8,128)S(1)}, f32[96,128]{1,0:T(8,128)S(1)}, u32[]{:S(2)}, u32[]{:S(2)}) collective-permute-start(f32[96,128]{1,0:T(8,128)S(1)} %get-tuple-element.33.z0), channel_id=1, source_target_pairs={{0,64},{1,65},{32,96},{33,97},{64,0},{65,1},{96,32},{97,33},{2,66}... | collective-permute-start | bytes 147464 | tf_op jit(solution)/shard_map/ppermute | solution.py:288
  38.8 4.5 %collective-permute-start.10 = (f32[96,128]{1,0:T(8,128)S(1)}, f32[96,128]{1,0:T(8,128)S(1)}, u32[]{:S(2)}, u32[]{:S(2)}) collective-permute-start(f32[96,128]{1,0:T(8,128)S(1)} %get-tuple-element.33.z0), channel_id=1, source_target_pairs={{0,33},{1,32},{32,1},{33,0},{64,97},{65,96},{96,65},{97,64},{2,35}... | collective-permute-start | bytes 147464 | tf_op jit(solution)/shard_map/ppermute | solution.py:288
  43.4 5.6 %collective-permute-start.15 = (f32[96,128]{1,0:T(8,128)S(1)}, f32[96,128]{1,0:T(8,128)S(1)}, u32[]{:S(2)}, u32[]{:S(2)}) collective-permute-start(f32[96,128]{1,0:T(8,128)S(1)} %normal.2.q0), channel_id=1, source_target_pairs={{0,25},{1,24},{8,17},{9,16},{16,9},{17,8},{24,1},{25,0},{2,27},{3,... | collective-permute-start | bytes 147464 | tf_op jit(solution)/shard_map/ppermute | solution.py:288
  44.9 5.0 %collective-permute-start.14 = (f32[96,128]{1,0:T(8,128)S(1)}, f32[96,128]{1,0:T(8,128)S(1)}, u32[]{:S(2)}, u32[]{:S(2)}) collective-permute-start(f32[96,128]{1,0:T(8,128)S(1)} %normal.2.q0), channel_id=1, source_target_pairs={{0,16},{1,17},{8,24},{9,25},{16,0},{17,1},{24,8},{25,9},{2,18},{3,... | collective-permute-start | bytes 147464 | tf_op jit(solution)/shard_map/ppermute | solution.py:288
  45.4 5.1 %collective-permute-start.13 = (f32[96,128]{1,0:T(8,128)S(1)}, f32[96,128]{1,0:T(8,128)S(1)}, u32[]{:S(2)}, u32[]{:S(2)}) collective-permute-start(f32[96,128]{1,0:T(8,128)S(1)} %normal.2.q0), channel_id=1, source_target_pairs={{0,9},{1,8},{8,1},{9,0},{16,25},{17,24},{24,17},{25,16},{2,11},{3,... | collective-permute-start | bytes 147464 | tf_op jit(solution)/shard_map/ppermute | solution.py:288
  50.5 2.1 %collective-permute-start.16 = (f32[392,128]{1,0:T(8,128)S(1)}, f32[392,128]{1,0:T(8,128)S(1)}, u32[]{:S(2)}, u32[]{:S(2)}) collective-permute-start(f32[392,128]{1,0:T(8,128)S(1)} %join.2.q_ref), channel_id=1, source_target_pairs={{0,1},{1,0},{2,3},{3,2},{4,5},{5,4},{6,7},{7,6},{8,9},{9,8},{10,11... | collective-permute-start | bytes 602120 | tf_op jit(solution)/shard_map/ppermute | solution.py:284
  54.1 3.9 %collective-permute-start.19 = (f32[16,192]{1,0:T(8,128)S(1)}, f32[16,192]{1,0:T(8,128)S(1)}, u32[]{:S(2)}, u32[]{:S(2)}) collective-permute-start(f32[16,192]{1,0:T(8,128)S(1)} %left_other.1.p0), channel_id=1, source_target_pairs={{0,96},{32,64},{64,32},{96,0},{1,97},{33,65},{65,33},{97,1},{2,98}... | collective-permute-start | bytes 36872 | tf_op jit(solution)/shard_map/ppermute | solution.py:284
  55.5 4.1 %collective-permute-start.18 = (f32[16,192]{1,0:T(8,128)S(1)}, f32[16,192]{1,0:T(8,128)S(1)}, u32[]{:S(2)}, u32[]{:S(2)}) collective-permute-start(f32[16,192]{1,0:T(8,128)S(1)} %left_other.1.p0), channel_id=1, source_target_pairs={{0,64},{32,96},{64,0},{96,32},{1,65},{33,97},{65,1},{97,33},{2,66}... | collective-permute-start | bytes 36872 | tf_op jit(solution)/shard_map/ppermute | solution.py:284
  56.4 3.2 %collective-permute-start.17 = (f32[16,192]{1,0:T(8,128)S(1)}, f32[16,192]{1,0:T(8,128)S(1)}, u32[]{:S(2)}, u32[]{:S(2)}) collective-permute-start(f32[16,192]{1,0:T(8,128)S(1)} %left_other.1.p0), channel_id=1, source_target_pairs={{0,32},{32,0},{64,96},{96,64},{1,33},{33,1},{65,97},{97,65},{2,34}... | collective-permute-start | bytes 36872 | tf_op jit(solution)/shard_map/ppermute | solution.py:284
  60.6 3.0 %collective-permute-start.20 = (f32[4,104,128]{2,1,0:T(8,128)S(1)}, f32[4,104,128]{2,1,0:T(8,128)S(1)}, u32[]{:S(2)}, u32[]{:S(2)}) collective-permute-start(f32[4,104,128]{2,1,0:T(8,128)S(1)} %right_other.3), channel_id=1, source_target_pairs={{0,1},{1,0},{2,3},{3,2},{4,5},{5,4},{6,7},{7,6},{8,9},{9,8},{10,11... | collective-permute-start | bytes 638984 | tf_op jit(solution)/shard_map/ppermute | solution.py:284
  63.6 4.5 %collective-permute-start.21 = (f32[104,128]{1,0:T(8,128)S(1)}, f32[104,128]{1,0:T(8,128)S(1)}, u32[]{:S(2)}, u32[]{:S(2)}) collective-permute-start(f32[104,128]{1,0:T(8,128)S(1)} %get-tuple-element.37), channel_id=1, source_target_pairs={{0,9},{1,8},{8,1},{9,0},{16,25},{17,24},{24,17},{25,16},{2,11},{3,... | collective-permute-start | bytes 159752 | tf_op jit(solution)/shard_map/ppermute | solution.py:288
  64.7 5.3 %collective-permute-start.22 = (f32[104,128]{1,0:T(8,128)S(1)}, f32[104,128]{1,0:T(8,128)S(1)}, u32[]{:S(2)}, u32[]{:S(2)}) collective-permute-start(f32[104,128]{1,0:T(8,128)S(1)} %get-tuple-element.38), channel_id=1, source_target_pairs={{0,16},{1,17},{8,24},{9,25},{16,0},{17,1},{24,8},{25,9},{2,18},{3,... | collective-permute-start | bytes 159752 | tf_op jit(solution)/shard_map/ppermute | solution.py:288
  66.8 5.1 %collective-permute-start.23 = (f32[104,128]{1,0:T(8,128)S(1)}, f32[104,128]{1,0:T(8,128)S(1)}, u32[]{:S(2)}, u32[]{:S(2)}) collective-permute-start(f32[104,128]{1,0:T(8,128)S(1)} %get-tuple-element.39), channel_id=1, source_target_pairs={{0,25},{1,24},{8,17},{9,16},{16,9},{17,8},{24,1},{25,0},{2,27},{3,... | collective-permute-start | bytes 159752 | tf_op jit(solution)/shard_map/ppermute | solution.py:288
  71.9 5.1 %collective-permute-start.26 = (f32[104,128]{1,0:T(8,128)S(1)}, f32[104,128]{1,0:T(8,128)S(1)}, u32[]{:S(2)}, u32[]{:S(2)}) collective-permute-start(f32[104,128]{1,0:T(8,128)S(1)} %add.6.a), channel_id=1, source_target_pairs={{0,7},{1,6},{2,5},{3,4},{4,3},{5,2},{6,1},{7,0},{8,15},{9,14},{10,... | collective-permute-start | bytes 159752 | tf_op jit(solution)/shard_map/ppermute | solution.py:288
  73.6 4.9 %collective-permute-start.25 = (f32[104,128]{1,0:T(8,128)S(1)}, f32[104,128]{1,0:T(8,128)S(1)}, u32[]{:S(2)}, u32[]{:S(2)}) collective-permute-start(f32[104,128]{1,0:T(8,128)S(1)} %add.6.a), channel_id=1, source_target_pairs={{0,4},{1,5},{2,6},{3,7},{4,0},{5,1},{6,2},{7,3},{8,12},{9,13},{10,... | collective-permute-start | bytes 159752 | tf_op jit(solution)/shard_map/ppermute | solution.py:288
  74.2 4.9 %collective-permute-start.24 = (f32[104,128]{1,0:T(8,128)S(1)}, f32[104,128]{1,0:T(8,128)S(1)}, u32[]{:S(2)}, u32[]{:S(2)}) collective-permute-start(f32[104,128]{1,0:T(8,128)S(1)} %add.6.a), channel_id=1, source_target_pairs={{0,3},{1,2},{2,1},{3,0},{4,7},{5,6},{6,5},{7,4},{8,11},{9,10},{10,... | collective-permute-start | bytes 159752 | tf_op jit(solution)/shard_map/ppermute | solution.py:288
  79.1 5.4 %collective-permute-start.29 = (f32[96,128]{1,0:T(8,128)S(1)}, f32[96,128]{1,0:T(8,128)S(1)}, u32[]{:S(2)}, u32[]{:S(2)}) collective-permute-start(f32[96,128]{1,0:T(8,128)S(1)} %get-tuple-element.40.z0), channel_id=1, source_target_pairs={{0,97},{1,96},{32,65},{33,64},{64,33},{65,32},{96,1},{97,0},{2,99}... | collective-permute-start | bytes 147464 | tf_op jit(solution)/shard_map/ppermute | solution.py:288
  80.5 4.4 %collective-permute-start.28 = (f32[96,128]{1,0:T(8,128)S(1)}, f32[96,128]{1,0:T(8,128)S(1)}, u32[]{:S(2)}, u32[]{:S(2)}) collective-permute-start(f32[96,128]{1,0:T(8,128)S(1)} %get-tuple-element.40.z0), channel_id=1, source_target_pairs={{0,64},{1,65},{32,96},{33,97},{64,0},{65,1},{96,32},{97,33},{2,66}... | collective-permute-start | bytes 147464 | tf_op jit(solution)/shard_map/ppermute | solution.py:288
  81.5 4.4 %collective-permute-start.27 = (f32[96,128]{1,0:T(8,128)S(1)}, f32[96,128]{1,0:T(8,128)S(1)}, u32[]{:S(2)}, u32[]{:S(2)}) collective-permute-start(f32[96,128]{1,0:T(8,128)S(1)} %get-tuple-element.40.z0), channel_id=1, source_target_pairs={{0,33},{1,32},{32,1},{33,0},{64,97},{65,96},{96,65},{97,64},{2,35}... | collective-permute-start | bytes 147464 | tf_op jit(solution)/shard_map/ppermute | solution.py:288
  86.1 5.0 %collective-permute-start.32 = (f32[96,128]{1,0:T(8,128)S(1)}, f32[96,128]{1,0:T(8,128)S(1)}, u32[]{:S(2)}, u32[]{:S(2)}) collective-permute-start(f32[96,128]{1,0:T(8,128)S(1)} %normal.3.q0), channel_id=1, source_target_pairs={{0,25},{1,24},{8,17},{9,16},{16,9},{17,8},{24,1},{25,0},{2,27},{3,... | collective-permute-start | bytes 147464 | tf_op jit(solution)/shard_map/ppermute | solution.py:288
  87.7 4.5 %collective-permute-start.31 = (f32[96,128]{1,0:T(8,128)S(1)}, f32[96,128]{1,0:T(8,128)S(1)}, u32[]{:S(2)}, u32[]{:S(2)}) collective-permute-start(f32[96,128]{1,0:T(8,128)S(1)} %normal.3.q0), channel_id=1, source_target_pairs={{0,16},{1,17},{8,24},{9,25},{16,0},{17,1},{24,8},{25,9},{2,18},{3,... | collective-permute-start | bytes 147464 | tf_op jit(solution)/shard_map/ppermute | solution.py:288
  87.9 5.1 %collective-permute-start.30 = (f32[96,128]{1,0:T(8,128)S(1)}, f32[96,128]{1,0:T(8,128)S(1)}, u32[]{:S(2)}, u32[]{:S(2)}) collective-permute-start(f32[96,128]{1,0:T(8,128)S(1)} %normal.3.q0), channel_id=1, source_target_pairs={{0,9},{1,8},{8,1},{9,0},{16,25},{17,24},{24,17},{25,16},{2,11},{3,... | collective-permute-start | bytes 147464 | tf_op jit(solution)/shard_map/ppermute | solution.py:288
  93.0 3.8 %collective-permute-start.33 = (f32[392,128]{1,0:T(8,128)S(1)}, f32[392,128]{1,0:T(8,128)S(1)}, u32[]{:S(2)}, u32[]{:S(2)}) collective-permute-start(f32[392,128]{1,0:T(8,128)S(1)} %join.3.q_ref), channel_id=1, source_target_pairs={{0,1},{1,0},{2,3},{3,2},{4,5},{5,4},{6,7},{7,6},{8,9},{9,8},{10,11... | collective-permute-start | bytes 602120 | tf_op jit(solution)/shard_map/ppermute | solution.py:284

commit v6 on v5

--- a/solution.py
+++ b/solution.py
@@ -134,27 +134,34 @@
     )(hbm(grads), hbm(errors), hbm(q))
 
 
-def left_kernel(slot, q_ref, g_ref, e_ref, *refs):
-    p_ref = refs[-1]
+def left_kernel(slot, ks, at, n_q, *refs):
+    q_refs, (g_ref, e_ref), acc_ref, o_ref = refs[:n_q], refs[n_q : n_q + 2], refs[n_q + 2 : -1], refs[-1]
     m = matrix(slot)
-    acc = jnp.zeros((24, ROWS), F32)
-    for k in range(SIDE):
+    acc = acc_ref[0][...] if acc_ref else jnp.zeros((24, ROWS), F32)
+    for i, k in enumerate(ks):
+        q_ref = q_refs[i if n_q > 1 else 0]
         for h in range(2):
-            q = three(block_of(q_ref, k, h))
+            q = three(block_of(q_ref, k if at else 0, h))
             acc = acc + lax.dot_general(q, g_ref[m, :, half(k, h)], NT, preferred_element_type=F32)
             acc = acc + lax.dot_general(q, e_ref[m, :, half(k, h)], NT, preferred_element_type=F32)
-    if slot == 0:
-        p_ref[...] = fold(acc)
-    else:
-        p_ref[rows(matrix(0)), :] = refs[0][...]
-        p_ref[rows(m), :] = fold(acc)
-
-
-def left(q_own, q_other, g, e):
-    own = kernel(functools.partial(left_kernel, 0), pltpu.VMEM((8, ROWS), F32), [IN_VMEM] * 3, "left_own", flops=10**9)(
-        vmem(q_own), vmem(g), vmem(e))
-    return kernel(functools.partial(left_kernel, 1), pltpu.VMEM((16, ROWS), F32), [IN_VMEM] * 4, "left_other")(
-        vmem(q_other), vmem(g), vmem(e), vmem(own))
+    o_ref[...] = acc
+
+
+def left_part(slot, ks, parts, g, e, acc=()):
+    at = parts[0].shape[0] > DEEP
+    return kernel(
+        functools.partial(left_kernel, slot, ks, at, len(parts)), pltpu.VMEM((24, ROWS), F32), [IN_VMEM] * (len(parts) + 2 + len(acc)),
+        "left_own" if slot == 0 else "left_other", flops=10**9,
+    )(*map(vmem, parts), vmem(g), vmem(e), *map(vmem, acc))
+
+
+def both_kernel(own_ref, other_ref, p_ref):
+    p_ref[rows(matrix(0)), :] = fold(own_ref[...])
+    p_ref[rows(matrix(1)), :] = fold(other_ref[...])
+
+
+def left_both(own, other):
+    return kernel(both_kernel, pltpu.VMEM((16, ROWS), F32), [IN_VMEM] * 2, "left_both")(vmem(own), vmem(other))
 
 
 def right_kernel(slot, p0, p1, p2, p3, g_ref, e_ref, o_ref, *mean_ref):
@@ -205,12 +212,23 @@
     return kernel(add_kernel, tuple(pltpu.VMEM((r, 128), F32) for r in rows), [IN_VMEM] * SIDE, "add")(*map(vmem, parts))
 
 
-def lower_kernel(gram_ref, o_ref):
-    o_ref[...] = inverse_lower(gram_ref[...])
-
-
-def lower_inverse(gram):
-    return kernel(lower_kernel, pltpu.VMEM((8, 128), F32), [IN_VMEM], "lower_inverse", flops=10**9)(vmem(gram))
+def hat_pieces(lower, p):
+    one, two, rest = split3(small_dot(lower, p))
+    pieces = jnp.concatenate([one, one, two, two, one, rest, jnp.zeros((80, ROWS), F32)], axis=0)
+    return jnp.concatenate([pieces, jnp.zeros((128, 64), F32)], axis=1).T.astype(BF16)
+
+
+def lower_kernel(gram_ref, *refs):
+    lower = inverse_lower(gram_ref[...])
+    if len(refs) > 1:
+        p_ref, o_ref, hat_ref = refs
+        hat_ref[...] = hat_pieces(lower, p_ref[rows(matrix(0)), :])
+    refs[-2 if len(refs) > 1 else 0][...] = lower
+
+
+def lower_inverse(gram, p):
+    out = (pltpu.VMEM((8, 128), F32),) + ((pltpu.VMEM((256, 128), BF16),) if p else ())
+    return kernel(lower_kernel, out, [IN_VMEM] * (1 + len(p)), "lower_inverse", flops=10**9)(vmem(gram), *map(vmem, p))
 
 
 def normal_kernel(z0, z1, z2, z3, lower_ref, o_ref):
@@ -234,24 +252,21 @@
     return kernel(join_kernel, pltpu.VMEM((SIDE * DEEP + 8, 128), F32), [IN_VMEM] * 5, "join")(*map(vmem, parts), vmem(lower))
 
 
-def final_kernel(slot, q_ref, p_ref, g_ref, e_ref, *refs):
-    a_hbm, n_hbm, q_hbm, p6, a_buf, n_buf, q_buf, a_sem, n_sem, q_sem = refs[-10:]
+def final_kernel(slot, ks, n_q, *refs):
+    q_refs, (p_ref, g_ref, e_ref), (a_hbm, n_hbm, q_hbm, a_buf, n_buf, q_buf, a_sem, n_sem, q_sem) = refs[:n_q], refs[n_q : n_q + 3], refs[-9:]
     m = matrix(slot)
     copies = []
-    one, two, rest = split3(small_dot(q_ref[SIDE * DEEP :, :], p_ref[rows(m), :]))
-    pieces = jnp.concatenate([one, one, two, two, one, rest, jnp.zeros((80, ROWS), F32)], axis=0)
-    pieces = jnp.concatenate([pieces, jnp.zeros((128, 64), F32)], axis=1)
-    p6[...] = pieces.T.astype(BF16)
-    left_pieces = p6[0:ROWS, 0:48]
-    for k in range(SIDE):
+    hat = p_ref[...] if slot == 0 else hat_pieces(q_refs[0][SIDE * DEEP :, :], p_ref[rows(m), :])
+    hat = hat[0:ROWS, 0:48]
+    for j, k in enumerate(ks):
         for h in range(2):
-            i = k * 2 + h
+            i = j * 2 + h
             s = half(k, h)
-            q = block_of(q_ref, k, h)
+            q = block_of(q_refs[j], 0, h) if slot == 0 else block_of(q_refs[0], k, h)
             q_buf[i] = q
             one, two, rest = split3(q)
             pieces = jnp.concatenate([one, two, one, two, rest, one], axis=0).astype(BF16)
-            full = jnp.dot(left_pieces, pieces, preferred_element_type=F32)
+            full = jnp.dot(hat, pieces, preferred_element_type=F32)
             a_buf[i] = full.astype(BF16)
             n_buf[i] = (g_ref[m, :, s].astype(F32) + e_ref[m, :, s].astype(F32) - full).astype(BF16)
             copies.append(pltpu.make_async_copy(a_buf.at[i], a_hbm.at[m, :, s], a_sem.at[i]))
@@ -263,21 +278,22 @@
         copy.wait()
 
 
-def final(slot, q, p, g, e, before=()):
-    n = SIDE * 2
+def final(slot, ks, parts, p, g, e, before=()):
+    n = len(ks) * 2
+    n_in = len(parts) + 3
     return pl.pallas_call(
-        functools.partial(final_kernel, slot),
-        in_specs=[IN_VMEM] * 4 + [ANYWHERE] * len(before),
+        functools.partial(final_kernel, slot, ks, len(parts)),
+        in_specs=[IN_VMEM] * n_in + [ANYWHERE] * len(before),
         out_specs=(ANYWHERE,) * 3,
         out_shape=(jax.ShapeDtypeStruct((MATS, ROWS, COLS), BF16), jax.ShapeDtypeStruct((1, MATS, ROWS, COLS), BF16),
                    jax.ShapeDtypeStruct((MATS, RANK, COLS), F32)),
-        scratch_shapes=[pltpu.VMEM((256, 128), BF16), pltpu.VMEM((n, ROWS, BLOCK), BF16), pltpu.VMEM((n, ROWS, BLOCK), BF16),
+        scratch_shapes=[pltpu.VMEM((n, ROWS, BLOCK), BF16), pltpu.VMEM((n, ROWS, BLOCK), BF16),
                         pltpu.VMEM((n, RANK, BLOCK), F32)] + [pltpu.SemaphoreType.DMA((n,))] * 3,
-        input_output_aliases={4 + i: i for i in range(len(before))},
+        input_output_aliases={n_in + i: i for i in range(len(before))},
         compiler_params=pltpu.CompilerParams(vmem_limit_bytes=16 * 1024 * 1024),
-        cost_estimate=pl.CostEstimate(flops=10**9, bytes_accessed=10**7, transcendentals=0),
+        cost_estimate=pl.CostEstimate(flops=10**9, bytes_accessed=10**6, transcendentals=0),
         name="residual_own" if slot == 0 else "residual_other",
-    )(*map(vmem, (q, p, g, e)), *before)
+    )(*map(vmem, (*parts, p, g, e)), *before)
 
 
 def swap(a, axis, k):
@@ -301,17 +317,30 @@
     (z,) = add((parts[0],) + tuple(cross(parts[k], "x", k) for k in (1, 2, 3)), DEEP + 8)
     z, gram = add(everyones(z, "y", cross), DEEP, 8)
     z_all = everyones(z, "dp", cross)
-    lower = lower_inverse(gram)
-    return join(everyones(normal(z_all, lower), "x", cross), lower), p
+    lower, *hat = lower_inverse(gram, p)
+    parts = everyones(normal(z_all, lower), "x", cross)
+    return parts, lower, p + hat
+
+
+def after(parts, out):
+    q1, q2, out = lax.optimization_barrier((parts[1], parts[2], out))
+    return (parts[0], q1, q2, parts[3]), out
 
 
 def per_device(grads, errors, q_init):
     p_own, g, e = first_left(grads, errors, jnp.swapaxes(q_init, 1, 2))
-    q_own, _ = right_sum(p_own, g, e, False)
-    p_own = left(q_own, swap(q_own, "core", 1), g, e)
-    q_own, (p,) = right_sum(p_own, g, e, True)
-    q_other = swap(q_own, "core", 1)
-    approx, errors_next, q_next = final(1, q_other, p, g, e, final(0, q_own, p, g, e))
+    parts, lower, _ = right_sum(p_own, g, e, False)
+    own = left_part(0, (0,), parts[:1], g, e)
+    parts, own = after(parts, left_part(0, (3,), parts[3:], g, e, (own,)))
+    q_other = swap(join(parts, lower), "core", 1)
+    own = left_part(0, (1, 2), parts[1:3], g, e, (own,))
+    p_own = left_both(own, left_part(1, (0, 1, 2, 3), (q_other,), g, e))
+    parts, lower, (p, hat) = right_sum(p_own, g, e, True)
+    out = final(0, (0,), parts[:1], hat, g, e)
+    parts, out = after(parts, final(0, (3,), parts[3:], hat, g, e, out))
+    q_other = swap(join(parts, lower), "core", 1)
+    out = final(0, (1, 2), parts[1:3], hat, g, e, out)
+    approx, errors_next, q_next = final(1, (0, 1, 2, 3), (q_other,), p, g, e, out)
     return approx, errors_next, jnp.swapaxes(q_next, 1, 2)
 
 

time: 100 us -> 98.6 us (0.986)
  waiting for transfers between devices: 32.5 us -> 29.1 us
  Pallas kernels: 19.7 us -> 21.6 us
    ppermute x24, waiting for transfers between devices: 26.7 us -> 23.1 us  [cross(): lax.ppermute(a, (axis, 'core'), [(i * 2 + c, (i ^ k) * 2 + (c ^ k & 1)) f...]
    pallas_call x6 -> x11, Pallas kernels: 10.2 us -> 12.1 us  [the longest x4 7.25 us: final(): pl.pallas_call(functools.partial(final_kernel, slot, ks, len(parts)), in_...]
  transfers between devices with their start and end apart: 34 -> 34, of which waited for: 26 -> 25; matrix products, arithmetic and copies ran while one was open for 0% -> 0% of each run, Pallas kernels for 8% -> 10%
where the time goes in v6:
time: 98.6 us; the launch traced here: 98.5 us
  starting transfers between devices  46.8 us (47%)
  waiting for transfers between devices  29.1 us (30%)
  Pallas kernels  21.6 us (22%)
    ppermute x24, starting transfers between devices, cross(): lax.ppermute(a, (axis, 'core'), [(i * 2 + c, (i ^ k) * 2 + (c ^ k & 1)) f...  32.6 us
    ppermute x24, waiting for transfers between devices, cross(): lax.ppermute(a, (axis, 'core'), [(i * 2 + c, (i ^ k) * 2 + (c ^ k & 1)) f...  23.1 us
    ppermute x10, starting transfers between devices, swap(): lax.ppermute(a, axis, [(i, i ^ k) for i in range(lax.axis_size(axis))])  14.2 us
    pallas_call x4, Pallas kernels, final(): pl.pallas_call(functools.partial(final_kernel, slot, ks, len(parts)), in_...  7.25 us
    ppermute x10, waiting for transfers between devices, swap(): lax.ppermute(a, axis, [(i, i ^ k) for i in range(lax.axis_size(axis))])  6.06 us
    pallas_call x1, Pallas kernels, first_left(): kernel(first_left_kernel, (pltpu.VMEM((16, ROWS), F32), wide, wide), [ANY...  5.25 us
    pallas_call x4, Pallas kernels, right(): kernel(functools.partial(right_kernel, slot), out, [IN_VMEM] * 6, 'right_...  3.89 us
    pallas_call x4, Pallas kernels, left_part(): kernel(functools.partial(left_kernel, slot, ks, at, len(parts)), pltpu.VM...  3.27 us
  transfers between devices with their start and end apart: 34, of which 25 were waited for; matrix products, arithmetic and copies ran while one was open for 0% of the time, Pallas kernels for 10%

profile of v6, /device:TPU:1, one launch (start us, length us, event | category | flops | bytes accessed | tf_op | source)
XLA Modules:
  0.0 98.5 jit_solution(1732185916280807628)
XLA Ops:
  0.6 5.3 %first_left.1 = (f32[16,192]{1,0:T(8,128)S(1)}, bf16[2,192,6144]{2,1,0:T(8,128)(2,1)S(1)}, bf16[2,192,6144]{2,1,0:T(8,128)(2,1)S(1)}) custom-call(bf16[1,2,192,6144]{3,2,1,0:T(8,128)(2,1)} %g_hbm.1, bf16[1,2,192,6144]{3,2,1,0:T(8,128)(2,1)} %e_hbm.1, f32[2,8,6144]{2,1,0:T(8,128)} %bitcast.3), custom_call_target="tpu_custom_call" | custom-call | flops 10000000 | bytes 1000000 | tf_op jit(solution)/shard_map/first_left/pallas_call | solution.py:131
  5.9 4.7 %collective-permute-start.2 = (f32[16,192]{1,0:T(8,128)S(1)}, f32[16,192]{1,0:T(8,128)S(1)}, u32[]{:S(2)}, u32[]{:S(2)}) collective-permute-start(f32[16,192]{1,0:T(8,128)S(1)} %get-tuple-element.42.p0), channel_id=1, source_target_pairs={{0,96},{32,64},{64,32},{96,0},{1,97},{33,65},{65,33},{97,1},{2,98}... | collective-permute-start | bytes 36872 | tf_op jit(solution)/shard_map/ppermute | solution.py:300
  11.7 3.0 %collective-permute-done.1.p2 = f32[16,192]{1,0:T(8,128)S(1)} collective-permute-done((f32[16,192]{1,0:T(8,128)S(1)}, f32[16,192]{1,0:T(8,128)S(1)}, u32[]{:S(2)}, u32[]{:S(2)}) %collective-permute-start.1) | collective-permute-done | bytes 12320 | tf_op jit(solution)/shard_map/ppermute | solution.py:300
  14.7 1.0 right_other.2
  15.6 2.2 %collective-permute-start.3 = (f32[4,104,128]{2,1,0:T(8,128)S(1)}, f32[4,104,128]{2,1,0:T(8,128)S(1)}, u32[]{:S(2)}, u32[]{:S(2)}) collective-permute-start(f32[4,104,128]{2,1,0:T(8,128)S(1)} %right_other.2), channel_id=1, source_target_pairs={{0,1},{1,0},{2,3},{3,2},{4,5},{5,4},{6,7},{7,6},{8,9},{9,8},{10,11... | collective-permute-start | bytes 638984 | tf_op jit(solution)/shard_map/ppermute | solution.py:300
  17.8 1.0 right_own.2.mine_ref
  18.9 1.6 %collective-permute-start.4 = (f32[104,128]{1,0:T(8,128)S(1)}, f32[104,128]{1,0:T(8,128)S(1)}, u32[]{:S(2)}, u32[]{:S(2)}) collective-permute-start(f32[104,128]{1,0:T(8,128)S(1)} %get-tuple-element.46), channel_id=1, source_target_pairs={{0,9},{1,8},{8,1},{9,0},{16,25},{17,24},{24,17},{25,16},{2,11},{3,... | collective-permute-start | bytes 159752 | tf_op jit(solution)/shard_map/ppermute | solution.py:304
  20.5 2.4 %collective-permute-start.5 = (f32[104,128]{1,0:T(8,128)S(1)}, f32[104,128]{1,0:T(8,128)S(1)}, u32[]{:S(2)}, u32[]{:S(2)}) collective-permute-start(f32[104,128]{1,0:T(8,128)S(1)} %get-tuple-element.47), channel_id=1, source_target_pairs={{0,16},{1,17},{8,24},{9,25},{16,0},{17,1},{24,8},{25,9},{2,18},{3,... | collective-permute-start | bytes 159752 | tf_op jit(solution)/shard_map/ppermute | solution.py:304
  23.5 2.7 %collective-permute-done.5.c = f32[104,128]{1,0:T(8,128)S(1)} collective-permute-done((f32[104,128]{1,0:T(8,128)S(1)}, f32[104,128]{1,0:T(8,128)S(1)}, u32[]{:S(2)}, u32[]{:S(2)}) %collective-permute-start.5) | collective-permute-done | bytes 53280 | tf_op jit(solution)/shard_map/ppermute | solution.py:304
  26.1 1.9 %collective-permute-done.6.d = f32[104,128]{1,0:T(8,128)S(1)} collective-permute-done((f32[104,128]{1,0:T(8,128)S(1)}, f32[104,128]{1,0:T(8,128)S(1)}, u32[]{:S(2)}, u32[]{:S(2)}) %collective-permute-start.6) | collective-permute-done | bytes 53280 | tf_op jit(solution)/shard_map/ppermute | solution.py:304
  28.1 3.1 %collective-permute-start.9 = (f32[104,128]{1,0:T(8,128)S(1)}, f32[104,128]{1,0:T(8,128)S(1)}, u32[]{:S(2)}, u32[]{:S(2)}) collective-permute-start(f32[104,128]{1,0:T(8,128)S(1)} %add.4.a), channel_id=1, source_target_pairs={{0,7},{1,6},{2,5},{3,4},{4,3},{5,2},{6,1},{7,0},{8,15},{9,14},{10,... | collective-permute-start | bytes 159752 | tf_op jit(solution)/shard_map/ppermute | solution.py:304
  32.1 1.4 %collective-permute-done.9.d = f32[104,128]{1,0:T(8,128)S(1)} collective-permute-done((f32[104,128]{1,0:T(8,128)S(1)}, f32[104,128]{1,0:T(8,128)S(1)}, u32[]{:S(2)}, u32[]{:S(2)}) %collective-permute-start.9) | collective-permute-done | bytes 53280 | tf_op jit(solution)/shard_map/ppermute | solution.py:304
  33.5 2.5 %collective-permute-done.8.c = f32[104,128]{1,0:T(8,128)S(1)} collective-permute-done((f32[104,128]{1,0:T(8,128)S(1)}, f32[104,128]{1,0:T(8,128)S(1)}, u32[]{:S(2)}, u32[]{:S(2)}) %collective-permute-start.8) | collective-permute-done | bytes 53280 | tf_op jit(solution)/shard_map/ppermute | solution.py:304
  36.1 1.9 %collective-permute-start.12 = (f32[96,128]{1,0:T(8,128)S(1)}, f32[96,128]{1,0:T(8,128)S(1)}, u32[]{:S(2)}, u32[]{:S(2)}) collective-permute-start(f32[96,128]{1,0:T(8,128)S(1)} %get-tuple-element.49.z0), channel_id=1, source_target_pairs={{0,97},{1,96},{32,65},{33,64},{64,33},{65,32},{96,1},{97,0},{2,99}... | collective-permute-start | bytes 147464 | tf_op jit(solution)/shard_map/ppermute | solution.py:304
  38.8 1.2 %collective-permute-start.10 = (f32[96,128]{1,0:T(8,128)S(1)}, f32[96,128]{1,0:T(8,128)S(1)}, u32[]{:S(2)}, u32[]{:S(2)}) collective-permute-start(f32[96,128]{1,0:T(8,128)S(1)} %get-tuple-element.49.z0), channel_id=1, source_target_pairs={{0,33},{1,32},{32,1},{33,0},{64,97},{65,96},{96,65},{97,64},{2,35}... | collective-permute-start | bytes 147464 | tf_op jit(solution)/shard_map/ppermute | solution.py:304
  40.9 2.4 %collective-permute-done.11.z2 = f32[96,128]{1,0:T(8,128)S(1)} collective-permute-done((f32[96,128]{1,0:T(8,128)S(1)}, f32[96,128]{1,0:T(8,128)S(1)}, u32[]{:S(2)}, u32[]{:S(2)}) %collective-permute-start.11) | collective-permute-done | bytes 49184 | tf_op jit(solution)/shard_map/ppermute | solution.py:304
  43.4 1.5 %collective-permute-start.15 = (f32[96,128]{1,0:T(8,128)S(1)}, f32[96,128]{1,0:T(8,128)S(1)}, u32[]{:S(2)}, u32[]{:S(2)}) collective-permute-start(f32[96,128]{1,0:T(8,128)S(1)} %normal.2.refs_0_.q0), channel_id=1, source_target_pairs={{0,25},{1,24},{8,17},{9,16},{16,9},{17,8},{24,1},{25,0},{2,27},{3,... | collective-permute-start | bytes 147464 | tf_op jit(solution)/shard_map/ppermute | solution.py:304
  45.4 1.9 %collective-permute-start.13 = (f32[96,128]{1,0:T(8,128)S(1)}, f32[96,128]{1,0:T(8,128)S(1)}, u32[]{:S(2)}, u32[]{:S(2)}) collective-permute-start(f32[96,128]{1,0:T(8,128)S(1)} %normal.2.refs_0_.q0), channel_id=1, source_target_pairs={{0,9},{1,8},{8,1},{9,0},{16,25},{17,24},{24,17},{25,16},{2,11},{3,... | collective-permute-start | bytes 147464 | tf_op jit(solution)/shard_map/ppermute | solution.py:304
  47.8 1.2 %collective-permute-done.15.refs_0_.q3 = f32[96,128]{1,0:T(8,128)S(1)} collective-permute-done((f32[96,128]{1,0:T(8,128)S(1)}, f32[96,128]{1,0:T(8,128)S(1)}, u32[]{:S(2)}, u32[]{:S(2)}) %collective-permute-start.15) | collective-permute-done | bytes 49184 | tf_op jit(solution)/shard_map/ppermute | solution.py:304
  52.0 1.5 %left_other.1.other_ref = f32[24,192]{1,0:T(8,128)S(1)} custom-call(f32[392,128]{1,0:T(8,128)S(1)} %collective-permute-done.16.refs_0_, bf16[2,192,6144]{2,1,0:T(8,128)(2,1)S(1)} %get-tuple-element.43.g_ref.refs_1_.refs_2_.refs_3_, bf16[2,192,6144]{2,1,0:T(8,128)(2,1)S(1)} %get-tuple-element.44.e_ref.refs_2_.refs_3_.refs_4_), custom_call_target="tpu_custom_call" | custom-call | flops 1000000000 | bytes 1000000 | tf_op jit(solution)/shard_map/left_other/pallas_call | solution.py:152
  53.6 1.4 %collective-permute-start.19 = (f32[16,192]{1,0:T(8,128)S(1)}, f32[16,192]{1,0:T(8,128)S(1)}, u32[]{:S(2)}, u32[]{:S(2)}) collective-permute-start(f32[16,192]{1,0:T(8,128)S(1)} %left_both.1.p0), channel_id=1, source_target_pairs={{0,96},{32,64},{64,32},{96,0},{1,97},{33,65},{65,33},{97,1},{2,98}... | collective-permute-start | bytes 36872 | tf_op jit(solution)/shard_map/ppermute | solution.py:300
  55.0 0.9 collective-permute-start.18
  55.9 1.0 %collective-permute-start.17 = (f32[16,192]{1,0:T(8,128)S(1)}, f32[16,192]{1,0:T(8,128)S(1)}, u32[]{:S(2)}, u32[]{:S(2)}) collective-permute-start(f32[16,192]{1,0:T(8,128)S(1)} %left_both.1.p0), channel_id=1, source_target_pairs={{0,32},{32,0},{64,96},{96,64},{1,33},{33,1},{65,97},{97,65},{2,34}... | collective-permute-start | bytes 36872 | tf_op jit(solution)/shard_map/ppermute | solution.py:300
  57.5 1.6 %collective-permute-done.18.p2 = f32[16,192]{1,0:T(8,128)S(1)} collective-permute-done((f32[16,192]{1,0:T(8,128)S(1)}, f32[16,192]{1,0:T(8,128)S(1)}, u32[]{:S(2)}, u32[]{:S(2)}) %collective-permute-start.18) | collective-permute-done | bytes 12320 | tf_op jit(solution)/shard_map/ppermute | solution.py:300
  59.1 1.0 right_other.3
  60.1 2.1 %collective-permute-start.20 = (f32[4,104,128]{2,1,0:T(8,128)S(1)}, f32[4,104,128]{2,1,0:T(8,128)S(1)}, u32[]{:S(2)}, u32[]{:S(2)}) collective-permute-start(f32[4,104,128]{2,1,0:T(8,128)S(1)} %right_other.3), channel_id=1, source_target_pairs={{0,1},{1,0},{2,3},{3,2},{4,5},{5,4},{6,7},{7,6},{8,9},{9,8},{10,11... | collective-permute-start | bytes 638984 | tf_op jit(solution)/shard_map/ppermute | solution.py:300
  62.1 1.0 right_own.3
  63.2 1.3 %collective-permute-start.21 = (f32[104,128]{1,0:T(8,128)S(1)}, f32[104,128]{1,0:T(8,128)S(1)}, u32[]{:S(2)}, u32[]{:S(2)}) collective-permute-start(f32[104,128]{1,0:T(8,128)S(1)} %get-tuple-element.56), channel_id=1, source_target_pairs={{0,9},{1,8},{8,1},{9,0},{16,25},{17,24},{24,17},{25,16},{2,11},{3,... | collective-permute-start | bytes 159752 | tf_op jit(solution)/shard_map/ppermute | solution.py:304
  64.5 2.1 %collective-permute-start.22 = (f32[104,128]{1,0:T(8,128)S(1)}, f32[104,128]{1,0:T(8,128)S(1)}, u32[]{:S(2)}, u32[]{:S(2)}) collective-permute-start(f32[104,128]{1,0:T(8,128)S(1)} %get-tuple-element.57), channel_id=1, source_target_pairs={{0,16},{1,17},{8,24},{9,25},{16,0},{17,1},{24,8},{25,9},{2,18},{3,... | collective-permute-start | bytes 159752 | tf_op jit(solution)/shard_map/ppermute | solution.py:304
  66.6 1.2 %collective-permute-start.23 = (f32[104,128]{1,0:T(8,128)S(1)}, f32[104,128]{1,0:T(8,128)S(1)}, u32[]{:S(2)}, u32[]{:S(2)}) collective-permute-start(f32[104,128]{1,0:T(8,128)S(1)} %get-tuple-element.58), channel_id=1, source_target_pairs={{0,25},{1,24},{8,17},{9,16},{16,9},{17,8},{24,1},{25,0},{2,27},{3,... | collective-permute-start | bytes 159752 | tf_op jit(solution)/shard_map/ppermute | solution.py:304
  67.8 2.0 %collective-permute-done.22.c = f32[104,128]{1,0:T(8,128)S(1)} collective-permute-done((f32[104,128]{1,0:T(8,128)S(1)}, f32[104,128]{1,0:T(8,128)S(1)}, u32[]{:S(2)}, u32[]{:S(2)}) %collective-permute-start.22) | collective-permute-done | bytes 53280 | tf_op jit(solution)/shard_map/ppermute | solution.py:304
  69.8 1.9 %collective-permute-done.23.d = f32[104,128]{1,0:T(8,128)S(1)} collective-permute-done((f32[104,128]{1,0:T(8,128)S(1)}, f32[104,128]{1,0:T(8,128)S(1)}, u32[]{:S(2)}, u32[]{:S(2)}) %collective-permute-start.23) | collective-permute-done | bytes 53280 | tf_op jit(solution)/shard_map/ppermute | solution.py:304
  71.7 1.7 %collective-permute-start.26 = (f32[104,128]{1,0:T(8,128)S(1)}, f32[104,128]{1,0:T(8,128)S(1)}, u32[]{:S(2)}, u32[]{:S(2)}) collective-permute-start(f32[104,128]{1,0:T(8,128)S(1)} %add.6.a), channel_id=1, source_target_pairs={{0,7},{1,6},{2,5},{3,4},{4,3},{5,2},{6,1},{7,0},{8,15},{9,14},{10,... | collective-permute-start | bytes 159752 | tf_op jit(solution)/shard_map/ppermute | solution.py:304
  73.9 1.7 %collective-permute-start.24 = (f32[104,128]{1,0:T(8,128)S(1)}, f32[104,128]{1,0:T(8,128)S(1)}, u32[]{:S(2)}, u32[]{:S(2)}) collective-permute-start(f32[104,128]{1,0:T(8,128)S(1)} %add.6.a), channel_id=1, source_target_pairs={{0,3},{1,2},{2,1},{3,0},{4,7},{5,6},{6,5},{7,4},{8,11},{9,10},{10,... | collective-permute-start | bytes 159752 | tf_op jit(solution)/shard_map/ppermute | solution.py:304
  75.6 1.2 %collective-permute-done.26.d = f32[104,128]{1,0:T(8,128)S(1)} collective-permute-done((f32[104,128]{1,0:T(8,128)S(1)}, f32[104,128]{1,0:T(8,128)S(1)}, u32[]{:S(2)}, u32[]{:S(2)}) %collective-permute-start.26) | collective-permute-done | bytes 53280 | tf_op jit(solution)/shard_map/ppermute | solution.py:304
  76.8 1.5 %collective-permute-done.25.c = f32[104,128]{1,0:T(8,128)S(1)} collective-permute-done((f32[104,128]{1,0:T(8,128)S(1)}, f32[104,128]{1,0:T(8,128)S(1)}, u32[]{:S(2)}, u32[]{:S(2)}) %collective-permute-start.25) | collective-permute-done | bytes 53280 | tf_op jit(solution)/shard_map/ppermute | solution.py:304
  78.9 1.5 %collective-permute-start.29 = (f32[96,128]{1,0:T(8,128)S(1)}, f32[96,128]{1,0:T(8,128)S(1)}, u32[]{:S(2)}, u32[]{:S(2)}) collective-permute-start(f32[96,128]{1,0:T(8,128)S(1)} %get-tuple-element.59.z0), channel_id=1, source_target_pairs={{0,97},{1,96},{32,65},{33,64},{64,33},{65,32},{96,1},{97,0},{2,99}... | collective-permute-start | bytes 147464 | tf_op jit(solution)/shard_map/ppermute | solution.py:304
  80.4 1.0 collective-permute-start.28
  81.3 1.5 %collective-permute-start.27 = (f32[96,128]{1,0:T(8,128)S(1)}, f32[96,128]{1,0:T(8,128)S(1)}, u32[]{:S(2)}, u32[]{:S(2)}) collective-permute-start(f32[96,128]{1,0:T(8,128)S(1)} %get-tuple-element.59.z0), channel_id=1, source_target_pairs={{0,33},{1,32},{32,1},{33,0},{64,97},{65,96},{96,65},{97,64},{2,35}... | collective-permute-start | bytes 147464 | tf_op jit(solution)/shard_map/ppermute | solution.py:304
  82.8 0.9 lower_inverse.3
  84.8 0.9 collective-permute-done.27.z1
  85.9 1.5 %collective-permute-start.32 = (f32[96,128]{1,0:T(8,128)S(1)}, f32[96,128]{1,0:T(8,128)S(1)}, u32[]{:S(2)}, u32[]{:S(2)}) collective-permute-start(f32[96,128]{1,0:T(8,128)S(1)} %normal.3.refs_0_.q0), channel_id=1, source_target_pairs={{0,25},{1,24},{8,17},{9,16},{16,9},{17,8},{24,1},{25,0},{2,27},{3,... | collective-permute-start | bytes 147464 | tf_op jit(solution)/shard_map/ppermute | solution.py:304
  87.7 2.1 %collective-permute-start.30 = (f32[96,128]{1,0:T(8,128)S(1)}, f32[96,128]{1,0:T(8,128)S(1)}, u32[]{:S(2)}, u32[]{:S(2)}) collective-permute-start(f32[96,128]{1,0:T(8,128)S(1)} %normal.3.refs_0_.q0), channel_id=1, source_target_pairs={{0,9},{1,8},{8,1},{9,0},{16,25},{17,24},{24,17},{25,16},{2,11},{3,... | collective-permute-start | bytes 147464 | tf_op jit(solution)/shard_map/ppermute | solution.py:304
  89.8 1.3 %residual_own.3 = (bf16[2,192,6144]{2,1,0:T(8,128)(2,1)}, bf16[1,2,192,6144]{3,2,1,0:T(8,128)(2,1)}, f32[2,8,6144]{2,1,0:T(8,128)}) custom-call(f32[96,128]{1,0:T(8,128)S(1)} %normal.3.refs_0_.q0, bf16[256,128]{1,0:T(8,128)(2,1)S(1)} %get-tuple-element.63.refs_1_.refs_2_, bf16[2,192,6144]{2,1,0:T(8,128)(2,1)S(1)} %get-tuple-element.43.g_ref.refs_1_.refs_2_.refs_3_, ...), custom_call_target="tpu_custom_call" | custom-call | flops 1000000000 | bytes 1000000 | tf_op jit(solution)/shard_map/residual_own/pallas_call | solution.py:284
  91.1 1.3 %residual_own.4 = (bf16[2,192,6144]{2,1,0:T(8,128)(2,1)}, bf16[1,2,192,6144]{3,2,1,0:T(8,128)(2,1)}, f32[2,8,6144]{2,1,0:T(8,128)}) custom-call(f32[96,128]{1,0:T(8,128)S(1)} %collective-permute-done.32.refs_0_.q3, bf16[256,128]{1,0:T(8,128)(2,1)S(1)} %get-tuple-element.63.refs_1_.refs_2_, ...), custom_call_target="tpu_custom_call", output_to_operand_aliasing={{0}: (4, {}), {1}: (5, {}), {2}: (6, {})} | custom-call | flops 1000000000 | bytes 1000000 | tf_op jit(solution)/shard_map/residual_own/pallas_call | solution.py:284
  92.8 0.8 collective-permute-start.33
  93.7 1.8 %residual_own.5 = (bf16[2,192,6144]{2,1,0:T(8,128)(2,1)}, bf16[1,2,192,6144]{3,2,1,0:T(8,128)(2,1)}, f32[2,8,6144]{2,1,0:T(8,128)}) custom-call(f32[96,128]{1,0:T(8,128)S(1)} %collective-permute-done.30.q1.refs_0_, f32[96,128]{1,0:T(8,128)S(1)} %collective-permute-done.31.q2.refs_1_, ...), custom_call_target="tpu_custom_call", output_to_operand_aliasing={{0}: (5, {}), {1}: (6, {}), {2}: (7, {})} | custom-call | flops 1000000000 | bytes 1000000 | tf_op jit(solution)/shard_map/residual_own/pallas_call | solution.py:284
  95.5 2.8 %residual_other.1 = (bf16[2,192,6144]{2,1,0:T(8,128)(2,1)}, bf16[1,2,192,6144]{3,2,1,0:T(8,128)(2,1)}, f32[2,8,6144]{2,1,0:T(8,128)}) custom-call(f32[392,128]{1,0:T(8,128)S(1)} %collective-permute-done.33.refs_0_, f32[16,192]{1,0:T(8,128)S(1)} %get-tuple-element.61.refs_0_.refs_1_, ...), custom_call_target="tpu_custom_call", output_to_operand_aliasing={{0}: (4, {}), {1}: (5, {}), {2}: (6, {})} | custom-call | flops 1000000000 | bytes 1000000 | tf_op jit(solution)/shard_map/residual_other/pallas_call | solution.py:284
  (46 shorter events, 12.3 us)
Async XLA Ops:
  5.9 5.8 %collective-permute-start.2 = (f32[16,192]{1,0:T(8,128)S(1)}, f32[16,192]{1,0:T(8,128)S(1)}, u32[]{:S(2)}, u32[]{:S(2)}) collective-permute-start(f32[16,192]{1,0:T(8,128)S(1)} %get-tuple-element.42.p0), channel_id=1, source_target_pairs={{0,96},{32,64},{64,32},{96,0},{1,97},{33,65},{65,33},{97,1},{2,98}... | collective-permute-start | bytes 36872 | tf_op jit(solution)/shard_map/ppermute | solution.py:300
  10.6 4.1 %collective-permute-start.1 = (f32[16,192]{1,0:T(8,128)S(1)}, f32[16,192]{1,0:T(8,128)S(1)}, u32[]{:S(2)}, u32[]{:S(2)}) collective-permute-start(f32[16,192]{1,0:T(8,128)S(1)} %get-tuple-element.42.p0), channel_id=1, source_target_pairs={{0,64},{32,96},{64,0},{96,32},{1,65},{33,97},{65,1},{97,33},{2,66}... | collective-permute-start | bytes 36872 | tf_op jit(solution)/shard_map/ppermute | solution.py:300
  10.6 4.1 %collective-permute-start = (f32[16,192]{1,0:T(8,128)S(1)}, f32[16,192]{1,0:T(8,128)S(1)}, u32[]{:S(2)}, u32[]{:S(2)}) collective-permute-start(f32[16,192]{1,0:T(8,128)S(1)} %get-tuple-element.42.p0), channel_id=1, source_target_pairs={{0,32},{32,0},{64,96},{96,64},{1,33},{33,1},{65,97},{97,65},{2,34}... | collective-permute-start | bytes 36872 | tf_op jit(solution)/shard_map/ppermute | solution.py:300
  15.6 3.3 %collective-permute-start.3 = (f32[4,104,128]{2,1,0:T(8,128)S(1)}, f32[4,104,128]{2,1,0:T(8,128)S(1)}, u32[]{:S(2)}, u32[]{:S(2)}) collective-permute-start(f32[4,104,128]{2,1,0:T(8,128)S(1)} %right_other.2), channel_id=1, source_target_pairs={{0,1},{1,0},{2,3},{3,2},{4,5},{5,4},{6,7},{7,6},{8,9},{9,8},{10,11... | collective-permute-start | bytes 638984 | tf_op jit(solution)/shard_map/ppermute | solution.py:300
  18.9 4.5 %collective-permute-start.4 = (f32[104,128]{1,0:T(8,128)S(1)}, f32[104,128]{1,0:T(8,128)S(1)}, u32[]{:S(2)}, u32[]{:S(2)}) collective-permute-start(f32[104,128]{1,0:T(8,128)S(1)} %get-tuple-element.46), channel_id=1, source_target_pairs={{0,9},{1,8},{8,1},{9,0},{16,25},{17,24},{24,17},{25,16},{2,11},{3,... | collective-permute-start | bytes 159752 | tf_op jit(solution)/shard_map/ppermute | solution.py:304
  20.5 5.7 %collective-permute-start.5 = (f32[104,128]{1,0:T(8,128)S(1)}, f32[104,128]{1,0:T(8,128)S(1)}, u32[]{:S(2)}, u32[]{:S(2)}) collective-permute-start(f32[104,128]{1,0:T(8,128)S(1)} %get-tuple-element.47), channel_id=1, source_target_pairs={{0,16},{1,17},{8,24},{9,25},{16,0},{17,1},{24,8},{25,9},{2,18},{3,... | collective-permute-start | bytes 159752 | tf_op jit(solution)/shard_map/ppermute | solution.py:304
  22.9 5.1 %collective-permute-start.6 = (f32[104,128]{1,0:T(8,128)S(1)}, f32[104,128]{1,0:T(8,128)S(1)}, u32[]{:S(2)}, u32[]{:S(2)}) collective-permute-start(f32[104,128]{1,0:T(8,128)S(1)} %get-tuple-element.48), channel_id=1, source_target_pairs={{0,25},{1,24},{8,17},{9,16},{16,9},{17,8},{24,1},{25,0},{2,27},{3,... | collective-permute-start | bytes 159752 | tf_op jit(solution)/shard_map/ppermute | solution.py:304
  28.1 5.5 %collective-permute-start.9 = (f32[104,128]{1,0:T(8,128)S(1)}, f32[104,128]{1,0:T(8,128)S(1)}, u32[]{:S(2)}, u32[]{:S(2)}) collective-permute-start(f32[104,128]{1,0:T(8,128)S(1)} %add.4.a), channel_id=1, source_target_pairs={{0,7},{1,6},{2,5},{3,4},{4,3},{5,2},{6,1},{7,0},{8,15},{9,14},{10,... | collective-permute-start | bytes 159752 | tf_op jit(solution)/shard_map/ppermute | solution.py:304
  31.2 4.9 %collective-permute-start.8 = (f32[104,128]{1,0:T(8,128)S(1)}, f32[104,128]{1,0:T(8,128)S(1)}, u32[]{:S(2)}, u32[]{:S(2)}) collective-permute-start(f32[104,128]{1,0:T(8,128)S(1)} %add.4.a), channel_id=1, source_target_pairs={{0,4},{1,5},{2,6},{3,7},{4,0},{5,1},{6,2},{7,3},{8,12},{9,13},{10,... | collective-permute-start | bytes 159752 | tf_op jit(solution)/shard_map/ppermute | solution.py:304
  31.5 4.5 %collective-permute-start.7 = (f32[104,128]{1,0:T(8,128)S(1)}, f32[104,128]{1,0:T(8,128)S(1)}, u32[]{:S(2)}, u32[]{:S(2)}) collective-permute-start(f32[104,128]{1,0:T(8,128)S(1)} %add.4.a), channel_id=1, source_target_pairs={{0,3},{1,2},{2,1},{3,0},{4,7},{5,6},{6,5},{7,4},{8,11},{9,10},{10,... | collective-permute-start | bytes 159752 | tf_op jit(solution)/shard_map/ppermute | solution.py:304
  36.1 4.8 %collective-permute-start.12 = (f32[96,128]{1,0:T(8,128)S(1)}, f32[96,128]{1,0:T(8,128)S(1)}, u32[]{:S(2)}, u32[]{:S(2)}) collective-permute-start(f32[96,128]{1,0:T(8,128)S(1)} %get-tuple-element.49.z0), channel_id=1, source_target_pairs={{0,97},{1,96},{32,65},{33,64},{64,33},{65,32},{96,1},{97,0},{2,99}... | collective-permute-start | bytes 147464 | tf_op jit(solution)/shard_map/ppermute | solution.py:304
  38.0 5.2 %collective-permute-start.11 = (f32[96,128]{1,0:T(8,128)S(1)}, f32[96,128]{1,0:T(8,128)S(1)}, u32[]{:S(2)}, u32[]{:S(2)}) collective-permute-start(f32[96,128]{1,0:T(8,128)S(1)} %get-tuple-element.49.z0), channel_id=1, source_target_pairs={{0,64},{1,65},{32,96},{33,97},{64,0},{65,1},{96,32},{97,33},{2,66}... | collective-permute-start | bytes 147464 | tf_op jit(solution)/shard_map/ppermute | solution.py:304
  38.8 4.5 %collective-permute-start.10 = (f32[96,128]{1,0:T(8,128)S(1)}, f32[96,128]{1,0:T(8,128)S(1)}, u32[]{:S(2)}, u32[]{:S(2)}) collective-permute-start(f32[96,128]{1,0:T(8,128)S(1)} %get-tuple-element.49.z0), channel_id=1, source_target_pairs={{0,33},{1,32},{32,1},{33,0},{64,97},{65,96},{96,65},{97,64},{2,35}... | collective-permute-start | bytes 147464 | tf_op jit(solution)/shard_map/ppermute | solution.py:304
  43.4 5.6 %collective-permute-start.15 = (f32[96,128]{1,0:T(8,128)S(1)}, f32[96,128]{1,0:T(8,128)S(1)}, u32[]{:S(2)}, u32[]{:S(2)}) collective-permute-start(f32[96,128]{1,0:T(8,128)S(1)} %normal.2.refs_0_.q0), channel_id=1, source_target_pairs={{0,25},{1,24},{8,17},{9,16},{16,9},{17,8},{24,1},{25,0},{2,27},{3,... | collective-permute-start | bytes 147464 | tf_op jit(solution)/shard_map/ppermute | solution.py:304
  44.9 5.0 %collective-permute-start.14 = (f32[96,128]{1,0:T(8,128)S(1)}, f32[96,128]{1,0:T(8,128)S(1)}, u32[]{:S(2)}, u32[]{:S(2)}) collective-permute-start(f32[96,128]{1,0:T(8,128)S(1)} %normal.2.refs_0_.q0), channel_id=1, source_target_pairs={{0,16},{1,17},{8,24},{9,25},{16,0},{17,1},{24,8},{25,9},{2,18},{3,... | collective-permute-start | bytes 147464 | tf_op jit(solution)/shard_map/ppermute | solution.py:304
  45.4 5.1 %collective-permute-start.13 = (f32[96,128]{1,0:T(8,128)S(1)}, f32[96,128]{1,0:T(8,128)S(1)}, u32[]{:S(2)}, u32[]{:S(2)}) collective-permute-start(f32[96,128]{1,0:T(8,128)S(1)} %normal.2.refs_0_.q0), channel_id=1, source_target_pairs={{0,9},{1,8},{8,1},{9,0},{16,25},{17,24},{24,17},{25,16},{2,11},{3,... | collective-permute-start | bytes 147464 | tf_op jit(solution)/shard_map/ppermute | solution.py:304
  50.5 1.6 %collective-permute-start.16 = (f32[392,128]{1,0:T(8,128)S(1)}, f32[392,128]{1,0:T(8,128)S(1)}, u32[]{:S(2)}, u32[]{:S(2)}) collective-permute-start(f32[392,128]{1,0:T(8,128)S(1)} %join.2), channel_id=1, source_target_pairs={{0,1},{1,0},{2,3},{3,2},{4,5},{5,4},{6,7},{7,6},{8,9},{9,8},{10,11... | collective-permute-start | bytes 602120 | tf_op jit(solution)/shard_map/ppermute | solution.py:300
  53.6 3.9 %collective-permute-start.19 = (f32[16,192]{1,0:T(8,128)S(1)}, f32[16,192]{1,0:T(8,128)S(1)}, u32[]{:S(2)}, u32[]{:S(2)}) collective-permute-start(f32[16,192]{1,0:T(8,128)S(1)} %left_both.1.p0), channel_id=1, source_target_pairs={{0,96},{32,64},{64,32},{96,0},{1,97},{33,65},{65,33},{97,1},{2,98}... | collective-permute-start | bytes 36872 | tf_op jit(solution)/shard_map/ppermute | solution.py:300
  55.0 4.1 %collective-permute-start.18 = (f32[16,192]{1,0:T(8,128)S(1)}, f32[16,192]{1,0:T(8,128)S(1)}, u32[]{:S(2)}, u32[]{:S(2)}) collective-permute-start(f32[16,192]{1,0:T(8,128)S(1)} %left_both.1.p0), channel_id=1, source_target_pairs={{0,64},{32,96},{64,0},{96,32},{1,65},{33,97},{65,1},{97,33},{2,66}... | collective-permute-start | bytes 36872 | tf_op jit(solution)/shard_map/ppermute | solution.py:300
  55.9 3.2 %collective-permute-start.17 = (f32[16,192]{1,0:T(8,128)S(1)}, f32[16,192]{1,0:T(8,128)S(1)}, u32[]{:S(2)}, u32[]{:S(2)}) collective-permute-start(f32[16,192]{1,0:T(8,128)S(1)} %left_both.1.p0), channel_id=1, source_target_pairs={{0,32},{32,0},{64,96},{96,64},{1,33},{33,1},{65,97},{97,65},{2,34}... | collective-permute-start | bytes 36872 | tf_op jit(solution)/shard_map/ppermute | solution.py:300
  60.1 3.2 %collective-permute-start.20 = (f32[4,104,128]{2,1,0:T(8,128)S(1)}, f32[4,104,128]{2,1,0:T(8,128)S(1)}, u32[]{:S(2)}, u32[]{:S(2)}) collective-permute-start(f32[4,104,128]{2,1,0:T(8,128)S(1)} %right_other.3), channel_id=1, source_target_pairs={{0,1},{1,0},{2,3},{3,2},{4,5},{5,4},{6,7},{7,6},{8,9},{9,8},{10,11... | collective-permute-start | bytes 638984 | tf_op jit(solution)/shard_map/ppermute | solution.py:300
  63.2 4.5 %collective-permute-start.21 = (f32[104,128]{1,0:T(8,128)S(1)}, f32[104,128]{1,0:T(8,128)S(1)}, u32[]{:S(2)}, u32[]{:S(2)}) collective-permute-start(f32[104,128]{1,0:T(8,128)S(1)} %get-tuple-element.56), channel_id=1, source_target_pairs={{0,9},{1,8},{8,1},{9,0},{16,25},{17,24},{24,17},{25,16},{2,11},{3,... | collective-permute-start | bytes 159752 | tf_op jit(solution)/shard_map/ppermute | solution.py:304
  64.5 5.3 %collective-permute-start.22 = (f32[104,128]{1,0:T(8,128)S(1)}, f32[104,128]{1,0:T(8,128)S(1)}, u32[]{:S(2)}, u32[]{:S(2)}) collective-permute-start(f32[104,128]{1,0:T(8,128)S(1)} %get-tuple-element.57), channel_id=1, source_target_pairs={{0,16},{1,17},{8,24},{9,25},{16,0},{17,1},{24,8},{25,9},{2,18},{3,... | collective-permute-start | bytes 159752 | tf_op jit(solution)/shard_map/ppermute | solution.py:304
  66.6 5.1 %collective-permute-start.23 = (f32[104,128]{1,0:T(8,128)S(1)}, f32[104,128]{1,0:T(8,128)S(1)}, u32[]{:S(2)}, u32[]{:S(2)}) collective-permute-start(f32[104,128]{1,0:T(8,128)S(1)} %get-tuple-element.58), channel_id=1, source_target_pairs={{0,25},{1,24},{8,17},{9,16},{16,9},{17,8},{24,1},{25,0},{2,27},{3,... | collective-permute-start | bytes 159752 | tf_op jit(solution)/shard_map/ppermute | solution.py:304
  71.7 5.1 %collective-permute-start.26 = (f32[104,128]{1,0:T(8,128)S(1)}, f32[104,128]{1,0:T(8,128)S(1)}, u32[]{:S(2)}, u32[]{:S(2)}) collective-permute-start(f32[104,128]{1,0:T(8,128)S(1)} %add.6.a), channel_id=1, source_target_pairs={{0,7},{1,6},{2,5},{3,4},{4,3},{5,2},{6,1},{7,0},{8,15},{9,14},{10,... | collective-permute-start | bytes 159752 | tf_op jit(solution)/shard_map/ppermute | solution.py:304
  73.4 4.9 %collective-permute-start.25 = (f32[104,128]{1,0:T(8,128)S(1)}, f32[104,128]{1,0:T(8,128)S(1)}, u32[]{:S(2)}, u32[]{:S(2)}) collective-permute-start(f32[104,128]{1,0:T(8,128)S(1)} %add.6.a), channel_id=1, source_target_pairs={{0,4},{1,5},{2,6},{3,7},{4,0},{5,1},{6,2},{7,3},{8,12},{9,13},{10,... | collective-permute-start | bytes 159752 | tf_op jit(solution)/shard_map/ppermute | solution.py:304
  73.9 5.0 %collective-permute-start.24 = (f32[104,128]{1,0:T(8,128)S(1)}, f32[104,128]{1,0:T(8,128)S(1)}, u32[]{:S(2)}, u32[]{:S(2)}) collective-permute-start(f32[104,128]{1,0:T(8,128)S(1)} %add.6.a), channel_id=1, source_target_pairs={{0,3},{1,2},{2,1},{3,0},{4,7},{5,6},{6,5},{7,4},{8,11},{9,10},{10,... | collective-permute-start | bytes 159752 | tf_op jit(solution)/shard_map/ppermute | solution.py:304
  78.9 5.4 %collective-permute-start.29 = (f32[96,128]{1,0:T(8,128)S(1)}, f32[96,128]{1,0:T(8,128)S(1)}, u32[]{:S(2)}, u32[]{:S(2)}) collective-permute-start(f32[96,128]{1,0:T(8,128)S(1)} %get-tuple-element.59.z0), channel_id=1, source_target_pairs={{0,97},{1,96},{32,65},{33,64},{64,33},{65,32},{96,1},{97,0},{2,99}... | collective-permute-start | bytes 147464 | tf_op jit(solution)/shard_map/ppermute | solution.py:304
  80.4 4.4 %collective-permute-start.28 = (f32[96,128]{1,0:T(8,128)S(1)}, f32[96,128]{1,0:T(8,128)S(1)}, u32[]{:S(2)}, u32[]{:S(2)}) collective-permute-start(f32[96,128]{1,0:T(8,128)S(1)} %get-tuple-element.59.z0), channel_id=1, source_target_pairs={{0,64},{1,65},{32,96},{33,97},{64,0},{65,1},{96,32},{97,33},{2,66}... | collective-permute-start | bytes 147464 | tf_op jit(solution)/shard_map/ppermute | solution.py:304
  81.3 4.4 %collective-permute-start.27 = (f32[96,128]{1,0:T(8,128)S(1)}, f32[96,128]{1,0:T(8,128)S(1)}, u32[]{:S(2)}, u32[]{:S(2)}) collective-permute-start(f32[96,128]{1,0:T(8,128)S(1)} %get-tuple-element.59.z0), channel_id=1, source_target_pairs={{0,33},{1,32},{32,1},{33,0},{64,97},{65,96},{96,65},{97,64},{2,35}... | collective-permute-start | bytes 147464 | tf_op jit(solution)/shard_map/ppermute | solution.py:304
  85.9 5.2 %collective-permute-start.32 = (f32[96,128]{1,0:T(8,128)S(1)}, f32[96,128]{1,0:T(8,128)S(1)}, u32[]{:S(2)}, u32[]{:S(2)}) collective-permute-start(f32[96,128]{1,0:T(8,128)S(1)} %normal.3.refs_0_.q0), channel_id=1, source_target_pairs={{0,25},{1,24},{8,17},{9,16},{16,9},{17,8},{24,1},{25,0},{2,27},{3,... | collective-permute-start | bytes 147464 | tf_op jit(solution)/shard_map/ppermute | solution.py:304
  87.4 5.0 %collective-permute-start.31 = (f32[96,128]{1,0:T(8,128)S(1)}, f32[96,128]{1,0:T(8,128)S(1)}, u32[]{:S(2)}, u32[]{:S(2)}) collective-permute-start(f32[96,128]{1,0:T(8,128)S(1)} %normal.3.refs_0_.q0), channel_id=1, source_target_pairs={{0,16},{1,17},{8,24},{9,25},{16,0},{17,1},{24,8},{25,9},{2,18},{3,... | collective-permute-start | bytes 147464 | tf_op jit(solution)/shard_map/ppermute | solution.py:304
  87.7 5.1 %collective-permute-start.30 = (f32[96,128]{1,0:T(8,128)S(1)}, f32[96,128]{1,0:T(8,128)S(1)}, u32[]{:S(2)}, u32[]{:S(2)}) collective-permute-start(f32[96,128]{1,0:T(8,128)S(1)} %normal.3.refs_0_.q0), channel_id=1, source_target_pairs={{0,9},{1,8},{8,1},{9,0},{16,25},{17,24},{24,17},{25,16},{2,11},{3,... | collective-permute-start | bytes 147464 | tf_op jit(solution)/shard_map/ppermute | solution.py:304
  92.8 2.6 %collective-permute-start.33 = (f32[392,128]{1,0:T(8,128)S(1)}, f32[392,128]{1,0:T(8,128)S(1)}, u32[]{:S(2)}, u32[]{:S(2)}) collective-permute-start(f32[392,128]{1,0:T(8,128)S(1)} %join.3), channel_id=1, source_target_pairs={{0,1},{1,0},{2,3},{3,2},{4,5},{5,4},{6,7},{7,6},{8,9},{9,8},{10,11... | collective-permute-start | bytes 602120 | tf_op jit(solution)/shard_map/ppermute | solution.py:300

commit v7 on v6

--- a/solution.py
+++ b/solution.py
@@ -28,7 +28,7 @@
     return pltpu.with_memory_space_constraint(a, pltpu.HBM)
 
 
-def kernel(body, out_shape, in_specs, name, scratch=(), limit=16, flops=10**7):
+def kernel(body, out_shape, in_specs, name, scratch=(), limit=16, flops=10**7, aliases=None):
     many = isinstance(out_shape, tuple)
     out_specs = tuple(ANYWHERE if isinstance(s, jax.ShapeDtypeStruct) else IN_VMEM for s in (out_shape if many else (out_shape,)))
     return pl.pallas_call(
@@ -37,6 +37,7 @@
         out_specs=out_specs if many else out_specs[0],
         out_shape=out_shape,
         scratch_shapes=list(scratch),
+        input_output_aliases=aliases or {},
         compiler_params=pltpu.CompilerParams(vmem_limit_bytes=limit * 1024 * 1024),
         cost_estimate=pl.CostEstimate(flops=flops, bytes_accessed=10**6, transcendentals=0),
         name=name,
@@ -91,6 +92,10 @@
 def matrix(slot):
     parity = lax.axis_index("x") ^ lax.axis_index("y") ^ lax.axis_index("dp")
     return lax.axis_index("core") ^ (parity & 1) ^ slot
+
+
+def here():
+    return lax.axis_index("core")
 
 
 def rows(m):
@@ -134,71 +139,122 @@
     )(hbm(grads), hbm(errors), hbm(q))
 
 
-def left_kernel(slot, ks, at, n_q, *refs):
-    q_refs, (g_ref, e_ref), acc_ref, o_ref = refs[:n_q], refs[n_q : n_q + 2], refs[n_q + 2 : -1], refs[-1]
+def working_kernel(g_ref, e_ref, o_ref):
+    m = matrix(1)
+    for c in range(STEPS):
+        o_ref[:, cols(c)] = g_ref[m, :, cols(c)].astype(F32) + e_ref[m, :, cols(c)].astype(F32)
+
+
+def working(g, e):
+    return kernel(working_kernel, pltpu.VMEM((ROWS, COLS), F32), [IN_VMEM] * 2, "working", flops=10**9)(vmem(g), vmem(e))
+
+
+def halves_kernel(w_ref, high_ref, low_ref):
+    for c in range(STEPS):
+        w = w_ref[:, cols(c)]
+        high = w.astype(BF16)
+        high_ref[:, cols(c)] = high
+        low_ref[:, cols(c)] = (w - high.astype(F32)).astype(BF16)
+
+
+def halves(w):
+    out = pltpu.VMEM((ROWS, COLS), BF16)
+    return kernel(halves_kernel, (out, out), [IN_VMEM], "halves", flops=10**9)(vmem(w))
+
+
+def left_kernel(ks, *refs):
+    n = len(ks)
+    q_refs, (g_ref, e_ref, high_ref, low_ref), acc_ref, o_ref = refs[:n], refs[n : n + 4], refs[n + 4 : -1], refs[-1]
+    m = matrix(0)
+    acc = [acc_ref[0][i] if acc_ref else jnp.zeros((24, ROWS), F32) for i in range(2)]
+    for q_ref, k in zip(q_refs, ks):
+        for h in range(2):
+            s = half(k, h)
+            q = three(block_of(q_ref, 0, h))
+            for w in (g_ref[m, :, s], e_ref[m, :, s]):
+                acc[0] = acc[0] + lax.dot_general(q, w, NT, preferred_element_type=F32)
+            for w in (high_ref[:, s], low_ref[:, s]):
+                acc[1] = acc[1] + lax.dot_general(q, w, NT, preferred_element_type=F32)
+    if len(o_ref.shape) == 3:
+        for i in range(2):
+            o_ref[i] = acc[i]
+    else:
+        for i in range(2):
+            o_ref[rows(here() ^ i), :] = fold(acc[i])
+
+
+def left_part(ks, parts, w, acc=(), last=False):
+    out = pltpu.VMEM((16, ROWS) if last else (2, 24, ROWS), F32)
+    return kernel(functools.partial(left_kernel, ks), out, [IN_VMEM] * (len(parts) + 4 + len(acc)), "left_factor", flops=10**9)(
+        *map(vmem, (*parts, *w, *acc)))
+
+
+def gram_tile(*ps):
+    gram = sum(lax.dot_general(p, p, NT, precision=lax.Precision.HIGHEST, preferred_element_type=F32) for p in ps)
+    return jnp.concatenate([gram, jnp.zeros((8, 120), F32)], axis=1)
+
+
+def mean_of(p0, p1, p2, p3):
+    return ((p0[...] + p1[...]) + (p2[...] + p3[...])) * (1.0 / SIDE)
+
+
+def put_tiles(o_ref, k, h, r):
+    for i in range(BLOCK // 128):
+        t = (h * (BLOCK // 128) + i) * 8
+        o_ref[(slice(t, t + 8),) if k is None else (k, slice(t, t + 8))] = r[:, i * 128 : (i + 1) * 128]
+
+
+def right_kernel(slot, p0, p1, p2, p3, g_ref, e_ref, o_ref):
     m = matrix(slot)
-    acc = acc_ref[0][...] if acc_ref else jnp.zeros((24, ROWS), F32)
-    for i, k in enumerate(ks):
-        q_ref = q_refs[i if n_q > 1 else 0]
-        for h in range(2):
-            q = three(block_of(q_ref, k if at else 0, h))
-            acc = acc + lax.dot_general(q, g_ref[m, :, half(k, h)], NT, preferred_element_type=F32)
-            acc = acc + lax.dot_general(q, e_ref[m, :, half(k, h)], NT, preferred_element_type=F32)
-    o_ref[...] = acc
-
-
-def left_part(slot, ks, parts, g, e, acc=()):
-    at = parts[0].shape[0] > DEEP
-    return kernel(
-        functools.partial(left_kernel, slot, ks, at, len(parts)), pltpu.VMEM((24, ROWS), F32), [IN_VMEM] * (len(parts) + 2 + len(acc)),
-        "left_own" if slot == 0 else "left_other", flops=10**9,
-    )(*map(vmem, parts), vmem(g), vmem(e), *map(vmem, acc))
-
-
-def both_kernel(own_ref, other_ref, p_ref):
-    p_ref[rows(matrix(0)), :] = fold(own_ref[...])
-    p_ref[rows(matrix(1)), :] = fold(other_ref[...])
-
-
-def left_both(own, other):
-    return kernel(both_kernel, pltpu.VMEM((16, ROWS), F32), [IN_VMEM] * 2, "left_both")(vmem(own), vmem(other))
-
-
-def right_kernel(slot, p0, p1, p2, p3, g_ref, e_ref, o_ref, *mean_ref):
-    m = matrix(slot)
-    p = ((p0[...] + p1[...]) + (p2[...] + p3[...])) * (1.0 / SIDE)
-    if mean_ref:
-        mean_ref[0][...] = p
+    p = mean_of(p0, p1, p2, p3)
     p = jnp.where(m == 0, p[0:8], p[8:16])
     pieces = three(p)
-    gram = lax.dot_general(p, p, NT, precision=lax.Precision.HIGHEST, preferred_element_type=F32)
-    gram = jnp.concatenate([gram, jnp.zeros((8, 120), F32)], axis=1)
+    gram = gram_tile(p)
     for k in range(SIDE):
         o_ref[k, DEEP : DEEP + 8, :] = gram
         for h in range(2):
             s = slice(k * QUARTER + h * BLOCK, k * QUARTER + (h + 1) * BLOCK)
             r = jnp.dot(pieces, g_ref[m, :, s], preferred_element_type=F32)
-            r = fold(r + jnp.dot(pieces, e_ref[m, :, s], preferred_element_type=F32))
-            for i in range(BLOCK // 128):
-                t = h * (BLOCK // 128) + i
-                o_ref[k, t * 8 : t * 8 + 8, :] = r[:, i * 128 : (i + 1) * 128]
-
-
-def right(slot, p_all, g, e, keep=False):
-    out = (pltpu.VMEM((SIDE, DEEP + 8, 128), F32),) + ((pltpu.VMEM((16, ROWS), F32),) if keep else ())
+            put_tiles(o_ref, k, h, fold(r + jnp.dot(pieces, e_ref[m, :, s], preferred_element_type=F32)))
+
+
+def right(slot, p_all, g, e):
     return kernel(
-        functools.partial(right_kernel, slot), out, [IN_VMEM] * 6, "right_own" if slot == 0 else "right_other", flops=10**9,
+        functools.partial(right_kernel, slot), pltpu.VMEM((SIDE, DEEP + 8, 128), F32), [IN_VMEM] * 6,
+        "right_own" if slot == 0 else "right_other", flops=10**9,
     )(*map(vmem, p_all), vmem(g), vmem(e))
 
 
-def pick_kernel(mine_ref, arrived_ref, *o_refs):
-    for k, o_ref in enumerate(o_refs):
+def right_both_kernel(ks, p0, p1, p2, p3, g_ref, e_ref, high_ref, low_ref, *o_refs):
+    m = matrix(0)
+    mean = mean_of(p0, p1, p2, p3)
+    if len(o_refs) > len(ks):
+        o_refs[-1][...] = mean
+    mine, theirs = (jnp.where(core == 0, mean[0:8], mean[8:16]) for core in (here(), here() ^ 1))
+    gram = gram_tile(mean[0:8], mean[8:16])
+    mine, theirs = three(mine), three(theirs)
+    for o_ref, k in zip(o_refs, ks):
+        o_ref[DEEP : DEEP + 8, :] = gram
+        for h in range(2):
+            s = half(k, h)
+            r = jnp.dot(mine, g_ref[m, :, s], preferred_element_type=F32) + jnp.dot(mine, e_ref[m, :, s], preferred_element_type=F32)
+            r = r + jnp.dot(theirs, high_ref[:, s], preferred_element_type=F32)
+            put_tiles(o_ref, None, h, fold(r + jnp.dot(theirs, low_ref[:, s], preferred_element_type=F32)))
+
+
+def right_both(ks, p_all, w, keep):
+    out = (pltpu.VMEM((DEEP + 8, 128), F32),) * len(ks) + ((pltpu.VMEM((16, ROWS), F32),) if keep else ())
+    return kernel(functools.partial(right_both_kernel, ks), out, [IN_VMEM] * 8, "right_both", flops=10**9)(*map(vmem, (*p_all, *w)))
+
+
+def pick_kernel(mine_ref, arrived_ref, _, *o_refs):
+    for k, o_ref in enumerate(o_refs[:SIDE]):
         o_ref[...] = mine_ref[lax.axis_index("x") ^ k] + arrived_ref[lax.axis_index("x") ^ k]
 
 
-def pick(mine, arrived):
-    return kernel(pick_kernel, (pltpu.VMEM((DEEP + 8, 128), F32),) * SIDE, [IN_VMEM] * 2, "pick")(
-        vmem(mine), vmem(arrived))
+def pick(mine, arrived, later):
+    out = (pltpu.VMEM((DEEP + 8, 128), F32),) * SIDE + (pltpu.VMEM(later.shape, later.dtype),)
+    return kernel(pick_kernel, out, [IN_VMEM] * 3, "pick", aliases={2: SIDE})(vmem(mine), vmem(arrived), vmem(later))
 
 
 def add_kernel(a, b, c, d, *o_refs):
@@ -222,7 +278,7 @@
     lower = inverse_lower(gram_ref[...])
     if len(refs) > 1:
         p_ref, o_ref, hat_ref = refs
-        hat_ref[...] = hat_pieces(lower, p_ref[rows(matrix(0)), :])
+        hat_ref[...] = hat_pieces(lower, p_ref[rows(here()), :])
     refs[-2 if len(refs) > 1 else 0][...] = lower
 
 
@@ -242,21 +298,30 @@
     return kernel(normal_kernel, pltpu.VMEM((DEEP, 128), F32), [IN_VMEM] * 5, "normal")(*map(vmem, z_all), vmem(lower))
 
 
-def join_kernel(q0, q1, q2, q3, lower_ref, o_ref):
+def join_kernel(q0, q1, q2, q3, lower_ref, p_ref, o_ref):
     for k, q_ref in enumerate((q0, q1, q2, q3)):
         o_ref[k * DEEP : (k + 1) * DEEP, :] = q_ref[...]
-    o_ref[SIDE * DEEP :, :] = lower_ref[...]
-
-
-def join(parts, lower):
-    return kernel(join_kernel, pltpu.VMEM((SIDE * DEEP + 8, 128), F32), [IN_VMEM] * 5, "join")(*map(vmem, parts), vmem(lower))
-
-
-def final_kernel(slot, ks, n_q, *refs):
-    q_refs, (p_ref, g_ref, e_ref), (a_hbm, n_hbm, q_hbm, a_buf, n_buf, q_buf, a_sem, n_sem, q_sem) = refs[:n_q], refs[n_q : n_q + 3], refs[-9:]
+    first = SIDE * DEEP
+    o_ref[first : first + 8, :] = lower_ref[...]
+    p = p_ref[rows(here() ^ 1), :]
+    o_ref[first + 8 : first + 16, :] = p[:, 0:128]
+    o_ref[first + 16 : first + 24, :] = jnp.concatenate([p[:, 128:ROWS], jnp.zeros((8, 256 - ROWS), F32)], axis=1)
+
+
+def join(parts, lower, p):
+    return kernel(join_kernel, pltpu.VMEM((SIDE * DEEP + 24, 128), F32), [IN_VMEM] * 6, "join")(*map(vmem, (*parts, lower, p)))
+
+
+def final_kernel(slot, ks, n_q, n_in, *refs):
+    q_refs, hat_ref, (g_ref, e_ref) = refs[:n_q], refs[n_q:n_in], refs[n_in : n_in + 2]
+    a_hbm, n_hbm, q_hbm, a_buf, n_buf, q_buf, a_sem, n_sem, q_sem = refs[-9:]
     m = matrix(slot)
     copies = []
-    hat = p_ref[...] if slot == 0 else hat_pieces(q_refs[0][SIDE * DEEP :, :], p_ref[rows(m), :])
+    if hat_ref:
+        hat = hat_ref[0][...]
+    else:
+        lower, p = q_refs[0][SIDE * DEEP : SIDE * DEEP + 8, :], q_refs[0][SIDE * DEEP + 8 :, :]
+        hat = hat_pieces(lower, jnp.concatenate([p[0:8], p[8:16, 0 : ROWS - 128]], axis=1))
     hat = hat[0:ROWS, 0:48]
     for j, k in enumerate(ks):
         for h in range(2):
@@ -278,22 +343,22 @@
         copy.wait()
 
 
-def final(slot, ks, parts, p, g, e, before=()):
+def final(slot, ks, parts, hat, g, e, before=()):
     n = len(ks) * 2
-    n_in = len(parts) + 3
+    n_in = len(parts) + len(hat)
     return pl.pallas_call(
-        functools.partial(final_kernel, slot, ks, len(parts)),
-        in_specs=[IN_VMEM] * n_in + [ANYWHERE] * len(before),
+        functools.partial(final_kernel, slot, ks, len(parts), n_in),
+        in_specs=[IN_VMEM] * (n_in + 2) + [ANYWHERE] * len(before),
         out_specs=(ANYWHERE,) * 3,
         out_shape=(jax.ShapeDtypeStruct((MATS, ROWS, COLS), BF16), jax.ShapeDtypeStruct((1, MATS, ROWS, COLS), BF16),
                    jax.ShapeDtypeStruct((MATS, RANK, COLS), F32)),
         scratch_shapes=[pltpu.VMEM((n, ROWS, BLOCK), BF16), pltpu.VMEM((n, ROWS, BLOCK), BF16),
                         pltpu.VMEM((n, RANK, BLOCK), F32)] + [pltpu.SemaphoreType.DMA((n,))] * 3,
-        input_output_aliases={n_in + i: i for i in range(len(before))},
+        input_output_aliases={n_in + 2 + i: i for i in range(len(before))},
         compiler_params=pltpu.CompilerParams(vmem_limit_bytes=16 * 1024 * 1024),
         cost_estimate=pl.CostEstimate(flops=10**9, bytes_accessed=10**6, transcendentals=0),
         name="residual_own" if slot == 0 else "residual_other",
-    )(*map(vmem, (*parts, p, g, e)), *before)
+    )(*map(vmem, (*parts, *hat, g, e)), *before)
 
 
 def swap(a, axis, k):
@@ -304,43 +369,45 @@
     return lax.ppermute(a, (axis, "core"), [(i * 2 + c, (i ^ k) * 2 + (c ^ (k & 1))) for i in range(SIDE) for c in range(2)])
 
 
-def everyones(a, axis, move):
-    return (a,) + tuple(move(a, axis, k) for k in (1, 2, 3))
-
-
-def right_sum(p_own, g, e, keep):
-    p_all = everyones(p_own, "dp", swap)
-    (theirs,) = right(1, p_all, g, e)
-    arrived = swap(theirs, "core", 1)
-    mine, *p = right(0, p_all, g, e, keep)
-    parts = pick(mine, arrived)
-    (z,) = add((parts[0],) + tuple(cross(parts[k], "x", k) for k in (1, 2, 3)), DEEP + 8)
+def everyones(a, axis, move, order=(1, 2, 3)):
+    moved = {k: move(a, axis, k) for k in order}
+    return (a, moved[1], moved[2], moved[3])
+
+
+def right_sum(parts, p=()):
+    (z,) = add(parts[:1] + tuple(cross(parts[k], "x", k) for k in (1, 2, 3)), DEEP + 8)
     z, gram = add(everyones(z, "y", cross), DEEP, 8)
     z_all = everyones(z, "dp", cross)
     lower, *hat = lower_inverse(gram, p)
-    parts = everyones(normal(z_all, lower), "x", cross)
-    return parts, lower, p + hat
-
-
-def after(parts, out):
-    q1, q2, out = lax.optimization_barrier((parts[1], parts[2], out))
-    return (parts[0], q1, q2, parts[3]), out
+    return everyones(normal(z_all, lower), "x", cross, (2, 1, 3)), lower, hat
+
+
+def after(parts, out, *ks):
+    *late, out = lax.optimization_barrier(tuple(parts[k] for k in ks) + (out,))
+    return tuple(late[ks.index(k)] if k in ks else parts[k] for k in range(SIDE)), out
 
 
 def per_device(grads, errors, q_init):
-    p_own, g, e = first_left(grads, errors, jnp.swapaxes(q_init, 1, 2))
-    parts, lower, _ = right_sum(p_own, g, e, False)
-    own = left_part(0, (0,), parts[:1], g, e)
-    parts, own = after(parts, left_part(0, (3,), parts[3:], g, e, (own,)))
-    q_other = swap(join(parts, lower), "core", 1)
-    own = left_part(0, (1, 2), parts[1:3], g, e, (own,))
-    p_own = left_both(own, left_part(1, (0, 1, 2, 3), (q_other,), g, e))
-    parts, lower, (p, hat) = right_sum(p_own, g, e, True)
+    p, g, e = first_left(grads, errors, jnp.swapaxes(q_init, 1, 2))
+    p_all = everyones(p, "dp", swap)
+    arrived = swap(right(1, p_all, g, e), "core", 1)
+    *parts, w = pick(right(0, p_all, g, e), arrived, working(g, e))
+    w = (g, e) + tuple(halves(swap(w, "core", 1)))
+    parts, _, _ = right_sum(tuple(parts))
+
+    acc = left_part((0,), parts[:1], w)
+    parts, acc = after(parts, left_part((3,), parts[3:], w, (acc,)), 1)
+    acc = left_part((1,), parts[1:2], w, (acc,))
+    p_all = everyones(left_part((2,), parts[2:3], w, (acc,), True), "dp", cross)
+    z2, z3, p = right_both((2, 3), p_all, w, True)
+    z1, z0 = right_both((1, 0), p_all, w, False)
+    parts, lower, hat = right_sum((z0, z1, z2, z3), (p,))
+
     out = final(0, (0,), parts[:1], hat, g, e)
-    parts, out = after(parts, final(0, (3,), parts[3:], hat, g, e, out))
-    q_other = swap(join(parts, lower), "core", 1)
+    parts, out = after(parts, final(0, (3,), parts[3:], hat, g, e, out), 1, 2)
+    other = swap(join(parts, lower, p), "core", 1)
     out = final(0, (1, 2), parts[1:3], hat, g, e, out)
-    approx, errors_next, q_next = final(1, (0, 1, 2, 3), (q_other,), p, g, e, out)
+    approx, errors_next, q_next = final(1, (0, 1, 2, 3), (other,), (), g, e, out)
     return approx, errors_next, jnp.swapaxes(q_next, 1, 2)
 
 

time: 98.6 us -> 95.3 us (0.967)
  waiting for transfers between devices: 29.1 us -> 26.6 us
  starting transfers between devices: 46.8 us -> 45.3 us
    ppermute x10 -> x6, starting transfers between devices: 14.2 us -> 8.55 us  [swap(): lax.ppermute(a, axis, [(i, i ^ k) for i in range(lax.axis_size(axis))])]
    ppermute x24 -> x27, starting transfers between devices: 32.6 us -> 36.7 us  [cross(): lax.ppermute(a, (axis, 'core'), [(i * 2 + c, (i ^ k) * 2 + (c ^ k & 1)) f...]
    ppermute x10 -> x6, waiting for transfers between devices: 6.06 us -> 3.43 us  [swap(): lax.ppermute(a, axis, [(i, i ^ k) for i in range(lax.axis_size(axis))])]
    pallas_call x17 -> x16, Pallas kernels: 14.5 us -> 15.2 us  [the longest x4 7.22 us: final(): pl.pallas_call(functools.partial(final_kernel, slot, ks, len(parts), n_in...]
    ppermute x24 -> x27, waiting for transfers between devices: 23.1 us -> 23.2 us  [cross(): lax.ppermute(a, (axis, 'core'), [(i * 2 + c, (i ^ k) * 2 + (c ^ k & 1)) f...]
  transfers between devices with their start and end apart: 34 -> 33, of which waited for: 25 -> 21; matrix products, arithmetic and copies ran while one was open for 0% -> 0% of each run, Pallas kernels for 10% -> 12%
where the time goes in v7:
time: 95.3 us; the launch traced here: 95.2 us
  starting transfers between devices  45.3 us (48%)
  waiting for transfers between devices  26.6 us (28%)
  Pallas kernels  22.3 us (23%)
  between operations  0.99 us (1%)
    ppermute x27, starting transfers between devices, cross(): lax.ppermute(a, (axis, 'core'), [(i * 2 + c, (i ^ k) * 2 + (c ^ k & 1)) f...  36.7 us
    ppermute x27, waiting for transfers between devices, cross(): lax.ppermute(a, (axis, 'core'), [(i * 2 + c, (i ^ k) * 2 + (c ^ k & 1)) f...  23.2 us
    ppermute x6, starting transfers between devices, swap(): lax.ppermute(a, axis, [(i, i ^ k) for i in range(lax.axis_size(axis))])  8.55 us
    pallas_call x4, Pallas kernels, final(): pl.pallas_call(functools.partial(final_kernel, slot, ks, len(parts), n_in...  7.22 us
    pallas_call x1, Pallas kernels, first_left(): kernel(first_left_kernel, (pltpu.VMEM((16, ROWS), F32), wide, wide), [ANY...  5.25 us
    ppermute x6, waiting for transfers between devices, swap(): lax.ppermute(a, axis, [(i, i ^ k) for i in range(lax.axis_size(axis))])  3.43 us
    pallas_call x4, Pallas kernels, left_part(): kernel(functools.partial(left_kernel, ks), out, [IN_VMEM] * (len(parts) +...  3.17 us
    pallas_call x2, Pallas kernels, right(): kernel(functools.partial(right_kernel, slot), pltpu.VMEM((SIDE, DEEP + 8,...  1.96 us
  transfers between devices with their start and end apart: 33, of which 21 were waited for; matrix products, arithmetic and copies ran while one was open for 0% of the time, Pallas kernels for 12%

profile of v7, /device:TPU:1, one launch (start us, length us, event | category | flops | bytes accessed | tf_op | source)
XLA Modules:
  0.0 95.2 jit_solution(10180645364951975478)
XLA Ops:
  0.6 5.3 %first_left.1 = (f32[16,192]{1,0:T(8,128)S(1)}, bf16[2,192,6144]{2,1,0:T(8,128)(2,1)S(1)}, bf16[2,192,6144]{2,1,0:T(8,128)(2,1)S(1)}) custom-call(bf16[1,2,192,6144]{3,2,1,0:T(8,128)(2,1)} %g_hbm.1, bf16[1,2,192,6144]{3,2,1,0:T(8,128)(2,1)} %e_hbm.1, f32[2,8,6144]{2,1,0:T(8,128)} %bitcast.3), custom_call_target="tpu_custom_call" | custom-call | flops 10000000 | bytes 1000000 | tf_op jit(solution)/shard_map/first_left/pallas_call | solution.py:136
  5.9 4.7 %collective-permute-start.2 = (f32[16,192]{1,0:T(8,128)S(1)}, f32[16,192]{1,0:T(8,128)S(1)}, u32[]{:S(2)}, u32[]{:S(2)}) collective-permute-start(f32[16,192]{1,0:T(8,128)S(1)} %get-tuple-element.43.p0), channel_id=1, source_target_pairs={{0,96},{32,64},{64,32},{96,0},{1,97},{33,65},{65,33},{97,1},{2,98}... | collective-permute-start | bytes 36872 | tf_op jit(solution)/shard_map/ppermute | solution.py:365
  11.7 3.0 %collective-permute-done.1.p2 = f32[16,192]{1,0:T(8,128)S(1)} collective-permute-done((f32[16,192]{1,0:T(8,128)S(1)}, f32[16,192]{1,0:T(8,128)S(1)}, u32[]{:S(2)}, u32[]{:S(2)}) %collective-permute-start.1) | collective-permute-done | bytes 12320 | tf_op jit(solution)/shard_map/ppermute | solution.py:365
  14.7 1.0 %right_other.1 = f32[4,104,128]{2,1,0:T(8,128)S(1)} custom-call(f32[16,192]{1,0:T(8,128)S(1)} %get-tuple-element.43.p0, f32[16,192]{1,0:T(8,128)S(1)} %collective-permute-done.p1, f32[16,192]{1,0:T(8,128)S(1)} %collective-permute-done.1.p2, f32[16,192]{1,0:T(8,128)S(1)} %collective-permute-done.2.p3, ...), custom_call_target="tpu_custom_call" | custom-call | flops 1000000000 | bytes 1000000 | tf_op jit(solution)/shard_map/right_other/pallas_call | solution.py:222
  15.6 2.2 %collective-permute-start.3 = (f32[4,104,128]{2,1,0:T(8,128)S(1)}, f32[4,104,128]{2,1,0:T(8,128)S(1)}, u32[]{:S(2)}, u32[]{:S(2)}) collective-permute-start(f32[4,104,128]{2,1,0:T(8,128)S(1)} %right_other.1), channel_id=1, source_target_pairs={{0,1},{1,0},{2,3},{3,2},{4,5},{5,4},{6,7},{7,6},{8,9},{9,8},{10,11... | collective-permute-start | bytes 638984 | tf_op jit(solution)/shard_map/ppermute | solution.py:365
  18.3 1.0 %right_own.1.mine_ref = f32[4,104,128]{2,1,0:T(8,128)S(1)} custom-call(f32[16,192]{1,0:T(8,128)S(1)} %get-tuple-element.43.p0, f32[16,192]{1,0:T(8,128)S(1)} %collective-permute-done.p1, f32[16,192]{1,0:T(8,128)S(1)} %collective-permute-done.1.p2, f32[16,192]{1,0:T(8,128)S(1)} %collective-permute-done.2.p3, ...), custom_call_target="tpu_custom_call" | custom-call | flops 1000000000 | bytes 1000000 | tf_op jit(solution)/shard_map/right_own/pallas_call | solution.py:222
  19.4 1.6 %collective-permute-start.4 = (f32[104,128]{1,0:T(8,128)S(1)}, f32[104,128]{1,0:T(8,128)S(1)}, u32[]{:S(2)}, u32[]{:S(2)}) collective-permute-start(f32[104,128]{1,0:T(8,128)S(1)} %get-tuple-element.47), channel_id=1, source_target_pairs={{0,9},{1,8},{8,1},{9,0},{16,25},{17,24},{24,17},{25,16},{2,11},{3,... | collective-permute-start | bytes 159752 | tf_op jit(solution)/shard_map/ppermute | solution.py:369
  21.0 2.5 %collective-permute-start.5 = (f32[104,128]{1,0:T(8,128)S(1)}, f32[104,128]{1,0:T(8,128)S(1)}, u32[]{:S(2)}, u32[]{:S(2)}) collective-permute-start(f32[104,128]{1,0:T(8,128)S(1)} %get-tuple-element.48), channel_id=1, source_target_pairs={{0,16},{1,17},{8,24},{9,25},{16,0},{17,1},{24,8},{25,9},{2,18},{3,... | collective-permute-start | bytes 159752 | tf_op jit(solution)/shard_map/ppermute | solution.py:369
  23.9 2.8 %collective-permute-done.5.c = f32[104,128]{1,0:T(8,128)S(1)} collective-permute-done((f32[104,128]{1,0:T(8,128)S(1)}, f32[104,128]{1,0:T(8,128)S(1)}, u32[]{:S(2)}, u32[]{:S(2)}) %collective-permute-start.5) | collective-permute-done | bytes 53280 | tf_op jit(solution)/shard_map/ppermute | solution.py:369
  26.7 1.8 %collective-permute-done.6.d = f32[104,128]{1,0:T(8,128)S(1)} collective-permute-done((f32[104,128]{1,0:T(8,128)S(1)}, f32[104,128]{1,0:T(8,128)S(1)}, u32[]{:S(2)}, u32[]{:S(2)}) %collective-permute-start.6) | collective-permute-done | bytes 53280 | tf_op jit(solution)/shard_map/ppermute | solution.py:369
  28.5 3.1 %collective-permute-start.9 = (f32[104,128]{1,0:T(8,128)S(1)}, f32[104,128]{1,0:T(8,128)S(1)}, u32[]{:S(2)}, u32[]{:S(2)}) collective-permute-start(f32[104,128]{1,0:T(8,128)S(1)} %add.4.a), channel_id=1, source_target_pairs={{0,7},{1,6},{2,5},{3,4},{4,3},{5,2},{6,1},{7,0},{8,15},{9,14},{10,... | collective-permute-start | bytes 159752 | tf_op jit(solution)/shard_map/ppermute | solution.py:369
  32.5 1.4 %collective-permute-done.9.d = f32[104,128]{1,0:T(8,128)S(1)} collective-permute-done((f32[104,128]{1,0:T(8,128)S(1)}, f32[104,128]{1,0:T(8,128)S(1)}, u32[]{:S(2)}, u32[]{:S(2)}) %collective-permute-start.9) | collective-permute-done | bytes 53280 | tf_op jit(solution)/shard_map/ppermute | solution.py:369
  33.9 2.2 %collective-permute-done.8.c = f32[104,128]{1,0:T(8,128)S(1)} collective-permute-done((f32[104,128]{1,0:T(8,128)S(1)}, f32[104,128]{1,0:T(8,128)S(1)}, u32[]{:S(2)}, u32[]{:S(2)}) %collective-permute-start.8) | collective-permute-done | bytes 53280 | tf_op jit(solution)/shard_map/ppermute | solution.py:369
  36.1 2.3 %collective-permute-start.12 = (f32[96,128]{1,0:T(8,128)S(1)}, f32[96,128]{1,0:T(8,128)S(1)}, u32[]{:S(2)}, u32[]{:S(2)}) collective-permute-start(f32[96,128]{1,0:T(8,128)S(1)} %get-tuple-element.50.z0), channel_id=1, source_target_pairs={{0,97},{1,96},{32,65},{33,64},{64,33},{65,32},{96,1},{97,0},{2,99}... | collective-permute-start | bytes 147464 | tf_op jit(solution)/shard_map/ppermute | solution.py:369
  39.1 0.8 collective-permute-start.10
  40.9 2.8 %collective-permute-done.11.z2 = f32[96,128]{1,0:T(8,128)S(1)} collective-permute-done((f32[96,128]{1,0:T(8,128)S(1)}, f32[96,128]{1,0:T(8,128)S(1)}, u32[]{:S(2)}, u32[]{:S(2)}) %collective-permute-start.11) | collective-permute-done | bytes 49184 | tf_op jit(solution)/shard_map/ppermute | solution.py:369
  43.8 1.6 %collective-permute-start.16 = (f32[96,128]{1,0:T(8,128)S(1)}, f32[96,128]{1,0:T(8,128)S(1)}, u32[]{:S(2)}, u32[]{:S(2)}) collective-permute-start(f32[96,128]{1,0:T(8,128)S(1)} %normal.2.refs_0_), channel_id=1, source_target_pairs={{0,25},{1,24},{8,17},{9,16},{16,9},{17,8},{24,1},{25,0},{2,27},{3,... | collective-permute-start | bytes 147464 | tf_op jit(solution)/shard_map/ppermute | solution.py:369
  45.4 2.6 %collective-permute-start.13 = (f32[96,128]{1,0:T(8,128)S(1)}, f32[96,128]{1,0:T(8,128)S(1)}, u32[]{:S(2)}, u32[]{:S(2)}) collective-permute-start(f32[96,128]{1,0:T(8,128)S(1)} %normal.2.refs_0_), channel_id=1, source_target_pairs={{0,16},{1,17},{8,24},{9,25},{16,0},{17,1},{24,8},{25,9},{2,18},{3,... | collective-permute-start | bytes 147464 | tf_op jit(solution)/shard_map/ppermute | solution.py:369
  51.1 0.8 left_factor.7.p0
  51.9 1.9 %collective-permute-start.19 = (f32[16,192]{1,0:T(8,128)S(1)}, f32[16,192]{1,0:T(8,128)S(1)}, u32[]{:S(2)}, u32[]{:S(2)}) collective-permute-start(f32[16,192]{1,0:T(8,128)S(1)} %left_factor.7.p0), channel_id=1, source_target_pairs={{0,97},{1,96},{32,65},{33,64},{64,33},{65,32},{96,1},{97,0},{2,99}... | collective-permute-start | bytes 36872 | tf_op jit(solution)/shard_map/ppermute | solution.py:369
  53.8 0.8 collective-permute-start.18
  54.6 1.2 %collective-permute-start.17 = (f32[16,192]{1,0:T(8,128)S(1)}, f32[16,192]{1,0:T(8,128)S(1)}, u32[]{:S(2)}, u32[]{:S(2)}) collective-permute-start(f32[16,192]{1,0:T(8,128)S(1)} %left_factor.7.p0), channel_id=1, source_target_pairs={{0,33},{1,32},{32,1},{33,0},{64,97},{65,96},{96,65},{97,64},{2,35}... | collective-permute-start | bytes 36872 | tf_op jit(solution)/shard_map/ppermute | solution.py:369
  55.8 0.9 collective-permute-done.19.p3
  56.7 1.2 %collective-permute-done.18.p2 = f32[16,192]{1,0:T(8,128)S(1)} collective-permute-done((f32[16,192]{1,0:T(8,128)S(1)}, f32[16,192]{1,0:T(8,128)S(1)}, u32[]{:S(2)}, u32[]{:S(2)}) %collective-permute-start.18) | collective-permute-done | bytes 12320 | tf_op jit(solution)/shard_map/ppermute | solution.py:369
  58.2 0.8 right_both.2
  59.0 1.4 %collective-permute-start.20 = (f32[104,128]{1,0:T(8,128)S(1)}, f32[104,128]{1,0:T(8,128)S(1)}, u32[]{:S(2)}, u32[]{:S(2)}) collective-permute-start(f32[104,128]{1,0:T(8,128)S(1)} %get-tuple-element.58), channel_id=1, source_target_pairs={{0,9},{1,8},{8,1},{9,0},{16,25},{17,24},{24,17},{25,16},{2,11},{3,... | collective-permute-start | bytes 159752 | tf_op jit(solution)/shard_map/ppermute | solution.py:369
  60.5 0.8 right_both.3
  61.3 1.8 %collective-permute-start.21 = (f32[104,128]{1,0:T(8,128)S(1)}, f32[104,128]{1,0:T(8,128)S(1)}, u32[]{:S(2)}, u32[]{:S(2)}) collective-permute-start(f32[104,128]{1,0:T(8,128)S(1)} %get-tuple-element.59), channel_id=1, source_target_pairs={{0,16},{1,17},{8,24},{9,25},{16,0},{17,1},{24,8},{25,9},{2,18},{3,... | collective-permute-start | bytes 159752 | tf_op jit(solution)/shard_map/ppermute | solution.py:369
  63.1 1.3 %collective-permute-start.22 = (f32[104,128]{1,0:T(8,128)S(1)}, f32[104,128]{1,0:T(8,128)S(1)}, u32[]{:S(2)}, u32[]{:S(2)}) collective-permute-start(f32[104,128]{1,0:T(8,128)S(1)} %get-tuple-element.60), channel_id=1, source_target_pairs={{0,25},{1,24},{8,17},{9,16},{16,9},{17,8},{24,1},{25,0},{2,27},{3,... | collective-permute-start | bytes 159752 | tf_op jit(solution)/shard_map/ppermute | solution.py:369
  64.4 1.9 %collective-permute-done.21.c = f32[104,128]{1,0:T(8,128)S(1)} collective-permute-done((f32[104,128]{1,0:T(8,128)S(1)}, f32[104,128]{1,0:T(8,128)S(1)}, u32[]{:S(2)}, u32[]{:S(2)}) %collective-permute-start.21) | collective-permute-done | bytes 53280 | tf_op jit(solution)/shard_map/ppermute | solution.py:369
  66.4 1.6 %collective-permute-done.22.d = f32[104,128]{1,0:T(8,128)S(1)} collective-permute-done((f32[104,128]{1,0:T(8,128)S(1)}, f32[104,128]{1,0:T(8,128)S(1)}, u32[]{:S(2)}, u32[]{:S(2)}) %collective-permute-start.22) | collective-permute-done | bytes 53280 | tf_op jit(solution)/shard_map/ppermute | solution.py:369
  68.0 1.1 %collective-permute-start.25 = (f32[104,128]{1,0:T(8,128)S(1)}, f32[104,128]{1,0:T(8,128)S(1)}, u32[]{:S(2)}, u32[]{:S(2)}) collective-permute-start(f32[104,128]{1,0:T(8,128)S(1)} %add.6.a), channel_id=1, source_target_pairs={{0,7},{1,6},{2,5},{3,4},{4,3},{5,2},{6,1},{7,0},{8,15},{9,14},{10,... | collective-permute-start | bytes 159752 | tf_op jit(solution)/shard_map/ppermute | solution.py:369
  69.1 0.9 collective-permute-start.24
  70.0 1.9 %collective-permute-start.23 = (f32[104,128]{1,0:T(8,128)S(1)}, f32[104,128]{1,0:T(8,128)S(1)}, u32[]{:S(2)}, u32[]{:S(2)}) collective-permute-start(f32[104,128]{1,0:T(8,128)S(1)} %add.6.a), channel_id=1, source_target_pairs={{0,3},{1,2},{2,1},{3,0},{4,7},{5,6},{6,5},{7,4},{8,11},{9,10},{10,... | collective-permute-start | bytes 159752 | tf_op jit(solution)/shard_map/ppermute | solution.py:369
  71.9 1.1 %collective-permute-done.25.d = f32[104,128]{1,0:T(8,128)S(1)} collective-permute-done((f32[104,128]{1,0:T(8,128)S(1)}, f32[104,128]{1,0:T(8,128)S(1)}, u32[]{:S(2)}, u32[]{:S(2)}) %collective-permute-start.25) | collective-permute-done | bytes 53280 | tf_op jit(solution)/shard_map/ppermute | solution.py:369
  73.6 1.5 %collective-permute-done.23.b = f32[104,128]{1,0:T(8,128)S(1)} collective-permute-done((f32[104,128]{1,0:T(8,128)S(1)}, f32[104,128]{1,0:T(8,128)S(1)}, u32[]{:S(2)}, u32[]{:S(2)}) %collective-permute-start.23) | collective-permute-done | bytes 53280 | tf_op jit(solution)/shard_map/ppermute | solution.py:369
  75.1 1.9 %collective-permute-start.28 = (f32[96,128]{1,0:T(8,128)S(1)}, f32[96,128]{1,0:T(8,128)S(1)}, u32[]{:S(2)}, u32[]{:S(2)}) collective-permute-start(f32[96,128]{1,0:T(8,128)S(1)} %get-tuple-element.61.z0), channel_id=1, source_target_pairs={{0,97},{1,96},{32,65},{33,64},{64,33},{65,32},{96,1},{97,0},{2,99}... | collective-permute-start | bytes 147464 | tf_op jit(solution)/shard_map/ppermute | solution.py:369
  77.7 1.3 %collective-permute-start.26 = (f32[96,128]{1,0:T(8,128)S(1)}, f32[96,128]{1,0:T(8,128)S(1)}, u32[]{:S(2)}, u32[]{:S(2)}) collective-permute-start(f32[96,128]{1,0:T(8,128)S(1)} %get-tuple-element.61.z0), channel_id=1, source_target_pairs={{0,33},{1,32},{32,1},{33,0},{64,97},{65,96},{96,65},{97,64},{2,35}... | collective-permute-start | bytes 147464 | tf_op jit(solution)/shard_map/ppermute | solution.py:369
  79.0 0.9 lower_inverse.3
  80.6 1.3 %collective-permute-done.27.z2 = f32[96,128]{1,0:T(8,128)S(1)} collective-permute-done((f32[96,128]{1,0:T(8,128)S(1)}, f32[96,128]{1,0:T(8,128)S(1)}, u32[]{:S(2)}, u32[]{:S(2)}) %collective-permute-start.27) | collective-permute-done | bytes 49184 | tf_op jit(solution)/shard_map/ppermute | solution.py:369
  82.4 1.8 %collective-permute-start.31 = (f32[96,128]{1,0:T(8,128)S(1)}, f32[96,128]{1,0:T(8,128)S(1)}, u32[]{:S(2)}, u32[]{:S(2)}) collective-permute-start(f32[96,128]{1,0:T(8,128)S(1)} %normal.3.refs_0_.q0), channel_id=1, source_target_pairs={{0,25},{1,24},{8,17},{9,16},{16,9},{17,8},{24,1},{25,0},{2,27},{3,... | collective-permute-start | bytes 147464 | tf_op jit(solution)/shard_map/ppermute | solution.py:369
  84.1 1.2 %collective-permute-start.30 = (f32[96,128]{1,0:T(8,128)S(1)}, f32[96,128]{1,0:T(8,128)S(1)}, u32[]{:S(2)}, u32[]{:S(2)}) collective-permute-start(f32[96,128]{1,0:T(8,128)S(1)} %normal.3.refs_0_.q0), channel_id=1, source_target_pairs={{0,16},{1,17},{8,24},{9,25},{16,0},{17,1},{24,8},{25,9},{2,18},{3,... | collective-permute-start | bytes 147464 | tf_op jit(solution)/shard_map/ppermute | solution.py:369
  85.3 0.9 collective-permute-start.29
  86.3 1.3 %residual_own.3 = (bf16[2,192,6144]{2,1,0:T(8,128)(2,1)}, bf16[1,2,192,6144]{3,2,1,0:T(8,128)(2,1)}, f32[2,8,6144]{2,1,0:T(8,128)}) custom-call(f32[96,128]{1,0:T(8,128)S(1)} %normal.3.refs_0_.q0, bf16[256,128]{1,0:T(8,128)(2,1)S(1)} %get-tuple-element.65.refs_1_.refs_2_, bf16[2,192,6144]{2,1,0:T(8,128)(2,1)S(1)} %get-tuple-element.44.g_ref.refs_1_.refs_2_.refs_3_, ...), custom_call_target="tpu_custom_call" | custom-call | flops 1000000000 | bytes 1000000 | tf_op jit(solution)/shard_map/residual_own/pallas_call | solution.py:349
  87.6 1.3 %residual_own.4 = (bf16[2,192,6144]{2,1,0:T(8,128)(2,1)}, bf16[1,2,192,6144]{3,2,1,0:T(8,128)(2,1)}, f32[2,8,6144]{2,1,0:T(8,128)}) custom-call(f32[96,128]{1,0:T(8,128)S(1)} %collective-permute-done.31.refs_0_.q3, bf16[256,128]{1,0:T(8,128)(2,1)S(1)} %get-tuple-element.65.refs_1_.refs_2_, ...), custom_call_target="tpu_custom_call", output_to_operand_aliasing={{0}: (4, {}), {1}: (5, {}), {2}: (6, {})} | custom-call | flops 1000000000 | bytes 1000000 | tf_op jit(solution)/shard_map/residual_own/pallas_call | solution.py:349
  89.5 0.9 collective-permute-start.32
  90.4 1.8 %residual_own.5 = (bf16[2,192,6144]{2,1,0:T(8,128)(2,1)}, bf16[1,2,192,6144]{3,2,1,0:T(8,128)(2,1)}, f32[2,8,6144]{2,1,0:T(8,128)}) custom-call(f32[96,128]{1,0:T(8,128)S(1)} %collective-permute-done.29.q1.refs_0_, f32[96,128]{1,0:T(8,128)S(1)} %collective-permute-done.30.q2.refs_1_, ...), custom_call_target="tpu_custom_call", output_to_operand_aliasing={{0}: (5, {}), {1}: (6, {}), {2}: (7, {})} | custom-call | flops 1000000000 | bytes 1000000 | tf_op jit(solution)/shard_map/residual_own/pallas_call | solution.py:349
  92.2 2.8 %residual_other.1 = (bf16[2,192,6144]{2,1,0:T(8,128)(2,1)}, bf16[1,2,192,6144]{3,2,1,0:T(8,128)(2,1)}, f32[2,8,6144]{2,1,0:T(8,128)}) custom-call(f32[408,128]{1,0:T(8,128)S(1)} %collective-permute-done.32.refs_0_, ...), custom_call_target="tpu_custom_call", output_to_operand_aliasing={{0}: (3, {}), {1}: (4, {}), {2}: (5, {})} | custom-call | flops 1000000000 | bytes 1000000 | tf_op jit(solution)/shard_map/residual_other/pallas_call | solution.py:349
  (43 shorter events, 11.5 us)
Async XLA Ops:
  5.9 5.8 %collective-permute-start.2 = (f32[16,192]{1,0:T(8,128)S(1)}, f32[16,192]{1,0:T(8,128)S(1)}, u32[]{:S(2)}, u32[]{:S(2)}) collective-permute-start(f32[16,192]{1,0:T(8,128)S(1)} %get-tuple-element.43.p0), channel_id=1, source_target_pairs={{0,96},{32,64},{64,32},{96,0},{1,97},{33,65},{65,33},{97,1},{2,98}... | collective-permute-start | bytes 36872 | tf_op jit(solution)/shard_map/ppermute | solution.py:365
  10.6 4.1 %collective-permute-start.1 = (f32[16,192]{1,0:T(8,128)S(1)}, f32[16,192]{1,0:T(8,128)S(1)}, u32[]{:S(2)}, u32[]{:S(2)}) collective-permute-start(f32[16,192]{1,0:T(8,128)S(1)} %get-tuple-element.43.p0), channel_id=1, source_target_pairs={{0,64},{32,96},{64,0},{96,32},{1,65},{33,97},{65,1},{97,33},{2,66}... | collective-permute-start | bytes 36872 | tf_op jit(solution)/shard_map/ppermute | solution.py:365
  10.6 4.1 %collective-permute-start = (f32[16,192]{1,0:T(8,128)S(1)}, f32[16,192]{1,0:T(8,128)S(1)}, u32[]{:S(2)}, u32[]{:S(2)}) collective-permute-start(f32[16,192]{1,0:T(8,128)S(1)} %get-tuple-element.43.p0), channel_id=1, source_target_pairs={{0,32},{32,0},{64,96},{96,64},{1,33},{33,1},{65,97},{97,65},{2,34}... | collective-permute-start | bytes 36872 | tf_op jit(solution)/shard_map/ppermute | solution.py:365
  15.6 3.6 %collective-permute-start.3 = (f32[4,104,128]{2,1,0:T(8,128)S(1)}, f32[4,104,128]{2,1,0:T(8,128)S(1)}, u32[]{:S(2)}, u32[]{:S(2)}) collective-permute-start(f32[4,104,128]{2,1,0:T(8,128)S(1)} %right_other.1), channel_id=1, source_target_pairs={{0,1},{1,0},{2,3},{3,2},{4,5},{5,4},{6,7},{7,6},{8,9},{9,8},{10,11... | collective-permute-start | bytes 638984 | tf_op jit(solution)/shard_map/ppermute | solution.py:365
  19.3 28.7 %collective-permute-start.14 = (f32[192,6144]{1,0:T(8,128)S(1)}, f32[192,6144]{1,0:T(8,128)S(1)}, u32[]{:S(2)}, u32[]{:S(2)}) collective-permute-start(f32[192,6144]{1,0:T(8,128)S(1)} %get-tuple-element.52), channel_id=1, source_target_pairs={{0,1},{1,0},{2,3},{3,2},{4,5},{5,4},{6,7},{7,6},{8,9},{9,8},{10,11... | collective-permute-start | bytes 14155784 | tf_op jit(solution)/shard_map/ppermute | solution.py:365
  19.4 4.5 %collective-permute-start.4 = (f32[104,128]{1,0:T(8,128)S(1)}, f32[104,128]{1,0:T(8,128)S(1)}, u32[]{:S(2)}, u32[]{:S(2)}) collective-permute-start(f32[104,128]{1,0:T(8,128)S(1)} %get-tuple-element.47), channel_id=1, source_target_pairs={{0,9},{1,8},{8,1},{9,0},{16,25},{17,24},{24,17},{25,16},{2,11},{3,... | collective-permute-start | bytes 159752 | tf_op jit(solution)/shard_map/ppermute | solution.py:369
  21.0 5.7 %collective-permute-start.5 = (f32[104,128]{1,0:T(8,128)S(1)}, f32[104,128]{1,0:T(8,128)S(1)}, u32[]{:S(2)}, u32[]{:S(2)}) collective-permute-start(f32[104,128]{1,0:T(8,128)S(1)} %get-tuple-element.48), channel_id=1, source_target_pairs={{0,16},{1,17},{8,24},{9,25},{16,0},{17,1},{24,8},{25,9},{2,18},{3,... | collective-permute-start | bytes 159752 | tf_op jit(solution)/shard_map/ppermute | solution.py:369
  23.5 5.0 %collective-permute-start.6 = (f32[104,128]{1,0:T(8,128)S(1)}, f32[104,128]{1,0:T(8,128)S(1)}, u32[]{:S(2)}, u32[]{:S(2)}) collective-permute-start(f32[104,128]{1,0:T(8,128)S(1)} %get-tuple-element.49), channel_id=1, source_target_pairs={{0,25},{1,24},{8,17},{9,16},{16,9},{17,8},{24,1},{25,0},{2,27},{3,... | collective-permute-start | bytes 159752 | tf_op jit(solution)/shard_map/ppermute | solution.py:369
  28.5 5.4 %collective-permute-start.9 = (f32[104,128]{1,0:T(8,128)S(1)}, f32[104,128]{1,0:T(8,128)S(1)}, u32[]{:S(2)}, u32[]{:S(2)}) collective-permute-start(f32[104,128]{1,0:T(8,128)S(1)} %add.4.a), channel_id=1, source_target_pairs={{0,7},{1,6},{2,5},{3,4},{4,3},{5,2},{6,1},{7,0},{8,15},{9,14},{10,... | collective-permute-start | bytes 159752 | tf_op jit(solution)/shard_map/ppermute | solution.py:369
  31.6 4.5 %collective-permute-start.8 = (f32[104,128]{1,0:T(8,128)S(1)}, f32[104,128]{1,0:T(8,128)S(1)}, u32[]{:S(2)}, u32[]{:S(2)}) collective-permute-start(f32[104,128]{1,0:T(8,128)S(1)} %add.4.a), channel_id=1, source_target_pairs={{0,4},{1,5},{2,6},{3,7},{4,0},{5,1},{6,2},{7,3},{8,12},{9,13},{10,... | collective-permute-start | bytes 159752 | tf_op jit(solution)/shard_map/ppermute | solution.py:369
  31.9 4.1 %collective-permute-start.7 = (f32[104,128]{1,0:T(8,128)S(1)}, f32[104,128]{1,0:T(8,128)S(1)}, u32[]{:S(2)}, u32[]{:S(2)}) collective-permute-start(f32[104,128]{1,0:T(8,128)S(1)} %add.4.a), channel_id=1, source_target_pairs={{0,3},{1,2},{2,1},{3,0},{4,7},{5,6},{6,5},{7,4},{8,11},{9,10},{10,... | collective-permute-start | bytes 159752 | tf_op jit(solution)/shard_map/ppermute | solution.py:369
  36.1 4.8 %collective-permute-start.12 = (f32[96,128]{1,0:T(8,128)S(1)}, f32[96,128]{1,0:T(8,128)S(1)}, u32[]{:S(2)}, u32[]{:S(2)}) collective-permute-start(f32[96,128]{1,0:T(8,128)S(1)} %get-tuple-element.50.z0), channel_id=1, source_target_pairs={{0,97},{1,96},{32,65},{33,64},{64,33},{65,32},{96,1},{97,0},{2,99}... | collective-permute-start | bytes 147464 | tf_op jit(solution)/shard_map/ppermute | solution.py:369
  38.4 5.2 %collective-permute-start.11 = (f32[96,128]{1,0:T(8,128)S(1)}, f32[96,128]{1,0:T(8,128)S(1)}, u32[]{:S(2)}, u32[]{:S(2)}) collective-permute-start(f32[96,128]{1,0:T(8,128)S(1)} %get-tuple-element.50.z0), channel_id=1, source_target_pairs={{0,64},{1,65},{32,96},{33,97},{64,0},{65,1},{96,32},{97,33},{2,66}... | collective-permute-start | bytes 147464 | tf_op jit(solution)/shard_map/ppermute | solution.py:369
  39.1 4.5 %collective-permute-start.10 = (f32[96,128]{1,0:T(8,128)S(1)}, f32[96,128]{1,0:T(8,128)S(1)}, u32[]{:S(2)}, u32[]{:S(2)}) collective-permute-start(f32[96,128]{1,0:T(8,128)S(1)} %get-tuple-element.50.z0), channel_id=1, source_target_pairs={{0,33},{1,32},{32,1},{33,0},{64,97},{65,96},{96,65},{97,64},{2,35}... | collective-permute-start | bytes 147464 | tf_op jit(solution)/shard_map/ppermute | solution.py:369
  43.8 5.7 %collective-permute-start.16 = (f32[96,128]{1,0:T(8,128)S(1)}, f32[96,128]{1,0:T(8,128)S(1)}, u32[]{:S(2)}, u32[]{:S(2)}) collective-permute-start(f32[96,128]{1,0:T(8,128)S(1)} %normal.2.refs_0_), channel_id=1, source_target_pairs={{0,25},{1,24},{8,17},{9,16},{16,9},{17,8},{24,1},{25,0},{2,27},{3,... | collective-permute-start | bytes 147464 | tf_op jit(solution)/shard_map/ppermute | solution.py:369
  45.4 4.9 %collective-permute-start.15 = (f32[96,128]{1,0:T(8,128)S(1)}, f32[96,128]{1,0:T(8,128)S(1)}, u32[]{:S(2)}, u32[]{:S(2)}) collective-permute-start(f32[96,128]{1,0:T(8,128)S(1)} %normal.2.refs_0_), channel_id=1, source_target_pairs={{0,9},{1,8},{8,1},{9,0},{16,25},{17,24},{24,17},{25,16},{2,11},{3,... | collective-permute-start | bytes 147464 | tf_op jit(solution)/shard_map/ppermute | solution.py:369
  45.4 5.7 %collective-permute-start.13 = (f32[96,128]{1,0:T(8,128)S(1)}, f32[96,128]{1,0:T(8,128)S(1)}, u32[]{:S(2)}, u32[]{:S(2)}) collective-permute-start(f32[96,128]{1,0:T(8,128)S(1)} %normal.2.refs_0_), channel_id=1, source_target_pairs={{0,16},{1,17},{8,24},{9,25},{16,0},{17,1},{24,8},{25,9},{2,18},{3,... | collective-permute-start | bytes 147464 | tf_op jit(solution)/shard_map/ppermute | solution.py:369
  51.9 4.8 %collective-permute-start.19 = (f32[16,192]{1,0:T(8,128)S(1)}, f32[16,192]{1,0:T(8,128)S(1)}, u32[]{:S(2)}, u32[]{:S(2)}) collective-permute-start(f32[16,192]{1,0:T(8,128)S(1)} %left_factor.7.p0), channel_id=1, source_target_pairs={{0,97},{1,96},{32,65},{33,64},{64,33},{65,32},{96,1},{97,0},{2,99}... | collective-permute-start | bytes 36872 | tf_op jit(solution)/shard_map/ppermute | solution.py:369
  53.8 4.1 %collective-permute-start.18 = (f32[16,192]{1,0:T(8,128)S(1)}, f32[16,192]{1,0:T(8,128)S(1)}, u32[]{:S(2)}, u32[]{:S(2)}) collective-permute-start(f32[16,192]{1,0:T(8,128)S(1)} %left_factor.7.p0), channel_id=1, source_target_pairs={{0,64},{1,65},{32,96},{33,97},{64,0},{65,1},{96,32},{97,33},{2,66}... | collective-permute-start | bytes 36872 | tf_op jit(solution)/shard_map/ppermute | solution.py:369
  54.6 3.6 %collective-permute-start.17 = (f32[16,192]{1,0:T(8,128)S(1)}, f32[16,192]{1,0:T(8,128)S(1)}, u32[]{:S(2)}, u32[]{:S(2)}) collective-permute-start(f32[16,192]{1,0:T(8,128)S(1)} %left_factor.7.p0), channel_id=1, source_target_pairs={{0,33},{1,32},{32,1},{33,0},{64,97},{65,96},{96,65},{97,64},{2,35}... | collective-permute-start | bytes 36872 | tf_op jit(solution)/shard_map/ppermute | solution.py:369
  59.0 5.4 %collective-permute-start.20 = (f32[104,128]{1,0:T(8,128)S(1)}, f32[104,128]{1,0:T(8,128)S(1)}, u32[]{:S(2)}, u32[]{:S(2)}) collective-permute-start(f32[104,128]{1,0:T(8,128)S(1)} %get-tuple-element.58), channel_id=1, source_target_pairs={{0,9},{1,8},{8,1},{9,0},{16,25},{17,24},{24,17},{25,16},{2,11},{3,... | collective-permute-start | bytes 159752 | tf_op jit(solution)/shard_map/ppermute | solution.py:369
  61.3 5.1 %collective-permute-start.21 = (f32[104,128]{1,0:T(8,128)S(1)}, f32[104,128]{1,0:T(8,128)S(1)}, u32[]{:S(2)}, u32[]{:S(2)}) collective-permute-start(f32[104,128]{1,0:T(8,128)S(1)} %get-tuple-element.59), channel_id=1, source_target_pairs={{0,16},{1,17},{8,24},{9,25},{16,0},{17,1},{24,8},{25,9},{2,18},{3,... | collective-permute-start | bytes 159752 | tf_op jit(solution)/shard_map/ppermute | solution.py:369
  63.1 4.8 %collective-permute-start.22 = (f32[104,128]{1,0:T(8,128)S(1)}, f32[104,128]{1,0:T(8,128)S(1)}, u32[]{:S(2)}, u32[]{:S(2)}) collective-permute-start(f32[104,128]{1,0:T(8,128)S(1)} %get-tuple-element.60), channel_id=1, source_target_pairs={{0,25},{1,24},{8,17},{9,16},{16,9},{17,8},{24,1},{25,0},{2,27},{3,... | collective-permute-start | bytes 159752 | tf_op jit(solution)/shard_map/ppermute | solution.py:369
  68.0 5.0 %collective-permute-start.25 = (f32[104,128]{1,0:T(8,128)S(1)}, f32[104,128]{1,0:T(8,128)S(1)}, u32[]{:S(2)}, u32[]{:S(2)}) collective-permute-start(f32[104,128]{1,0:T(8,128)S(1)} %add.6.a), channel_id=1, source_target_pairs={{0,7},{1,6},{2,5},{3,4},{4,3},{5,2},{6,1},{7,0},{8,15},{9,14},{10,... | collective-permute-start | bytes 159752 | tf_op jit(solution)/shard_map/ppermute | solution.py:369
  69.1 4.5 %collective-permute-start.24 = (f32[104,128]{1,0:T(8,128)S(1)}, f32[104,128]{1,0:T(8,128)S(1)}, u32[]{:S(2)}, u32[]{:S(2)}) collective-permute-start(f32[104,128]{1,0:T(8,128)S(1)} %add.6.a), channel_id=1, source_target_pairs={{0,4},{1,5},{2,6},{3,7},{4,0},{5,1},{6,2},{7,3},{8,12},{9,13},{10,... | collective-permute-start | bytes 159752 | tf_op jit(solution)/shard_map/ppermute | solution.py:369
  70.0 5.1 %collective-permute-start.23 = (f32[104,128]{1,0:T(8,128)S(1)}, f32[104,128]{1,0:T(8,128)S(1)}, u32[]{:S(2)}, u32[]{:S(2)}) collective-permute-start(f32[104,128]{1,0:T(8,128)S(1)} %add.6.a), channel_id=1, source_target_pairs={{0,3},{1,2},{2,1},{3,0},{4,7},{5,6},{6,5},{7,4},{8,11},{9,10},{10,... | collective-permute-start | bytes 159752 | tf_op jit(solution)/shard_map/ppermute | solution.py:369
  75.1 5.5 %collective-permute-start.28 = (f32[96,128]{1,0:T(8,128)S(1)}, f32[96,128]{1,0:T(8,128)S(1)}, u32[]{:S(2)}, u32[]{:S(2)}) collective-permute-start(f32[96,128]{1,0:T(8,128)S(1)} %get-tuple-element.61.z0), channel_id=1, source_target_pairs={{0,97},{1,96},{32,65},{33,64},{64,33},{65,32},{96,1},{97,0},{2,99}... | collective-permute-start | bytes 147464 | tf_op jit(solution)/shard_map/ppermute | solution.py:369
  77.0 4.9 %collective-permute-start.27 = (f32[96,128]{1,0:T(8,128)S(1)}, f32[96,128]{1,0:T(8,128)S(1)}, u32[]{:S(2)}, u32[]{:S(2)}) collective-permute-start(f32[96,128]{1,0:T(8,128)S(1)} %get-tuple-element.61.z0), channel_id=1, source_target_pairs={{0,64},{1,65},{32,96},{33,97},{64,0},{65,1},{96,32},{97,33},{2,66}... | collective-permute-start | bytes 147464 | tf_op jit(solution)/shard_map/ppermute | solution.py:369
  77.7 4.6 %collective-permute-start.26 = (f32[96,128]{1,0:T(8,128)S(1)}, f32[96,128]{1,0:T(8,128)S(1)}, u32[]{:S(2)}, u32[]{:S(2)}) collective-permute-start(f32[96,128]{1,0:T(8,128)S(1)} %get-tuple-element.61.z0), channel_id=1, source_target_pairs={{0,33},{1,32},{32,1},{33,0},{64,97},{65,96},{96,65},{97,64},{2,35}... | collective-permute-start | bytes 147464 | tf_op jit(solution)/shard_map/ppermute | solution.py:369
  82.4 5.3 %collective-permute-start.31 = (f32[96,128]{1,0:T(8,128)S(1)}, f32[96,128]{1,0:T(8,128)S(1)}, u32[]{:S(2)}, u32[]{:S(2)}) collective-permute-start(f32[96,128]{1,0:T(8,128)S(1)} %normal.3.refs_0_.q0), channel_id=1, source_target_pairs={{0,25},{1,24},{8,17},{9,16},{16,9},{17,8},{24,1},{25,0},{2,27},{3,... | collective-permute-start | bytes 147464 | tf_op jit(solution)/shard_map/ppermute | solution.py:369
  84.1 4.8 %collective-permute-start.30 = (f32[96,128]{1,0:T(8,128)S(1)}, f32[96,128]{1,0:T(8,128)S(1)}, u32[]{:S(2)}, u32[]{:S(2)}) collective-permute-start(f32[96,128]{1,0:T(8,128)S(1)} %normal.3.refs_0_.q0), channel_id=1, source_target_pairs={{0,16},{1,17},{8,24},{9,25},{16,0},{17,1},{24,8},{25,9},{2,18},{3,... | collective-permute-start | bytes 147464 | tf_op jit(solution)/shard_map/ppermute | solution.py:369
  85.3 4.1 %collective-permute-start.29 = (f32[96,128]{1,0:T(8,128)S(1)}, f32[96,128]{1,0:T(8,128)S(1)}, u32[]{:S(2)}, u32[]{:S(2)}) collective-permute-start(f32[96,128]{1,0:T(8,128)S(1)} %normal.3.refs_0_.q0), channel_id=1, source_target_pairs={{0,9},{1,8},{8,1},{9,0},{16,25},{17,24},{24,17},{25,16},{2,11},{3,... | collective-permute-start | bytes 147464 | tf_op jit(solution)/shard_map/ppermute | solution.py:369
  89.5 2.7 %collective-permute-start.32 = (f32[408,128]{1,0:T(8,128)S(1)}, f32[408,128]{1,0:T(8,128)S(1)}, u32[]{:S(2)}, u32[]{:S(2)}) collective-permute-start(f32[408,128]{1,0:T(8,128)S(1)} %join.1), channel_id=1, source_target_pairs={{0,1},{1,0},{2,3},{3,2},{4,5},{5,4},{6,7},{7,6},{8,9},{9,8},{10,11... | collective-permute-start | bytes 626696 | tf_op jit(solution)/shard_map/ppermute | solution.py:365

commit v8 on v7

--- a/solution.py
+++ b/solution.py
@@ -287,15 +287,16 @@
     return kernel(lower_kernel, out, [IN_VMEM] * (1 + len(p)), "lower_inverse", flops=10**9)(vmem(gram), *map(vmem, p))
 
 
-def normal_kernel(z0, z1, z2, z3, lower_ref, o_ref):
+def normal_kernel(z0, z1, z2, z3, lower_ref, *refs):
+    o_ref = refs[-1]
     total = ((z0[...] + z1[...]) + (z2[...] + z3[...])) * (1.0 / SIDE)
     lower = lower_ref[...]
     for t in range(DEEP // 8):
         o_ref[t * 8 : t * 8 + 8, :] = small_dot(lower, total[t * 8 : t * 8 + 8])
 
 
-def normal(z_all, lower):
-    return kernel(normal_kernel, pltpu.VMEM((DEEP, 128), F32), [IN_VMEM] * 5, "normal")(*map(vmem, z_all), vmem(lower))
+def normal(z_all, lower, first):
+    return kernel(normal_kernel, pltpu.VMEM((DEEP, 128), F32), [IN_VMEM] * (5 + len(first)), "normal")(*map(vmem, (*z_all, lower, *first)))
 
 
 def join_kernel(q0, q1, q2, q3, lower_ref, p_ref, o_ref):
@@ -374,12 +375,12 @@
     return (a, moved[1], moved[2], moved[3])
 
 
-def right_sum(parts, p=()):
+def right_sum(parts, p=(), first=()):
     (z,) = add(parts[:1] + tuple(cross(parts[k], "x", k) for k in (1, 2, 3)), DEEP + 8)
     z, gram = add(everyones(z, "y", cross), DEEP, 8)
     z_all = everyones(z, "dp", cross)
     lower, *hat = lower_inverse(gram, p)
-    return everyones(normal(z_all, lower), "x", cross, (2, 1, 3)), lower, hat
+    return everyones(normal(z_all, lower, first), "x", cross, (2, 1, 3)), lower, hat
 
 
 def after(parts, out, *ks):
@@ -393,7 +394,7 @@
     arrived = swap(right(1, p_all, g, e), "core", 1)
     *parts, w = pick(right(0, p_all, g, e), arrived, working(g, e))
     w = (g, e) + tuple(halves(swap(w, "core", 1)))
-    parts, _, _ = right_sum(tuple(parts))
+    parts, _, _ = right_sum(tuple(parts), first=w[2:])
 
     acc = left_part((0,), parts[:1], w)
     parts, acc = after(parts, left_part((3,), parts[3:], w, (acc,)), 1)

time: 95.3 us -> 95 us (level)
  no operation moved by 1% of the time
where the time goes in v8:
time: 95 us; the launch traced here: 94.9 us
  starting transfers between devices  45 us (47%)
  waiting for transfers between devices  26.5 us (28%)
  Pallas kernels  22.4 us (24%)
  between operations  1 us (1%)
    ppermute x27, starting transfers between devices, cross(): lax.ppermute(a, (axis, 'core'), [(i * 2 + c, (i ^ k) * 2 + (c ^ k & 1)) f...  36.7 us
    ppermute x27, waiting for transfers between devices, cross(): lax.ppermute(a, (axis, 'core'), [(i * 2 + c, (i ^ k) * 2 + (c ^ k & 1)) f...  23.1 us
    ppermute x6, starting transfers between devices, swap(): lax.ppermute(a, axis, [(i, i ^ k) for i in range(lax.axis_size(axis))])  8.27 us
    pallas_call x4, Pallas kernels, final(): pl.pallas_call(functools.partial(final_kernel, slot, ks, len(parts), n_in...  7.22 us
    pallas_call x1, Pallas kernels, first_left(): kernel(first_left_kernel, (pltpu.VMEM((16, ROWS), F32), wide, wide), [ANY...  5.25 us
    ppermute x6, waiting for transfers between devices, swap(): lax.ppermute(a, axis, [(i, i ^ k) for i in range(lax.axis_size(axis))])  3.43 us
    pallas_call x4, Pallas kernels, left_part(): kernel(functools.partial(left_kernel, ks), out, [IN_VMEM] * (len(parts) +...  3.16 us
    pallas_call x2, Pallas kernels, right(): kernel(functools.partial(right_kernel, slot), pltpu.VMEM((SIDE, DEEP + 8,...  1.96 us
  transfers between devices with their start and end apart: 33, of which 21 were waited for; matrix products, arithmetic and copies ran while one was open for 0% of the time, Pallas kernels for 12%

profile of v8, /device:TPU:1, one launch (start us, length us, event | category | flops | bytes accessed | tf_op | source)
XLA Modules:
  0.0 94.9 jit_solution(9638491217233076049)
XLA Ops:
  0.6 5.3 %first_left.1 = (f32[16,192]{1,0:T(8,128)S(1)}, bf16[2,192,6144]{2,1,0:T(8,128)(2,1)S(1)}, bf16[2,192,6144]{2,1,0:T(8,128)(2,1)S(1)}) custom-call(bf16[1,2,192,6144]{3,2,1,0:T(8,128)(2,1)} %g_hbm.1, bf16[1,2,192,6144]{3,2,1,0:T(8,128)(2,1)} %e_hbm.1, f32[2,8,6144]{2,1,0:T(8,128)} %bitcast.3), custom_call_target="tpu_custom_call" | custom-call | flops 10000000 | bytes 1000000 | tf_op jit(solution)/shard_map/first_left/pallas_call | solution.py:136
  5.9 4.7 %collective-permute-start.2 = (f32[16,192]{1,0:T(8,128)S(1)}, f32[16,192]{1,0:T(8,128)S(1)}, u32[]{:S(2)}, u32[]{:S(2)}) collective-permute-start(f32[16,192]{1,0:T(8,128)S(1)} %get-tuple-element.43.p0), channel_id=1, source_target_pairs={{0,96},{32,64},{64,32},{96,0},{1,97},{33,65},{65,33},{97,1},{2,98}... | collective-permute-start | bytes 36872 | tf_op jit(solution)/shard_map/ppermute | solution.py:366
  11.7 3.0 %collective-permute-done.1.p2 = f32[16,192]{1,0:T(8,128)S(1)} collective-permute-done((f32[16,192]{1,0:T(8,128)S(1)}, f32[16,192]{1,0:T(8,128)S(1)}, u32[]{:S(2)}, u32[]{:S(2)}) %collective-permute-start.1) | collective-permute-done | bytes 12320 | tf_op jit(solution)/shard_map/ppermute | solution.py:366
  14.7 1.0 %right_other.1 = f32[4,104,128]{2,1,0:T(8,128)S(1)} custom-call(f32[16,192]{1,0:T(8,128)S(1)} %get-tuple-element.43.p0, f32[16,192]{1,0:T(8,128)S(1)} %collective-permute-done.p1, f32[16,192]{1,0:T(8,128)S(1)} %collective-permute-done.1.p2, f32[16,192]{1,0:T(8,128)S(1)} %collective-permute-done.2.p3, ...), custom_call_target="tpu_custom_call" | custom-call | flops 1000000000 | bytes 1000000 | tf_op jit(solution)/shard_map/right_other/pallas_call | solution.py:222
  15.6 2.2 %collective-permute-start.3 = (f32[4,104,128]{2,1,0:T(8,128)S(1)}, f32[4,104,128]{2,1,0:T(8,128)S(1)}, u32[]{:S(2)}, u32[]{:S(2)}) collective-permute-start(f32[4,104,128]{2,1,0:T(8,128)S(1)} %right_other.1), channel_id=1, source_target_pairs={{0,1},{1,0},{2,3},{3,2},{4,5},{5,4},{6,7},{7,6},{8,9},{9,8},{10,11... | collective-permute-start | bytes 638984 | tf_op jit(solution)/shard_map/ppermute | solution.py:366
  18.3 1.0 %right_own.1.mine_ref = f32[4,104,128]{2,1,0:T(8,128)S(1)} custom-call(f32[16,192]{1,0:T(8,128)S(1)} %get-tuple-element.43.p0, f32[16,192]{1,0:T(8,128)S(1)} %collective-permute-done.p1, f32[16,192]{1,0:T(8,128)S(1)} %collective-permute-done.1.p2, f32[16,192]{1,0:T(8,128)S(1)} %collective-permute-done.2.p3, ...), custom_call_target="tpu_custom_call" | custom-call | flops 1000000000 | bytes 1000000 | tf_op jit(solution)/shard_map/right_own/pallas_call | solution.py:222
  19.4 1.6 %collective-permute-start.4 = (f32[104,128]{1,0:T(8,128)S(1)}, f32[104,128]{1,0:T(8,128)S(1)}, u32[]{:S(2)}, u32[]{:S(2)}) collective-permute-start(f32[104,128]{1,0:T(8,128)S(1)} %get-tuple-element.47), channel_id=1, source_target_pairs={{0,9},{1,8},{8,1},{9,0},{16,25},{17,24},{24,17},{25,16},{2,11},{3,... | collective-permute-start | bytes 159752 | tf_op jit(solution)/shard_map/ppermute | solution.py:370
  21.0 2.5 %collective-permute-start.5 = (f32[104,128]{1,0:T(8,128)S(1)}, f32[104,128]{1,0:T(8,128)S(1)}, u32[]{:S(2)}, u32[]{:S(2)}) collective-permute-start(f32[104,128]{1,0:T(8,128)S(1)} %get-tuple-element.48), channel_id=1, source_target_pairs={{0,16},{1,17},{8,24},{9,25},{16,0},{17,1},{24,8},{25,9},{2,18},{3,... | collective-permute-start | bytes 159752 | tf_op jit(solution)/shard_map/ppermute | solution.py:370
  23.9 2.8 %collective-permute-done.5.c = f32[104,128]{1,0:T(8,128)S(1)} collective-permute-done((f32[104,128]{1,0:T(8,128)S(1)}, f32[104,128]{1,0:T(8,128)S(1)}, u32[]{:S(2)}, u32[]{:S(2)}) %collective-permute-start.5) | collective-permute-done | bytes 53280 | tf_op jit(solution)/shard_map/ppermute | solution.py:370
  26.7 1.8 %collective-permute-done.6.d = f32[104,128]{1,0:T(8,128)S(1)} collective-permute-done((f32[104,128]{1,0:T(8,128)S(1)}, f32[104,128]{1,0:T(8,128)S(1)}, u32[]{:S(2)}, u32[]{:S(2)}) %collective-permute-start.6) | collective-permute-done | bytes 53280 | tf_op jit(solution)/shard_map/ppermute | solution.py:370
  28.5 3.1 %collective-permute-start.9 = (f32[104,128]{1,0:T(8,128)S(1)}, f32[104,128]{1,0:T(8,128)S(1)}, u32[]{:S(2)}, u32[]{:S(2)}) collective-permute-start(f32[104,128]{1,0:T(8,128)S(1)} %add.4.a), channel_id=1, source_target_pairs={{0,7},{1,6},{2,5},{3,4},{4,3},{5,2},{6,1},{7,0},{8,15},{9,14},{10,... | collective-permute-start | bytes 159752 | tf_op jit(solution)/shard_map/ppermute | solution.py:370
  32.5 1.4 %collective-permute-done.9.d = f32[104,128]{1,0:T(8,128)S(1)} collective-permute-done((f32[104,128]{1,0:T(8,128)S(1)}, f32[104,128]{1,0:T(8,128)S(1)}, u32[]{:S(2)}, u32[]{:S(2)}) %collective-permute-start.9) | collective-permute-done | bytes 53280 | tf_op jit(solution)/shard_map/ppermute | solution.py:370
  33.9 2.2 %collective-permute-done.8.c = f32[104,128]{1,0:T(8,128)S(1)} collective-permute-done((f32[104,128]{1,0:T(8,128)S(1)}, f32[104,128]{1,0:T(8,128)S(1)}, u32[]{:S(2)}, u32[]{:S(2)}) %collective-permute-start.8) | collective-permute-done | bytes 53280 | tf_op jit(solution)/shard_map/ppermute | solution.py:370
  36.1 2.3 %collective-permute-start.12 = (f32[96,128]{1,0:T(8,128)S(1)}, f32[96,128]{1,0:T(8,128)S(1)}, u32[]{:S(2)}, u32[]{:S(2)}) collective-permute-start(f32[96,128]{1,0:T(8,128)S(1)} %get-tuple-element.50.z0), channel_id=1, source_target_pairs={{0,97},{1,96},{32,65},{33,64},{64,33},{65,32},{96,1},{97,0},{2,99}... | collective-permute-start | bytes 147464 | tf_op jit(solution)/shard_map/ppermute | solution.py:370
  39.1 0.8 collective-permute-start.10
  41.4 2.2 %collective-permute-done.11.z2 = f32[96,128]{1,0:T(8,128)S(1)} collective-permute-done((f32[96,128]{1,0:T(8,128)S(1)}, f32[96,128]{1,0:T(8,128)S(1)}, u32[]{:S(2)}, u32[]{:S(2)}) %collective-permute-start.11) | collective-permute-done | bytes 49184 | tf_op jit(solution)/shard_map/ppermute | solution.py:370
  43.8 1.6 %collective-permute-start.16 = (f32[96,128]{1,0:T(8,128)S(1)}, f32[96,128]{1,0:T(8,128)S(1)}, u32[]{:S(2)}, u32[]{:S(2)}) collective-permute-start(f32[96,128]{1,0:T(8,128)S(1)} %normal.2.refs_0_), channel_id=1, source_target_pairs={{0,25},{1,24},{8,17},{9,16},{16,9},{17,8},{24,1},{25,0},{2,27},{3,... | collective-permute-start | bytes 147464 | tf_op jit(solution)/shard_map/ppermute | solution.py:370
  45.4 2.6 %collective-permute-start.14 = (f32[96,128]{1,0:T(8,128)S(1)}, f32[96,128]{1,0:T(8,128)S(1)}, u32[]{:S(2)}, u32[]{:S(2)}) collective-permute-start(f32[96,128]{1,0:T(8,128)S(1)} %normal.2.refs_0_), channel_id=1, source_target_pairs={{0,16},{1,17},{8,24},{9,25},{16,0},{17,1},{24,8},{25,9},{2,18},{3,... | collective-permute-start | bytes 147464 | tf_op jit(solution)/shard_map/ppermute | solution.py:370
  49.1 0.8 left_factor.5.refs_5_
  49.9 0.8 left_factor.6.refs_5_
  50.7 0.8 left_factor.7.p0
  51.5 2.2 %collective-permute-start.19 = (f32[16,192]{1,0:T(8,128)S(1)}, f32[16,192]{1,0:T(8,128)S(1)}, u32[]{:S(2)}, u32[]{:S(2)}) collective-permute-start(f32[16,192]{1,0:T(8,128)S(1)} %left_factor.7.p0), channel_id=1, source_target_pairs={{0,97},{1,96},{32,65},{33,64},{64,33},{65,32},{96,1},{97,0},{2,99}... | collective-permute-start | bytes 36872 | tf_op jit(solution)/shard_map/ppermute | solution.py:370
  53.8 0.9 collective-permute-start.18
  54.6 0.8 collective-permute-start.17
  56.0 1.9 %collective-permute-done.18.p2 = f32[16,192]{1,0:T(8,128)S(1)} collective-permute-done((f32[16,192]{1,0:T(8,128)S(1)}, f32[16,192]{1,0:T(8,128)S(1)}, u32[]{:S(2)}, u32[]{:S(2)}) %collective-permute-start.18) | collective-permute-done | bytes 12320 | tf_op jit(solution)/shard_map/ppermute | solution.py:370
  58.1 0.8 right_both.2
  58.9 1.6 %collective-permute-start.20 = (f32[104,128]{1,0:T(8,128)S(1)}, f32[104,128]{1,0:T(8,128)S(1)}, u32[]{:S(2)}, u32[]{:S(2)}) collective-permute-start(f32[104,128]{1,0:T(8,128)S(1)} %get-tuple-element.58), channel_id=1, source_target_pairs={{0,9},{1,8},{8,1},{9,0},{16,25},{17,24},{24,17},{25,16},{2,11},{3,... | collective-permute-start | bytes 159752 | tf_op jit(solution)/shard_map/ppermute | solution.py:370
  60.4 0.8 right_both.3
  61.3 1.8 %collective-permute-start.21 = (f32[104,128]{1,0:T(8,128)S(1)}, f32[104,128]{1,0:T(8,128)S(1)}, u32[]{:S(2)}, u32[]{:S(2)}) collective-permute-start(f32[104,128]{1,0:T(8,128)S(1)} %get-tuple-element.59), channel_id=1, source_target_pairs={{0,16},{1,17},{8,24},{9,25},{16,0},{17,1},{24,8},{25,9},{2,18},{3,... | collective-permute-start | bytes 159752 | tf_op jit(solution)/shard_map/ppermute | solution.py:370
  63.1 1.2 %collective-permute-start.22 = (f32[104,128]{1,0:T(8,128)S(1)}, f32[104,128]{1,0:T(8,128)S(1)}, u32[]{:S(2)}, u32[]{:S(2)}) collective-permute-start(f32[104,128]{1,0:T(8,128)S(1)} %get-tuple-element.60), channel_id=1, source_target_pairs={{0,25},{1,24},{8,17},{9,16},{16,9},{17,8},{24,1},{25,0},{2,27},{3,... | collective-permute-start | bytes 159752 | tf_op jit(solution)/shard_map/ppermute | solution.py:370
  64.3 2.1 %collective-permute-done.21.c = f32[104,128]{1,0:T(8,128)S(1)} collective-permute-done((f32[104,128]{1,0:T(8,128)S(1)}, f32[104,128]{1,0:T(8,128)S(1)}, u32[]{:S(2)}, u32[]{:S(2)}) %collective-permute-start.21) | collective-permute-done | bytes 53280 | tf_op jit(solution)/shard_map/ppermute | solution.py:370
  66.4 1.6 %collective-permute-done.22.d = f32[104,128]{1,0:T(8,128)S(1)} collective-permute-done((f32[104,128]{1,0:T(8,128)S(1)}, f32[104,128]{1,0:T(8,128)S(1)}, u32[]{:S(2)}, u32[]{:S(2)}) %collective-permute-start.22) | collective-permute-done | bytes 53280 | tf_op jit(solution)/shard_map/ppermute | solution.py:370
  67.9 1.1 %collective-permute-start.25 = (f32[104,128]{1,0:T(8,128)S(1)}, f32[104,128]{1,0:T(8,128)S(1)}, u32[]{:S(2)}, u32[]{:S(2)}) collective-permute-start(f32[104,128]{1,0:T(8,128)S(1)} %add.6.a), channel_id=1, source_target_pairs={{0,7},{1,6},{2,5},{3,4},{4,3},{5,2},{6,1},{7,0},{8,15},{9,14},{10,... | collective-permute-start | bytes 159752 | tf_op jit(solution)/shard_map/ppermute | solution.py:370
  69.1 0.9 collective-permute-start.24
  70.0 1.9 %collective-permute-start.23 = (f32[104,128]{1,0:T(8,128)S(1)}, f32[104,128]{1,0:T(8,128)S(1)}, u32[]{:S(2)}, u32[]{:S(2)}) collective-permute-start(f32[104,128]{1,0:T(8,128)S(1)} %add.6.a), channel_id=1, source_target_pairs={{0,3},{1,2},{2,1},{3,0},{4,7},{5,6},{6,5},{7,4},{8,11},{9,10},{10,... | collective-permute-start | bytes 159752 | tf_op jit(solution)/shard_map/ppermute | solution.py:370
  71.8 1.1 %collective-permute-done.25.d = f32[104,128]{1,0:T(8,128)S(1)} collective-permute-done((f32[104,128]{1,0:T(8,128)S(1)}, f32[104,128]{1,0:T(8,128)S(1)}, u32[]{:S(2)}, u32[]{:S(2)}) %collective-permute-start.25) | collective-permute-done | bytes 53280 | tf_op jit(solution)/shard_map/ppermute | solution.py:370
  73.5 1.5 %collective-permute-done.23.b = f32[104,128]{1,0:T(8,128)S(1)} collective-permute-done((f32[104,128]{1,0:T(8,128)S(1)}, f32[104,128]{1,0:T(8,128)S(1)}, u32[]{:S(2)}, u32[]{:S(2)}) %collective-permute-start.23) | collective-permute-done | bytes 53280 | tf_op jit(solution)/shard_map/ppermute | solution.py:370
  75.0 1.9 %collective-permute-start.28 = (f32[96,128]{1,0:T(8,128)S(1)}, f32[96,128]{1,0:T(8,128)S(1)}, u32[]{:S(2)}, u32[]{:S(2)}) collective-permute-start(f32[96,128]{1,0:T(8,128)S(1)} %get-tuple-element.61.z0), channel_id=1, source_target_pairs={{0,97},{1,96},{32,65},{33,64},{64,33},{65,32},{96,1},{97,0},{2,99}... | collective-permute-start | bytes 147464 | tf_op jit(solution)/shard_map/ppermute | solution.py:370
  77.6 1.3 %collective-permute-start.26 = (f32[96,128]{1,0:T(8,128)S(1)}, f32[96,128]{1,0:T(8,128)S(1)}, u32[]{:S(2)}, u32[]{:S(2)}) collective-permute-start(f32[96,128]{1,0:T(8,128)S(1)} %get-tuple-element.61.z0), channel_id=1, source_target_pairs={{0,33},{1,32},{32,1},{33,0},{64,97},{65,96},{96,65},{97,64},{2,35}... | collective-permute-start | bytes 147464 | tf_op jit(solution)/shard_map/ppermute | solution.py:370
  78.9 0.9 lower_inverse.3
  80.6 1.3 %collective-permute-done.27.z2 = f32[96,128]{1,0:T(8,128)S(1)} collective-permute-done((f32[96,128]{1,0:T(8,128)S(1)}, f32[96,128]{1,0:T(8,128)S(1)}, u32[]{:S(2)}, u32[]{:S(2)}) %collective-permute-start.27) | collective-permute-done | bytes 49184 | tf_op jit(solution)/shard_map/ppermute | solution.py:370
  82.3 1.6 %collective-permute-start.31 = (f32[96,128]{1,0:T(8,128)S(1)}, f32[96,128]{1,0:T(8,128)S(1)}, u32[]{:S(2)}, u32[]{:S(2)}) collective-permute-start(f32[96,128]{1,0:T(8,128)S(1)} %normal.3.refs_0_.q0), channel_id=1, source_target_pairs={{0,25},{1,24},{8,17},{9,16},{16,9},{17,8},{24,1},{25,0},{2,27},{3,... | collective-permute-start | bytes 147464 | tf_op jit(solution)/shard_map/ppermute | solution.py:370
  84.0 1.2 %collective-permute-start.30 = (f32[96,128]{1,0:T(8,128)S(1)}, f32[96,128]{1,0:T(8,128)S(1)}, u32[]{:S(2)}, u32[]{:S(2)}) collective-permute-start(f32[96,128]{1,0:T(8,128)S(1)} %normal.3.refs_0_.q0), channel_id=1, source_target_pairs={{0,16},{1,17},{8,24},{9,25},{16,0},{17,1},{24,8},{25,9},{2,18},{3,... | collective-permute-start | bytes 147464 | tf_op jit(solution)/shard_map/ppermute | solution.py:370
  85.2 1.0 %collective-permute-start.29 = (f32[96,128]{1,0:T(8,128)S(1)}, f32[96,128]{1,0:T(8,128)S(1)}, u32[]{:S(2)}, u32[]{:S(2)}) collective-permute-start(f32[96,128]{1,0:T(8,128)S(1)} %normal.3.refs_0_.q0), channel_id=1, source_target_pairs={{0,9},{1,8},{8,1},{9,0},{16,25},{17,24},{24,17},{25,16},{2,11},{3,... | collective-permute-start | bytes 147464 | tf_op jit(solution)/shard_map/ppermute | solution.py:370
  86.2 1.3 %residual_own.3 = (bf16[2,192,6144]{2,1,0:T(8,128)(2,1)}, bf16[1,2,192,6144]{3,2,1,0:T(8,128)(2,1)}, f32[2,8,6144]{2,1,0:T(8,128)}) custom-call(f32[96,128]{1,0:T(8,128)S(1)} %normal.3.refs_0_.q0, bf16[256,128]{1,0:T(8,128)(2,1)S(1)} %get-tuple-element.65.refs_1_.refs_2_, bf16[2,192,6144]{2,1,0:T(8,128)(2,1)S(1)} %get-tuple-element.44.g_ref.refs_1_.refs_2_.refs_3_, ...), custom_call_target="tpu_custom_call" | custom-call | flops 1000000000 | bytes 1000000 | tf_op jit(solution)/shard_map/residual_own/pallas_call | solution.py:350
  87.6 1.3 %residual_own.4 = (bf16[2,192,6144]{2,1,0:T(8,128)(2,1)}, bf16[1,2,192,6144]{3,2,1,0:T(8,128)(2,1)}, f32[2,8,6144]{2,1,0:T(8,128)}) custom-call(f32[96,128]{1,0:T(8,128)S(1)} %collective-permute-done.31.refs_0_.q3, bf16[256,128]{1,0:T(8,128)(2,1)S(1)} %get-tuple-element.65.refs_1_.refs_2_, ...), custom_call_target="tpu_custom_call", output_to_operand_aliasing={{0}: (4, {}), {1}: (5, {}), {2}: (6, {})} | custom-call | flops 1000000000 | bytes 1000000 | tf_op jit(solution)/shard_map/residual_own/pallas_call | solution.py:350
  90.1 1.8 %residual_own.5 = (bf16[2,192,6144]{2,1,0:T(8,128)(2,1)}, bf16[1,2,192,6144]{3,2,1,0:T(8,128)(2,1)}, f32[2,8,6144]{2,1,0:T(8,128)}) custom-call(f32[96,128]{1,0:T(8,128)S(1)} %collective-permute-done.29.q1.refs_0_, f32[96,128]{1,0:T(8,128)S(1)} %collective-permute-done.30.q2.refs_1_, ...), custom_call_target="tpu_custom_call", output_to_operand_aliasing={{0}: (5, {}), {1}: (6, {}), {2}: (7, {})} | custom-call | flops 1000000000 | bytes 1000000 | tf_op jit(solution)/shard_map/residual_own/pallas_call | solution.py:350
  91.9 2.8 %residual_other.1 = (bf16[2,192,6144]{2,1,0:T(8,128)(2,1)}, bf16[1,2,192,6144]{3,2,1,0:T(8,128)(2,1)}, f32[2,8,6144]{2,1,0:T(8,128)}) custom-call(f32[408,128]{1,0:T(8,128)S(1)} %collective-permute-done.32.refs_0_, ...), custom_call_target="tpu_custom_call", output_to_operand_aliasing={{0}: (3, {}), {1}: (4, {}), {2}: (5, {})} | custom-call | flops 1000000000 | bytes 1000000 | tf_op jit(solution)/shard_map/residual_other/pallas_call | solution.py:350
  (43 shorter events, 11.1 us)
Async XLA Ops:
  5.9 5.8 %collective-permute-start.2 = (f32[16,192]{1,0:T(8,128)S(1)}, f32[16,192]{1,0:T(8,128)S(1)}, u32[]{:S(2)}, u32[]{:S(2)}) collective-permute-start(f32[16,192]{1,0:T(8,128)S(1)} %get-tuple-element.43.p0), channel_id=1, source_target_pairs={{0,96},{32,64},{64,32},{96,0},{1,97},{33,65},{65,33},{97,1},{2,98}... | collective-permute-start | bytes 36872 | tf_op jit(solution)/shard_map/ppermute | solution.py:366
  10.6 4.1 %collective-permute-start.1 = (f32[16,192]{1,0:T(8,128)S(1)}, f32[16,192]{1,0:T(8,128)S(1)}, u32[]{:S(2)}, u32[]{:S(2)}) collective-permute-start(f32[16,192]{1,0:T(8,128)S(1)} %get-tuple-element.43.p0), channel_id=1, source_target_pairs={{0,64},{32,96},{64,0},{96,32},{1,65},{33,97},{65,1},{97,33},{2,66}... | collective-permute-start | bytes 36872 | tf_op jit(solution)/shard_map/ppermute | solution.py:366
  10.6 4.1 %collective-permute-start = (f32[16,192]{1,0:T(8,128)S(1)}, f32[16,192]{1,0:T(8,128)S(1)}, u32[]{:S(2)}, u32[]{:S(2)}) collective-permute-start(f32[16,192]{1,0:T(8,128)S(1)} %get-tuple-element.43.p0), channel_id=1, source_target_pairs={{0,32},{32,0},{64,96},{96,64},{1,33},{33,1},{65,97},{97,65},{2,34}... | collective-permute-start | bytes 36872 | tf_op jit(solution)/shard_map/ppermute | solution.py:366
  15.6 3.6 %collective-permute-start.3 = (f32[4,104,128]{2,1,0:T(8,128)S(1)}, f32[4,104,128]{2,1,0:T(8,128)S(1)}, u32[]{:S(2)}, u32[]{:S(2)}) collective-permute-start(f32[4,104,128]{2,1,0:T(8,128)S(1)} %right_other.1), channel_id=1, source_target_pairs={{0,1},{1,0},{2,3},{3,2},{4,5},{5,4},{6,7},{7,6},{8,9},{9,8},{10,11... | collective-permute-start | bytes 638984 | tf_op jit(solution)/shard_map/ppermute | solution.py:366
  19.3 21.3 %collective-permute-start.13 = (f32[192,6144]{1,0:T(8,128)S(1)}, f32[192,6144]{1,0:T(8,128)S(1)}, u32[]{:S(2)}, u32[]{:S(2)}) collective-permute-start(f32[192,6144]{1,0:T(8,128)S(1)} %get-tuple-element.52), channel_id=1, source_target_pairs={{0,1},{1,0},{2,3},{3,2},{4,5},{5,4},{6,7},{7,6},{8,9},{9,8},{10,11... | collective-permute-start | bytes 14155784 | tf_op jit(solution)/shard_map/ppermute | solution.py:366
  19.4 4.5 %collective-permute-start.4 = (f32[104,128]{1,0:T(8,128)S(1)}, f32[104,128]{1,0:T(8,128)S(1)}, u32[]{:S(2)}, u32[]{:S(2)}) collective-permute-start(f32[104,128]{1,0:T(8,128)S(1)} %get-tuple-element.47), channel_id=1, source_target_pairs={{0,9},{1,8},{8,1},{9,0},{16,25},{17,24},{24,17},{25,16},{2,11},{3,... | collective-permute-start | bytes 159752 | tf_op jit(solution)/shard_map/ppermute | solution.py:370
  21.0 5.7 %collective-permute-start.5 = (f32[104,128]{1,0:T(8,128)S(1)}, f32[104,128]{1,0:T(8,128)S(1)}, u32[]{:S(2)}, u32[]{:S(2)}) collective-permute-start(f32[104,128]{1,0:T(8,128)S(1)} %get-tuple-element.48), channel_id=1, source_target_pairs={{0,16},{1,17},{8,24},{9,25},{16,0},{17,1},{24,8},{25,9},{2,18},{3,... | collective-permute-start | bytes 159752 | tf_op jit(solution)/shard_map/ppermute | solution.py:370
  23.5 5.0 %collective-permute-start.6 = (f32[104,128]{1,0:T(8,128)S(1)}, f32[104,128]{1,0:T(8,128)S(1)}, u32[]{:S(2)}, u32[]{:S(2)}) collective-permute-start(f32[104,128]{1,0:T(8,128)S(1)} %get-tuple-element.49), channel_id=1, source_target_pairs={{0,25},{1,24},{8,17},{9,16},{16,9},{17,8},{24,1},{25,0},{2,27},{3,... | collective-permute-start | bytes 159752 | tf_op jit(solution)/shard_map/ppermute | solution.py:370
  28.5 5.4 %collective-permute-start.9 = (f32[104,128]{1,0:T(8,128)S(1)}, f32[104,128]{1,0:T(8,128)S(1)}, u32[]{:S(2)}, u32[]{:S(2)}) collective-permute-start(f32[104,128]{1,0:T(8,128)S(1)} %add.4.a), channel_id=1, source_target_pairs={{0,7},{1,6},{2,5},{3,4},{4,3},{5,2},{6,1},{7,0},{8,15},{9,14},{10,... | collective-permute-start | bytes 159752 | tf_op jit(solution)/shard_map/ppermute | solution.py:370
  31.6 4.5 %collective-permute-start.8 = (f32[104,128]{1,0:T(8,128)S(1)}, f32[104,128]{1,0:T(8,128)S(1)}, u32[]{:S(2)}, u32[]{:S(2)}) collective-permute-start(f32[104,128]{1,0:T(8,128)S(1)} %add.4.a), channel_id=1, source_target_pairs={{0,4},{1,5},{2,6},{3,7},{4,0},{5,1},{6,2},{7,3},{8,12},{9,13},{10,... | collective-permute-start | bytes 159752 | tf_op jit(solution)/shard_map/ppermute | solution.py:370
  31.9 4.1 %collective-permute-start.7 = (f32[104,128]{1,0:T(8,128)S(1)}, f32[104,128]{1,0:T(8,128)S(1)}, u32[]{:S(2)}, u32[]{:S(2)}) collective-permute-start(f32[104,128]{1,0:T(8,128)S(1)} %add.4.a), channel_id=1, source_target_pairs={{0,3},{1,2},{2,1},{3,0},{4,7},{5,6},{6,5},{7,4},{8,11},{9,10},{10,... | collective-permute-start | bytes 159752 | tf_op jit(solution)/shard_map/ppermute | solution.py:370
  36.1 5.4 %collective-permute-start.12 = (f32[96,128]{1,0:T(8,128)S(1)}, f32[96,128]{1,0:T(8,128)S(1)}, u32[]{:S(2)}, u32[]{:S(2)}) collective-permute-start(f32[96,128]{1,0:T(8,128)S(1)} %get-tuple-element.50.z0), channel_id=1, source_target_pairs={{0,97},{1,96},{32,65},{33,64},{64,33},{65,32},{96,1},{97,0},{2,99}... | collective-permute-start | bytes 147464 | tf_op jit(solution)/shard_map/ppermute | solution.py:370
  38.4 5.2 %collective-permute-start.11 = (f32[96,128]{1,0:T(8,128)S(1)}, f32[96,128]{1,0:T(8,128)S(1)}, u32[]{:S(2)}, u32[]{:S(2)}) collective-permute-start(f32[96,128]{1,0:T(8,128)S(1)} %get-tuple-element.50.z0), channel_id=1, source_target_pairs={{0,64},{1,65},{32,96},{33,97},{64,0},{65,1},{96,32},{97,33},{2,66}... | collective-permute-start | bytes 147464 | tf_op jit(solution)/shard_map/ppermute | solution.py:370
  39.1 4.5 %collective-permute-start.10 = (f32[96,128]{1,0:T(8,128)S(1)}, f32[96,128]{1,0:T(8,128)S(1)}, u32[]{:S(2)}, u32[]{:S(2)}) collective-permute-start(f32[96,128]{1,0:T(8,128)S(1)} %get-tuple-element.50.z0), channel_id=1, source_target_pairs={{0,33},{1,32},{32,1},{33,0},{64,97},{65,96},{96,65},{97,64},{2,35}... | collective-permute-start | bytes 147464 | tf_op jit(solution)/shard_map/ppermute | solution.py:370
  43.8 5.3 %collective-permute-start.16 = (f32[96,128]{1,0:T(8,128)S(1)}, f32[96,128]{1,0:T(8,128)S(1)}, u32[]{:S(2)}, u32[]{:S(2)}) collective-permute-start(f32[96,128]{1,0:T(8,128)S(1)} %normal.2.refs_0_), channel_id=1, source_target_pairs={{0,25},{1,24},{8,17},{9,16},{16,9},{17,8},{24,1},{25,0},{2,27},{3,... | collective-permute-start | bytes 147464 | tf_op jit(solution)/shard_map/ppermute | solution.py:370
  45.4 4.5 %collective-permute-start.15 = (f32[96,128]{1,0:T(8,128)S(1)}, f32[96,128]{1,0:T(8,128)S(1)}, u32[]{:S(2)}, u32[]{:S(2)}) collective-permute-start(f32[96,128]{1,0:T(8,128)S(1)} %normal.2.refs_0_), channel_id=1, source_target_pairs={{0,9},{1,8},{8,1},{9,0},{16,25},{17,24},{24,17},{25,16},{2,11},{3,... | collective-permute-start | bytes 147464 | tf_op jit(solution)/shard_map/ppermute | solution.py:370
  45.4 5.4 %collective-permute-start.14 = (f32[96,128]{1,0:T(8,128)S(1)}, f32[96,128]{1,0:T(8,128)S(1)}, u32[]{:S(2)}, u32[]{:S(2)}) collective-permute-start(f32[96,128]{1,0:T(8,128)S(1)} %normal.2.refs_0_), channel_id=1, source_target_pairs={{0,16},{1,17},{8,24},{9,25},{16,0},{17,1},{24,8},{25,9},{2,18},{3,... | collective-permute-start | bytes 147464 | tf_op jit(solution)/shard_map/ppermute | solution.py:370
  51.5 4.5 %collective-permute-start.19 = (f32[16,192]{1,0:T(8,128)S(1)}, f32[16,192]{1,0:T(8,128)S(1)}, u32[]{:S(2)}, u32[]{:S(2)}) collective-permute-start(f32[16,192]{1,0:T(8,128)S(1)} %left_factor.7.p0), channel_id=1, source_target_pairs={{0,97},{1,96},{32,65},{33,64},{64,33},{65,32},{96,1},{97,0},{2,99}... | collective-permute-start | bytes 36872 | tf_op jit(solution)/shard_map/ppermute | solution.py:370
  53.8 4.1 %collective-permute-start.18 = (f32[16,192]{1,0:T(8,128)S(1)}, f32[16,192]{1,0:T(8,128)S(1)}, u32[]{:S(2)}, u32[]{:S(2)}) collective-permute-start(f32[16,192]{1,0:T(8,128)S(1)} %left_factor.7.p0), channel_id=1, source_target_pairs={{0,64},{1,65},{32,96},{33,97},{64,0},{65,1},{96,32},{97,33},{2,66}... | collective-permute-start | bytes 36872 | tf_op jit(solution)/shard_map/ppermute | solution.py:370
  54.6 3.5 %collective-permute-start.17 = (f32[16,192]{1,0:T(8,128)S(1)}, f32[16,192]{1,0:T(8,128)S(1)}, u32[]{:S(2)}, u32[]{:S(2)}) collective-permute-start(f32[16,192]{1,0:T(8,128)S(1)} %left_factor.7.p0), channel_id=1, source_target_pairs={{0,33},{1,32},{32,1},{33,0},{64,97},{65,96},{96,65},{97,64},{2,35}... | collective-permute-start | bytes 36872 | tf_op jit(solution)/shard_map/ppermute | solution.py:370
  58.9 5.4 %collective-permute-start.20 = (f32[104,128]{1,0:T(8,128)S(1)}, f32[104,128]{1,0:T(8,128)S(1)}, u32[]{:S(2)}, u32[]{:S(2)}) collective-permute-start(f32[104,128]{1,0:T(8,128)S(1)} %get-tuple-element.58), channel_id=1, source_target_pairs={{0,9},{1,8},{8,1},{9,0},{16,25},{17,24},{24,17},{25,16},{2,11},{3,... | collective-permute-start | bytes 159752 | tf_op jit(solution)/shard_map/ppermute | solution.py:370
  61.3 5.1 %collective-permute-start.21 = (f32[104,128]{1,0:T(8,128)S(1)}, f32[104,128]{1,0:T(8,128)S(1)}, u32[]{:S(2)}, u32[]{:S(2)}) collective-permute-start(f32[104,128]{1,0:T(8,128)S(1)} %get-tuple-element.59), channel_id=1, source_target_pairs={{0,16},{1,17},{8,24},{9,25},{16,0},{17,1},{24,8},{25,9},{2,18},{3,... | collective-permute-start | bytes 159752 | tf_op jit(solution)/shard_map/ppermute | solution.py:370
  63.1 4.9 %collective-permute-start.22 = (f32[104,128]{1,0:T(8,128)S(1)}, f32[104,128]{1,0:T(8,128)S(1)}, u32[]{:S(2)}, u32[]{:S(2)}) collective-permute-start(f32[104,128]{1,0:T(8,128)S(1)} %get-tuple-element.60), channel_id=1, source_target_pairs={{0,25},{1,24},{8,17},{9,16},{16,9},{17,8},{24,1},{25,0},{2,27},{3,... | collective-permute-start | bytes 159752 | tf_op jit(solution)/shard_map/ppermute | solution.py:370
  67.9 5.0 %collective-permute-start.25 = (f32[104,128]{1,0:T(8,128)S(1)}, f32[104,128]{1,0:T(8,128)S(1)}, u32[]{:S(2)}, u32[]{:S(2)}) collective-permute-start(f32[104,128]{1,0:T(8,128)S(1)} %add.6.a), channel_id=1, source_target_pairs={{0,7},{1,6},{2,5},{3,4},{4,3},{5,2},{6,1},{7,0},{8,15},{9,14},{10,... | collective-permute-start | bytes 159752 | tf_op jit(solution)/shard_map/ppermute | solution.py:370
  69.1 4.5 %collective-permute-start.24 = (f32[104,128]{1,0:T(8,128)S(1)}, f32[104,128]{1,0:T(8,128)S(1)}, u32[]{:S(2)}, u32[]{:S(2)}) collective-permute-start(f32[104,128]{1,0:T(8,128)S(1)} %add.6.a), channel_id=1, source_target_pairs={{0,4},{1,5},{2,6},{3,7},{4,0},{5,1},{6,2},{7,3},{8,12},{9,13},{10,... | collective-permute-start | bytes 159752 | tf_op jit(solution)/shard_map/ppermute | solution.py:370
  70.0 5.1 %collective-permute-start.23 = (f32[104,128]{1,0:T(8,128)S(1)}, f32[104,128]{1,0:T(8,128)S(1)}, u32[]{:S(2)}, u32[]{:S(2)}) collective-permute-start(f32[104,128]{1,0:T(8,128)S(1)} %add.6.a), channel_id=1, source_target_pairs={{0,3},{1,2},{2,1},{3,0},{4,7},{5,6},{6,5},{7,4},{8,11},{9,10},{10,... | collective-permute-start | bytes 159752 | tf_op jit(solution)/shard_map/ppermute | solution.py:370
  75.0 5.5 %collective-permute-start.28 = (f32[96,128]{1,0:T(8,128)S(1)}, f32[96,128]{1,0:T(8,128)S(1)}, u32[]{:S(2)}, u32[]{:S(2)}) collective-permute-start(f32[96,128]{1,0:T(8,128)S(1)} %get-tuple-element.61.z0), channel_id=1, source_target_pairs={{0,97},{1,96},{32,65},{33,64},{64,33},{65,32},{96,1},{97,0},{2,99}... | collective-permute-start | bytes 147464 | tf_op jit(solution)/shard_map/ppermute | solution.py:370
  76.9 4.9 %collective-permute-start.27 = (f32[96,128]{1,0:T(8,128)S(1)}, f32[96,128]{1,0:T(8,128)S(1)}, u32[]{:S(2)}, u32[]{:S(2)}) collective-permute-start(f32[96,128]{1,0:T(8,128)S(1)} %get-tuple-element.61.z0), channel_id=1, source_target_pairs={{0,64},{1,65},{32,96},{33,97},{64,0},{65,1},{96,32},{97,33},{2,66}... | collective-permute-start | bytes 147464 | tf_op jit(solution)/shard_map/ppermute | solution.py:370
  77.6 4.6 %collective-permute-start.26 = (f32[96,128]{1,0:T(8,128)S(1)}, f32[96,128]{1,0:T(8,128)S(1)}, u32[]{:S(2)}, u32[]{:S(2)}) collective-permute-start(f32[96,128]{1,0:T(8,128)S(1)} %get-tuple-element.61.z0), channel_id=1, source_target_pairs={{0,33},{1,32},{32,1},{33,0},{64,97},{65,96},{96,65},{97,64},{2,35}... | collective-permute-start | bytes 147464 | tf_op jit(solution)/shard_map/ppermute | solution.py:370
  82.3 5.3 %collective-permute-start.31 = (f32[96,128]{1,0:T(8,128)S(1)}, f32[96,128]{1,0:T(8,128)S(1)}, u32[]{:S(2)}, u32[]{:S(2)}) collective-permute-start(f32[96,128]{1,0:T(8,128)S(1)} %normal.3.refs_0_.q0), channel_id=1, source_target_pairs={{0,25},{1,24},{8,17},{9,16},{16,9},{17,8},{24,1},{25,0},{2,27},{3,... | collective-permute-start | bytes 147464 | tf_op jit(solution)/shard_map/ppermute | solution.py:370
  84.0 5.0 %collective-permute-start.30 = (f32[96,128]{1,0:T(8,128)S(1)}, f32[96,128]{1,0:T(8,128)S(1)}, u32[]{:S(2)}, u32[]{:S(2)}) collective-permute-start(f32[96,128]{1,0:T(8,128)S(1)} %normal.3.refs_0_.q0), channel_id=1, source_target_pairs={{0,16},{1,17},{8,24},{9,25},{16,0},{17,1},{24,8},{25,9},{2,18},{3,... | collective-permute-start | bytes 147464 | tf_op jit(solution)/shard_map/ppermute | solution.py:370
  85.2 4.2 %collective-permute-start.29 = (f32[96,128]{1,0:T(8,128)S(1)}, f32[96,128]{1,0:T(8,128)S(1)}, u32[]{:S(2)}, u32[]{:S(2)}) collective-permute-start(f32[96,128]{1,0:T(8,128)S(1)} %normal.3.refs_0_.q0), channel_id=1, source_target_pairs={{0,9},{1,8},{8,1},{9,0},{16,25},{17,24},{24,17},{25,16},{2,11},{3,... | collective-permute-start | bytes 147464 | tf_op jit(solution)/shard_map/ppermute | solution.py:370
  89.5 2.4 %collective-permute-start.32 = (f32[408,128]{1,0:T(8,128)S(1)}, f32[408,128]{1,0:T(8,128)S(1)}, u32[]{:S(2)}, u32[]{:S(2)}) collective-permute-start(f32[408,128]{1,0:T(8,128)S(1)} %join.1), channel_id=1, source_target_pairs={{0,1},{1,0},{2,3},{3,2},{4,5},{5,4},{6,7},{7,6},{8,9},{9,8},{10,11... | collective-permute-start | bytes 626696 | tf_op jit(solution)/shard_map/ppermute | solution.py:366

commit v9 on v8

--- a/solution.py
+++ b/solution.py
@@ -248,7 +248,7 @@
 
 
 def pick_kernel(mine_ref, arrived_ref, _, *o_refs):
-    for k, o_ref in enumerate(o_refs[:SIDE]):
+    for k, o_ref in zip((3, 2, 1, 0), o_refs):
         o_ref[...] = mine_ref[lax.axis_index("x") ^ k] + arrived_ref[lax.axis_index("x") ^ k]
 
 
@@ -376,7 +376,8 @@
 
 
 def right_sum(parts, p=(), first=()):
-    (z,) = add(parts[:1] + tuple(cross(parts[k], "x", k) for k in (1, 2, 3)), DEEP + 8)
+    moved = [cross(parts[k], "x", k) for k in (3, 2, 1)]
+    (z,) = add((*moved, parts[0]), DEEP + 8)
     z, gram = add(everyones(z, "y", cross), DEEP, 8)
     z_all = everyones(z, "dp", cross)
     lower, *hat = lower_inverse(gram, p)
@@ -392,9 +393,9 @@
     p, g, e = first_left(grads, errors, jnp.swapaxes(q_init, 1, 2))
     p_all = everyones(p, "dp", swap)
     arrived = swap(right(1, p_all, g, e), "core", 1)
-    *parts, w = pick(right(0, p_all, g, e), arrived, working(g, e))
+    z3, z2, z1, z0, w = pick(right(0, p_all, g, e), arrived, working(g, e))
     w = (g, e) + tuple(halves(swap(w, "core", 1)))
-    parts, _, _ = right_sum(tuple(parts), first=w[2:])
+    parts, _, _ = right_sum((z0, z1, z2, z3), first=w[2:])
 
     acc = left_part((0,), parts[:1], w)
     parts, acc = after(parts, left_part((3,), parts[3:], w, (acc,)), 1)

time: 95 us -> 95 us (level)
  starting transfers between devices: 45 us -> 43.8 us
  waiting for transfers between devices: 26.5 us -> 27.7 us
    ppermute x27, waiting for transfers between devices: 23.1 us -> 24.3 us  [cross(): lax.ppermute(a, (axis, 'core'), [(i * 2 + c, (i ^ k) * 2 + (c ^ k & 1)) f...]
  transfers between devices with their start and end apart: 33 -> 33, of which waited for: 21 -> 20; matrix products, arithmetic and copies ran while one was open for 0% -> 0% of each run, Pallas kernels for 12% -> 12%
where the time goes in v9:
time: 95 us; the launch traced here: 94.9 us
  starting transfers between devices  43.8 us (46%)
  waiting for transfers between devices  27.7 us (29%)
  Pallas kernels  22.4 us (24%)
  between operations  1.02 us (1%)
    ppermute x27, starting transfers between devices, cross(): lax.ppermute(a, (axis, 'core'), [(i * 2 + c, (i ^ k) * 2 + (c ^ k & 1)) f...  36.1 us
    ppermute x27, waiting for transfers between devices, cross(): lax.ppermute(a, (axis, 'core'), [(i * 2 + c, (i ^ k) * 2 + (c ^ k & 1)) f...  24.3 us
    ppermute x6, starting transfers between devices, swap(): lax.ppermute(a, axis, [(i, i ^ k) for i in range(lax.axis_size(axis))])  7.72 us
    pallas_call x4, Pallas kernels, final(): pl.pallas_call(functools.partial(final_kernel, slot, ks, len(parts), n_in...  7.23 us
    pallas_call x1, Pallas kernels, first_left(): kernel(first_left_kernel, (pltpu.VMEM((16, ROWS), F32), wide, wide), [ANY...  5.25 us
    ppermute x6, waiting for transfers between devices, swap(): lax.ppermute(a, axis, [(i, i ^ k) for i in range(lax.axis_size(axis))])  3.43 us
    pallas_call x4, Pallas kernels, left_part(): kernel(functools.partial(left_kernel, ks), out, [IN_VMEM] * (len(parts) +...  3.17 us
    pallas_call x2, Pallas kernels, right(): kernel(functools.partial(right_kernel, slot), pltpu.VMEM((SIDE, DEEP + 8,...  1.96 us
  transfers between devices with their start and end apart: 33, of which 20 were waited for; matrix products, arithmetic and copies ran while one was open for 0% of the time, Pallas kernels for 12%

profile of v9, /device:TPU:1, one launch (start us, length us, event | category | flops | bytes accessed | tf_op | source)
XLA Modules:
  0.0 94.9 jit_solution(3578100963225768392)
XLA Ops:
  0.6 5.3 %first_left.1 = (f32[16,192]{1,0:T(8,128)S(1)}, bf16[2,192,6144]{2,1,0:T(8,128)(2,1)S(1)}, bf16[2,192,6144]{2,1,0:T(8,128)(2,1)S(1)}) custom-call(bf16[1,2,192,6144]{3,2,1,0:T(8,128)(2,1)} %g_hbm.1, bf16[1,2,192,6144]{3,2,1,0:T(8,128)(2,1)} %e_hbm.1, f32[2,8,6144]{2,1,0:T(8,128)} %bitcast.3), custom_call_target="tpu_custom_call" | custom-call | flops 10000000 | bytes 1000000 | tf_op jit(solution)/shard_map/first_left/pallas_call | solution.py:136
  5.9 4.7 %collective-permute-start.2 = (f32[16,192]{1,0:T(8,128)S(1)}, f32[16,192]{1,0:T(8,128)S(1)}, u32[]{:S(2)}, u32[]{:S(2)}) collective-permute-start(f32[16,192]{1,0:T(8,128)S(1)} %get-tuple-element.43.p0), channel_id=1, source_target_pairs={{0,96},{32,64},{64,32},{96,0},{1,97},{33,65},{65,33},{97,1},{2,98}... | collective-permute-start | bytes 36872 | tf_op jit(solution)/shard_map/ppermute | solution.py:366
  11.7 3.0 %collective-permute-done.1.p2 = f32[16,192]{1,0:T(8,128)S(1)} collective-permute-done((f32[16,192]{1,0:T(8,128)S(1)}, f32[16,192]{1,0:T(8,128)S(1)}, u32[]{:S(2)}, u32[]{:S(2)}) %collective-permute-start.1) | collective-permute-done | bytes 12320 | tf_op jit(solution)/shard_map/ppermute | solution.py:366
  14.7 1.0 %right_other.1 = f32[4,104,128]{2,1,0:T(8,128)S(1)} custom-call(f32[16,192]{1,0:T(8,128)S(1)} %get-tuple-element.43.p0, f32[16,192]{1,0:T(8,128)S(1)} %collective-permute-done.p1, f32[16,192]{1,0:T(8,128)S(1)} %collective-permute-done.1.p2, f32[16,192]{1,0:T(8,128)S(1)} %collective-permute-done.2.p3, ...), custom_call_target="tpu_custom_call" | custom-call | flops 1000000000 | bytes 1000000 | tf_op jit(solution)/shard_map/right_other/pallas_call | solution.py:222
  15.6 2.2 %collective-permute-start.3 = (f32[4,104,128]{2,1,0:T(8,128)S(1)}, f32[4,104,128]{2,1,0:T(8,128)S(1)}, u32[]{:S(2)}, u32[]{:S(2)}) collective-permute-start(f32[4,104,128]{2,1,0:T(8,128)S(1)} %right_other.1), channel_id=1, source_target_pairs={{0,1},{1,0},{2,3},{3,2},{4,5},{5,4},{6,7},{7,6},{8,9},{9,8},{10,11... | collective-permute-start | bytes 638984 | tf_op jit(solution)/shard_map/ppermute | solution.py:366
  18.3 1.0 %right_own.1.mine_ref = f32[4,104,128]{2,1,0:T(8,128)S(1)} custom-call(f32[16,192]{1,0:T(8,128)S(1)} %get-tuple-element.43.p0, f32[16,192]{1,0:T(8,128)S(1)} %collective-permute-done.p1, f32[16,192]{1,0:T(8,128)S(1)} %collective-permute-done.1.p2, f32[16,192]{1,0:T(8,128)S(1)} %collective-permute-done.2.p3, ...), custom_call_target="tpu_custom_call" | custom-call | flops 1000000000 | bytes 1000000 | tf_op jit(solution)/shard_map/right_own/pallas_call | solution.py:222
  19.4 2.8 %collective-permute-start.4 = (f32[104,128]{1,0:T(8,128)S(1)}, f32[104,128]{1,0:T(8,128)S(1)}, u32[]{:S(2)}, u32[]{:S(2)}) collective-permute-start(f32[104,128]{1,0:T(8,128)S(1)} %get-tuple-element.46), channel_id=1, source_target_pairs={{0,25},{1,24},{8,17},{9,16},{16,9},{17,8},{24,1},{25,0},{2,27},{3,... | collective-permute-start | bytes 159752 | tf_op jit(solution)/shard_map/ppermute | solution.py:370
  23.3 1.3 %collective-permute-done.4.a = f32[104,128]{1,0:T(8,128)S(1)} collective-permute-done((f32[104,128]{1,0:T(8,128)S(1)}, f32[104,128]{1,0:T(8,128)S(1)}, u32[]{:S(2)}, u32[]{:S(2)}) %collective-permute-start.4) | collective-permute-done | bytes 53280 | tf_op jit(solution)/shard_map/ppermute | solution.py:370
  24.6 2.6 %collective-permute-done.5.b = f32[104,128]{1,0:T(8,128)S(1)} collective-permute-done((f32[104,128]{1,0:T(8,128)S(1)}, f32[104,128]{1,0:T(8,128)S(1)}, u32[]{:S(2)}, u32[]{:S(2)}) %collective-permute-start.5) | collective-permute-done | bytes 53280 | tf_op jit(solution)/shard_map/ppermute | solution.py:370
  27.2 3.9 %collective-permute-start.9 = (f32[104,128]{1,0:T(8,128)S(1)}, f32[104,128]{1,0:T(8,128)S(1)}, u32[]{:S(2)}, u32[]{:S(2)}) collective-permute-start(f32[104,128]{1,0:T(8,128)S(1)} %add.4.a), channel_id=1, source_target_pairs={{0,7},{1,6},{2,5},{3,4},{4,3},{5,2},{6,1},{7,0},{8,15},{9,14},{10,... | collective-permute-start | bytes 159752 | tf_op jit(solution)/shard_map/ppermute | solution.py:370
  32.1 1.2 %collective-permute-done.9.d = f32[104,128]{1,0:T(8,128)S(1)} collective-permute-done((f32[104,128]{1,0:T(8,128)S(1)}, f32[104,128]{1,0:T(8,128)S(1)}, u32[]{:S(2)}, u32[]{:S(2)}) %collective-permute-start.9) | collective-permute-done | bytes 53280 | tf_op jit(solution)/shard_map/ppermute | solution.py:370
  33.2 2.7 %collective-permute-done.8.c = f32[104,128]{1,0:T(8,128)S(1)} collective-permute-done((f32[104,128]{1,0:T(8,128)S(1)}, f32[104,128]{1,0:T(8,128)S(1)}, u32[]{:S(2)}, u32[]{:S(2)}) %collective-permute-start.8) | collective-permute-done | bytes 53280 | tf_op jit(solution)/shard_map/ppermute | solution.py:370
  36.0 1.0 %collective-permute-start.12 = (f32[96,128]{1,0:T(8,128)S(1)}, f32[96,128]{1,0:T(8,128)S(1)}, u32[]{:S(2)}, u32[]{:S(2)}) collective-permute-start(f32[96,128]{1,0:T(8,128)S(1)} %get-tuple-element.50.z0), channel_id=1, source_target_pairs={{0,97},{1,96},{32,65},{33,64},{64,33},{65,32},{96,1},{97,0},{2,99}... | collective-permute-start | bytes 147464 | tf_op jit(solution)/shard_map/ppermute | solution.py:370
  37.0 0.9 collective-permute-start.11
  37.9 2.0 %collective-permute-start.10 = (f32[96,128]{1,0:T(8,128)S(1)}, f32[96,128]{1,0:T(8,128)S(1)}, u32[]{:S(2)}, u32[]{:S(2)}) collective-permute-start(f32[96,128]{1,0:T(8,128)S(1)} %get-tuple-element.50.z0), channel_id=1, source_target_pairs={{0,33},{1,32},{32,1},{33,0},{64,97},{65,96},{96,65},{97,64},{2,35}... | collective-permute-start | bytes 147464 | tf_op jit(solution)/shard_map/ppermute | solution.py:370
  41.6 1.1 %collective-permute-done.10.z1 = f32[96,128]{1,0:T(8,128)S(1)} collective-permute-done((f32[96,128]{1,0:T(8,128)S(1)}, f32[96,128]{1,0:T(8,128)S(1)}, u32[]{:S(2)}, u32[]{:S(2)}) %collective-permute-start.10) | collective-permute-done | bytes 49184 | tf_op jit(solution)/shard_map/ppermute | solution.py:370
  42.8 1.8 %collective-permute-start.16 = (f32[96,128]{1,0:T(8,128)S(1)}, f32[96,128]{1,0:T(8,128)S(1)}, u32[]{:S(2)}, u32[]{:S(2)}) collective-permute-start(f32[96,128]{1,0:T(8,128)S(1)} %normal.2.refs_0_), channel_id=1, source_target_pairs={{0,25},{1,24},{8,17},{9,16},{16,9},{17,8},{24,1},{25,0},{2,27},{3,... | collective-permute-start | bytes 147464 | tf_op jit(solution)/shard_map/ppermute | solution.py:370
  44.6 2.4 %collective-permute-start.14 = (f32[96,128]{1,0:T(8,128)S(1)}, f32[96,128]{1,0:T(8,128)S(1)}, u32[]{:S(2)}, u32[]{:S(2)}) collective-permute-start(f32[96,128]{1,0:T(8,128)S(1)} %normal.2.refs_0_), channel_id=1, source_target_pairs={{0,16},{1,17},{8,24},{9,25},{16,0},{17,1},{24,8},{25,9},{2,18},{3,... | collective-permute-start | bytes 147464 | tf_op jit(solution)/shard_map/ppermute | solution.py:370
  47.0 0.8 left_factor.4.refs_5_
  47.8 0.8 left_factor.5.refs_5_
  48.6 0.8 left_factor.6.refs_5_
  50.1 0.8 left_factor.7.p0
  50.9 2.3 %collective-permute-start.19 = (f32[16,192]{1,0:T(8,128)S(1)}, f32[16,192]{1,0:T(8,128)S(1)}, u32[]{:S(2)}, u32[]{:S(2)}) collective-permute-start(f32[16,192]{1,0:T(8,128)S(1)} %left_factor.7.p0), channel_id=1, source_target_pairs={{0,97},{1,96},{32,65},{33,64},{64,33},{65,32},{96,1},{97,0},{2,99}... | collective-permute-start | bytes 36872 | tf_op jit(solution)/shard_map/ppermute | solution.py:370
  53.2 1.0 %collective-permute-start.18 = (f32[16,192]{1,0:T(8,128)S(1)}, f32[16,192]{1,0:T(8,128)S(1)}, u32[]{:S(2)}, u32[]{:S(2)}) collective-permute-start(f32[16,192]{1,0:T(8,128)S(1)} %left_factor.7.p0), channel_id=1, source_target_pairs={{0,64},{1,65},{32,96},{33,97},{64,0},{65,1},{96,32},{97,33},{2,66}... | collective-permute-start | bytes 36872 | tf_op jit(solution)/shard_map/ppermute | solution.py:370
  54.8 1.0 %collective-permute-done.19.p3 = f32[16,192]{1,0:T(8,128)S(1)} collective-permute-done((f32[16,192]{1,0:T(8,128)S(1)}, f32[16,192]{1,0:T(8,128)S(1)}, u32[]{:S(2)}, u32[]{:S(2)}) %collective-permute-start.19) | collective-permute-done | bytes 12320 | tf_op jit(solution)/shard_map/ppermute | solution.py:370
  55.8 1.6 %collective-permute-done.18.p2 = f32[16,192]{1,0:T(8,128)S(1)} collective-permute-done((f32[16,192]{1,0:T(8,128)S(1)}, f32[16,192]{1,0:T(8,128)S(1)}, u32[]{:S(2)}, u32[]{:S(2)}) %collective-permute-start.18) | collective-permute-done | bytes 12320 | tf_op jit(solution)/shard_map/ppermute | solution.py:370
  57.4 0.8 right_both.3
  58.2 1.6 %collective-permute-start.22 = (f32[104,128]{1,0:T(8,128)S(1)}, f32[104,128]{1,0:T(8,128)S(1)}, u32[]{:S(2)}, u32[]{:S(2)}) collective-permute-start(f32[104,128]{1,0:T(8,128)S(1)} %get-tuple-element.59), channel_id=1, source_target_pairs={{0,9},{1,8},{8,1},{9,0},{16,25},{17,24},{24,17},{25,16},{2,11},{3,... | collective-permute-start | bytes 159752 | tf_op jit(solution)/shard_map/ppermute | solution.py:370
  59.8 0.8 right_both.2
  60.7 1.7 %collective-permute-start.20 = (f32[104,128]{1,0:T(8,128)S(1)}, f32[104,128]{1,0:T(8,128)S(1)}, u32[]{:S(2)}, u32[]{:S(2)}) collective-permute-start(f32[104,128]{1,0:T(8,128)S(1)} %get-tuple-element.57), channel_id=1, source_target_pairs={{0,25},{1,24},{8,17},{9,16},{16,9},{17,8},{24,1},{25,0},{2,27},{3,... | collective-permute-start | bytes 159752 | tf_op jit(solution)/shard_map/ppermute | solution.py:370
  62.7 2.8 %collective-permute-done.20.a = f32[104,128]{1,0:T(8,128)S(1)} collective-permute-done((f32[104,128]{1,0:T(8,128)S(1)}, f32[104,128]{1,0:T(8,128)S(1)}, u32[]{:S(2)}, u32[]{:S(2)}) %collective-permute-start.20) | collective-permute-done | bytes 53280 | tf_op jit(solution)/shard_map/ppermute | solution.py:370
  65.5 2.1 %collective-permute-done.21.b = f32[104,128]{1,0:T(8,128)S(1)} collective-permute-done((f32[104,128]{1,0:T(8,128)S(1)}, f32[104,128]{1,0:T(8,128)S(1)}, u32[]{:S(2)}, u32[]{:S(2)}) %collective-permute-start.21) | collective-permute-done | bytes 53280 | tf_op jit(solution)/shard_map/ppermute | solution.py:370
  67.7 1.9 %collective-permute-start.25 = (f32[104,128]{1,0:T(8,128)S(1)}, f32[104,128]{1,0:T(8,128)S(1)}, u32[]{:S(2)}, u32[]{:S(2)}) collective-permute-start(f32[104,128]{1,0:T(8,128)S(1)} %add.6.a), channel_id=1, source_target_pairs={{0,7},{1,6},{2,5},{3,4},{4,3},{5,2},{6,1},{7,0},{8,15},{9,14},{10,... | collective-permute-start | bytes 159752 | tf_op jit(solution)/shard_map/ppermute | solution.py:370
  70.0 1.5 %collective-permute-start.23 = (f32[104,128]{1,0:T(8,128)S(1)}, f32[104,128]{1,0:T(8,128)S(1)}, u32[]{:S(2)}, u32[]{:S(2)}) collective-permute-start(f32[104,128]{1,0:T(8,128)S(1)} %add.6.a), channel_id=1, source_target_pairs={{0,3},{1,2},{2,1},{3,0},{4,7},{5,6},{6,5},{7,4},{8,11},{9,10},{10,... | collective-permute-start | bytes 159752 | tf_op jit(solution)/shard_map/ppermute | solution.py:370
  71.6 1.2 %collective-permute-done.25.d = f32[104,128]{1,0:T(8,128)S(1)} collective-permute-done((f32[104,128]{1,0:T(8,128)S(1)}, f32[104,128]{1,0:T(8,128)S(1)}, u32[]{:S(2)}, u32[]{:S(2)}) %collective-permute-start.25) | collective-permute-done | bytes 53280 | tf_op jit(solution)/shard_map/ppermute | solution.py:370
  72.8 1.7 %collective-permute-done.24.c = f32[104,128]{1,0:T(8,128)S(1)} collective-permute-done((f32[104,128]{1,0:T(8,128)S(1)}, f32[104,128]{1,0:T(8,128)S(1)}, u32[]{:S(2)}, u32[]{:S(2)}) %collective-permute-start.24) | collective-permute-done | bytes 53280 | tf_op jit(solution)/shard_map/ppermute | solution.py:370
  74.8 1.5 %collective-permute-start.28 = (f32[96,128]{1,0:T(8,128)S(1)}, f32[96,128]{1,0:T(8,128)S(1)}, u32[]{:S(2)}, u32[]{:S(2)}) collective-permute-start(f32[96,128]{1,0:T(8,128)S(1)} %get-tuple-element.61.z0), channel_id=1, source_target_pairs={{0,97},{1,96},{32,65},{33,64},{64,33},{65,32},{96,1},{97,0},{2,99}... | collective-permute-start | bytes 147464 | tf_op jit(solution)/shard_map/ppermute | solution.py:370
  76.8 2.0 %collective-permute-start.26 = (f32[96,128]{1,0:T(8,128)S(1)}, f32[96,128]{1,0:T(8,128)S(1)}, u32[]{:S(2)}, u32[]{:S(2)}) collective-permute-start(f32[96,128]{1,0:T(8,128)S(1)} %get-tuple-element.61.z0), channel_id=1, source_target_pairs={{0,33},{1,32},{32,1},{33,0},{64,97},{65,96},{96,65},{97,64},{2,35}... | collective-permute-start | bytes 147464 | tf_op jit(solution)/shard_map/ppermute | solution.py:370
  78.7 0.9 lower_inverse.3
  80.2 1.1 %collective-permute-done.27.z2 = f32[96,128]{1,0:T(8,128)S(1)} collective-permute-done((f32[96,128]{1,0:T(8,128)S(1)}, f32[96,128]{1,0:T(8,128)S(1)}, u32[]{:S(2)}, u32[]{:S(2)}) %collective-permute-start.27) | collective-permute-done | bytes 49184 | tf_op jit(solution)/shard_map/ppermute | solution.py:370
  81.3 1.1 %collective-permute-done.26.z1 = f32[96,128]{1,0:T(8,128)S(1)} collective-permute-done((f32[96,128]{1,0:T(8,128)S(1)}, f32[96,128]{1,0:T(8,128)S(1)}, u32[]{:S(2)}, u32[]{:S(2)}) %collective-permute-start.26) | collective-permute-done | bytes 49184 | tf_op jit(solution)/shard_map/ppermute | solution.py:370
  82.5 0.9 collective-permute-start.31
  84.0 2.4 %collective-permute-start.29 = (f32[96,128]{1,0:T(8,128)S(1)}, f32[96,128]{1,0:T(8,128)S(1)}, u32[]{:S(2)}, u32[]{:S(2)}) collective-permute-start(f32[96,128]{1,0:T(8,128)S(1)} %normal.3.refs_0_.q0), channel_id=1, source_target_pairs={{0,9},{1,8},{8,1},{9,0},{16,25},{17,24},{24,17},{25,16},{2,11},{3,... | collective-permute-start | bytes 147464 | tf_op jit(solution)/shard_map/ppermute | solution.py:370
  86.4 1.3 %residual_own.3 = (bf16[2,192,6144]{2,1,0:T(8,128)(2,1)}, bf16[1,2,192,6144]{3,2,1,0:T(8,128)(2,1)}, f32[2,8,6144]{2,1,0:T(8,128)}) custom-call(f32[96,128]{1,0:T(8,128)S(1)} %normal.3.refs_0_.q0, bf16[256,128]{1,0:T(8,128)(2,1)S(1)} %get-tuple-element.65.refs_1_.refs_2_, bf16[2,192,6144]{2,1,0:T(8,128)(2,1)S(1)} %get-tuple-element.44.g_ref.refs_1_.refs_2_.refs_3_, ...), custom_call_target="tpu_custom_call" | custom-call | flops 1000000000 | bytes 1000000 | tf_op jit(solution)/shard_map/residual_own/pallas_call | solution.py:350
  87.7 1.0 %collective-permute-done.31.refs_0_.q3 = f32[96,128]{1,0:T(8,128)S(1)} collective-permute-done((f32[96,128]{1,0:T(8,128)S(1)}, f32[96,128]{1,0:T(8,128)S(1)}, u32[]{:S(2)}, u32[]{:S(2)}) %collective-permute-start.31) | collective-permute-done | bytes 49184 | tf_op jit(solution)/shard_map/ppermute | solution.py:370
  88.7 1.3 %residual_own.4 = (bf16[2,192,6144]{2,1,0:T(8,128)(2,1)}, bf16[1,2,192,6144]{3,2,1,0:T(8,128)(2,1)}, f32[2,8,6144]{2,1,0:T(8,128)}) custom-call(f32[96,128]{1,0:T(8,128)S(1)} %collective-permute-done.31.refs_0_.q3, bf16[256,128]{1,0:T(8,128)(2,1)S(1)} %get-tuple-element.65.refs_1_.refs_2_, ...), custom_call_target="tpu_custom_call", output_to_operand_aliasing={{0}: (4, {}), {1}: (5, {}), {2}: (6, {})} | custom-call | flops 1000000000 | bytes 1000000 | tf_op jit(solution)/shard_map/residual_own/pallas_call | solution.py:350
  90.1 1.8 %residual_own.5 = (bf16[2,192,6144]{2,1,0:T(8,128)(2,1)}, bf16[1,2,192,6144]{3,2,1,0:T(8,128)(2,1)}, f32[2,8,6144]{2,1,0:T(8,128)}) custom-call(f32[96,128]{1,0:T(8,128)S(1)} %collective-permute-done.29.q1.refs_0_, f32[96,128]{1,0:T(8,128)S(1)} %collective-permute-done.30.q2.refs_1_, ...), custom_call_target="tpu_custom_call", output_to_operand_aliasing={{0}: (5, {}), {1}: (6, {}), {2}: (7, {})} | custom-call | flops 1000000000 | bytes 1000000 | tf_op jit(solution)/shard_map/residual_own/pallas_call | solution.py:350
  91.9 2.8 %residual_other.1 = (bf16[2,192,6144]{2,1,0:T(8,128)(2,1)}, bf16[1,2,192,6144]{3,2,1,0:T(8,128)(2,1)}, f32[2,8,6144]{2,1,0:T(8,128)}) custom-call(f32[408,128]{1,0:T(8,128)S(1)} %collective-permute-done.32.refs_0_, ...), custom_call_target="tpu_custom_call", output_to_operand_aliasing={{0}: (3, {}), {1}: (4, {}), {2}: (5, {})} | custom-call | flops 1000000000 | bytes 1000000 | tf_op jit(solution)/shard_map/residual_other/pallas_call | solution.py:350
  (43 shorter events, 9.7 us)
Async XLA Ops:
  5.9 5.8 %collective-permute-start.2 = (f32[16,192]{1,0:T(8,128)S(1)}, f32[16,192]{1,0:T(8,128)S(1)}, u32[]{:S(2)}, u32[]{:S(2)}) collective-permute-start(f32[16,192]{1,0:T(8,128)S(1)} %get-tuple-element.43.p0), channel_id=1, source_target_pairs={{0,96},{32,64},{64,32},{96,0},{1,97},{33,65},{65,33},{97,1},{2,98}... | collective-permute-start | bytes 36872 | tf_op jit(solution)/shard_map/ppermute | solution.py:366
  10.6 4.1 %collective-permute-start.1 = (f32[16,192]{1,0:T(8,128)S(1)}, f32[16,192]{1,0:T(8,128)S(1)}, u32[]{:S(2)}, u32[]{:S(2)}) collective-permute-start(f32[16,192]{1,0:T(8,128)S(1)} %get-tuple-element.43.p0), channel_id=1, source_target_pairs={{0,64},{32,96},{64,0},{96,32},{1,65},{33,97},{65,1},{97,33},{2,66}... | collective-permute-start | bytes 36872 | tf_op jit(solution)/shard_map/ppermute | solution.py:366
  10.6 4.1 %collective-permute-start = (f32[16,192]{1,0:T(8,128)S(1)}, f32[16,192]{1,0:T(8,128)S(1)}, u32[]{:S(2)}, u32[]{:S(2)}) collective-permute-start(f32[16,192]{1,0:T(8,128)S(1)} %get-tuple-element.43.p0), channel_id=1, source_target_pairs={{0,32},{32,0},{64,96},{96,64},{1,33},{33,1},{65,97},{97,65},{2,34}... | collective-permute-start | bytes 36872 | tf_op jit(solution)/shard_map/ppermute | solution.py:366
  15.6 3.6 %collective-permute-start.3 = (f32[4,104,128]{2,1,0:T(8,128)S(1)}, f32[4,104,128]{2,1,0:T(8,128)S(1)}, u32[]{:S(2)}, u32[]{:S(2)}) collective-permute-start(f32[4,104,128]{2,1,0:T(8,128)S(1)} %right_other.1), channel_id=1, source_target_pairs={{0,1},{1,0},{2,3},{3,2},{4,5},{5,4},{6,7},{7,6},{8,9},{9,8},{10,11... | collective-permute-start | bytes 638984 | tf_op jit(solution)/shard_map/ppermute | solution.py:366
  19.3 21.2 %collective-permute-start.13 = (f32[192,6144]{1,0:T(8,128)S(1)}, f32[192,6144]{1,0:T(8,128)S(1)}, u32[]{:S(2)}, u32[]{:S(2)}) collective-permute-start(f32[192,6144]{1,0:T(8,128)S(1)} %get-tuple-element.52), channel_id=1, source_target_pairs={{0,1},{1,0},{2,3},{3,2},{4,5},{5,4},{6,7},{7,6},{8,9},{9,8},{10,11... | collective-permute-start | bytes 14155784 | tf_op jit(solution)/shard_map/ppermute | solution.py:366
  19.4 5.1 %collective-permute-start.4 = (f32[104,128]{1,0:T(8,128)S(1)}, f32[104,128]{1,0:T(8,128)S(1)}, u32[]{:S(2)}, u32[]{:S(2)}) collective-permute-start(f32[104,128]{1,0:T(8,128)S(1)} %get-tuple-element.46), channel_id=1, source_target_pairs={{0,25},{1,24},{8,17},{9,16},{16,9},{17,8},{24,1},{25,0},{2,27},{3,... | collective-permute-start | bytes 159752 | tf_op jit(solution)/shard_map/ppermute | solution.py:370
  22.3 4.9 %collective-permute-start.5 = (f32[104,128]{1,0:T(8,128)S(1)}, f32[104,128]{1,0:T(8,128)S(1)}, u32[]{:S(2)}, u32[]{:S(2)}) collective-permute-start(f32[104,128]{1,0:T(8,128)S(1)} %get-tuple-element.47), channel_id=1, source_target_pairs={{0,16},{1,17},{8,24},{9,25},{16,0},{17,1},{24,8},{25,9},{2,18},{3,... | collective-permute-start | bytes 159752 | tf_op jit(solution)/shard_map/ppermute | solution.py:370
  22.8 4.4 %collective-permute-start.6 = (f32[104,128]{1,0:T(8,128)S(1)}, f32[104,128]{1,0:T(8,128)S(1)}, u32[]{:S(2)}, u32[]{:S(2)}) collective-permute-start(f32[104,128]{1,0:T(8,128)S(1)} %get-tuple-element.48), channel_id=1, source_target_pairs={{0,9},{1,8},{8,1},{9,0},{16,25},{17,24},{24,17},{25,16},{2,11},{3,... | collective-permute-start | bytes 159752 | tf_op jit(solution)/shard_map/ppermute | solution.py:370
  27.2 6.0 %collective-permute-start.9 = (f32[104,128]{1,0:T(8,128)S(1)}, f32[104,128]{1,0:T(8,128)S(1)}, u32[]{:S(2)}, u32[]{:S(2)}) collective-permute-start(f32[104,128]{1,0:T(8,128)S(1)} %add.4.a), channel_id=1, source_target_pairs={{0,7},{1,6},{2,5},{3,4},{4,3},{5,2},{6,1},{7,0},{8,15},{9,14},{10,... | collective-permute-start | bytes 159752 | tf_op jit(solution)/shard_map/ppermute | solution.py:370
  31.1 4.9 %collective-permute-start.8 = (f32[104,128]{1,0:T(8,128)S(1)}, f32[104,128]{1,0:T(8,128)S(1)}, u32[]{:S(2)}, u32[]{:S(2)}) collective-permute-start(f32[104,128]{1,0:T(8,128)S(1)} %add.4.a), channel_id=1, source_target_pairs={{0,4},{1,5},{2,6},{3,7},{4,0},{5,1},{6,2},{7,3},{8,12},{9,13},{10,... | collective-permute-start | bytes 159752 | tf_op jit(solution)/shard_map/ppermute | solution.py:370
  31.5 4.5 %collective-permute-start.7 = (f32[104,128]{1,0:T(8,128)S(1)}, f32[104,128]{1,0:T(8,128)S(1)}, u32[]{:S(2)}, u32[]{:S(2)}) collective-permute-start(f32[104,128]{1,0:T(8,128)S(1)} %add.4.a), channel_id=1, source_target_pairs={{0,3},{1,2},{2,1},{3,0},{4,7},{5,6},{6,5},{7,4},{8,11},{9,10},{10,... | collective-permute-start | bytes 159752 | tf_op jit(solution)/shard_map/ppermute | solution.py:370
  36.0 5.4 %collective-permute-start.12 = (f32[96,128]{1,0:T(8,128)S(1)}, f32[96,128]{1,0:T(8,128)S(1)}, u32[]{:S(2)}, u32[]{:S(2)}) collective-permute-start(f32[96,128]{1,0:T(8,128)S(1)} %get-tuple-element.50.z0), channel_id=1, source_target_pairs={{0,97},{1,96},{32,65},{33,64},{64,33},{65,32},{96,1},{97,0},{2,99}... | collective-permute-start | bytes 147464 | tf_op jit(solution)/shard_map/ppermute | solution.py:370
  37.0 4.5 %collective-permute-start.11 = (f32[96,128]{1,0:T(8,128)S(1)}, f32[96,128]{1,0:T(8,128)S(1)}, u32[]{:S(2)}, u32[]{:S(2)}) collective-permute-start(f32[96,128]{1,0:T(8,128)S(1)} %get-tuple-element.50.z0), channel_id=1, source_target_pairs={{0,64},{1,65},{32,96},{33,97},{64,0},{65,1},{96,32},{97,33},{2,66}... | collective-permute-start | bytes 147464 | tf_op jit(solution)/shard_map/ppermute | solution.py:370
  37.9 4.8 %collective-permute-start.10 = (f32[96,128]{1,0:T(8,128)S(1)}, f32[96,128]{1,0:T(8,128)S(1)}, u32[]{:S(2)}, u32[]{:S(2)}) collective-permute-start(f32[96,128]{1,0:T(8,128)S(1)} %get-tuple-element.50.z0), channel_id=1, source_target_pairs={{0,33},{1,32},{32,1},{33,0},{64,97},{65,96},{96,65},{97,64},{2,35}... | collective-permute-start | bytes 147464 | tf_op jit(solution)/shard_map/ppermute | solution.py:370
  42.8 5.0 %collective-permute-start.16 = (f32[96,128]{1,0:T(8,128)S(1)}, f32[96,128]{1,0:T(8,128)S(1)}, u32[]{:S(2)}, u32[]{:S(2)}) collective-permute-start(f32[96,128]{1,0:T(8,128)S(1)} %normal.2.refs_0_), channel_id=1, source_target_pairs={{0,25},{1,24},{8,17},{9,16},{16,9},{17,8},{24,1},{25,0},{2,27},{3,... | collective-permute-start | bytes 147464 | tf_op jit(solution)/shard_map/ppermute | solution.py:370
  44.6 4.0 %collective-permute-start.15 = (f32[96,128]{1,0:T(8,128)S(1)}, f32[96,128]{1,0:T(8,128)S(1)}, u32[]{:S(2)}, u32[]{:S(2)}) collective-permute-start(f32[96,128]{1,0:T(8,128)S(1)} %normal.2.refs_0_), channel_id=1, source_target_pairs={{0,9},{1,8},{8,1},{9,0},{16,25},{17,24},{24,17},{25,16},{2,11},{3,... | collective-permute-start | bytes 147464 | tf_op jit(solution)/shard_map/ppermute | solution.py:370
  44.6 5.5 %collective-permute-start.14 = (f32[96,128]{1,0:T(8,128)S(1)}, f32[96,128]{1,0:T(8,128)S(1)}, u32[]{:S(2)}, u32[]{:S(2)}) collective-permute-start(f32[96,128]{1,0:T(8,128)S(1)} %normal.2.refs_0_), channel_id=1, source_target_pairs={{0,16},{1,17},{8,24},{9,25},{16,0},{17,1},{24,8},{25,9},{2,18},{3,... | collective-permute-start | bytes 147464 | tf_op jit(solution)/shard_map/ppermute | solution.py:370
  50.9 4.9 %collective-permute-start.19 = (f32[16,192]{1,0:T(8,128)S(1)}, f32[16,192]{1,0:T(8,128)S(1)}, u32[]{:S(2)}, u32[]{:S(2)}) collective-permute-start(f32[16,192]{1,0:T(8,128)S(1)} %left_factor.7.p0), channel_id=1, source_target_pairs={{0,97},{1,96},{32,65},{33,64},{64,33},{65,32},{96,1},{97,0},{2,99}... | collective-permute-start | bytes 36872 | tf_op jit(solution)/shard_map/ppermute | solution.py:370
  53.2 4.2 %collective-permute-start.18 = (f32[16,192]{1,0:T(8,128)S(1)}, f32[16,192]{1,0:T(8,128)S(1)}, u32[]{:S(2)}, u32[]{:S(2)}) collective-permute-start(f32[16,192]{1,0:T(8,128)S(1)} %left_factor.7.p0), channel_id=1, source_target_pairs={{0,64},{1,65},{32,96},{33,97},{64,0},{65,1},{96,32},{97,33},{2,66}... | collective-permute-start | bytes 36872 | tf_op jit(solution)/shard_map/ppermute | solution.py:370
  54.2 3.2 %collective-permute-start.17 = (f32[16,192]{1,0:T(8,128)S(1)}, f32[16,192]{1,0:T(8,128)S(1)}, u32[]{:S(2)}, u32[]{:S(2)}) collective-permute-start(f32[16,192]{1,0:T(8,128)S(1)} %left_factor.7.p0), channel_id=1, source_target_pairs={{0,33},{1,32},{32,1},{33,0},{64,97},{65,96},{96,65},{97,64},{2,35}... | collective-permute-start | bytes 36872 | tf_op jit(solution)/shard_map/ppermute | solution.py:370
  58.2 4.5 %collective-permute-start.22 = (f32[104,128]{1,0:T(8,128)S(1)}, f32[104,128]{1,0:T(8,128)S(1)}, u32[]{:S(2)}, u32[]{:S(2)}) collective-permute-start(f32[104,128]{1,0:T(8,128)S(1)} %get-tuple-element.59), channel_id=1, source_target_pairs={{0,9},{1,8},{8,1},{9,0},{16,25},{17,24},{24,17},{25,16},{2,11},{3,... | collective-permute-start | bytes 159752 | tf_op jit(solution)/shard_map/ppermute | solution.py:370
  60.7 4.8 %collective-permute-start.20 = (f32[104,128]{1,0:T(8,128)S(1)}, f32[104,128]{1,0:T(8,128)S(1)}, u32[]{:S(2)}, u32[]{:S(2)}) collective-permute-start(f32[104,128]{1,0:T(8,128)S(1)} %get-tuple-element.57), channel_id=1, source_target_pairs={{0,25},{1,24},{8,17},{9,16},{16,9},{17,8},{24,1},{25,0},{2,27},{3,... | collective-permute-start | bytes 159752 | tf_op jit(solution)/shard_map/ppermute | solution.py:370
  62.3 5.3 %collective-permute-start.21 = (f32[104,128]{1,0:T(8,128)S(1)}, f32[104,128]{1,0:T(8,128)S(1)}, u32[]{:S(2)}, u32[]{:S(2)}) collective-permute-start(f32[104,128]{1,0:T(8,128)S(1)} %get-tuple-element.58), channel_id=1, source_target_pairs={{0,16},{1,17},{8,24},{9,25},{16,0},{17,1},{24,8},{25,9},{2,18},{3,... | collective-permute-start | bytes 159752 | tf_op jit(solution)/shard_map/ppermute | solution.py:370
  67.7 5.1 %collective-permute-start.25 = (f32[104,128]{1,0:T(8,128)S(1)}, f32[104,128]{1,0:T(8,128)S(1)}, u32[]{:S(2)}, u32[]{:S(2)}) collective-permute-start(f32[104,128]{1,0:T(8,128)S(1)} %add.6.a), channel_id=1, source_target_pairs={{0,7},{1,6},{2,5},{3,4},{4,3},{5,2},{6,1},{7,0},{8,15},{9,14},{10,... | collective-permute-start | bytes 159752 | tf_op jit(solution)/shard_map/ppermute | solution.py:370
  69.5 4.9 %collective-permute-start.24 = (f32[104,128]{1,0:T(8,128)S(1)}, f32[104,128]{1,0:T(8,128)S(1)}, u32[]{:S(2)}, u32[]{:S(2)}) collective-permute-start(f32[104,128]{1,0:T(8,128)S(1)} %add.6.a), channel_id=1, source_target_pairs={{0,4},{1,5},{2,6},{3,7},{4,0},{5,1},{6,2},{7,3},{8,12},{9,13},{10,... | collective-permute-start | bytes 159752 | tf_op jit(solution)/shard_map/ppermute | solution.py:370
  70.0 4.8 %collective-permute-start.23 = (f32[104,128]{1,0:T(8,128)S(1)}, f32[104,128]{1,0:T(8,128)S(1)}, u32[]{:S(2)}, u32[]{:S(2)}) collective-permute-start(f32[104,128]{1,0:T(8,128)S(1)} %add.6.a), channel_id=1, source_target_pairs={{0,3},{1,2},{2,1},{3,0},{4,7},{5,6},{6,5},{7,4},{8,11},{9,10},{10,... | collective-permute-start | bytes 159752 | tf_op jit(solution)/shard_map/ppermute | solution.py:370
  74.8 5.3 %collective-permute-start.28 = (f32[96,128]{1,0:T(8,128)S(1)}, f32[96,128]{1,0:T(8,128)S(1)}, u32[]{:S(2)}, u32[]{:S(2)}) collective-permute-start(f32[96,128]{1,0:T(8,128)S(1)} %get-tuple-element.61.z0), channel_id=1, source_target_pairs={{0,97},{1,96},{32,65},{33,64},{64,33},{65,32},{96,1},{97,0},{2,99}... | collective-permute-start | bytes 147464 | tf_op jit(solution)/shard_map/ppermute | solution.py:370
  76.3 5.0 %collective-permute-start.27 = (f32[96,128]{1,0:T(8,128)S(1)}, f32[96,128]{1,0:T(8,128)S(1)}, u32[]{:S(2)}, u32[]{:S(2)}) collective-permute-start(f32[96,128]{1,0:T(8,128)S(1)} %get-tuple-element.61.z0), channel_id=1, source_target_pairs={{0,64},{1,65},{32,96},{33,97},{64,0},{65,1},{96,32},{97,33},{2,66}... | collective-permute-start | bytes 147464 | tf_op jit(solution)/shard_map/ppermute | solution.py:370
  76.8 5.6 %collective-permute-start.26 = (f32[96,128]{1,0:T(8,128)S(1)}, f32[96,128]{1,0:T(8,128)S(1)}, u32[]{:S(2)}, u32[]{:S(2)}) collective-permute-start(f32[96,128]{1,0:T(8,128)S(1)} %get-tuple-element.61.z0), channel_id=1, source_target_pairs={{0,33},{1,32},{32,1},{33,0},{64,97},{65,96},{96,65},{97,64},{2,35}... | collective-permute-start | bytes 147464 | tf_op jit(solution)/shard_map/ppermute | solution.py:370
  82.5 6.2 %collective-permute-start.31 = (f32[96,128]{1,0:T(8,128)S(1)}, f32[96,128]{1,0:T(8,128)S(1)}, u32[]{:S(2)}, u32[]{:S(2)}) collective-permute-start(f32[96,128]{1,0:T(8,128)S(1)} %normal.3.refs_0_.q0), channel_id=1, source_target_pairs={{0,25},{1,24},{8,17},{9,16},{16,9},{17,8},{24,1},{25,0},{2,27},{3,... | collective-permute-start | bytes 147464 | tf_op jit(solution)/shard_map/ppermute | solution.py:370
  83.4 6.6 %collective-permute-start.30 = (f32[96,128]{1,0:T(8,128)S(1)}, f32[96,128]{1,0:T(8,128)S(1)}, u32[]{:S(2)}, u32[]{:S(2)}) collective-permute-start(f32[96,128]{1,0:T(8,128)S(1)} %normal.3.refs_0_.q0), channel_id=1, source_target_pairs={{0,16},{1,17},{8,24},{9,25},{16,0},{17,1},{24,8},{25,9},{2,18},{3,... | collective-permute-start | bytes 147464 | tf_op jit(solution)/shard_map/ppermute | solution.py:370
  84.0 6.1 %collective-permute-start.29 = (f32[96,128]{1,0:T(8,128)S(1)}, f32[96,128]{1,0:T(8,128)S(1)}, u32[]{:S(2)}, u32[]{:S(2)}) collective-permute-start(f32[96,128]{1,0:T(8,128)S(1)} %normal.3.refs_0_.q0), channel_id=1, source_target_pairs={{0,9},{1,8},{8,1},{9,0},{16,25},{17,24},{24,17},{25,16},{2,11},{3,... | collective-permute-start | bytes 147464 | tf_op jit(solution)/shard_map/ppermute | solution.py:370
  90.0 1.9 %collective-permute-start.32 = (f32[408,128]{1,0:T(8,128)S(1)}, f32[408,128]{1,0:T(8,128)S(1)}, u32[]{:S(2)}, u32[]{:S(2)}) collective-permute-start(f32[408,128]{1,0:T(8,128)S(1)} %join.1), channel_id=1, source_target_pairs={{0,1},{1,0},{2,3},{3,2},{4,5},{5,4},{6,7},{7,6},{8,9},{9,8},{10,11... | collective-permute-start | bytes 626696 | tf_op jit(solution)/shard_map/ppermute | solution.py:366
